TPU v7x, 32 devices: a whole 2x2x4 slice. The times are simulated.
32 devices in a mesh: tm: 8 (over y, x, core), freq: 4 (over z).
Axes of the slice: x: 2, y: 2, z: 4, core: 2. Of those that a mesh axis runs over, the one named last changes fastest.
Arguments:
- increments: float32 [1024, 4, 128], P('tm'), may hold values from -6 to 6
- projections: float32 [128, 3, 4096], P(None, None, 'freq'), may hold values from -0.5 to 0.5
- phases: float32 [3, 4096], P(None, 'freq'), may hold values from -3.140625 to 3.140625
- groups: int32 [4], replicated, may hold values from 0 to 1, as said below
Outputs:
- grad_increments: float32 [1024, 4, 128], P(('tm', 'freq'))
- grad_projections: float32 [128, 3, 4096], P('tm', None, 'freq')
Inputs may be any that keep to these rules, and one draw needn't show every extreme that they name: `groups`: exactly 2 sequences have 1.
All inputs are finite; a program needn't handle non-finite values.
Results may differ from a plain program's by a relative error of at most 0.0003.
Values sent between devices are 32-bit elements; how exact they have to be, the bound alone decides.
No kernel may reach another device: no remote copies, remote signals or barrier semaphores. Data moves between devices by JAX's collectives and lax.ppermute only.
A program may use at most 64 MiB of HBM per device.

v0:
```python
import math

import jax
import jax.numpy as jnp
from jax import lax
from jax.sharding import PartitionSpec as P

highest = lax.Precision.HIGHEST


def prefix(part, axis, combine, identity, reverse):
    count = lax.axis_size(axis)
    place = lax.axis_index(axis)
    ahead = count - 1 - place if reverse else place
    gathered = lax.all_gather(part, axis)
    state = jnp.zeros_like(part) + jnp.asarray(identity, part.dtype)

    def one(step, state):
        source = count - 1 - step if reverse else step
        return combine(state, lax.dynamic_index_in_dim(gathered, source, 0, False))

    return lax.fori_loop(0, ahead, one, state)


def add_terms(early, late):
    return early + late


def carry_forward(values):
    return prefix(values, "tm", add_terms, jnp.zeros_like(values), False)


def carry_backward(values):
    return prefix(values, "tm", add_terms, jnp.zeros_like(values), True)


def global_gaps(totals, set_weight):
    stacked = jnp.stack([jnp.sum(set_weight * total, axis=0) for total in totals], axis=0)
    return lax.psum(stacked, "tm")


def tiled_sum(values, forward):
    steps, batch, width = values.shape
    tile = min(128, steps)
    count = steps // tile
    row_ids = lax.broadcasted_iota(jnp.int32, (tile, tile), 0)
    col_ids = lax.broadcasted_iota(jnp.int32, (tile, tile), 1)
    if forward:
        tri_mask = (col_ids < row_ids).astype(jnp.float32)
    else:
        tri_mask = (col_ids > row_ids).astype(jnp.float32)
    blocks = values.reshape(count, tile, batch, width)
    inner = jnp.einsum("ts,nsbf->ntbf", tri_mask, blocks, precision=highest)
    block_sums = jnp.sum(blocks, axis=1)
    running = jnp.cumsum(block_sums, axis=0)
    if forward:
        outer = running - block_sums
    else:
        outer = running - running
    return (inner + outer[:, None]).reshape(steps, batch, width)


def on_device(increments, projections, phases, groups):
    steps, batch, chans = increments.shape
    length = steps * lax.axis_size("tm")
    amplitude = math.sqrt(2.0 / length)
    set_weight = jnp.where(groups == 1, 2.0 / batch, -2.0 / batch).astype(jnp.float32)[:, None]

    def before(values):
        return tiled_sum(values, True)

    def after(values):
        return tiled_sum(values, False)

    angles = [
        jnp.einsum("tbc,cf->tbf", increments, projections[:, degree, :], precision=highest)
        + phases[degree][None, None, :]
        for degree in range(3)
    ]
    waves = [amplitude * jnp.cos(angle) for angle in angles]
    entry1 = carry_forward(jnp.sum(waves[0], axis=0))
    front1 = entry1[None] + before(waves[0])
    term2 = front1 * waves[1]
    entry2 = carry_forward(jnp.sum(term2, axis=0))
    front2 = entry2[None] + before(term2)
    totals = (jnp.sum(waves[0], axis=0), jnp.sum(term2, axis=0), jnp.sum(front2 * waves[2], axis=0))
    gaps = global_gaps(totals, set_weight)
    seeds = [2.0 * set_weight * gaps[degree][None, :] for degree in range(3)]
    tail3 = carry_backward(jnp.sum(waves[2], axis=0))
    adjoint1 = seeds[1][None] + seeds[2][None] * (tail3[None] + after(waves[2]))
    product = adjoint1 * waves[1]
    tail2 = carry_backward(jnp.sum(product, axis=0))
    adjoint0 = seeds[0][None] + tail2[None] + after(product)
    directions = [adjoint0, adjoint1 * front1, seeds[2][None] * front2]
    slopes = [-amplitude * jnp.sin(angles[degree]) * directions[degree] for degree in range(3)]
    piece = increments
    grad_projections = lax.psum_scatter(
        jnp.stack(
            [jnp.einsum("tbc,tbf->cf", piece, slope, precision=highest) for slope in slopes], axis=1
        ),
        "tm",
        scatter_dimension=0,
        tiled=True,
    )
    result = jnp.zeros(
        (lax.axis_size("freq") * (steps // lax.axis_size("freq")), batch, chans), jnp.float32
    )
    for degree in range(3):
        piece = slopes[degree]
        result = result + jnp.einsum(
            "tbf,cf->tbc", piece, projections[:, degree, :], precision=highest
        )
    grad_increments = lax.psum_scatter(result, "freq", scatter_dimension=0, tiled=True)
    return (grad_increments, grad_projections)


def solution(mesh):
    placed = (P("tm", None, None), P(None, None, "freq"), P(None, "freq"), P())
    return jax.shard_map(
        on_device,
        mesh=mesh,
        in_specs=placed,
        out_specs=(P(("tm", "freq"), None, None), P("tm", None, "freq")),
        check_vma=False,
    )
```

profile of v0, /device:TPU:0, one launch (start us, length us, event | category | flops | bytes accessed | tf_op | source)
XLA Modules:
  0.0 279.2 jit_solution(2539248831738838316)
XLA Ops:
  8.9 2.9 %fusion.15 = f32[128,4,1024]{2,0,1:T(8,128)S(1)} fusion(f32[128,3,1024]{2,0,1:T(8,128)} %param.13, f32[128,4,128]{2,1,0:T(4,128)} %param.12), kind=kOutput, calls=%fused_computation.38 | convolution fusion | flops 805306368 | bytes 2883584 | tf_op jit(solution)/shard_map/tbc,cf->tbf/dot_general | solution.py:76
  11.8 10.0 %fusion.5 = (f32[4,1024]{1,0:T(4,128)S(1)}, f32[128,4,1024]{2,0,1:T(8,128)S(1)}) fusion(f32[1024]{0:T(1024)S(1)} %bitcast.166, f32[128,3,1024]{2,0,1:T(8,128)} %param.13, f32[128,4,128]{2,1,0:T(4,128)S(1)} %copy-done.6), kind=kOutput, calls=%fused_computation.23 | convolution fusion | flops 806875136 | bytes 2904064 | tf_op jit(solution)/shard_map/tbc,cf->tbf/dot_general | solution.py:76
  21.9 1.3 copy-done
  23.2 9.9 %fusion.4 = f32[4,1024,128]{1,2,0:T(8,128)} fusion(f32[128,4,1024]{2,0,1:T(8,128)S(1)} %get-tuple-element.218, f32[1024]{0:T(1024)S(1)} %bitcast.167), kind=kOutput, calls=%fused_computation.22 | convolution fusion | flops 806371328 | bytes 4198400 | tf_op jit(solution)/shard_map/ts,nsbf->ntbf/dot_general | solution.py:53
  33.1 10.7 %all-gather.4 = f32[8,4,1024]{2,1,0:T(4,128)S(1)} all-gather(f32[1,4,1024]{2,1,0:T(4,128)S(1)} %bitcast.154), channel_id=2, replica_groups=mesh['tm'=8,'freq'=4] {'tm'}, dimensions={0}, use_global_device_ids=true | all-gather | bytes 147456 | tf_op jit(solution)/shard_map/all_gather | solution.py:15
  43.8 11.1 %fusion.32 = (f32[4,1024]{1,0:T(4,128)S(1)}, f32[128,4,1024]{2,0,1:T(8,128)}) fusion(f32[1024]{0:T(1024)S(1)} %bitcast.158, f32[4,1024]{1,0:T(4,128)S(1)} %sub.52, f32[4,1024,128]{1,2,0:T(8,128)} %fusion.4, f32[4,1024]{1,0:T(4,128)S(1)} %get-tuple-element.160, f32[128,3,1024]{2,0,1:T(8,128)} %param.13, f32[128,4,128]{2,1,0:T(4,128)S(1)} %copy-done.6), kind=kOutput, calls=%fused_computation.54 | convolution fusion | flops 808448000 | bytes 5033984 | tf_op jit(solution)/shard_map/tbc,cf->tbf/dot_general | solution.py:76
  54.9 9.3 %all-gather.5 = f32[8,4,1024]{2,1,0:T(4,128)S(1)} all-gather(f32[1,4,1024]{2,1,0:T(4,128)S(1)} %bitcast.155), channel_id=3, replica_groups=mesh['tm'=8,'freq'=4] {'tm'}, dimensions={0}, use_global_device_ids=true | all-gather | bytes 147456 | tf_op jit(solution)/shard_map/all_gather | solution.py:15
  64.2 17.5 %multiply_reduce_fusion = (f32[4,1024]{1,0:T(4,128)S(1)}, f32[4,1024]{1,0:T(4,128)S(1)}, f32[4,1024,128]{1,2,0:T(8,128)}) fusion(f32[128,4,1024]{2,0,1:T(8,128)S(1)} %fusion.15, f32[1024]{0:T(1024)S(1)} %bitcast.162, f32[4,1024]{1,0:T(4,128)S(1)} %sub.53, f32[4,1024]{1,0:T(4,128)S(1)} %get-tuple-element.161, f32[4,1024,128]{1,2,0:T(8,128)} %fusion.4, ...), kind=kOutput, calls=%fused_computation.17 | convolution fusion | flops 811606016 | bytes 8495104 | tf_op jit(solution)/shard_map/ts,nsbf->ntbf/dot_general | solution.py:53
  81.8 8.5 %all-gather.6 = f32[8,4,1024]{2,1,0:T(4,128)S(1)} all-gather(f32[1,4,1024]{2,1,0:T(4,128)S(1)} %bitcast.157), channel_id=4, replica_groups=mesh['tm'=8,'freq'=4] {'tm'}, dimensions={0}, use_global_device_ids=true | all-gather | bytes 147456 | tf_op jit(solution)/shard_map/all_gather | solution.py:15
  90.3 13.0 %while.46 = (s32[]{:T(128)}, f32[4,1024]{1,0:T(4,128)S(1)}, s32[]{:T(128)}, f32[8,4,1024]{2,1,0:T(4,128)S(1)}, s32[]{:T(128)}, /*index=5*/s32[]{:T(128)}, s32[]{:T(128)}, s32[]{:T(128)}) while((s32[]{:T(128)}, f32[4,1024]{1,0:T(4,128)S(1)}, s32[]{:T(128)}, f32[8,4,1024]{2,1,0:T(4,128)S(1)}, s32[]{:T(128)}, /*index=5*/s32[]{:T(128)}, ...), condition=%wide.region_13.14_spmd, body=%wide.region_12.13_spmd.sunk | while | flops 4102 | bytes 49295 | solution.py:22
  103.4 23.3 %psum.7 = f32[3,1024]{1,0:T(4,128)S(1)} all-reduce(f32[3,1024]{1,0:T(4,128)S(1)} %pad_maximum_fusion.1), channel_id=1, replica_groups=mesh['tm'=8,'freq'=4] {'tm'}, use_global_device_ids=true, to_apply=%region_10.11 | all-reduce | flops 3072 | bytes 24576 | tf_op jit(solution)/shard_map/psum | solution.py:39
  126.8 19.4 %multiply_multiply_fusion.1 = (f32[128,4,1024]{2,0,1:T(8,128)}, f32[4,1024]{1,0:T(4,128)S(1)}, f32[128,4,1024]{2,0,1:T(8,128)}) fusion(f32[128,4,1024]{2,0,1:T(8,128)} %get-tuple-element.220, f32[4,1024,128]{1,2,0:T(8,128)} %fusion.4, f32[1024]{0:T(1024)S(1)} %bitcast.160, f32[4,1024]{1,0:T(4,128)S(1)} %sub.52, f32[4,1024]{1,0:T(4,128)S(1)} %get-tuple-element.160, ...), kind=kOutput, calls=%fused_computation.16 | convolution fusion | flops 813182976 | bytes 10608640 | tf_op jit(solution)/shard_map/ts,nsbf->ntbf/dot_general | solution.py:53
  146.2 9.4 %all-gather.7 = f32[8,4,1024]{2,1,0:T(4,128)S(1)} all-gather(f32[1,4,1024]{2,1,0:T(4,128)S(1)} %bitcast.156), channel_id=5, replica_groups=mesh['tm'=8,'freq'=4] {'tm'}, dimensions={0}, use_global_device_ids=true | all-gather | bytes 147456 | tf_op jit(solution)/shard_map/all_gather | solution.py:15
  156.0 16.6 %fusion = f32[128,4,1024]{2,0,1:T(8,128)S(1)} fusion(f32[128,4,1024]{2,0,1:T(8,128)} %copy-done, f32[4,1024]{1,0:T(4,128)S(1)} %sub.56, f32[4,1024]{1,0:T(4,128)S(1)} %multiply_add_fusion, f32[1024]{0:T(1024)S(1)} %bitcast.168, f32[128,4,1024]{2,0,1:T(8,128)} %get-tuple-element.222, f32[128,4,1024]{2,0,1:T(8,128)} %get-tuple-element.220, f32[1024]{0:T(1024)S(1)} %bitcast.161), kind=kOutput, calls=%fused_computation.5 | convolution fusion | flops 809517056 | bytes 8429568 | tf_op jit(solution)/shard_map/ts,nsbf->ntbf/dot_general | solution.py:53
  172.5 1.3 copy-done.3
  173.9 1.8 fusion.20
  175.7 1.8 convolution_add_fusion.1
  177.5 9.8 %convolution_add_fusion = f32[128,4,128]{2,0,1:T(8,128)} fusion(f32[128,4,128]{2,0,1:T(8,128)S(1)} %convolution_add_fusion.1, f32[128,3,1024]{2,0,1:T(8,128)S(1)} %copy-done.7, f32[128,4,1024]{2,0,1:T(8,128)S(1)} %fusion.15, f32[4,1024,128]{1,2,0:T(8,128)S(1)} %copy-done.1, f32[4,1024]{1,0:T(4,128)S(1)} %get-tuple-element.214, f32[1024]{0:T(1024)S(1)} %bitcast.164, ...), kind=kOutput, calls=%fused_computation.30 | convolution fusion | flops 808517632 | bytes 5296128 | tf_op jit(solution)/shard_map/tbf,cf->tbc/dot_general | solution.py:110
  187.4 5.2 %convolution_bitcast_fusion.1 = f32[128,1,1024]{0,2,1:T(8,128)S(1)} fusion(f32[128,4,1024]{2,0,1:T(8,128)} %get-tuple-element.205, f32[128,4,128]{2,1,0:T(4,128)S(1)} %copy-done.6), kind=kOutput, calls=%fused_computation.28 | convolution fusion | flops 805306368 | bytes 2883584 | tf_op jit(solution)/shard_map/tbc,tbf->cf/dot_general | solution.py:99
  192.6 3.4 %convolution_bitcast_fusion.2 = f32[128,1,1024]{0,2,1:T(8,128)S(1)} fusion(f32[128,4,1024]{2,0,1:T(8,128)S(1)} %copy-done.4, f32[128,4,128]{2,1,0:T(4,128)S(1)} %copy-done.6), kind=kOutput, calls=%fused_computation.29 | convolution fusion | flops 805306368 | bytes 2883584 | tf_op jit(solution)/shard_map/tbc,tbf->cf/dot_general | solution.py:99
  196.1 10.4 %convolution_bitcast_fusion = f32[128,1,1024]{0,2,1:T(8,128)S(1)} fusion(f32[128,4,128]{2,1,0:T(4,128)S(1)} %copy-done.6, f32[128,4,1024]{2,0,1:T(8,128)S(1)} %fusion.15, f32[4,1024,128]{1,2,0:T(8,128)S(1)} %copy-done.2, f32[4,1024]{1,0:T(4,128)S(1)} %get-tuple-element.214, f32[1024]{0:T(1024)S(1)} %bitcast.165, f32[4,1024]{1,0:T(4,128)S(1)} %sub.53, ...), kind=kOutput, calls=%fused_computation.27 | convolution fusion | flops 808452096 | bytes 5033984 | tf_op jit(solution)/shard_map/tbc,tbf->cf/dot_general | solution.py:99
  206.6 1.9 copy.30
  209.8 1.5 copy.31
  211.3 58.5 %all-reduce.3.cloned.1.call-done = f32[128,3,1024]{2,1,0:T(4,128)} async-done(((f32[128,3,1024]{2,1,0:T(4,128)}), f32[128,3,1024]{2,1,0:T(4,128)}) %all-reduce.3.cloned.1.call-update) | async-done | bytes 1572880
  (59 shorter events, 4.3 us)
Async XLA Ops:
  8.0 3.8 %copy-start.6 = (f32[128,4,128]{2,1,0:T(4,128)S(1)}, f32[128,4,128]{2,1,0:T(4,128)}, u32[]{:S(2)}) copy-start(f32[128,4,128]{2,1,0:T(4,128)} %param.12) | copy-start | bytes 786436
  8.0 201.8 %reduce-scatter.2.cloned.1.call-start = ((), (), s32[]{:S(2)}) async-start(), calls=%async_computation.1 | async-start | bytes 327680 | tf_op jit(solution)/shard_map/reduce_scatter | solution.py:113
  21.9 1.3 copy-start
  64.2 39.0 %copy-start.8 = (s32[4]{0:T(128)S(1)}, s32[4]{0:T(128)}, u32[]{:S(2)}) copy-start(s32[4]{0:T(128)} %param.15) | copy-start | bytes 52
  156.0 17.9 %copy-start.7 = (f32[128,3,1024]{2,0,1:T(8,128)S(1)}, f32[128,3,1024]{2,0,1:T(8,128)}, u32[]{:S(2)}) copy-start(f32[128,3,1024]{2,0,1:T(8,128)} %param.13) | copy-start | bytes 4718596
  172.5 1.3 copy-start.3
  173.9 1.8 copy-start.5
  175.7 1.8 copy-start.1
  187.4 82.4 %all-reduce.3.cloned.1.call-start = ((), (), s32[]{:S(2)}) async-start(), calls=%async_computation.2 | async-start | bytes 4194304
  187.4 5.2 %copy-start.4 = (f32[128,4,1024]{2,0,1:T(8,128)S(1)}, f32[128,4,1024]{2,0,1:T(8,128)}, u32[]{:S(2)}) copy-start(f32[128,4,1024]{2,0,1:T(8,128)} %copy-done.3) | copy-start | bytes 6291460
  192.6 3.4 %copy-start.2 = (f32[4,1024,128]{1,2,0:T(8,128)S(1)}, f32[4,1024,128]{1,2,0:T(8,128)}, u32[]{:S(2)}) copy-start(f32[4,1024,128]{1,2,0:T(8,128)} %get-tuple-element.221) | copy-start | bytes 6291460
  206.6 2.0 copy-start.9
Sparse Core Ops, SparseCore 0:
  187.5 19.6 reduce-scatter.1
Sparse Core Ops, SparseCore 1:
  208.6 61.1 all-reduce.2
where the time goes:
time: 282 us; the launch traced here: 279 us
  matrix products  120 us (43%)
  blocking collectives  61.2 us (22%)
  waiting for transfers between devices  58.5 us (21%)
  between operations  16.6 us (6%)
  loops' own time  13 us (5%)
  local copies, waits for them, and re-layouts  9.34 us (3%)
    dot_general x4, matrix products, tiled_sum(): inner = jnp.einsum('ts,nsbf->ntbf', tri_mask, blocks, precision=highest)  63.4 us
    unnamed x3, waiting for transfers between devices  58.5 us
    all_gather x4, blocking collectives, prefix(): gathered = lax.all_gather(part, axis)  37.8 us
    dot_general x3, matrix products, on_device(): jnp.einsum('tbc,cf->tbf', increments, projections[:, degree, :], precisio...  24.1 us
    psum x1, blocking collectives, global_gaps(): return lax.psum(stacked, 'tm')  23.3 us
    dot_general x3, matrix products, on_device(): jnp.einsum('tbc,tbf->cf', piece, slope, precision=highest)  19 us
    dot_general x3, matrix products, on_device(): jnp.einsum('tbf,cf->tbc', piece, projections[:, degree, :], precision=hig...  13.4 us
    another operation x4, loops' own time, prefix(): return lax.fori_loop(0, ahead, one, state)  13 us
  transfers between devices with their start and end apart: 2, of which 1 were waited for; matrix products, arithmetic and copies ran while one was open for 8% of the time, Pallas kernels for 0%

commit v1 on v0

v1 whole, which is shorter than its diff:
```python
import math

import jax
import jax.numpy as jnp
from jax import lax
from jax.experimental import pallas as pl
from jax.experimental.pallas import tpu as pltpu
from jax.sharding import PartitionSpec as P

f32, bf16 = jnp.float32, jnp.bfloat16
SUB = 8
WIDE = 256
MAGIC = 12582912.0
SIN = (3.141582022150658, -5.167142796368909, 2.541899027590427, -0.5546361970970186)
COS = (
    0.9999999534666683,
    -4.934792858675264,
    4.058411914167107,
    -1.3318801612488937,
    0.2196967986036905,
)
NT = (((1,), (1,)), ((), ()))


def horner(z, coefs):
    acc = z * coefs[-1] + coefs[-2]
    for coef in coefs[-3::-1]:
        acc = acc * z + coef
    return acc


def split(value):
    high = value.astype(bf16)
    return high, (value - high.astype(f32)).astype(bf16)


def pair_rows(low, high):
    top = lax.broadcasted_iota(jnp.int32, low.shape, 0) < SUB // 2
    first = jnp.where(top, low, pltpu.roll(high, SUB // 2, 0))
    second = jnp.where(top, pltpu.roll(low, SUB // 2, 0), high)
    return first, second


def waves_kernel(amplitude, x_ref, p_ref, ph_ref, c_ref, s_ref, loc_ref, snd_ref, xs_ref, ang_ref):
    rows, chans = x_ref.shape
    half = rows // 2
    wide = p_ref.shape[2]
    inv = 1.0 / (2.0 * math.pi)
    root = math.sqrt(2.0 * amplitude)
    sin_coefs = [root * coef for coef in SIN]
    cos_coefs = [-root * coef for coef in COS]

    @pl.when(pl.program_id(0) == 0)
    def _():
        def one(k, _):
            at = pl.multiple_of(k * SUB, SUB)
            first, second = pair_rows(x_ref[pl.ds(at, SUB), :], x_ref[pl.ds(half + at, SUB), :])
            high, low = split(jnp.concatenate([first, second], axis=0))
            to = pl.ds(pl.multiple_of(k * 2 * SUB, 2 * SUB), 2 * SUB)
            xs_ref[to, :] = jnp.concatenate([high, low, high, low], axis=1)
            return 0

        lax.fori_loop(0, half // SUB, one, 0, unroll=4)

    for level in range(3):
        high, low = split(p_ref[level] * inv)
        stacked = jnp.concatenate([high, high, low, low], axis=0)
        turns = jnp.dot(xs_ref[...], stacked, preferred_element_type=f32)
        ang_ref[level] = turns + ph_ref[level : level + 1, :] * inv

    zero = jnp.zeros((SUB, wide), f32)

    def step(i, carry):
        s0, s1, s2, s01, s12, s012 = carry
        at = pl.ds(pl.multiple_of(i * SUB, SUB), SUB)
        cosines = []
        for level in range(3):
            turn = ang_ref[level, at, :]
            r = turn - ((turn + MAGIC) - MAGIC)
            z = r * r
            sine = r * horner(z, sin_coefs)
            cosine = horner(z, cos_coefs)
            wave = amplitude - sine * sine
            c_ref[0, level, at, :] = wave
            s_ref[0, level, at, :] = sine * cosine
            cosines.append(wave)
        c0, c1, c2 = cosines
        s012 = s012 + s01 * c2
        s12 = s12 + s1 * c2
        s01 = s01 + s0 * c1
        return (s0 + c0, s1 + c1, s2 + c2, s01, s12, s012)

    sums = lax.fori_loop(0, rows // SUB, step, (zero,) * 6, unroll=4)
    for k in range(6):
        loc_ref[SUB * k : SUB * (k + 1), :] = sums[k]
    hb = SUB // 2
    a0, a1, a2, a01, a12, a012 = [v[:hb] for v in sums]
    b0, b1, b2, b01, b12, b012 = [v[hb:] for v in sums]
    both = (
        a0 + b0,
        a1 + b1,
        a2 + b2,
        a01 + b01 + a0 * b1,
        a12 + b12 + a1 * b2,
        a012 + b012 + a0 * b12 + a01 * b2,
    )
    for k in range(6):
        snd_ref[hb * k : hb * (k + 1), :] = both[k]


def grads_kernel(sizes, place_ref, groups_ref, *refs):
    n_tm, n_freq, batch = sizes
    x_ref, p_ref, c_ref, s_ref, loc_ref = refs[:5]
    got = refs[5 : 5 + n_tm]
    gk_ref, gs_ref, gi_ref = refs[5 + n_tm : 8 + n_tm]
    xt_ref, all_ref, u1_ref, sh_ref, sl_ref, w_ref, gp_ref, acc_ref, flat_ref = refs[8 + n_tm :]
    rows, chans = x_ref.shape
    half = rows // 2
    wide = p_ref.shape[2]
    hb = SUB // 2
    me, z = place_ref[0], place_ref[1]
    chunk = pl.program_id(0)

    @pl.when(chunk == 0)
    def _():
        def one(k, _):
            at = pl.multiple_of(k * SUB, SUB)
            first, second = pair_rows(x_ref[pl.ds(at, SUB), :], x_ref[pl.ds(half + at, SUB), :])
            to = pl.multiple_of(k * 2 * SUB, 2 * SUB)
            flat_ref[pl.ds(to, SUB), :] = first
            flat_ref[pl.ds(to + SUB, SUB), :] = second
            return 0

        lax.fori_loop(0, half // SUB, one, 0, unroll=4)
        high, low = split(flat_ref[...].T)
        xt_ref[:chans, :] = high
        xt_ref[chans:, :] = low
        acc_ref[...] = jnp.zeros_like(acc_ref)

    for d in range(n_tm):
        all_ref[jnp.bitwise_xor(me, d)] = got[d][...]

    def sums_of(j):
        return [all_ref[j, hb * k : hb * (k + 1), :] for k in range(6)]

    def forward(j, carry):
        p0, p01, p012 = carry
        b0, b1, b2, b01, b12, b012 = sums_of(j)
        p012 = p012 + b012 + p0 * b12 + p01 * b2
        p01 = p01 + b01 + p0 * b1
        return (p0 + b0, p01, p012)

    def backward(step, carry):
        t1, t2, t12 = carry
        b0, b1, b2, b01, b12, b012 = sums_of(n_tm - 1 - step)
        t12 = t12 + b12 + b1 * t2
        return (t1 + b1, t2 + b2, t12)

    zero = jnp.zeros((hb, wide), f32)
    entry = lax.fori_loop(0, me, forward, (zero,) * 3)
    e1, e2 = entry[:2]
    totals = lax.fori_loop(me, n_tm, forward, entry)
    t1, t2, t12 = lax.fori_loop(0, n_tm - 1 - me, backward, (zero,) * 3)

    row = lax.broadcasted_iota(jnp.int32, (hb, wide), 0)
    weight = zero
    for b in range(batch):
        value = jnp.where(groups_ref[b] == 1, 2.0 / batch, -2.0 / batch)
        weight = jnp.where(row == b, value, weight)
    seeds = [2.0 * weight * jnp.sum(weight * total, axis=0, keepdims=True) for total in totals]

    def local(k):
        return loc_ref[SUB * k : SUB * k + hb, :], loc_ref[SUB * k + hb : SUB * (k + 1), :]

    a0, _ = local(0)
    a1, b1 = local(1)
    _, b2 = local(2)
    a01, _ = local(3)
    _, b12 = local(4)

    def tall(first, second):
        return jnp.concatenate([first, second], axis=0)

    front1 = tall(e1, e1 + a0)
    front2 = tall(e2, e2 + a01 + e1 * a1)
    tail2 = tall(t2 + b2, t2)
    tail1 = tall(t1 + b1, t1)
    tail12 = tall(t12 + b12 + b1 * t2, t12)
    d0, d1, d2 = [tall(seed, seed) for seed in seeds]
    adjoint1 = d1 + d2 * tail2
    adjoint0 = d0 + d1 * tail1 + d2 * tail12

    def fwd(pair, carry):
        f1, f2 = carry
        slopes = []
        for which in range(2):
            at = pl.ds(pl.multiple_of((2 * pair + which) * SUB, SUB), SUB)
            u1_ref[at, :] = s_ref[0, 1, at, :] * f1
            slopes.append(s_ref[0, 2, at, :] * (d2 * f2))
            f2 = f2 + f1 * c_ref[0, 1, at, :]
            f1 = f1 + c_ref[0, 0, at, :]
        at = pl.ds(pl.multiple_of(pair * 2 * SUB, 2 * SUB), 2 * SUB)
        high, low = split(jnp.concatenate(slopes, axis=0))
        sh_ref[at, 2 * wide :] = high
        sl_ref[at, 2 * wide :] = low
        return f1, f2

    lax.fori_loop(0, rows // (2 * SUB), fwd, (front1, front2), unroll=2)

    def bwd(step, carry):
        g1, g0 = carry
        pair = rows // (2 * SUB) - 1 - step
        slope0, slope1 = [], []
        for which in (1, 0):
            at = pl.ds(pl.multiple_of((2 * pair + which) * SUB, SUB), SUB)
            slope1.append(u1_ref[at, :] * g1)
            slope0.append(s_ref[0, 0, at, :] * g0)
            g0 = g0 + g1 * c_ref[0, 1, at, :]
            g1 = g1 + d2 * c_ref[0, 2, at, :]
        at = pl.ds(pl.multiple_of(pair * 2 * SUB, 2 * SUB), 2 * SUB)
        for level, slopes in enumerate((slope0, slope1)):
            high, low = split(jnp.concatenate(slopes[::-1], axis=0))
            sh_ref[at, level * wide : (level + 1) * wide] = high
            sl_ref[at, level * wide : (level + 1) * wide] = low
        return g1, g0

    lax.fori_loop(0, rows // (2 * SUB), bwd, (adjoint1, adjoint0), unroll=2)

    each = chans // n_tm
    for level in range(3):
        cols = slice(level * wide, (level + 1) * wide)
        high, low = split(p_ref[level])
        w_ref[:chans, cols] = high
        w_ref[chans:, cols] = low
        main = jnp.dot(xt_ref[...], sh_ref[:, cols], preferred_element_type=f32)
        rest = jnp.dot(xt_ref[:chans, :], sl_ref[:, cols], preferred_element_type=f32)
        grad = main[:chans] + main[chans:] + rest
        for d in range(n_tm):
            gp_ref[d] = grad[each * d : each * (d + 1)]
        for j in range(n_tm // 2):
            keep = jnp.bitwise_xor(me, 2 * j)
            gk_ref[j, level] = gp_ref[keep]
            gs_ref[j, level] = gp_ref[jnp.bitwise_xor(keep, 1)]

    main = lax.dot_general(sh_ref[...], w_ref[...], NT, preferred_element_type=f32)
    rest = lax.dot_general(sl_ref[...], w_ref[:chans, :], NT, preferred_element_type=f32)
    acc_ref[...] += main[:, :chans] + main[:, chans:] + rest

    @pl.when(chunk == pl.num_programs(0) - 1)
    def _():
        def one(k, _):
            at = pl.multiple_of(k * SUB, SUB)
            to = pl.multiple_of(k * 2 * SUB, 2 * SUB)
            low, high = pair_rows(acc_ref[pl.ds(to, SUB), :], acc_ref[pl.ds(to + SUB, SUB), :])
            flat_ref[pl.ds(at, SUB), :] = low
            flat_ref[pl.ds(half + at, SUB), :] = high
            return 0

        lax.fori_loop(0, half // SUB, one, 0, unroll=4)
        piece = rows // n_freq
        for j in range(n_freq):
            at = pl.multiple_of(jnp.bitwise_xor(z, j) * piece, piece)
            gi_ref[j] = flat_ref[pl.ds(at, piece), :]


def swap(value, axis, distance):
    count = lax.axis_size(axis)
    return lax.ppermute(value, axis, [(i, i ^ distance) for i in range(count)])


def on_device(increments, projections, phases, groups):
    steps, batch, chans = increments.shape
    freqs = phases.shape[1]
    n_tm, n_freq = lax.axis_size("tm"), lax.axis_size("freq")
    amplitude = math.sqrt(2.0 / (steps * n_tm))
    rows = steps * batch
    wide = min(WIDE, freqs)
    chunks = freqs // wide
    each = chans // n_tm
    x = increments.reshape(rows, chans)
    p = jnp.transpose(projections, (1, 0, 2))
    params = pltpu.CompilerParams(vmem_limit_bytes=48 * 1024 * 1024)

    def waves_body(*refs):
        waves_kernel(amplitude, *refs)

    tall = lambda n: pl.BlockSpec((n, wide), lambda i: (0, i))
    big = pl.BlockSpec((1, 3, rows, wide), lambda i: (i, 0, 0, 0))
    cosines, sines, local, own = pl.pallas_call(
        waves_body,
        grid=(chunks,),
        in_specs=[
            pl.BlockSpec((rows, chans), lambda i: (0, 0)),
            pl.BlockSpec((3, chans, wide), lambda i: (0, 0, i)),
            pl.BlockSpec((3, wide), lambda i: (0, i)),
        ],
        out_specs=[big, big, tall(6 * SUB), tall(3 * SUB)],
        out_shape=[
            jax.ShapeDtypeStruct((chunks, 3, rows, wide), f32),
            jax.ShapeDtypeStruct((chunks, 3, rows, wide), f32),
            jax.ShapeDtypeStruct((6 * SUB, freqs), f32),
            jax.ShapeDtypeStruct((3 * SUB, freqs), f32),
        ],
        scratch_shapes=[pltpu.VMEM((rows, 4 * chans), bf16), pltpu.VMEM((3, rows, wide), f32)],
        compiler_params=params,
        name="waves",
    )(x, p, phases)

    got = [own] + [swap(own, "tm", d) for d in range(1, n_tm)]
    place = jnp.stack([lax.axis_index("tm"), lax.axis_index("freq")]).astype(jnp.int32)

    def grads_body(*refs):
        grads_kernel((n_tm, n_freq, batch), *refs)

    fixed = lambda *shape: pl.BlockSpec(shape, lambda i, *_: (0,) * len(shape))
    tall = lambda n: pl.BlockSpec((n, wide), lambda i, *_: (0, i))
    big = pl.BlockSpec((1, 3, rows, wide), lambda i, *_: (i, 0, 0, 0))
    gspec = pl.BlockSpec((n_tm // 2, 3, each, wide), lambda i, *_: (0, 0, 0, i))
    gshape = jax.ShapeDtypeStruct((n_tm // 2, 3, each, freqs), f32)
    kept, sent, pieces = pl.pallas_call(
        grads_body,
        grid_spec=pltpu.PrefetchScalarGridSpec(
            num_scalar_prefetch=2,
            grid=(chunks,),
            in_specs=[
                fixed(rows, chans),
                pl.BlockSpec((3, chans, wide), lambda i, *_: (0, 0, i)),
                big,
                big,
                tall(6 * SUB),
            ]
            + [tall(3 * SUB)] * n_tm,
            out_specs=[gspec, gspec, fixed(n_freq, rows // n_freq, chans)],
            scratch_shapes=[
                pltpu.VMEM((2 * chans, rows), bf16),
                pltpu.VMEM((n_tm, 3 * SUB, wide), f32),
                pltpu.VMEM((rows, wide), f32),
                pltpu.VMEM((rows, 3 * wide), bf16),
                pltpu.VMEM((rows, 3 * wide), bf16),
                pltpu.VMEM((2 * chans, 3 * wide), bf16),
                pltpu.VMEM((n_tm, each, wide), f32),
                pltpu.VMEM((rows, chans), f32),
                pltpu.VMEM((rows, chans), f32),
            ],
        ),
        out_shape=[gshape, gshape, jax.ShapeDtypeStruct((n_freq, rows // n_freq, chans), f32)],
        compiler_params=params,
        name="grads",
    )(place, groups, x, p, cosines, sines, local, *got)

    mine = kept + swap(sent, "tm", 1)
    total = mine[0]
    for j in range(1, n_tm // 2):
        total = total + swap(mine[j], "tm", 2 * j)
    grad_projections = jnp.transpose(total, (1, 0, 2))
    result = pieces[0]
    for j in range(1, n_freq):
        result = result + swap(pieces[j], "freq", j)
    grad_increments = result.reshape(steps // n_freq, batch, chans)
    return (grad_increments, grad_projections)


def solution(mesh):
    placed = (P("tm", None, None), P(None, None, "freq"), P(None, "freq"), P())
    return jax.shard_map(
        on_device,
        mesh=mesh,
        in_specs=placed,
        out_specs=(P(("tm", "freq"), None, None), P("tm", None, "freq")),
        check_vma=False,
    )
```

time: 282 us -> 60 us (0.21)
  matrix products: 120 us -> 0 us
  blocking collectives: 61.2 us -> 0 us
  waiting for transfers between devices: 58.5 us -> 13.8 us
  Pallas kernels: 0 us -> 20.6 us
  starting transfers between devices: 0.08 us -> 16.9 us
  between operations: 16.6 us -> 0.68 us
  loops' own time: 13 us -> 0 us
  local copies, waits for them, and re-layouts: 9.34 us -> 6.14 us
    dot_general x13 -> x0, matrix products: 120 us -> none  [the longest x4 63.4 us: tiled_sum(): inner = jnp.einsum('ts,nsbf->ntbf', tri_mask, blocks, precision=highest)]
    unnamed x3 -> x0, waiting for transfers between devices: 58.5 us -> none
    all_gather x4 -> x0, blocking collectives: 37.8 us -> none  [prefix(): gathered = lax.all_gather(part, axis)]
    psum x1 -> x0, blocking collectives: 23.3 us -> none  [global_gaps(): return lax.psum(stacked, 'tm')]
    pallas_call x0 -> x2, Pallas kernels: none -> 20.6 us  [the longest x1 10.5 us: on_device(): pl.pallas_call(waves_body, grid=(chunks,), in_specs=[pl.BlockSpec((rows,...]
    ppermute x0 -> x14, starting transfers between devices: none -> 16.9 us  [swap(): return lax.ppermute(value, axis, [(i, i ^ distance) for i in range(count)])]
    ppermute x0 -> x14, waiting for transfers between devices: none -> 13.8 us  [swap(): return lax.ppermute(value, axis, [(i, i ^ distance) for i in range(count)])]
    another operation x4 -> x0, loops' own time: 13 us -> none  [prefix(): return lax.fori_loop(0, ahead, one, state)]
  transfers between devices with their start and end apart: 2 -> 14, of which waited for: 1 -> 9; matrix products, arithmetic and copies ran while one was open for 8% -> 1% of each run, Pallas kernels for 0% -> 0%
where the time goes in v1:
time: 60 us; the launch traced here: 59.7 us
  Pallas kernels  20.6 us (34%)
  starting transfers between devices  16.9 us (28%)
  waiting for transfers between devices  13.8 us (23%)
  local copies, waits for them, and re-layouts  6.14 us (10%)
  other arithmetic  1.56 us (3%)
  between operations  0.68 us (1%)
    ppermute x14, starting transfers between devices, swap(): return lax.ppermute(value, axis, [(i, i ^ distance) for i in range(count)])  16.9 us
    ppermute x14, waiting for transfers between devices, swap(): return lax.ppermute(value, axis, [(i, i ^ distance) for i in range(count)])  13.8 us
    pallas_call x1, Pallas kernels, on_device(): pl.pallas_call(waves_body, grid=(chunks,), in_specs=[pl.BlockSpec((rows,...  10.5 us
    pallas_call x1, Pallas kernels, on_device(): pl.pallas_call(grads_body, grid_spec=pltpu.PrefetchScalarGridSpec(num_sca...  10.1 us
    unnamed x12, local copies, waits for them, and re-layouts  6.08 us
  transfers between devices with their start and end apart: 14, of which 9 were waited for; matrix products, arithmetic and copies ran while one was open for 1% of the time, Pallas kernels for 0%

profile of v1, /device:TPU:0, one launch (start us, length us, event | category | flops | bytes accessed | tf_op | source)
XLA Modules:
  0.0 59.7 jit_solution(119132467916247372)
XLA Ops:
  0.6 1.4 %copy-done = f32[128,3,1024]{2,0,1:T(8,128)S(1)} copy-done((f32[128,3,1024]{2,0,1:T(8,128)S(1)}, f32[128,3,1024]{2,0,1:T(8,128)}, u32[]{:S(2)}) %copy-start) | copy-done | bytes 1572888
  2.0 0.9 %copy-done.2 = f32[128,4,128]{2,1,0:T(4,128)S(1)} copy-done((f32[128,4,128]{2,1,0:T(4,128)S(1)}, f32[128,4,128]{2,1,0:T(4,128)}, u32[]{:S(2)}) %copy-start.2) | copy-done | bytes 262168
  3.0 0.7 %copy-done.4 = f32[3,1024]{1,0:T(4,128)S(1)} copy-done((f32[3,1024]{1,0:T(4,128)S(1)}, f32[3,1024]{1,0:T(4,128)}, u32[]{:S(2)}) %copy-start.4) | copy-done | bytes 12312
  3.7 10.5 %waves.1 = (f32[4,3,512,256]{3,2,1,0:T(8,128)}, f32[4,3,512,256]{3,2,1,0:T(8,128)}, f32[48,1024]{1,0:T(8,128)S(1)}, f32[24,1024]{1,0:T(8,128)S(1)}) custom-call(f32[512,128]{1,0:T(8,128)S(1)} %bitcast.37, f32[3,128,1024]{2,1,0:T(8,128)S(1)} %bitcast.35, f32[3,1024]{1,0:T(4,128)S(1)} %copy-done.4), custom_call_target="tpu_custom_call" | custom-call | tf_op jit(solution)/shard_map/waves/pallas_call | solution.py:289
  14.2 3.3 %collective-permute-start.6 = (f32[24,1024]{1,0:T(8,128)S(1)}, f32[24,1024]{1,0:T(8,128)S(1)}, u32[]{:S(2)}, u32[]{:S(2)}) collective-permute-start(f32[24,1024]{1,0:T(8,128)S(1)} %get-tuple-element.12.refs_7_), channel_id=1, source_target_pairs={{0,28},{4,24},{8,20},{12,16},{16,12},{20,8},{24,4},{28,0},{1,29},{... | collective-permute-start | bytes 294920 | tf_op jit(solution)/shard_map/ppermute | solution.py:268
  18.1 1.4 %collective-permute-start.4 = (f32[24,1024]{1,0:T(8,128)S(1)}, f32[24,1024]{1,0:T(8,128)S(1)}, u32[]{:S(2)}, u32[]{:S(2)}) collective-permute-start(f32[24,1024]{1,0:T(8,128)S(1)} %get-tuple-element.12.refs_7_), channel_id=1, source_target_pairs={{0,20},{4,16},{8,28},{12,24},{16,4},{20,0},{24,12},{28,8},{1,21},{... | collective-permute-start | bytes 294920 | tf_op jit(solution)/shard_map/ppermute | solution.py:268
  19.9 1.2 %collective-permute-start.2 = (f32[24,1024]{1,0:T(8,128)S(1)}, f32[24,1024]{1,0:T(8,128)S(1)}, u32[]{:S(2)}, u32[]{:S(2)}) collective-permute-start(f32[24,1024]{1,0:T(8,128)S(1)} %get-tuple-element.12.refs_7_), channel_id=1, source_target_pairs={{0,12},{4,8},{8,4},{12,0},{16,28},{20,24},{24,20},{28,16},{1,13},{... | collective-permute-start | bytes 294920 | tf_op jit(solution)/shard_map/ppermute | solution.py:268
  21.0 2.2 %collective-permute-start.1 = (f32[24,1024]{1,0:T(8,128)S(1)}, f32[24,1024]{1,0:T(8,128)S(1)}, u32[]{:S(2)}, u32[]{:S(2)}) collective-permute-start(f32[24,1024]{1,0:T(8,128)S(1)} %get-tuple-element.12.refs_7_), channel_id=1, source_target_pairs={{0,8},{4,12},{8,0},{12,4},{16,24},{20,28},{24,16},{28,20},{1,9},{5... | collective-permute-start | bytes 294920 | tf_op jit(solution)/shard_map/ppermute | solution.py:268
  23.2 0.7 %collective-permute-done.5.refs_13_ = f32[24,1024]{1,0:T(8,128)S(1)} collective-permute-done((f32[24,1024]{1,0:T(8,128)S(1)}, f32[24,1024]{1,0:T(8,128)S(1)}, u32[]{:S(2)}, u32[]{:S(2)}) %collective-permute-start.5) | collective-permute-done | bytes 98336 | tf_op jit(solution)/shard_map/ppermute | solution.py:268
  24.0 1.1 %collective-permute-done.4.refs_12_ = f32[24,1024]{1,0:T(8,128)S(1)} collective-permute-done((f32[24,1024]{1,0:T(8,128)S(1)}, f32[24,1024]{1,0:T(8,128)S(1)}, u32[]{:S(2)}, u32[]{:S(2)}) %collective-permute-start.4) | collective-permute-done | bytes 98336 | tf_op jit(solution)/shard_map/ppermute | solution.py:268
  25.1 2.4 %collective-permute-done.3.refs_11_ = f32[24,1024]{1,0:T(8,128)S(1)} collective-permute-done((f32[24,1024]{1,0:T(8,128)S(1)}, f32[24,1024]{1,0:T(8,128)S(1)}, u32[]{:S(2)}, u32[]{:S(2)}) %collective-permute-start.3) | collective-permute-done | bytes 98336 | tf_op jit(solution)/shard_map/ppermute | solution.py:268
  28.1 1.4 %copy-done.1 = f32[128,3,1024]{2,0,1:T(8,128)S(1)} copy-done((f32[128,3,1024]{2,0,1:T(8,128)S(1)}, f32[128,3,1024]{2,0,1:T(8,128)}, u32[]{:S(2)}) %copy-start.1) | copy-done | bytes 1572888
  29.5 0.9 %copy-done.3 = f32[128,4,128]{2,1,0:T(4,128)S(1)} copy-done((f32[128,4,128]{2,1,0:T(4,128)S(1)}, f32[128,4,128]{2,1,0:T(4,128)}, u32[]{:S(2)}) %copy-start.3) | copy-done | bytes 262168
  31.1 10.1 %grads.1 = (f32[4,3,16,1024]{3,2,1,0:T(8,128)S(1)}, f32[4,3,16,1024]{3,2,1,0:T(8,128)S(1)}, f32[4,128,128]{2,1,0:T(8,128)S(1)}) custom-call(s32[2]{0:T(128)S(1)} %pad_add_fusion.refs_0_, s32[4]{0:T(128)S(1)} %copy-done.5, f32[512,128]{1,0:T(8,128)S(1)} %bitcast.38, f32[3,128,1024]{2,1,0:T(8,128)S(1)} %bitcast.36, ...), custom_call_target="tpu_custom_call" | custom-call | tf_op jit(solution)/shard_map/grads/pallas_call | solution.py:320
  41.4 1.6 %collective-permute-start.7 = (f32[128,128]{1,0:T(8,128)S(1)}, f32[128,128]{1,0:T(8,128)S(1)}, u32[]{:S(2)}, u32[]{:S(2)}) collective-permute-start(f32[128,128]{1,0:T(8,128)S(1)} %get-tuple-element.19), channel_id=1, source_target_pairs={{0,1},{1,0},{2,3},{3,2},{4,5},{5,4},{6,7},{7,6},{8,9},{9,8},{10,11... | collective-permute-start | bytes 196616 | tf_op jit(solution)/shard_map/ppermute | solution.py:268
  43.0 2.5 %collective-permute-start.9 = (f32[128,128]{1,0:T(8,128)S(1)}, f32[128,128]{1,0:T(8,128)S(1)}, u32[]{:S(2)}, u32[]{:S(2)}) collective-permute-start(f32[128,128]{1,0:T(8,128)S(1)} %get-tuple-element.20), channel_id=1, source_target_pairs={{0,3},{1,2},{2,1},{3,0},{4,7},{5,6},{6,5},{7,4},{8,11},{9,10},{10,... | collective-permute-start | bytes 196616 | tf_op jit(solution)/shard_map/ppermute | solution.py:268
  45.8 1.5 %collective-permute-start.11 = (f32[3,16,1024]{2,1,0:T(8,128)S(1)}, f32[3,16,1024]{2,1,0:T(8,128)S(1)}, u32[]{:S(2)}, u32[]{:S(2)}) collective-permute-start(f32[3,16,1024]{2,1,0:T(8,128)S(1)} %get-tuple-element.16), channel_id=1, source_target_pairs={{0,8},{4,12},{8,0},{12,4},{16,24},{20,28},{24,16},{28,20},{1,9},{5... | collective-permute-start | bytes 589832 | tf_op jit(solution)/shard_map/ppermute | solution.py:268
  47.3 1.3 %collective-permute-start.13 = (f32[3,16,1024]{2,1,0:T(8,128)S(1)}, f32[3,16,1024]{2,1,0:T(8,128)S(1)}, u32[]{:S(2)}, u32[]{:S(2)}) collective-permute-start(f32[3,16,1024]{2,1,0:T(8,128)S(1)} %get-tuple-element.17), channel_id=1, source_target_pairs={{0,24},{4,28},{8,16},{12,20},{16,8},{20,12},{24,0},{28,4},{1,25},{... | collective-permute-start | bytes 589832 | tf_op jit(solution)/shard_map/ppermute | solution.py:268
  48.6 0.7 %collective-permute-start.12 = (f32[3,16,1024]{2,1,0:T(8,128)S(1)}, f32[3,16,1024]{2,1,0:T(8,128)S(1)}, u32[]{:S(2)}, u32[]{:S(2)}) collective-permute-start(f32[3,16,1024]{2,1,0:T(8,128)S(1)} %get-tuple-element.18), channel_id=1, source_target_pairs={{0,16},{4,20},{8,24},{12,28},{16,0},{20,4},{24,8},{28,12},{1,17},{... | collective-permute-start | bytes 589832 | tf_op jit(solution)/shard_map/ppermute | solution.py:268
  49.7 2.5 %collective-permute-done.8 = f32[128,128]{1,0:T(8,128)S(1)} collective-permute-done((f32[128,128]{1,0:T(8,128)S(1)}, f32[128,128]{1,0:T(8,128)S(1)}, u32[]{:S(2)}, u32[]{:S(2)}) %collective-permute-start.8) | collective-permute-done | bytes 65568 | tf_op jit(solution)/shard_map/ppermute | solution.py:268
  52.9 0.7 %collective-permute-done.11 = f32[3,16,1024]{2,1,0:T(8,128)S(1)} collective-permute-done((f32[3,16,1024]{2,1,0:T(8,128)S(1)}, f32[3,16,1024]{2,1,0:T(8,128)S(1)}, u32[]{:S(2)}, u32[]{:S(2)}) %collective-permute-start.11) | collective-permute-done | bytes 196640 | tf_op jit(solution)/shard_map/ppermute | solution.py:268
  53.6 4.0 %collective-permute-done.13 = f32[3,16,1024]{2,1,0:T(8,128)S(1)} collective-permute-done((f32[3,16,1024]{2,1,0:T(8,128)S(1)}, f32[3,16,1024]{2,1,0:T(8,128)S(1)}, u32[]{:S(2)}, u32[]{:S(2)}) %collective-permute-start.13) | collective-permute-done | bytes 196640 | tf_op jit(solution)/shard_map/ppermute | solution.py:268
  57.6 1.4 %collective-permute-done.12 = f32[3,16,1024]{2,1,0:T(8,128)S(1)} collective-permute-done((f32[3,16,1024]{2,1,0:T(8,128)S(1)}, f32[3,16,1024]{2,1,0:T(8,128)S(1)}, u32[]{:S(2)}, u32[]{:S(2)}) %collective-permute-start.12) | collective-permute-done | bytes 196640 | tf_op jit(solution)/shard_map/ppermute | solution.py:268
  59.0 0.7 %fusion.3 = f32[16,3,1024]{2,0,1:T(8,128)} fusion(f32[3,16,1024]{2,1,0:T(8,128)S(1)} %collective-permute-done.13, f32[3,16,1024]{2,1,0:T(8,128)S(1)} %collective-permute-done.12, f32[3,16,1024]{2,1,0:T(8,128)S(1)} %collective-permute-done.11, f32[4,3,16,1024]{3,2,1,0:T(8,128)S(1)} %add.24), kind=kLoop, calls=%fused_computation.7 | loop fusion | flops 147456 | bytes 983040 | tf_op jit(solution)/shard_map/transpose | solution.py:355
  (24 shorter events, 3.8 us)
Async XLA Ops:
  0.6 1.4 %copy-start = (f32[128,3,1024]{2,0,1:T(8,128)S(1)}, f32[128,3,1024]{2,0,1:T(8,128)}, u32[]{:S(2)}) copy-start(f32[128,3,1024]{2,0,1:T(8,128)} %param.5) | copy-start | bytes 4718596
  2.0 0.9 %copy-start.2 = (f32[128,4,128]{2,1,0:T(4,128)S(1)}, f32[128,4,128]{2,1,0:T(4,128)}, u32[]{:S(2)}) copy-start(f32[128,4,128]{2,1,0:T(4,128)} %param.4) | copy-start | bytes 786436
  3.0 0.7 %copy-start.4 = (f32[3,1024]{1,0:T(4,128)S(1)}, f32[3,1024]{1,0:T(4,128)}, u32[]{:S(2)}) copy-start(f32[3,1024]{1,0:T(4,128)} %refs_2_.1) | copy-start | bytes 36868
  14.2 6.8 %collective-permute-start.6 = (f32[24,1024]{1,0:T(8,128)S(1)}, f32[24,1024]{1,0:T(8,128)S(1)}, u32[]{:S(2)}, u32[]{:S(2)}) collective-permute-start(f32[24,1024]{1,0:T(8,128)S(1)} %get-tuple-element.12.refs_7_), channel_id=1, source_target_pairs={{0,28},{4,24},{8,20},{12,16},{16,12},{20,8},{24,4},{28,0},{1,29},{... | collective-permute-start | bytes 294920 | tf_op jit(solution)/shard_map/ppermute | solution.py:268
  17.6 6.4 %collective-permute-start.5 = (f32[24,1024]{1,0:T(8,128)S(1)}, f32[24,1024]{1,0:T(8,128)S(1)}, u32[]{:S(2)}, u32[]{:S(2)}) collective-permute-start(f32[24,1024]{1,0:T(8,128)S(1)} %get-tuple-element.12.refs_7_), channel_id=1, source_target_pairs={{0,24},{4,28},{8,16},{12,20},{16,8},{20,12},{24,0},{28,4},{1,25},{... | collective-permute-start | bytes 294920 | tf_op jit(solution)/shard_map/ppermute | solution.py:268
  18.1 6.9 %collective-permute-start.4 = (f32[24,1024]{1,0:T(8,128)S(1)}, f32[24,1024]{1,0:T(8,128)S(1)}, u32[]{:S(2)}, u32[]{:S(2)}) collective-permute-start(f32[24,1024]{1,0:T(8,128)S(1)} %get-tuple-element.12.refs_7_), channel_id=1, source_target_pairs={{0,20},{4,16},{8,28},{12,24},{16,4},{20,0},{24,12},{28,8},{1,21},{... | collective-permute-start | bytes 294920 | tf_op jit(solution)/shard_map/ppermute | solution.py:268
  19.6 7.9 %collective-permute-start.3 = (f32[24,1024]{1,0:T(8,128)S(1)}, f32[24,1024]{1,0:T(8,128)S(1)}, u32[]{:S(2)}, u32[]{:S(2)}) collective-permute-start(f32[24,1024]{1,0:T(8,128)S(1)} %get-tuple-element.12.refs_7_), channel_id=1, source_target_pairs={{0,16},{4,20},{8,24},{12,28},{16,0},{20,4},{24,8},{28,12},{1,17},{... | collective-permute-start | bytes 294920 | tf_op jit(solution)/shard_map/ppermute | solution.py:268
  19.9 7.6 %collective-permute-start.2 = (f32[24,1024]{1,0:T(8,128)S(1)}, f32[24,1024]{1,0:T(8,128)S(1)}, u32[]{:S(2)}, u32[]{:S(2)}) collective-permute-start(f32[24,1024]{1,0:T(8,128)S(1)} %get-tuple-element.12.refs_7_), channel_id=1, source_target_pairs={{0,12},{4,8},{8,4},{12,0},{16,28},{20,24},{24,20},{28,16},{1,13},{... | collective-permute-start | bytes 294920 | tf_op jit(solution)/shard_map/ppermute | solution.py:268
  21.0 7.1 %collective-permute-start.1 = (f32[24,1024]{1,0:T(8,128)S(1)}, f32[24,1024]{1,0:T(8,128)S(1)}, u32[]{:S(2)}, u32[]{:S(2)}) collective-permute-start(f32[24,1024]{1,0:T(8,128)S(1)} %get-tuple-element.12.refs_7_), channel_id=1, source_target_pairs={{0,8},{4,12},{8,0},{12,4},{16,24},{20,28},{24,16},{28,20},{1,9},{5... | collective-permute-start | bytes 294920 | tf_op jit(solution)/shard_map/ppermute | solution.py:268
  23.9 4.2 %collective-permute-start = (f32[24,1024]{1,0:T(8,128)S(1)}, f32[24,1024]{1,0:T(8,128)S(1)}, u32[]{:S(2)}, u32[]{:S(2)}) collective-permute-start(f32[24,1024]{1,0:T(8,128)S(1)} %get-tuple-element.12.refs_7_), channel_id=1, source_target_pairs={{0,4},{4,0},{8,12},{12,8},{16,20},{20,16},{24,28},{28,24},{1,5},{5... | collective-permute-start | bytes 294920 | tf_op jit(solution)/shard_map/ppermute | solution.py:268
  28.1 1.4 %copy-start.1 = (f32[128,3,1024]{2,0,1:T(8,128)S(1)}, f32[128,3,1024]{2,0,1:T(8,128)}, u32[]{:S(2)}) copy-start(f32[128,3,1024]{2,0,1:T(8,128)} %param.5) | copy-start | bytes 4718596
  29.5 0.9 %copy-start.3 = (f32[128,4,128]{2,1,0:T(4,128)S(1)}, f32[128,4,128]{2,1,0:T(4,128)}, u32[]{:S(2)}) copy-start(f32[128,4,128]{2,1,0:T(4,128)} %param.4) | copy-start | bytes 786436
  30.4 0.7 %copy-start.5 = (s32[4]{0:T(128)S(1)}, s32[4]{0:T(128)}, u32[]{:S(2)}) copy-start(s32[4]{0:T(128)} %refs_1_.1) | copy-start | bytes 52
  41.2 4.4 %collective-permute-start.10 = (f32[4,3,16,1024]{3,2,1,0:T(8,128)S(1)}, f32[4,3,16,1024]{3,2,1,0:T(8,128)S(1)}, u32[]{:S(2)}, u32[]{:S(2)}) collective-permute-start(f32[4,3,16,1024]{3,2,1,0:T(8,128)S(1)} %get-tuple-element.15), channel_id=1, source_target_pairs={{0,4},{4,0},{8,12},{12,8},{16,20},{20,16},{24,28},{28,24},{1,5},{5... | collective-permute-start | bytes 2359304 | tf_op jit(solution)/shard_map/ppermute | solution.py:268
  41.4 7.3 %collective-permute-start.7 = (f32[128,128]{1,0:T(8,128)S(1)}, f32[128,128]{1,0:T(8,128)S(1)}, u32[]{:S(2)}, u32[]{:S(2)}) collective-permute-start(f32[128,128]{1,0:T(8,128)S(1)} %get-tuple-element.19), channel_id=1, source_target_pairs={{0,1},{1,0},{2,3},{3,2},{4,5},{5,4},{6,7},{7,6},{8,9},{9,8},{10,11... | collective-permute-start | bytes 196616 | tf_op jit(solution)/shard_map/ppermute | solution.py:268
  43.0 6.7 %collective-permute-start.9 = (f32[128,128]{1,0:T(8,128)S(1)}, f32[128,128]{1,0:T(8,128)S(1)}, u32[]{:S(2)}, u32[]{:S(2)}) collective-permute-start(f32[128,128]{1,0:T(8,128)S(1)} %get-tuple-element.20), channel_id=1, source_target_pairs={{0,3},{1,2},{2,1},{3,0},{4,7},{5,6},{6,5},{7,4},{8,11},{9,10},{10,... | collective-permute-start | bytes 196616 | tf_op jit(solution)/shard_map/ppermute | solution.py:268
  45.5 6.7 %collective-permute-start.8 = (f32[128,128]{1,0:T(8,128)S(1)}, f32[128,128]{1,0:T(8,128)S(1)}, u32[]{:S(2)}, u32[]{:S(2)}) collective-permute-start(f32[128,128]{1,0:T(8,128)S(1)} %get-tuple-element.21), channel_id=1, source_target_pairs={{0,2},{1,3},{2,0},{3,1},{4,6},{5,7},{6,4},{7,5},{8,10},{9,11},{10,... | collective-permute-start | bytes 196616 | tf_op jit(solution)/shard_map/ppermute | solution.py:268
  45.8 7.8 %collective-permute-start.11 = (f32[3,16,1024]{2,1,0:T(8,128)S(1)}, f32[3,16,1024]{2,1,0:T(8,128)S(1)}, u32[]{:S(2)}, u32[]{:S(2)}) collective-permute-start(f32[3,16,1024]{2,1,0:T(8,128)S(1)} %get-tuple-element.16), channel_id=1, source_target_pairs={{0,8},{4,12},{8,0},{12,4},{16,24},{20,28},{24,16},{28,20},{1,9},{5... | collective-permute-start | bytes 589832 | tf_op jit(solution)/shard_map/ppermute | solution.py:268
  47.3 10.3 %collective-permute-start.13 = (f32[3,16,1024]{2,1,0:T(8,128)S(1)}, f32[3,16,1024]{2,1,0:T(8,128)S(1)}, u32[]{:S(2)}, u32[]{:S(2)}) collective-permute-start(f32[3,16,1024]{2,1,0:T(8,128)S(1)} %get-tuple-element.17), channel_id=1, source_target_pairs={{0,24},{4,28},{8,16},{12,20},{16,8},{20,12},{24,0},{28,4},{1,25},{... | collective-permute-start | bytes 589832 | tf_op jit(solution)/shard_map/ppermute | solution.py:268
  48.6 10.4 %collective-permute-start.12 = (f32[3,16,1024]{2,1,0:T(8,128)S(1)}, f32[3,16,1024]{2,1,0:T(8,128)S(1)}, u32[]{:S(2)}, u32[]{:S(2)}) collective-permute-start(f32[3,16,1024]{2,1,0:T(8,128)S(1)} %get-tuple-element.18), channel_id=1, source_target_pairs={{0,16},{4,20},{8,24},{12,28},{16,0},{20,4},{24,8},{28,12},{1,17},{... | collective-permute-start | bytes 589832 | tf_op jit(solution)/shard_map/ppermute | solution.py:268

commit v2 on v0

v2 whole, which is shorter than its diff:
```python
import math

import jax
import jax.numpy as jnp
from jax import lax
from jax.experimental import pallas as pl
from jax.experimental.pallas import tpu as pltpu
from jax.sharding import PartitionSpec as P

f32, bf16 = jnp.float32, jnp.bfloat16
SUB = 8
HALF = SUB // 2
WIDE = 256
MAGIC = 12582912.0
SIN = (3.141582022150658, -5.167142796368909, 2.541899027590427, -0.5546361970970186)
COS = (
    0.9999999534666683,
    -4.934792858675264,
    4.058411914167107,
    -1.3318801612488937,
    0.2196967986036905,
)
NT = (((1,), (1,)), ((), ()))


def horner(z, coefs):
    acc = z * coefs[-1] + coefs[-2]
    for coef in coefs[-3::-1]:
        acc = acc * z + coef
    return acc


def split(value):
    high = value.astype(bf16)
    return high, (value - high.astype(f32)).astype(bf16)


def pair_rows(low, high):
    top = lax.broadcasted_iota(jnp.int32, low.shape, 0) < HALF
    first = jnp.where(top, low, pltpu.roll(high, HALF, 0))
    second = jnp.where(top, pltpu.roll(low, HALF, 0), high)
    return first, second


def tile(i, count=1):
    return pl.ds(pl.multiple_of(i * (count * SUB), count * SUB), count * SUB)


def by_core(core, own, sibling, body):
    @pl.when(core == 0)
    def _():
        body(own, sibling)

    @pl.when(core == 1)
    def _():
        body(sibling, own)


def waves_kernel(amplitude, wide, place_ref, x_hbm, y_ref, p_hbm, ph_hbm, *rest):
    c_ref, s_ref, loc_ref, snd_ref, xt_ref, w_ref = rest[:6]
    xs_ref, ang_ref, flat_ref, x_ref, p_ref, ph_ref, sems = rest[6:]
    rows, chans = flat_ref.shape
    core = place_ref[0] & 1
    chunks = c_ref.shape[0]

    def columns(chunk):
        return pl.ds(pl.multiple_of((core * chunks + chunk) * wide, wide), wide)

    fetch_x = pltpu.make_async_copy(x_hbm, x_ref, sems.at[0])
    fetch_ph = pltpu.make_async_copy(ph_hbm, ph_ref, sems.at[1])
    fetch_p = [
        pltpu.make_async_copy(p_hbm.at[:, :, columns(k)], p_ref.at[k], sems.at[2 + k])
        for k in range(chunks)
    ]
    for copy in [fetch_x, fetch_ph] + fetch_p:
        copy.start()
    inv = 1.0 / (2.0 * math.pi)
    root = math.sqrt(2.0 * amplitude)
    sin_coefs = [root * coef for coef in SIN]
    cos_coefs = [-root * coef for coef in COS]

    lane = lax.broadcasted_iota(jnp.int32, (2 * SUB, chans), 1)
    ones = jnp.where(lane < 3, 1.0, 0.0).astype(bf16)

    def pairs(even_ref, odd_ref):
        def one(k, _):
            first, second = pair_rows(even_ref[tile(k), :], odd_ref[tile(k), :])
            both = jnp.concatenate([first, second], axis=0)
            flat_ref[tile(k, 2), :] = both
            high, low = split(both)
            xs_ref[tile(k, 2), :] = jnp.concatenate([high, low, high, ones], axis=1)
            return 0

        lax.fori_loop(0, rows // (2 * SUB), one, 0, unroll=4)

    fetch_x.wait()
    by_core(core, x_ref, y_ref, pairs)
    high, low = split(flat_ref[...].T)
    xt_ref[:chans, :] = high
    xt_ref[chans:, :] = low
    fetch_ph.wait()

    zero = jnp.zeros((SUB, wide), f32)
    row = lax.broadcasted_iota(jnp.int32, (chans, wide), 0)
    for chunk in range(chunks):
        fetch_p[chunk].wait()
        for level in range(3):
            high, low = split(p_ref[chunk, level])
            w_ref[chunk, :chans, level * wide : (level + 1) * wide] = high
            w_ref[chunk, chans:, level * wide : (level + 1) * wide] = low
            high, low = split(p_ref[chunk, level] * inv)
            phase = ph_ref[level : level + 1, columns(chunk)] * inv
            phase0 = phase.astype(bf16).astype(f32)
            phase1 = (phase - phase0).astype(bf16).astype(f32)
            phase2 = phase - phase0 - phase1
            extra = jnp.where(row == 0, phase0, jnp.where(row == 1, phase1, phase2))
            extra = jnp.where(row < 3, extra, 0.0).astype(bf16)
            stacked = jnp.concatenate([high, high, low, extra], axis=0)
            ang_ref[level] = jnp.dot(xs_ref[...], stacked, preferred_element_type=f32)

        def step(i, carry):
            s0, s1, s2, s01, s12, s012 = carry
            cosines = []
            for level in range(3):
                turn = ang_ref[level, tile(i), :]
                r = turn - ((turn + MAGIC) - MAGIC)
                z = r * r
                sine = r * horner(z, sin_coefs)
                cosine = horner(z, cos_coefs)
                wave = amplitude - sine * sine
                c_ref[chunk, level, tile(i), :] = wave
                s_ref[chunk, level, tile(i), :] = sine * cosine
                cosines.append(wave)
            c0, c1, c2 = cosines
            s012 = s012 + s01 * c2
            s12 = s12 + s1 * c2
            s01 = s01 + s0 * c1
            return (s0 + c0, s1 + c1, s2 + c2, s01, s12, s012)

        sums = lax.fori_loop(0, rows // SUB, step, (zero,) * 6, unroll=4)
        for k in range(6):
            loc_ref[chunk, SUB * k : SUB * (k + 1), :] = sums[k]
        a0, a1, a2, a01, a12, a012 = [v[:HALF] for v in sums]
        b0, b1, b2, b01, b12, b012 = [v[HALF:] for v in sums]
        both = (
            a0 + b0,
            a1 + b1,
            a2 + b2,
            a01 + b01 + a0 * b1,
            a12 + b12 + a1 * b2,
            a012 + b012 + a0 * b12 + a01 * b2,
        )
        for k in range(6):
            snd_ref[chunk, HALF * k : HALF * (k + 1), :] = both[k]


def grads_kernel(sizes, place_ref, c_ref, s_ref, loc_ref, xt_ref, w_ref, *refs):
    n_tm, n_freq, batch, wide = sizes
    chips = n_tm // 2
    got = refs[:chips]
    gp_ref, gk_ref, gs_ref = refs[chips : chips + 3]
    all_ref, u1_ref, sh_ref, sl_ref, acc_ref, flat_ref = refs[chips + 3 :]
    rows, chans = acc_ref.shape
    core, chip, z = place_ref[0] & 1, place_ref[0] >> 1, place_ref[1]
    chunks = c_ref.shape[0]
    each = chans // n_tm

    for d in range(chips):
        all_ref[jnp.bitwise_xor(chip, d)] = got[d][...]

    row = lax.broadcasted_iota(jnp.int32, (HALF, wide), 0)
    zero = jnp.zeros((HALF, wide), f32)
    weight = zero
    for b in range(batch):
        value = jnp.where(place_ref[2 + b] == 1, 2.0 / batch, -2.0 / batch)
        weight = jnp.where(row == b, value, weight)

    def tall(first, second):
        return jnp.concatenate([first, second], axis=0)

    for chunk in range(chunks):

        def sums_of(j):
            return [all_ref[j, chunk, HALF * k : HALF * (k + 1), :] for k in range(6)]

        def forward(j, carry):
            p0, p01, p012 = carry
            b0, b1, b2, b01, b12, b012 = sums_of(j)
            p012 = p012 + b012 + p0 * b12 + p01 * b2
            p01 = p01 + b01 + p0 * b1
            return (p0 + b0, p01, p012)

        def backward(step, carry):
            t1, t2, t12 = carry
            b0, b1, b2, b01, b12, b012 = sums_of(chips - 1 - step)
            t12 = t12 + b12 + b1 * t2
            return (t1 + b1, t2 + b2, t12)

        entry = lax.fori_loop(0, chip, forward, (zero,) * 3)
        e1, e2 = entry[:2]
        totals = lax.fori_loop(chip, chips, forward, entry)
        t1, t2, t12 = lax.fori_loop(0, chips - 1 - chip, backward, (zero,) * 3)
        seeds = [2.0 * weight * jnp.sum(weight * total, axis=0, keepdims=True) for total in totals]

        def local(k):
            value = loc_ref[chunk, SUB * k : SUB * (k + 1), :]
            return value[:HALF], value[HALF:]

        a0, _ = local(0)
        a1, b1 = local(1)
        _, b2 = local(2)
        a01, _ = local(3)
        _, b12 = local(4)
        front1 = tall(e1, e1 + a0)
        front2 = tall(e2, e2 + a01 + e1 * a1)
        tail2 = tall(t2 + b2, t2)
        tail1 = tall(t1 + b1, t1)
        tail12 = tall(t12 + b12 + b1 * t2, t12)
        d0, d1, d2 = [tall(seed, seed) for seed in seeds]
        adjoint1 = d1 + d2 * tail2
        adjoint0 = d0 + d1 * tail1 + d2 * tail12

        def fwd(pair, carry):
            f1, f2 = carry
            slopes = []
            for which in range(2):
                at = tile(2 * pair + which)
                u1_ref[at, :] = s_ref[chunk, 1, at, :] * f1
                slopes.append(s_ref[chunk, 2, at, :] * (d2 * f2))
                f2 = f2 + f1 * c_ref[chunk, 1, at, :]
                f1 = f1 + c_ref[chunk, 0, at, :]
            high, low = split(jnp.concatenate(slopes, axis=0))
            sh_ref[tile(pair, 2), 2 * wide :] = high
            sl_ref[tile(pair, 2), 2 * wide :] = low
            return f1, f2

        lax.fori_loop(0, rows // (2 * SUB), fwd, (front1, front2), unroll=2)

        def bwd(step, carry):
            g1, g0 = carry
            pair = rows // (2 * SUB) - 1 - step
            slope0, slope1 = [], []
            for which in (1, 0):
                at = tile(2 * pair + which)
                slope1.append(u1_ref[at, :] * g1)
                slope0.append(s_ref[chunk, 0, at, :] * g0)
                g0 = g0 + g1 * c_ref[chunk, 1, at, :]
                g1 = g1 + d2 * c_ref[chunk, 2, at, :]
            for level, slopes in enumerate((slope0, slope1)):
                high, low = split(jnp.concatenate(slopes[::-1], axis=0))
                sh_ref[tile(pair, 2), level * wide : (level + 1) * wide] = high
                sl_ref[tile(pair, 2), level * wide : (level + 1) * wide] = low
            return g1, g0

        lax.fori_loop(0, rows // (2 * SUB), bwd, (adjoint1, adjoint0), unroll=2)

        for level in range(3):
            cols = slice(level * wide, (level + 1) * wide)
            main = jnp.dot(xt_ref[...], sh_ref[:, cols], preferred_element_type=f32)
            rest = jnp.dot(xt_ref[:chans, :], sl_ref[:, cols], preferred_element_type=f32)
            grad = main[:chans] + main[chans:] + rest
            for d in range(n_tm):
                gp_ref[d, level, :, chunk * wide : (chunk + 1) * wide] = grad[each * d : each * (d + 1)]

        main = lax.dot_general(sh_ref[...], w_ref[chunk], NT, preferred_element_type=f32)
        rest = lax.dot_general(sl_ref[...], w_ref[chunk, :chans, :], NT, preferred_element_type=f32)
        total = main[:, :chans] + main[:, chans:] + rest
        if chunk == 0:
            acc_ref[...] = total
        else:
            acc_ref[...] += total

    def one(k, _):
        even, odd = pair_rows(acc_ref[tile(2 * k), :], acc_ref[tile(2 * k + 1), :])
        flat_ref[0, tile(k), :] = even
        flat_ref[1, tile(k), :] = odd
        return 0

    lax.fori_loop(0, rows // (2 * SUB), one, 0, unroll=4)
    piece = rows // 2 // n_freq
    for j in range(n_freq):
        at = pl.ds(pl.multiple_of(jnp.bitwise_xor(z, j) * piece, piece), piece)
        gk_ref[j] = flat_ref[core, at, :]
        gs_ref[j] = flat_ref[1 - core, at, :]


def swap(value, axis, distance):
    count = lax.axis_size(axis)
    return lax.ppermute(value, axis, [(i, i ^ distance) for i in range(count)])


def resident(value):
    return pltpu.with_memory_space_constraint(value, pltpu.HBM)


def on_device(increments, projections, phases, groups):
    steps, batch, chans = increments.shape
    freqs = phases.shape[1]
    n_tm, n_freq = lax.axis_size("tm"), lax.axis_size("freq")
    amplitude = math.sqrt(2.0 / (steps * n_tm))
    rows = 2 * steps * batch
    mine = freqs // 2
    wide = min(WIDE, mine)
    chunks = mine // wide
    each = chans // n_tm
    x = increments.reshape(rows // 2, chans)
    p = jnp.transpose(projections, (1, 0, 2))
    here = jnp.stack([lax.axis_index("tm"), lax.axis_index("freq")]).astype(jnp.int32)
    place = jnp.concatenate([here, groups])
    params = pltpu.CompilerParams(vmem_limit_bytes=32 * 1024 * 1024)
    scalars = pl.BlockSpec(memory_space=pltpu.SMEM)
    vectors = pl.BlockSpec(memory_space=pltpu.VMEM)

    def waves_body(*refs):
        waves_kernel(amplitude, wide, *refs)

    y = swap(x, "tm", 1)
    stay = pl.BlockSpec(memory_space=pltpu.HBM)
    cosines, sines, local, own, xt, weights = pl.pallas_call(
        waves_body,
        in_specs=[scalars, stay, vectors, stay, stay],
        out_specs=[vectors] * 6,
        out_shape=[
            pltpu.VMEM((chunks, 3, rows, wide), f32),
            pltpu.VMEM((chunks, 3, rows, wide), f32),
            pltpu.VMEM((chunks, 6 * SUB, wide), f32),
            jax.ShapeDtypeStruct((chunks, 3 * SUB, wide), f32),
            pltpu.VMEM((2 * chans, rows), bf16),
            pltpu.VMEM((chunks, 2 * chans, 3 * wide), bf16),
        ],
        scratch_shapes=[
            pltpu.VMEM((rows, 4 * chans), bf16),
            pltpu.VMEM((3, rows, wide), f32),
            pltpu.VMEM((rows, chans), f32),
            pltpu.VMEM((rows // 2, chans), f32),
            pltpu.VMEM((chunks, 3, chans, wide), f32),
            pltpu.VMEM((3, freqs), f32),
            pltpu.SemaphoreType.DMA((2 + chunks,)),
        ],
        compiler_params=params,
        name="waves",
    )(place, resident(x), y, resident(p), resident(phases))

    got = [own] + [swap(own, "tm", 2 * d) for d in range(1, n_tm // 2)]

    def grads_body(*refs):
        grads_kernel((n_tm, n_freq, batch, wide), *refs)

    gshape = jax.ShapeDtypeStruct((n_freq, rows // 2 // n_freq, chans), f32)
    parts, kept, sent = pl.pallas_call(
        grads_body,
        in_specs=[scalars] + [vectors] * (5 + n_tm // 2),
        out_specs=[vectors] * 3,
        out_shape=[jax.ShapeDtypeStruct((n_tm, 3, each, mine), f32), gshape, gshape],
        scratch_shapes=[
            pltpu.VMEM((n_tm // 2, chunks, 3 * SUB, wide), f32),
            pltpu.VMEM((rows, wide), f32),
            pltpu.VMEM((rows, 3 * wide), bf16),
            pltpu.VMEM((rows, 3 * wide), bf16),
            pltpu.VMEM((rows, chans), f32),
            pltpu.VMEM((2, rows // 2, chans), f32),
        ],
        compiler_params=params,
        name="grads",
    )(place, cosines, sines, local, xt, weights, *got)

    pieces = kept + swap(sent, "tm", 1)
    result = pieces[0]
    for j in range(1, n_freq):
        result = result + swap(pieces[j], "freq", j)
    grad_increments = result.reshape(steps // n_freq, batch, chans)
    parts = lax.all_to_all(parts, "tm", 0, 0, tiled=True)
    total = jnp.sum(parts.reshape(n_tm // 2, 2, 3, each, mine), axis=0)
    grad_projections = jnp.transpose(total, (2, 1, 0, 3)).reshape(each, 3, freqs)
    return (grad_increments, grad_projections)


def solution(mesh):
    placed = (P("tm", None, None), P(None, None, "freq"), P(None, "freq"), P())
    return jax.shard_map(
        on_device,
        mesh=mesh,
        in_specs=placed,
        out_specs=(P(("tm", "freq"), None, None), P("tm", None, "freq")),
        check_vma=False,
    )
```

time: 282 us -> 47.5 us (0.17)
  matrix products: 120 us -> 0 us
  blocking collectives: 61.2 us -> 0 us
  waiting for transfers between devices: 58.5 us -> 12.2 us
  Pallas kernels: 0 us -> 19.4 us
  between operations: 16.6 us -> 0.68 us
  loops' own time: 13 us -> 0 us
  starting transfers between devices: 0.08 us -> 12.8 us
  local copies, waits for them, and re-layouts: 9.34 us -> 0.71 us
    dot_general x13 -> x0, matrix products: 120 us -> none  [the longest x4 63.4 us: tiled_sum(): inner = jnp.einsum('ts,nsbf->ntbf', tri_mask, blocks, precision=highest)]
    unnamed x3 -> x0, waiting for transfers between devices: 58.5 us -> none
    all_gather x4 -> x0, blocking collectives: 37.8 us -> none  [prefix(): gathered = lax.all_gather(part, axis)]
    psum x1 -> x0, blocking collectives: 23.3 us -> none  [global_gaps(): return lax.psum(stacked, 'tm')]
    pallas_call x0 -> x2, Pallas kernels: none -> 19.4 us  [the longest x1 10.7 us: on_device(): pl.pallas_call(waves_body, in_specs=[scalars, stay, vectors, stay, stay],...]
    another operation x4 -> x0, loops' own time: 13 us -> none  [prefix(): return lax.fori_loop(0, ahead, one, state)]
    ppermute x0 -> x8, waiting for transfers between devices: none -> 11.2 us  [swap(): return lax.ppermute(value, axis, [(i, i ^ distance) for i in range(count)])]
    ppermute x0 -> x8, starting transfers between devices: none -> 9.28 us  [swap(): return lax.ppermute(value, axis, [(i, i ^ distance) for i in range(count)])]
  transfers between devices with their start and end apart: 2 -> 9, of which waited for: 1 -> 8; matrix products, arithmetic and copies ran while one was open for 8% -> 3% of each run, Pallas kernels for 0% -> 0%
where the time goes in v2:
time: 47.5 us; the launch traced here: 47.3 us
  Pallas kernels  19.4 us (41%)
  starting transfers between devices  12.8 us (27%)
  waiting for transfers between devices  12.2 us (26%)
  other arithmetic  1.47 us (3%)
  local copies, waits for them, and re-layouts  0.71 us (1%)
  between operations  0.68 us (1%)
    ppermute x8, waiting for transfers between devices, swap(): return lax.ppermute(value, axis, [(i, i ^ distance) for i in range(count)])  11.2 us
    pallas_call x1, Pallas kernels, on_device(): pl.pallas_call(waves_body, in_specs=[scalars, stay, vectors, stay, stay],...  10.7 us
    ppermute x8, starting transfers between devices, swap(): return lax.ppermute(value, axis, [(i, i ^ distance) for i in range(count)])  9.28 us
    pallas_call x1, Pallas kernels, on_device(): pl.pallas_call(grads_body, in_specs=[scalars] + [vectors] * (5 + n_tm //...  8.77 us
    all_to_all x1, starting transfers between devices, on_device(): parts = lax.all_to_all(parts, 'tm', 0, 0, tiled=True)  3.55 us
  transfers between devices with their start and end apart: 9, of which 8 were waited for; matrix products, arithmetic and copies ran while one was open for 3% of the time, Pallas kernels for 0%

profile of v2, /device:TPU:0, one launch (start us, length us, event | category | flops | bytes accessed | tf_op | source)
XLA Modules:
  0.0 47.3 jit_solution(5147392880549451550)
XLA Ops:
  0.6 0.5 %collective-permute-start = (f32[512,128]{1,0:T(8,128)}, f32[512,128]{1,0:T(8,128)S(1)}, u32[]{:S(2)}, u32[]{:S(2)}) collective-permute-start(f32[512,128]{1,0:T(8,128)} %bitcast.26), channel_id=1, source_target_pairs={{0,4},{4,0},{8,12},{12,8},{16,20},{20,16},{24,28},{28,24},{1,5},{5... | collective-permute-start | bytes 786440 | tf_op jit(solution)/shard_map/ppermute | solution.py:289
  1.1 0.7 %pad_add_fusion.refs_0_ = s32[6]{0:T(128)S(1)} fusion(s32[4]{0:T(128)} %param.7, s32[1]{0:T(128)} %bitcast.1, s32[1]{0:T(128)} %bitcast), kind=kLoop, calls=%fused_computation.7 | loop fusion | flops 12 | bytes 48 | tf_op jit(solution)/shard_map/concatenate | solution.py:309
  1.9 0.6 %collective-permute-done.refs_2_ = f32[512,128]{1,0:T(8,128)S(1)} collective-permute-done((f32[512,128]{1,0:T(8,128)}, f32[512,128]{1,0:T(8,128)S(1)}, u32[]{:S(2)}, u32[]{:S(2)}) %collective-permute-start) | collective-permute-done | bytes 262176 | tf_op jit(solution)/shard_map/ppermute | solution.py:289
  2.5 10.7 %waves.1 = (f32[2,3,1024,256]{3,2,1,0:T(8,128)S(1)}, f32[2,3,1024,256]{3,2,1,0:T(8,128)S(1)}, f32[2,48,256]{2,1,0:T(8,128)S(1)}, f32[2,24,256]{2,1,0:T(8,128)S(1...) custom-call(s32[6]{0:T(128)S(1)} %pad_add_fusion.refs_0_, f32[512,128]{1,0:T(8,128)} %bitcast.27, ...), custom_call_target="tpu_custom_call" | custom-call | tf_op jit(solution)/shard_map/waves/pallas_call | solution.py:319
  13.2 3.9 %collective-permute-start.3 = (f32[2,24,256]{2,1,0:T(8,128)S(1)}, f32[2,24,256]{2,1,0:T(8,128)S(1)}, u32[]{:S(2)}, u32[]{:S(2)}) collective-permute-start(f32[2,24,256]{2,1,0:T(8,128)S(1)} %get-tuple-element.16.refs_6_), channel_id=1, source_target_pairs={{0,24},{4,28},{8,16},{12,20},{16,8},{20,12},{24,0},{28,4},{1,25},{... | collective-permute-start | bytes 147464 | tf_op jit(solution)/shard_map/ppermute | solution.py:289
  17.1 0.5 %collective-permute-start.2 = (f32[2,24,256]{2,1,0:T(8,128)S(1)}, f32[2,24,256]{2,1,0:T(8,128)S(1)}, u32[]{:S(2)}, u32[]{:S(2)}) collective-permute-start(f32[2,24,256]{2,1,0:T(8,128)S(1)} %get-tuple-element.16.refs_6_), channel_id=1, source_target_pairs={{0,16},{4,20},{8,24},{12,28},{16,0},{20,4},{24,8},{28,12},{1,17},{... | collective-permute-start | bytes 147464 | tf_op jit(solution)/shard_map/ppermute | solution.py:289
  17.6 0.1 collective-permute-start.1
  17.7 1.4 %collective-permute-done.3.refs_9_ = f32[2,24,256]{2,1,0:T(8,128)S(1)} collective-permute-done((f32[2,24,256]{2,1,0:T(8,128)S(1)}, f32[2,24,256]{2,1,0:T(8,128)S(1)}, u32[]{:S(2)}, u32[]{:S(2)}) %collective-permute-start.3) | collective-permute-done | bytes 49184 | tf_op jit(solution)/shard_map/ppermute | solution.py:289
  19.2 2.0 %collective-permute-done.2.refs_8_ = f32[2,24,256]{2,1,0:T(8,128)S(1)} collective-permute-done((f32[2,24,256]{2,1,0:T(8,128)S(1)}, f32[2,24,256]{2,1,0:T(8,128)S(1)}, u32[]{:S(2)}, u32[]{:S(2)}) %collective-permute-start.2) | collective-permute-done | bytes 49184 | tf_op jit(solution)/shard_map/ppermute | solution.py:289
  21.2 0.5 %collective-permute-done.1.refs_7_ = f32[2,24,256]{2,1,0:T(8,128)S(1)} collective-permute-done((f32[2,24,256]{2,1,0:T(8,128)S(1)}, f32[2,24,256]{2,1,0:T(8,128)S(1)}, u32[]{:S(2)}, u32[]{:S(2)}) %collective-permute-start.1) | collective-permute-done | bytes 49184 | tf_op jit(solution)/shard_map/ppermute | solution.py:289
  21.7 8.8 %grads.1 = (f32[8,3,16,512]{3,2,1,0:T(8,128)}, f32[4,128,128]{2,1,0:T(8,128)S(1)}, f32[4,128,128]{2,1,0:T(8,128)S(1)}) custom-call(s32[6]{0:T(128)S(1)} %pad_add_fusion.refs_0_, f32[2,3,1024,256]{3,2,1,0:T(8,128)S(1)} %get-tuple-element.11.refs_1_, f32[2,3,1024,256]{3,2,1,0:T(8,128)S(1)} %get-tuple-element.12.refs_2_, ...), custom_call_target="tpu_custom_call" | custom-call | tf_op jit(solution)/shard_map/grads/pallas_call | solution.py:350
  30.4 0.0 collective-permute-start.4
  30.5 3.5 %all-to-all-start = ((f32[8,3,16,512]{3,2,1,0:T(8,128)}), f32[8,3,16,512]{3,2,1,0:T(8,128)S(1)}, u32[]{:S(2)}, u32[]{:S(2)}) async-start(f32[8,3,16,512]{3,2,1,0:T(8,128)} %get-tuple-element.19), calls=%async_computation | async-start | bytes 1572864 | tf_op jit(solution)/shard_map/all_to_all | solution.py:372
  34.0 0.0 collective-permute-done.4
  34.1 1.6 %collective-permute-start.5 = (f32[128,128]{1,0:T(8,128)S(1)}, f32[128,128]{1,0:T(8,128)S(1)}, u32[]{:S(2)}, u32[]{:S(2)}) collective-permute-start(f32[128,128]{1,0:T(8,128)S(1)} %get-tuple-element.20), channel_id=1, source_target_pairs={{0,1},{1,0},{2,3},{3,2},{4,5},{5,4},{6,7},{7,6},{8,9},{9,8},{10,11... | collective-permute-start | bytes 196616 | tf_op jit(solution)/shard_map/ppermute | solution.py:289
  35.7 2.5 %collective-permute-start.7 = (f32[128,128]{1,0:T(8,128)S(1)}, f32[128,128]{1,0:T(8,128)S(1)}, u32[]{:S(2)}, u32[]{:S(2)}) collective-permute-start(f32[128,128]{1,0:T(8,128)S(1)} %get-tuple-element.21), channel_id=1, source_target_pairs={{0,3},{1,2},{2,1},{3,0},{4,7},{5,6},{6,5},{7,4},{8,11},{9,10},{10,... | collective-permute-start | bytes 196616 | tf_op jit(solution)/shard_map/ppermute | solution.py:289
  38.2 0.1 collective-permute-start.6
  38.3 0.3 collective-permute-done.5
  38.6 3.9 %collective-permute-done.7 = f32[128,128]{1,0:T(8,128)S(1)} collective-permute-done((f32[128,128]{1,0:T(8,128)S(1)}, f32[128,128]{1,0:T(8,128)S(1)}, u32[]{:S(2)}, u32[]{:S(2)}) %collective-permute-start.7) | collective-permute-done | bytes 65568 | tf_op jit(solution)/shard_map/ppermute | solution.py:289
  42.5 2.5 %collective-permute-done.6 = f32[128,128]{1,0:T(8,128)S(1)} collective-permute-done((f32[128,128]{1,0:T(8,128)S(1)}, f32[128,128]{1,0:T(8,128)S(1)}, u32[]{:S(2)}, u32[]{:S(2)}) %collective-permute-start.6) | collective-permute-done | bytes 65568 | tf_op jit(solution)/shard_map/ppermute | solution.py:289
  45.0 0.6 %fusion.2 = f32[128,128]{1,0:T(8,128)} fusion(f32[128,128]{1,0:T(8,128)S(1)} %collective-permute-done.7, f32[128,128]{1,0:T(8,128)S(1)} %collective-permute-done.6, f32[128,128]{1,0:T(8,128)S(1)} %collective-permute-done.5, f32[4,128,128]{2,1,0:T(8,128)S(1)} %add.12), kind=kLoop, calls=%fused_computation.6 | loop fusion | flops 49152 | bytes 327680 | tf_op jit(solution)/shard_map/add | solution.py:370
  45.6 0.9 %all-to-all-done = f32[8,3,16,512]{3,2,1,0:T(8,128)S(1)} async-done(((f32[8,3,16,512]{3,2,1,0:T(8,128)}), f32[8,3,16,512]{3,2,1,0:T(8,128)S(1)}, u32[]{:S(2)}, u32[]{:S(2)}) %all-to-all-start) | async-done | bytes 786464 | tf_op jit(solution)/shard_map/all_to_all | solution.py:372
  46.5 0.1 reduce_sum.9
  46.6 0.7 %copy.7 = f32[2,3,2,8,512]{4,3,0,2,1:T(8,128)} copy(f32[2,3,2,8,512]{4,3,2,1,0:T(8,128)S(1)} %bitcast.25) | data formatting | bytes 393216 | tf_op jit(solution)/shard_map/reshape | solution.py:374
  (2 shorter events, 0.0 us)
Async XLA Ops:
  0.6 1.9 %collective-permute-start = (f32[512,128]{1,0:T(8,128)}, f32[512,128]{1,0:T(8,128)S(1)}, u32[]{:S(2)}, u32[]{:S(2)}) collective-permute-start(f32[512,128]{1,0:T(8,128)} %bitcast.26), channel_id=1, source_target_pairs={{0,4},{4,0},{8,12},{12,8},{16,20},{20,16},{24,28},{28,24},{1,5},{5... | collective-permute-start | bytes 786440 | tf_op jit(solution)/shard_map/ppermute | solution.py:289
  13.2 6.0 %collective-permute-start.3 = (f32[2,24,256]{2,1,0:T(8,128)S(1)}, f32[2,24,256]{2,1,0:T(8,128)S(1)}, u32[]{:S(2)}, u32[]{:S(2)}) collective-permute-start(f32[2,24,256]{2,1,0:T(8,128)S(1)} %get-tuple-element.16.refs_6_), channel_id=1, source_target_pairs={{0,24},{4,28},{8,16},{12,20},{16,8},{20,12},{24,0},{28,4},{1,25},{... | collective-permute-start | bytes 147464 | tf_op jit(solution)/shard_map/ppermute | solution.py:289
  17.1 4.1 %collective-permute-start.2 = (f32[2,24,256]{2,1,0:T(8,128)S(1)}, f32[2,24,256]{2,1,0:T(8,128)S(1)}, u32[]{:S(2)}, u32[]{:S(2)}) collective-permute-start(f32[2,24,256]{2,1,0:T(8,128)S(1)} %get-tuple-element.16.refs_6_), channel_id=1, source_target_pairs={{0,16},{4,20},{8,24},{12,28},{16,0},{20,4},{24,8},{28,12},{1,17},{... | collective-permute-start | bytes 147464 | tf_op jit(solution)/shard_map/ppermute | solution.py:289
  17.6 4.1 %collective-permute-start.1 = (f32[2,24,256]{2,1,0:T(8,128)S(1)}, f32[2,24,256]{2,1,0:T(8,128)S(1)}, u32[]{:S(2)}, u32[]{:S(2)}) collective-permute-start(f32[2,24,256]{2,1,0:T(8,128)S(1)} %get-tuple-element.16.refs_6_), channel_id=1, source_target_pairs={{0,8},{4,12},{8,0},{12,4},{16,24},{20,28},{24,16},{28,20},{1,9},{5... | collective-permute-start | bytes 147464 | tf_op jit(solution)/shard_map/ppermute | solution.py:289
  30.4 3.6 %collective-permute-start.4 = (f32[4,128,128]{2,1,0:T(8,128)S(1)}, f32[4,128,128]{2,1,0:T(8,128)S(1)}, u32[]{:S(2)}, u32[]{:S(2)}) collective-permute-start(f32[4,128,128]{2,1,0:T(8,128)S(1)} %get-tuple-element.18), channel_id=1, source_target_pairs={{0,4},{4,0},{8,12},{12,8},{16,20},{20,16},{24,28},{28,24},{1,5},{5... | collective-permute-start | bytes 786440 | tf_op jit(solution)/shard_map/ppermute | solution.py:289
  30.5 16.1 %all-to-all-start = ((f32[8,3,16,512]{3,2,1,0:T(8,128)}), f32[8,3,16,512]{3,2,1,0:T(8,128)S(1)}, u32[]{:S(2)}, u32[]{:S(2)}) async-start(f32[8,3,16,512]{3,2,1,0:T(8,128)} %get-tuple-element.19), calls=%async_computation | async-start | bytes 1572864 | tf_op jit(solution)/shard_map/all_to_all | solution.py:372
  34.1 4.5 %collective-permute-start.5 = (f32[128,128]{1,0:T(8,128)S(1)}, f32[128,128]{1,0:T(8,128)S(1)}, u32[]{:S(2)}, u32[]{:S(2)}) collective-permute-start(f32[128,128]{1,0:T(8,128)S(1)} %get-tuple-element.20), channel_id=1, source_target_pairs={{0,1},{1,0},{2,3},{3,2},{4,5},{5,4},{6,7},{7,6},{8,9},{9,8},{10,11... | collective-permute-start | bytes 196616 | tf_op jit(solution)/shard_map/ppermute | solution.py:289
  35.7 6.7 %collective-permute-start.7 = (f32[128,128]{1,0:T(8,128)S(1)}, f32[128,128]{1,0:T(8,128)S(1)}, u32[]{:S(2)}, u32[]{:S(2)}) collective-permute-start(f32[128,128]{1,0:T(8,128)S(1)} %get-tuple-element.21), channel_id=1, source_target_pairs={{0,3},{1,2},{2,1},{3,0},{4,7},{5,6},{6,5},{7,4},{8,11},{9,10},{10,... | collective-permute-start | bytes 196616 | tf_op jit(solution)/shard_map/ppermute | solution.py:289
  38.2 6.8 %collective-permute-start.6 = (f32[128,128]{1,0:T(8,128)S(1)}, f32[128,128]{1,0:T(8,128)S(1)}, u32[]{:S(2)}, u32[]{:S(2)}) collective-permute-start(f32[128,128]{1,0:T(8,128)S(1)} %get-tuple-element.22), channel_id=1, source_target_pairs={{0,2},{1,3},{2,0},{3,1},{4,6},{5,7},{6,4},{7,5},{8,10},{9,11},{10,... | collective-permute-start | bytes 196616 | tf_op jit(solution)/shard_map/ppermute | solution.py:289

commit v3 on v0

v3 whole, which is shorter than its diff:
```python
import math

import jax
import jax.numpy as jnp
from jax import lax
from jax.experimental import pallas as pl
from jax.experimental.pallas import tpu as pltpu
from jax.sharding import PartitionSpec as P

f32, bf16 = jnp.float32, jnp.bfloat16
SUB = 8
HALF = SUB // 2
WIDE = 256
MAGIC = 12582912.0
SIN = (3.141582022150658, -5.167142796368909, 2.541899027590427, -0.5546361970970186)
COS = (
    0.9999999534666683,
    -4.934792858675264,
    4.058411914167107,
    -1.3318801612488937,
    0.2196967986036905,
)
NT = (((1,), (1,)), ((), ()))
PARAMS = pltpu.CompilerParams(vmem_limit_bytes=24 * 1024 * 1024)
SCALARS = pl.BlockSpec(memory_space=pltpu.SMEM)
VECTORS = pl.BlockSpec(memory_space=pltpu.VMEM)
STAY = pl.BlockSpec(memory_space=pltpu.HBM)


def horner(z, coefs):
    acc = z * coefs[-1] + coefs[-2]
    for coef in coefs[-3::-1]:
        acc = acc * z + coef
    return acc


def split(value):
    high = value.astype(bf16)
    return high, (value - high.astype(f32)).astype(bf16)


def pair_rows(low, high):
    top = lax.broadcasted_iota(jnp.int32, low.shape, 0) < HALF
    first = jnp.where(top, low, pltpu.roll(high, HALF, 0))
    second = jnp.where(top, pltpu.roll(low, HALF, 0), high)
    return first, second


def tile(i, count=1):
    return pl.ds(pl.multiple_of(i * (count * SUB), count * SUB), count * SUB)


def tall(first, second):
    return jnp.concatenate([first, second], axis=0)


def call(body, name, ins, outs, scratch, *operands):
    return pl.pallas_call(
        body,
        in_specs=ins,
        out_specs=[VECTORS] * len(outs),
        out_shape=outs,
        scratch_shapes=scratch,
        compiler_params=PARAMS,
        name=name,
    )(*operands)


def prepare_kernel(place_ref, x_hbm, p_hbm, ph_hbm, x_ref, w_ref, r_ref, p_ref, ph_ref, sems):
    chunks, _, chans, wide = p_ref.shape
    core = place_ref[0] & 1
    inv = 1.0 / (2.0 * math.pi)

    def columns(chunk):
        return pl.ds(pl.multiple_of((core * chunks + chunk) * wide, wide), wide)

    fetch = [pltpu.make_async_copy(ph_hbm, ph_ref, sems.at[0])]
    for k in range(chunks):
        fetch.append(
            pltpu.make_async_copy(p_hbm.at[:, :, columns(k)], p_ref.at[k], sems.at[1 + k])
        )
    fetch_x = pltpu.make_async_copy(x_hbm, x_ref, sems.at[1 + chunks])
    for copy in fetch + [fetch_x]:
        copy.start()
    fetch[0].wait()
    row = lax.broadcasted_iota(jnp.int32, (chans, wide), 0)
    for chunk in range(chunks):
        fetch[1 + chunk].wait()
        for level in range(3):
            high, low = split(p_ref[chunk, level])
            w_ref[chunk, :chans, level * wide : (level + 1) * wide] = high
            w_ref[chunk, chans:, level * wide : (level + 1) * wide] = low
            high, low = split(p_ref[chunk, level] * inv)
            phase = ph_ref[level : level + 1, columns(chunk)] * inv
            phase0 = phase.astype(bf16).astype(f32)
            phase1 = (phase - phase0).astype(bf16).astype(f32)
            phase2 = phase - phase0 - phase1
            extra = jnp.where(row == 0, phase0, jnp.where(row == 1, phase1, phase2))
            extra = jnp.where(row < 3, extra, 0.0).astype(bf16)
            for k, part in enumerate((high, high, low, extra)):
                r_ref[chunk, level, chans * k : chans * (k + 1), :] = part
    fetch_x.wait()


def pairs_kernel(place_ref, x_ref, y_ref, xs_ref, xt_ref, flat_ref):
    rows, chans = flat_ref.shape
    core = place_ref[0] & 1
    lane = lax.broadcasted_iota(jnp.int32, (2 * SUB, chans), 1)
    ones = jnp.where(lane < 3, 1.0, 0.0).astype(bf16)

    def pairs(even_ref, odd_ref):
        def one(k, _):
            both = tall(*pair_rows(even_ref[tile(k), :], odd_ref[tile(k), :]))
            flat_ref[tile(k, 2), :] = both
            high, low = split(both)
            xs_ref[tile(k, 2), :] = jnp.concatenate([high, low, high, ones], axis=1)
            return 0

        lax.fori_loop(0, rows // (2 * SUB), one, 0, unroll=4)

    @pl.when(core == 0)
    def _():
        pairs(x_ref, y_ref)

    @pl.when(core == 1)
    def _():
        pairs(y_ref, x_ref)

    high, low = split(flat_ref[...].T)
    xt_ref[:chans, :] = high
    xt_ref[chans:, :] = low


def waves_kernel(amplitude, chunk, xs_ref, r_ref, c_ref, s_ref, loc_ref, snd_ref, ang_ref):
    _, rows, wide = ang_ref.shape
    root = math.sqrt(2.0 * amplitude)
    sin_coefs = [root * coef for coef in SIN]
    cos_coefs = [-root * coef for coef in COS]
    for level in range(3):
        ang_ref[level] = jnp.dot(xs_ref[...], r_ref[chunk, level], preferred_element_type=f32)

    def step(i, carry):
        s0, s1, s2, s01, s12, s012 = carry
        cosines = []
        for level in range(3):
            turn = ang_ref[level, tile(i), :]
            r = turn - ((turn + MAGIC) - MAGIC)
            z = r * r
            sine = r * horner(z, sin_coefs)
            cosine = horner(z, cos_coefs)
            wave = amplitude - sine * sine
            c_ref[level, tile(i), :] = wave
            s_ref[level, tile(i), :] = sine * cosine
            cosines.append(wave)
        c0, c1, c2 = cosines
        s012 = s012 + s01 * c2
        s12 = s12 + s1 * c2
        s01 = s01 + s0 * c1
        return (s0 + c0, s1 + c1, s2 + c2, s01, s12, s012)

    zero = jnp.zeros((SUB, wide), f32)
    sums = lax.fori_loop(0, rows // SUB, step, (zero,) * 6, unroll=4)
    for k in range(6):
        loc_ref[SUB * k : SUB * (k + 1), :] = sums[k]
    a0, a1, a2, a01, a12, a012 = [v[:HALF] for v in sums]
    b0, b1, b2, b01, b12, b012 = [v[HALF:] for v in sums]
    both = (
        a0 + b0,
        a1 + b1,
        a2 + b2,
        a01 + b01 + a0 * b1,
        a12 + b12 + a1 * b2,
        a012 + b012 + a0 * b12 + a01 * b2,
    )
    for k in range(6):
        snd_ref[HALF * k : HALF * (k + 1), :] = both[k]


def frequency_grads(xt_ref, sh_ref, sl_ref, gp_ref):
    count, _, each, wide = gp_ref.shape
    chans = count * each
    for level in range(3):
        cols = slice(level * wide, (level + 1) * wide)
        main = jnp.dot(xt_ref[...], sh_ref[:, cols], preferred_element_type=f32)
        rest = jnp.dot(xt_ref[:chans, :], sl_ref[:, cols], preferred_element_type=f32)
        grad = main[:chans] + main[chans:] + rest
        for d in range(count):
            gp_ref[d, level] = grad[each * d : each * (d + 1)]


def increment_grads(w_ref, sh_ref, sl_ref):
    chans = w_ref.shape[0] // 2
    main = lax.dot_general(sh_ref[...], w_ref[...], NT, preferred_element_type=f32)
    rest = lax.dot_general(sl_ref[...], w_ref[:chans, :], NT, preferred_element_type=f32)
    return main[:, :chans] + main[:, chans:] + rest


def slopes_kernel(sizes, chunk, place_ref, c_ref, s_ref, loc_ref, xt_ref, w_all_ref, *refs):
    n_tm, n_freq, batch, chunks = sizes
    chips = n_tm // 2
    got, refs = refs[:chips], refs[chips:]
    first, last = chunk == 0, chunk == chunks - 1
    before_ref = None
    if not first:
        before_ref, refs = refs[0], refs[1:]
    if last:
        gk_ref, gs_ref, sh_ref, sl_ref, all_ref, u1_ref, acc_ref, flat_ref = refs
    else:
        gp_ref, acc_ref, all_ref, u1_ref, sh_ref, sl_ref = refs
    rows, chans = acc_ref.shape
    wide = u1_ref.shape[1]
    w_ref = w_all_ref.at[chunk]
    core, chip = place_ref[0] & 1, place_ref[0] >> 1

    for d in range(chips):
        all_ref[jnp.bitwise_xor(chip, d)] = got[d][...]

    row = lax.broadcasted_iota(jnp.int32, (HALF, wide), 0)
    zero = jnp.zeros((HALF, wide), f32)
    weight = zero
    for b in range(batch):
        value = jnp.where(place_ref[2 + b] == 1, 2.0 / batch, -2.0 / batch)
        weight = jnp.where(row == b, value, weight)

    def sums_of(j):
        return [all_ref[j, HALF * k : HALF * (k + 1), :] for k in range(6)]

    def forward(j, carry):
        p0, p01, p012 = carry
        b0, b1, b2, b01, b12, b012 = sums_of(j)
        p012 = p012 + b012 + p0 * b12 + p01 * b2
        p01 = p01 + b01 + p0 * b1
        return (p0 + b0, p01, p012)

    def backward(step, carry):
        t1, t2, t12 = carry
        b0, b1, b2, b01, b12, b012 = sums_of(chips - 1 - step)
        t12 = t12 + b12 + b1 * t2
        return (t1 + b1, t2 + b2, t12)

    entry = lax.fori_loop(0, chip, forward, (zero,) * 3)
    e1, e2 = entry[:2]
    totals = lax.fori_loop(chip, chips, forward, entry)
    t1, t2, t12 = lax.fori_loop(0, chips - 1 - chip, backward, (zero,) * 3)
    seeds = [2.0 * weight * jnp.sum(weight * total, axis=0, keepdims=True) for total in totals]

    def local(k):
        value = loc_ref[SUB * k : SUB * (k + 1), :]
        return value[:HALF], value[HALF:]

    a0, _ = local(0)
    a1, b1 = local(1)
    _, b2 = local(2)
    a01, _ = local(3)
    _, b12 = local(4)
    front1 = tall(e1, e1 + a0)
    front2 = tall(e2, e2 + a01 + e1 * a1)
    tail2 = tall(t2 + b2, t2)
    tail1 = tall(t1 + b1, t1)
    tail12 = tall(t12 + b12 + b1 * t2, t12)
    d0, d1, d2 = [tall(seed, seed) for seed in seeds]
    adjoint1 = d1 + d2 * tail2
    adjoint0 = d0 + d1 * tail1 + d2 * tail12

    def fwd(pair, carry):
        f1, f2 = carry
        slopes = []
        for which in range(2):
            at = tile(2 * pair + which)
            u1_ref[at, :] = s_ref[1, at, :] * f1
            slopes.append(s_ref[2, at, :] * (d2 * f2))
            f2 = f2 + f1 * c_ref[1, at, :]
            f1 = f1 + c_ref[0, at, :]
        high, low = split(tall(*slopes))
        sh_ref[tile(pair, 2), 2 * wide :] = high
        sl_ref[tile(pair, 2), 2 * wide :] = low
        return f1, f2

    lax.fori_loop(0, rows // (2 * SUB), fwd, (front1, front2), unroll=2)

    def bwd(step, carry):
        g1, g0 = carry
        pair = rows // (2 * SUB) - 1 - step
        slope0, slope1 = [], []
        for which in (1, 0):
            at = tile(2 * pair + which)
            slope1.append(u1_ref[at, :] * g1)
            slope0.append(s_ref[0, at, :] * g0)
            g0 = g0 + g1 * c_ref[1, at, :]
            g1 = g1 + d2 * c_ref[2, at, :]
        for level, slopes in enumerate((slope0, slope1)):
            high, low = split(tall(*slopes[::-1]))
            sh_ref[tile(pair, 2), level * wide : (level + 1) * wide] = high
            sl_ref[tile(pair, 2), level * wide : (level + 1) * wide] = low
        return g1, g0

    lax.fori_loop(0, rows // (2 * SUB), bwd, (adjoint1, adjoint0), unroll=2)

    if not last:
        frequency_grads(xt_ref, sh_ref, sl_ref, gp_ref)
    total = increment_grads(w_ref, sh_ref, sl_ref)
    if not first:
        total = total + before_ref[...]
    acc_ref[...] = total
    if not last:
        return

    def one(k, _):
        even, odd = pair_rows(acc_ref[tile(2 * k), :], acc_ref[tile(2 * k + 1), :])
        flat_ref[0, tile(k), :] = even
        flat_ref[1, tile(k), :] = odd
        return 0

    lax.fori_loop(0, rows // (2 * SUB), one, 0, unroll=4)
    piece = rows // 2 // n_freq
    for j in range(n_freq):
        gk_ref[j] = flat_ref[core, piece * j : piece * (j + 1), :]
        gs_ref[j] = flat_ref[1 - core, piece * j : piece * (j + 1), :]


def swap(value, axis, distance):
    count = lax.axis_size(axis)
    return lax.ppermute(value, axis, [(i, i ^ distance) for i in range(count)])


def resident(value):
    return pltpu.with_memory_space_constraint(value, pltpu.HBM)


def on_device(increments, projections, phases, groups):
    steps, batch, chans = increments.shape
    freqs = phases.shape[1]
    n_tm, n_freq = lax.axis_size("tm"), lax.axis_size("freq")
    amplitude = math.sqrt(2.0 / (steps * n_tm))
    rows = 2 * steps * batch
    mine = freqs // 2
    wide = min(WIDE, mine)
    chunks = mine // wide
    each = chans // n_tm
    chips = n_tm // 2
    x = increments.reshape(rows // 2, chans)
    p = jnp.transpose(projections, (1, 0, 2))
    here = jnp.stack([lax.axis_index("tm"), lax.axis_index("freq")]).astype(jnp.int32)
    place = jnp.concatenate([here, groups])

    y = swap(x, "tm", 1)
    x, weights, turns = call(
        prepare_kernel,
        "prepare",
        [SCALARS] + [STAY] * 3,
        [
            pltpu.VMEM((rows // 2, chans), f32),
            pltpu.VMEM((chunks, 2 * chans, 3 * wide), bf16),
            pltpu.VMEM((chunks, 3, 4 * chans, wide), bf16),
        ],
        [
            pltpu.VMEM((chunks, 3, chans, wide), f32),
            pltpu.VMEM((3, freqs), f32),
            pltpu.SemaphoreType.DMA((2 + chunks,)),
        ],
        place,
        resident(x),
        resident(p),
        resident(phases),
    )
    xs, xt = call(
        pairs_kernel,
        "pairs",
        [SCALARS] + [VECTORS] * 2,
        [pltpu.VMEM((rows, 4 * chans), bf16), pltpu.VMEM((2 * chans, rows), bf16)],
        [pltpu.VMEM((rows, chans), f32)],
        place,
        x,
        y,
    )

    waves, got = [], []
    for chunk in range(chunks):

        def waves_body(*refs, chunk=chunk):
            waves_kernel(amplitude, chunk, *refs)

        *keep, own = call(
            waves_body,
            f"waves{chunk}",
            [VECTORS] * 2,
            [
                pltpu.VMEM((3, rows, wide), f32),
                pltpu.VMEM((3, rows, wide), f32),
                pltpu.VMEM((6 * SUB, wide), f32),
                jax.ShapeDtypeStruct((3 * SUB, wide), f32),
            ],
            [pltpu.VMEM((3, rows, wide), f32)],
            xs,
            turns,
        )
        waves.append(keep)
        got.append([own] + [swap(own, "tm", 2 * d) for d in range(1, chips)])

    parts = []
    before = []
    pshape = jax.ShapeDtypeStruct((n_tm, 3, each, wide), f32)
    gshape = jax.ShapeDtypeStruct((n_freq, rows // 2 // n_freq, chans), f32)
    slopes = [pltpu.VMEM((rows, 3 * wide), bf16)] * 2
    scratch = [pltpu.VMEM((chips, 3 * SUB, wide), f32), pltpu.VMEM((rows, wide), f32)]
    total = pltpu.VMEM((rows, chans), f32)
    for chunk in range(chunks):
        last = chunk == chunks - 1

        def slopes_body(*refs, chunk=chunk):
            slopes_kernel((n_tm, n_freq, batch, chunks), chunk, *refs)

        operands = [place, *waves[chunk], xt, weights, *got[chunk], *before]
        outs = call(
            slopes_body,
            f"slopes{chunk}",
            [SCALARS] + [VECTORS] * (len(operands) - 1),
            [gshape, gshape] + slopes if last else [pshape, total],
            scratch + ([total, pltpu.VMEM((2, rows // 2, chans), f32)] if last else slopes),
            *operands,
        )
        if last:
            kept, sent, high, low = outs
        else:
            parts.append(lax.all_to_all(outs[0], "tm", 0, 0, tiled=True))
            before = [outs[1]]

    other = swap(sent, "tm", 1)
    (final,) = call(frequency_grads, "last", [VECTORS] * 3, [pshape], [], xt, high, low)
    pieces, final = lax.optimization_barrier((kept + other, final))
    pieces = lax.all_to_all(pieces, "freq", 0, 0, tiled=True)
    parts.append(lax.all_to_all(final, "tm", 0, 0, tiled=True))

    grad_increments = jnp.sum(pieces, axis=0).reshape(steps // n_freq, batch, chans)
    sums = [jnp.sum(part.reshape(chips, 2, 3, each, wide), axis=0) for part in parts]
    total = jnp.concatenate(sums, axis=-1)
    grad_projections = jnp.transpose(total, (2, 1, 0, 3)).reshape(each, 3, freqs)
    return (grad_increments, grad_projections)


def solution(mesh):
    placed = (P("tm", None, None), P(None, None, "freq"), P(None, "freq"), P())
    return jax.shard_map(
        on_device,
        mesh=mesh,
        in_specs=placed,
        out_specs=(P(("tm", "freq"), None, None), P("tm", None, "freq")),
        check_vma=False,
    )
```

time: 282 us -> 68.6 us (0.24)
  matrix products: 120 us -> 0 us
  blocking collectives: 61.2 us -> 10.9 us
  waiting for transfers between devices: 58.5 us -> 15 us
  Pallas kernels: 0 us -> 18.5 us
  starting transfers between devices: 0.08 us -> 17.3 us
  between operations: 16.6 us -> 0.75 us
  loops' own time: 13 us -> 0 us
  local copies, waits for them, and re-layouts: 9.34 us -> 2.55 us
    dot_general x13 -> x0, matrix products: 120 us -> none  [the longest x4 63.4 us: tiled_sum(): inner = jnp.einsum('ts,nsbf->ntbf', tri_mask, blocks, precision=highest)]
    unnamed x3 -> x0, waiting for transfers between devices: 58.5 us -> none
    all_gather x4 -> x0, blocking collectives: 37.8 us -> none  [prefix(): gathered = lax.all_gather(part, axis)]
    psum x1 -> x0, blocking collectives: 23.3 us -> none  [global_gaps(): return lax.psum(stacked, 'tm')]
    pallas_call x0 -> x7, Pallas kernels: none -> 18.5 us  [call(): pl.pallas_call(body, in_specs=ins, out_specs=[VECTORS] * len(outs), out_s...]
    another operation x4 -> x0, loops' own time: 13 us -> none  [prefix(): return lax.fori_loop(0, ahead, one, state)]
    all_to_all x0 -> x1, blocking collectives: none -> 10.9 us  [on_device(): parts.append(lax.all_to_all(final, 'tm', 0, 0, tiled=True))]
    all_to_all x0 -> x2, starting transfers between devices: none -> 8.96 us  [the longest x1 4.87 us: on_device(): pieces = lax.all_to_all(pieces, 'freq', 0, 0, tiled=True)]
  transfers between devices with their start and end apart: 2 -> 10, of which waited for: 1 -> 8; matrix products, arithmetic and copies ran while one was open for 8% -> 5% of each run, Pallas kernels for 0% -> 14%
where the time goes in v3:
time: 68.6 us; the launch traced here: 68.1 us
  Pallas kernels  18.5 us (27%)
  starting transfers between devices  17.3 us (25%)
  waiting for transfers between devices  15 us (22%)
  blocking collectives  10.9 us (16%)
  other arithmetic  3.18 us (5%)
  local copies, waits for them, and re-layouts  2.55 us (4%)
  between operations  0.75 us (1%)
    pallas_call x7, Pallas kernels, call(): pl.pallas_call(body, in_specs=ins, out_specs=[VECTORS] * len(outs), out_s...  18.5 us
    all_to_all x1, blocking collectives, on_device(): parts.append(lax.all_to_all(final, 'tm', 0, 0, tiled=True))  10.9 us
    ppermute x8, starting transfers between devices, swap(): return lax.ppermute(value, axis, [(i, i ^ distance) for i in range(count)])  8.33 us
    ppermute x8, waiting for transfers between devices, swap(): return lax.ppermute(value, axis, [(i, i ^ distance) for i in range(count)])  8.08 us
    all_to_all x1, waiting for transfers between devices, on_device(): pieces = lax.all_to_all(pieces, 'freq', 0, 0, tiled=True)  6.89 us
    all_to_all x1, starting transfers between devices, on_device(): pieces = lax.all_to_all(pieces, 'freq', 0, 0, tiled=True)  4.87 us
    all_to_all x1, starting transfers between devices, on_device(): parts.append(lax.all_to_all(outs[0], 'tm', 0, 0, tiled=True))  4.09 us
    unnamed x8, local copies, waits for them, and re-layouts  1.86 us
  transfers between devices with their start and end apart: 10, of which 8 were waited for; matrix products, arithmetic and copies ran while one was open for 5% of the time, Pallas kernels for 14%

profile of v3, /device:TPU:0, one launch (start us, length us, event | category | flops | bytes accessed | tf_op | source)
XLA Modules:
  0.0 68.1 jit_solution(13949043429844842032)
XLA Ops:
  1.1 0.7 %pad_add_fusion.place_ref.refs_0_ = s32[6]{0:T(128)S(1)} fusion(s32[4]{0:T(128)} %param.7, s32[1]{0:T(128)} %bitcast.1, s32[1]{0:T(128)} %bitcast), kind=kLoop, calls=%fused_computation.1 | loop fusion | flops 12 | bytes 48 | tf_op jit(solution)/shard_map/concatenate | solution.py:344
  1.9 1.9 %prepare.1 = (f32[512,128]{1,0:T(8,128)S(1)}, bf16[2,256,768]{2,1,0:T(8,128)(2,1)S(1)}, bf16[2,3,512,256]{3,2,1,0:T(8,128)(2,1)S(1)}) custom-call(s32[6]{0:T(128)S(1)} %pad_add_fusion.place_ref.refs_0_, f32[512,128]{1,0:T(8,128)} %bitcast.14, f32[3,128,1024]{2,1,0:T(8,128)} %bitcast.12, f32[3,1024]{1,0:T(4,128)} %ph_hbm.1), custom_call_target="tpu_custom_call" | custom-call | tf_op jit(solution)/shard_map/prepare/pallas_call | solution.py:58
  3.8 1.0 %pairs.1 = (bf16[1024,512]{1,0:T(8,128)(2,1)S(1)}, bf16[256,1024]{1,0:T(8,128)(2,1)S(1)}) custom-call(s32[6]{0:T(128)S(1)} %pad_add_fusion.place_ref.refs_0_, f32[512,128]{1,0:T(8,128)S(1)} %get-tuple-element.23.x_ref, f32[512,128]{1,0:T(8,128)S(1)} %collective-permute-done.y_ref), custom_call_target="tpu_custom_call" | custom-call | tf_op jit(solution)/shard_map/pairs/pallas_call | solution.py:58
  4.8 4.0 %waves0.1 = (f32[3,1024,256]{2,1,0:T(8,128)S(1)}, f32[3,1024,256]{2,1,0:T(8,128)S(1)}, f32[48,256]{1,0:T(8,128)S(1)}, f32[24,256]{1,0:T(8,128)S(1)}) custom-call(bf16[1024,512]{1,0:T(8,128)(2,1)S(1)} %get-tuple-element.24.refs_0_, bf16[2,3,512,256]{3,2,1,0:T(8,128)(2,1)S(1)} %get-tuple-element.25.refs_1_), custom_call_target="tpu_custom_call" | custom-call | tf_op jit(solution)/shard_map/waves0/pallas_call | solution.py:58
  8.8 3.5 %collective-permute-start.6 = (f32[24,256]{1,0:T(8,128)S(1)}, f32[24,256]{1,0:T(8,128)S(1)}, u32[]{:S(2)}, u32[]{:S(2)}) collective-permute-start(f32[24,256]{1,0:T(8,128)S(1)} %get-tuple-element.35.refs_6_), channel_id=1, source_target_pairs={{0,24},{4,28},{8,16},{12,20},{16,8},{20,12},{24,0},{28,4},{1,25},{... | collective-permute-start | bytes 73736 | tf_op jit(solution)/shard_map/ppermute | solution.py:323
  13.0 1.2 %collective-permute-done.6.refs_9_ = f32[24,256]{1,0:T(8,128)S(1)} collective-permute-done((f32[24,256]{1,0:T(8,128)S(1)}, f32[24,256]{1,0:T(8,128)S(1)}, u32[]{:S(2)}, u32[]{:S(2)}) %collective-permute-start.6) | collective-permute-done | bytes 24608 | tf_op jit(solution)/shard_map/ppermute | solution.py:323
  14.2 2.0 %collective-permute-done.5.refs_8_ = f32[24,256]{1,0:T(8,128)S(1)} collective-permute-done((f32[24,256]{1,0:T(8,128)S(1)}, f32[24,256]{1,0:T(8,128)S(1)}, u32[]{:S(2)}, u32[]{:S(2)}) %collective-permute-start.5) | collective-permute-done | bytes 24608 | tf_op jit(solution)/shard_map/ppermute | solution.py:323
  16.7 3.7 %slopes0.1 = (f32[8,3,16,256]{3,2,1,0:T(8,128)}, f32[1024,128]{1,0:T(8,128)S(1)}) custom-call(s32[6]{0:T(128)S(1)} %pad_add_fusion.place_ref.refs_0_, f32[3,1024,256]{2,1,0:T(8,128)S(1)} %get-tuple-element.32.refs_1_, f32[3,1024,256]{2,1,0:T(8,128)S(1)} %get-tuple-element.33.refs_2_, f32[48,256]{1,0:T(8,128)S(1)} %get-tuple-element.34.refs_3_, ...), custom_call_target="tpu_custom_call" | custom-call | tf_op jit(solution)/shard_map/slopes0/pallas_call | solution.py:58
  20.4 0.8 %copy-done.2 = f32[1024,128]{1,0:T(8,128)} copy-done((f32[1024,128]{1,0:T(8,128)}, f32[1024,128]{1,0:T(8,128)S(1)}, u32[]{:S(2)}) %copy-start.2) | copy-done | bytes 524312
  21.2 4.1 %all-to-all-start.1 = ((f32[8,3,16,256]{3,2,1,0:T(8,128)}), f32[8,3,16,256]{3,2,1,0:T(8,128)}, u32[]{:S(2)}, u32[]{:S(2)}) async-start(f32[8,3,16,256]{3,2,1,0:T(8,128)} %get-tuple-element.42), calls=%async_computation.1 | async-start | bytes 786432 | tf_op jit(solution)/shard_map/all_to_all | solution.py:425
  25.3 4.0 %waves1.1 = (f32[3,1024,256]{2,1,0:T(8,128)S(1)}, f32[3,1024,256]{2,1,0:T(8,128)S(1)}, f32[48,256]{1,0:T(8,128)S(1)}, f32[24,256]{1,0:T(8,128)S(1)}) custom-call(bf16[1024,512]{1,0:T(8,128)(2,1)S(1)} %get-tuple-element.24.refs_0_, bf16[2,3,512,256]{3,2,1,0:T(8,128)(2,1)S(1)} %get-tuple-element.25.refs_1_), custom_call_target="tpu_custom_call" | custom-call | tf_op jit(solution)/shard_map/waves1/pallas_call | solution.py:58
  29.3 2.9 %collective-permute-start.3 = (f32[24,256]{1,0:T(8,128)S(1)}, f32[24,256]{1,0:T(8,128)S(1)}, u32[]{:S(2)}, u32[]{:S(2)}) collective-permute-start(f32[24,256]{1,0:T(8,128)S(1)} %get-tuple-element.31.refs_6_), channel_id=1, source_target_pairs={{0,24},{4,28},{8,16},{12,20},{16,8},{20,12},{24,0},{28,4},{1,25},{... | collective-permute-start | bytes 73736 | tf_op jit(solution)/shard_map/ppermute | solution.py:323
  32.9 1.2 %collective-permute-done.3.refs_9_ = f32[24,256]{1,0:T(8,128)S(1)} collective-permute-done((f32[24,256]{1,0:T(8,128)S(1)}, f32[24,256]{1,0:T(8,128)S(1)}, u32[]{:S(2)}, u32[]{:S(2)}) %collective-permute-start.3) | collective-permute-done | bytes 24608 | tf_op jit(solution)/shard_map/ppermute | solution.py:323
  34.1 1.9 %collective-permute-done.2.refs_8_ = f32[24,256]{1,0:T(8,128)S(1)} collective-permute-done((f32[24,256]{1,0:T(8,128)S(1)}, f32[24,256]{1,0:T(8,128)S(1)}, u32[]{:S(2)}, u32[]{:S(2)}) %collective-permute-start.2) | collective-permute-done | bytes 24608 | tf_op jit(solution)/shard_map/ppermute | solution.py:323
  36.6 1.0 %copy-done.3 = f32[1024,128]{1,0:T(8,128)S(1)} copy-done((f32[1024,128]{1,0:T(8,128)S(1)}, f32[1024,128]{1,0:T(8,128)}, u32[]{:S(2)}) %copy-start.3) | copy-done | bytes 524312
  37.6 3.1 %slopes1.1 = (f32[4,128,128]{2,1,0:T(8,128)S(1)}, f32[4,128,128]{2,1,0:T(8,128)S(1)}, bf16[1024,768]{1,0:T(8,128)(2,1)S(1)}, bf16[1024,768]{1,0:T(8,128)(2,1)S(1)}) custom-call(s32[6]{0:T(128)S(1)} %pad_add_fusion.place_ref.refs_0_, f32[3,1024,256]{2,1,0:T(8,128)S(1)} %get-tuple-element.26.refs_1_, f32[3,1024,256]{2,1,0:T(8,128)S(1)} %get-tuple-element.27.refs_2_, ...), custom_call_target="tpu_custom_call" | custom-call | tf_op jit(solution)/shard_map/slopes1/pallas_call | solution.py:58
  40.8 0.8 %last.1 = f32[8,3,16,256]{3,2,1,0:T(8,128)S(1)} custom-call(bf16[256,1024]{1,0:T(8,128)(2,1)S(1)} %get-tuple-element.29.refs_4_.xt_ref, bf16[1024,768]{1,0:T(8,128)(2,1)S(1)} %get-tuple-element.39.sh_ref, bf16[1024,768]{1,0:T(8,128)(2,1)S(1)} %get-tuple-element.40.sl_ref), custom_call_target="tpu_custom_call" | custom-call | tf_op jit(solution)/shard_map/last/pallas_call | solution.py:58
  41.6 0.7 %collective-permute-done.7 = f32[4,128,128]{2,1,0:T(8,128)S(1)} collective-permute-done((f32[4,128,128]{2,1,0:T(8,128)S(1)}, f32[4,128,128]{2,1,0:T(8,128)S(1)}, u32[]{:S(2)}, u32[]{:S(2)}) %collective-permute-start.7) | collective-permute-done | bytes 262176 | tf_op jit(solution)/shard_map/ppermute | solution.py:323
  42.3 0.7 %add.3 = f32[4,128,128]{2,1,0:T(8,128)} add(f32[4,128,128]{2,1,0:T(8,128)S(1)} %get-tuple-element.37, f32[4,128,128]{2,1,0:T(8,128)S(1)} %collective-permute-done.7) | non-fusion elementwise | flops 65536 | bytes 786432 | tf_op jit(solution)/shard_map/add | solution.py:430
  43.1 10.9 %all_to_all.15 = f32[8,3,16,256]{3,2,1,0:T(8,128)S(1)} all-to-all(f32[8,3,16,256]{3,2,1,0:T(8,128)S(1)} %last.1), channel_id=1, replica_groups=mesh['tm'=8,'freq'=4] {'tm'}, dimensions={0} | all-to-all | bytes 786432 | tf_op jit(solution)/shard_map/all_to_all | solution.py:432
  53.9 4.9 %all-to-all-start = ((f32[4,128,128]{2,1,0:T(8,128)}), f32[4,128,128]{2,1,0:T(8,128)S(1)}, u32[]{:S(2)}, u32[]{:S(2)}) async-start(f32[4,128,128]{2,1,0:T(8,128)} %add.3), calls=%async_computation | async-start | bytes 524288 | tf_op jit(solution)/shard_map/all_to_all | solution.py:431
  58.8 1.0 %reduce_sum.28 = f32[2,3,16,256]{3,2,1,0:T(8,128)S(1)} reduce(f32[4,2,3,16,256]{4,3,2,1,0:T(8,128)} %bitcast.5, f32[]{:T(128)} %constant.10.clone.1), dimensions={0}, to_apply=%region_1.0 | reduce | flops 73728 | bytes 491524 | tf_op jit(solution)/shard_map/reduce_sum | solution.py:435
  59.9 0.7 %copy.7 = f32[2,3,2,8,512]{4,3,0,2,1:T(8,128)} copy(f32[2,3,2,8,512]{4,3,2,1,0:T(8,128)S(1)} %maximum_bitcast_fusion) | data formatting | bytes 393216 | tf_op jit(solution)/shard_map/reshape | solution.py:437
  60.6 6.9 %all-to-all-done = f32[4,128,128]{2,1,0:T(8,128)S(1)} async-done(((f32[4,128,128]{2,1,0:T(8,128)}), f32[4,128,128]{2,1,0:T(8,128)S(1)}, u32[]{:S(2)}, u32[]{:S(2)}) %all-to-all-start) | async-done | bytes 262176 | tf_op jit(solution)/shard_map/all_to_all | solution.py:431
  (19 shorter events, 3.7 us)
Async XLA Ops:
  0.6 3.2 %collective-permute-start = (f32[512,128]{1,0:T(8,128)}, f32[512,128]{1,0:T(8,128)S(1)}, u32[]{:S(2)}, u32[]{:S(2)}) collective-permute-start(f32[512,128]{1,0:T(8,128)} %bitcast.13), channel_id=1, source_target_pairs={{0,4},{4,0},{8,12},{12,8},{16,20},{20,16},{24,28},{28,24},{1,5},{5... | collective-permute-start | bytes 786440 | tf_op jit(solution)/shard_map/ppermute | solution.py:323
  3.8 16.6 %copy-start = (bf16[2,256,768]{2,1,0:T(8,128)(2,1)}, bf16[2,256,768]{2,1,0:T(8,128)(2,1)S(1)}, u32[]{:S(2)}) copy-start(bf16[2,256,768]{2,1,0:T(8,128)(2,1)S(1)} %get-tuple-element.30.refs_5_) | copy-start | bytes 2359300
  8.8 5.4 %collective-permute-start.6 = (f32[24,256]{1,0:T(8,128)S(1)}, f32[24,256]{1,0:T(8,128)S(1)}, u32[]{:S(2)}, u32[]{:S(2)}) collective-permute-start(f32[24,256]{1,0:T(8,128)S(1)} %get-tuple-element.35.refs_6_), channel_id=1, source_target_pairs={{0,24},{4,28},{8,16},{12,20},{16,8},{20,12},{24,0},{28,4},{1,25},{... | collective-permute-start | bytes 73736 | tf_op jit(solution)/shard_map/ppermute | solution.py:323
  12.4 3.8 %collective-permute-start.5 = (f32[24,256]{1,0:T(8,128)S(1)}, f32[24,256]{1,0:T(8,128)S(1)}, u32[]{:S(2)}, u32[]{:S(2)}) collective-permute-start(f32[24,256]{1,0:T(8,128)S(1)} %get-tuple-element.35.refs_6_), channel_id=1, source_target_pairs={{0,16},{4,20},{8,24},{12,28},{16,0},{20,4},{24,8},{28,12},{1,17},{... | collective-permute-start | bytes 73736 | tf_op jit(solution)/shard_map/ppermute | solution.py:323
  12.9 3.8 %collective-permute-start.4 = (f32[24,256]{1,0:T(8,128)S(1)}, f32[24,256]{1,0:T(8,128)S(1)}, u32[]{:S(2)}, u32[]{:S(2)}) collective-permute-start(f32[24,256]{1,0:T(8,128)S(1)} %get-tuple-element.35.refs_6_), channel_id=1, source_target_pairs={{0,8},{4,12},{8,0},{12,4},{16,24},{20,28},{24,16},{28,20},{1,9},{5... | collective-permute-start | bytes 73736 | tf_op jit(solution)/shard_map/ppermute | solution.py:323
  20.4 0.8 %copy-start.2 = (f32[1024,128]{1,0:T(8,128)}, f32[1024,128]{1,0:T(8,128)S(1)}, u32[]{:S(2)}) copy-start(f32[1024,128]{1,0:T(8,128)S(1)} %get-tuple-element.36.refs_10_) | copy-start | bytes 1572868
  21.2 21.9 %all-to-all-start.1 = ((f32[8,3,16,256]{3,2,1,0:T(8,128)}), f32[8,3,16,256]{3,2,1,0:T(8,128)}, u32[]{:S(2)}, u32[]{:S(2)}) async-start(f32[8,3,16,256]{3,2,1,0:T(8,128)} %get-tuple-element.42), calls=%async_computation.1 | async-start | bytes 786432 | tf_op jit(solution)/shard_map/all_to_all | solution.py:425
  25.3 11.3 %copy-start.1 = (bf16[2,256,768]{2,1,0:T(8,128)(2,1)S(1)}, bf16[2,256,768]{2,1,0:T(8,128)(2,1)}, u32[]{:S(2)}) copy-start(bf16[2,256,768]{2,1,0:T(8,128)(2,1)} %copy-done) | copy-start | bytes 2359300
  29.3 4.8 %collective-permute-start.3 = (f32[24,256]{1,0:T(8,128)S(1)}, f32[24,256]{1,0:T(8,128)S(1)}, u32[]{:S(2)}, u32[]{:S(2)}) collective-permute-start(f32[24,256]{1,0:T(8,128)S(1)} %get-tuple-element.31.refs_6_), channel_id=1, source_target_pairs={{0,24},{4,28},{8,16},{12,20},{16,8},{20,12},{24,0},{28,4},{1,25},{... | collective-permute-start | bytes 73736 | tf_op jit(solution)/shard_map/ppermute | solution.py:323
  32.2 3.8 %collective-permute-start.2 = (f32[24,256]{1,0:T(8,128)S(1)}, f32[24,256]{1,0:T(8,128)S(1)}, u32[]{:S(2)}, u32[]{:S(2)}) collective-permute-start(f32[24,256]{1,0:T(8,128)S(1)} %get-tuple-element.31.refs_6_), channel_id=1, source_target_pairs={{0,16},{4,20},{8,24},{12,28},{16,0},{20,4},{24,8},{28,12},{1,17},{... | collective-permute-start | bytes 73736 | tf_op jit(solution)/shard_map/ppermute | solution.py:323
  32.8 3.8 %collective-permute-start.1 = (f32[24,256]{1,0:T(8,128)S(1)}, f32[24,256]{1,0:T(8,128)S(1)}, u32[]{:S(2)}, u32[]{:S(2)}) collective-permute-start(f32[24,256]{1,0:T(8,128)S(1)} %get-tuple-element.31.refs_6_), channel_id=1, source_target_pairs={{0,8},{4,12},{8,0},{12,4},{16,24},{20,28},{24,16},{28,20},{1,9},{5... | collective-permute-start | bytes 73736 | tf_op jit(solution)/shard_map/ppermute | solution.py:323
  36.6 1.0 %copy-start.3 = (f32[1024,128]{1,0:T(8,128)S(1)}, f32[1024,128]{1,0:T(8,128)}, u32[]{:S(2)}) copy-start(f32[1024,128]{1,0:T(8,128)} %copy-done.2) | copy-start | bytes 1572868
  40.7 1.6 %collective-permute-start.7 = (f32[4,128,128]{2,1,0:T(8,128)S(1)}, f32[4,128,128]{2,1,0:T(8,128)S(1)}, u32[]{:S(2)}, u32[]{:S(2)}) collective-permute-start(f32[4,128,128]{2,1,0:T(8,128)S(1)} %get-tuple-element.38), channel_id=1, source_target_pairs={{0,4},{4,0},{8,12},{12,8},{16,20},{20,16},{24,28},{28,24},{1,5},{5... | collective-permute-start | bytes 786440 | tf_op jit(solution)/shard_map/ppermute | solution.py:323
  53.9 13.5 %all-to-all-start = ((f32[4,128,128]{2,1,0:T(8,128)}), f32[4,128,128]{2,1,0:T(8,128)S(1)}, u32[]{:S(2)}, u32[]{:S(2)}) async-start(f32[4,128,128]{2,1,0:T(8,128)} %add.3), calls=%async_computation | async-start | bytes 524288 | tf_op jit(solution)/shard_map/all_to_all | solution.py:431

commit v4 on v2

v4 whole, which is shorter than its diff:
```python
import math

import jax
import jax.numpy as jnp
from jax import lax
from jax.experimental import pallas as pl
from jax.experimental.pallas import tpu as pltpu
from jax.sharding import PartitionSpec as P

f32, bf16 = jnp.float32, jnp.bfloat16
SUB = 8
HALF = SUB // 2
WIDE = 256
MAGIC = 12582912.0
SIN = (3.141582022150658, -5.167142796368909, 2.541899027590427, -0.5546361970970186)
COS = (
    0.9999999534666683,
    -4.934792858675264,
    4.058411914167107,
    -1.3318801612488937,
    0.2196967986036905,
)
NT = (((1,), (1,)), ((), ()))
PARAMS = pltpu.CompilerParams(vmem_limit_bytes=24 * 1024 * 1024)
VECTORS = pl.BlockSpec(memory_space=pltpu.VMEM)
STAY = pl.BlockSpec(memory_space=pltpu.HBM)


def horner(z, coefs):
    acc = z * coefs[-1] + coefs[-2]
    for coef in coefs[-3::-1]:
        acc = acc * z + coef
    return acc


def split(value):
    high = value.astype(bf16)
    return high, (value - high.astype(f32)).astype(bf16)


def pair_rows(low, high):
    top = lax.broadcasted_iota(jnp.int32, low.shape, 0) < HALF
    first = jnp.where(top, low, pltpu.roll(high, HALF, 0))
    second = jnp.where(top, pltpu.roll(low, HALF, 0), high)
    return first, second


def tile(i, count=1):
    return pl.ds(pl.multiple_of(i * (count * SUB), count * SUB), count * SUB)


def tall(first, second):
    return jnp.concatenate([first, second], axis=0)


def call(body, name, micros, ins, outs, scratch, *operands):
    return pl.pallas_call(
        body,
        in_specs=ins,
        out_specs=[VECTORS] * len(outs),
        out_shape=outs,
        scratch_shapes=scratch,
        compiler_params=PARAMS,
        cost_estimate=pl.CostEstimate(
            flops=int(micros * 1.1e9), bytes_accessed=int(micros * 3e6), transcendentals=0
        ),
        name=name,
    )(*operands)


def prepare_kernel(x_hbm, p_hbm, ph_hbm, g_hbm, x_ref, w_ref, r_ref, weight_ref, *rest):
    p_ref, ph_ref, g_ref, sems = rest
    chunks, _, chans, wide = p_ref.shape
    batch = g_ref.shape[0]
    core = lax.axis_index("tm") & 1
    inv = 1.0 / (2.0 * math.pi)

    def columns(chunk):
        return pl.ds(pl.multiple_of((core * chunks + chunk) * wide, wide), wide)

    fetch = [pltpu.make_async_copy(ph_hbm, ph_ref, sems.at[0])]
    for k in range(chunks):
        fetch.append(
            pltpu.make_async_copy(p_hbm.at[:, :, columns(k)], p_ref.at[k], sems.at[1 + k])
        )
    fetch_x = pltpu.make_async_copy(x_hbm, x_ref, sems.at[1 + chunks])
    fetch_g = pltpu.make_async_copy(g_hbm, g_ref, sems.at[2 + chunks])
    for copy in fetch + [fetch_x, fetch_g]:
        copy.start()
    fetch[0].wait()
    row = lax.broadcasted_iota(jnp.int32, (chans, wide), 0)
    for chunk in range(chunks):
        fetch[1 + chunk].wait()
        for level in range(3):
            cols = slice((3 * chunk + level) * wide, (3 * chunk + level + 1) * wide)
            high, low = split(p_ref[chunk, level])
            w_ref[:chans, cols] = high
            w_ref[chans:, cols] = low
            high, low = split(p_ref[chunk, level] * inv)
            phase = ph_ref[level : level + 1, columns(chunk)] * inv
            phase0 = phase.astype(bf16).astype(f32)
            phase1 = (phase - phase0).astype(bf16).astype(f32)
            phase2 = phase - phase0 - phase1
            extra = jnp.where(row == 0, phase0, jnp.where(row == 1, phase1, phase2))
            extra = jnp.where(row < 3, extra, 0.0).astype(bf16)
            for k, part in enumerate((high, high, low, extra)):
                r_ref[chans * k : chans * (k + 1), cols] = part
    fetch_g.wait()
    row = lax.broadcasted_iota(jnp.int32, weight_ref.shape, 0)
    weight = jnp.zeros(weight_ref.shape, f32)
    for b in range(batch):
        value = jnp.where(g_ref[b] == 1, 2.0 / batch, -2.0 / batch)
        weight = jnp.where(row == b, value, weight)
    weight_ref[...] = weight
    fetch_x.wait()


def turn_kernel(flat_ref, xt_ref):
    chans = flat_ref.shape[1]
    high, low = split(flat_ref[...].T)
    xt_ref[:chans, :] = high
    xt_ref[chans:, :] = low


def waves_kernel(amplitude, wide, x_ref, y_ref, r_ref, *rest):
    c_ref, s_ref, loc_ref, snd_ref, flat_ref, xs_ref, ang_ref = rest
    rows, chans = flat_ref.shape
    chunks = c_ref.shape[0]
    core = lax.axis_index("tm") & 1
    root = math.sqrt(2.0 * amplitude)
    sin_coefs = [root * coef for coef in SIN]
    cos_coefs = [-root * coef for coef in COS]
    lane = lax.broadcasted_iota(jnp.int32, (2 * SUB, chans), 1)
    ones = jnp.where(lane < 3, 1.0, 0.0).astype(bf16)

    def pairs(even_ref, odd_ref):
        def one(k, _):
            both = tall(*pair_rows(even_ref[tile(k), :], odd_ref[tile(k), :]))
            flat_ref[tile(k, 2), :] = both
            high, low = split(both)
            xs_ref[tile(k, 2), :] = jnp.concatenate([high, low, high, ones], axis=1)
            return 0

        lax.fori_loop(0, rows // (2 * SUB), one, 0, unroll=8)

    @pl.when(core == 0)
    def _():
        pairs(x_ref, y_ref)

    @pl.when(core == 1)
    def _():
        pairs(y_ref, x_ref)

    ang_ref[...] = jnp.dot(xs_ref[...], r_ref[...], preferred_element_type=f32)
    zero = jnp.zeros((SUB, wide), f32)
    for chunk in range(chunks):
        here = slice(chunk * wide, (chunk + 1) * wide)

        def step(i, carry):
            s0, s1, s2, s01, s12, s012 = carry
            cosines = []
            for level in range(3):
                at = (3 * chunk + level) * wide
                turn = ang_ref[tile(i), at : at + wide]
                r = turn - ((turn + MAGIC) - MAGIC)
                z = r * r
                sine = r * horner(z, sin_coefs)
                cosine = horner(z, cos_coefs)
                wave = amplitude - sine * sine
                c_ref[chunk, level, tile(i), :] = wave
                s_ref[chunk, level, tile(i), :] = sine * cosine
                cosines.append(wave)
            c0, c1, c2 = cosines
            s012 = s012 + s01 * c2
            s12 = s12 + s1 * c2
            s01 = s01 + s0 * c1
            return (s0 + c0, s1 + c1, s2 + c2, s01, s12, s012)

        sums = lax.fori_loop(0, rows // SUB, step, (zero,) * 6, unroll=16)
        for k in range(6):
            loc_ref[SUB * k : SUB * (k + 1), here] = sums[k]
        a0, a1, a2, a01, a12, a012 = [v[:HALF] for v in sums]
        b0, b1, b2, b01, b12, b012 = [v[HALF:] for v in sums]
        both = (
            a0 + b0,
            a1 + b1,
            a2 + b2,
            a01 + b01 + a0 * b1,
            a12 + b12 + a1 * b2,
            a012 + b012 + a0 * b12 + a01 * b2,
        )
        for k in range(6):
            snd_ref[HALF * k : HALF * (k + 1), here] = both[k]


def grads_kernel(sizes, c_ref, s_ref, loc_ref, xt_ref, w_ref, weight_ref, *refs):
    n_tm, n_freq, wide = sizes
    chips = n_tm // 2
    got, refs = refs[:chips], refs[chips:]
    gp_ref, gk_ref, gs_ref, sh_ref, sl_ref, all_ref, u1_ref, acc_ref, flat_ref = refs
    rows, chans = acc_ref.shape
    chunks = c_ref.shape[0]
    me = lax.axis_index("tm")
    core, chip, z = me & 1, me >> 1, lax.axis_index("freq")

    for d in range(chips):
        all_ref[jnp.bitwise_xor(chip, d)] = got[d][...]

    weight = weight_ref[:HALF]
    zero = jnp.zeros(weight.shape, f32)

    def sums_of(j):
        return [all_ref[j, HALF * k : HALF * (k + 1), :] for k in range(6)]

    def forward(j, carry):
        p0, p01, p012 = carry
        b0, b1, b2, b01, b12, b012 = sums_of(j)
        p012 = p012 + b012 + p0 * b12 + p01 * b2
        p01 = p01 + b01 + p0 * b1
        return (p0 + b0, p01, p012)

    def backward(step, carry):
        t1, t2, t12 = carry
        b0, b1, b2, b01, b12, b012 = sums_of(chips - 1 - step)
        t12 = t12 + b12 + b1 * t2
        return (t1 + b1, t2 + b2, t12)

    entry = lax.fori_loop(0, chip, forward, (zero,) * 3)
    e1, e2 = entry[:2]
    totals = lax.fori_loop(chip, chips, forward, entry)
    t1, t2, t12 = lax.fori_loop(0, chips - 1 - chip, backward, (zero,) * 3)
    seeds = [2.0 * weight * jnp.sum(weight * total, axis=0, keepdims=True) for total in totals]

    def local(k):
        value = loc_ref[SUB * k : SUB * (k + 1), :]
        return value[:HALF], value[HALF:]

    a0, _ = local(0)
    a1, b1 = local(1)
    _, b2 = local(2)
    a01, _ = local(3)
    _, b12 = local(4)
    d0, d1, d2 = [tall(seed, seed) for seed in seeds]
    tail2 = tall(t2 + b2, t2)
    tail1 = tall(t1 + b1, t1)
    tail12 = tall(t12 + b12 + b1 * t2, t12)
    starts = (
        d2,
        tall(e1, e1 + a0),
        tall(e2, e2 + a01 + e1 * a1),
        d1 + d2 * tail2,
        d0 + d1 * tail1 + d2 * tail12,
    )

    for chunk in range(chunks):
        scale, front1, front2, adjoint1, adjoint0 = [
            v[:, chunk * wide : (chunk + 1) * wide] for v in starts
        ]

        def keep(pair, level, slopes):
            high, low = split(tall(*slopes))
            at = (3 * chunk + level) * wide
            sh_ref[tile(pair, 2), at : at + wide] = high
            sl_ref[tile(pair, 2), at : at + wide] = low

        def fwd(pair, carry):
            f1, f2 = carry
            slopes = []
            for which in range(2):
                at = tile(2 * pair + which)
                u1_ref[at, :] = s_ref[chunk, 1, at, :] * f1
                slopes.append(s_ref[chunk, 2, at, :] * (scale * f2))
                f2 = f2 + f1 * c_ref[chunk, 1, at, :]
                f1 = f1 + c_ref[chunk, 0, at, :]
            keep(pair, 2, slopes)
            return f1, f2

        lax.fori_loop(0, rows // (2 * SUB), fwd, (front1, front2), unroll=8)

        def bwd(step, carry):
            g1, g0 = carry
            pair = rows // (2 * SUB) - 1 - step
            slope0, slope1 = [], []
            for which in (1, 0):
                at = tile(2 * pair + which)
                slope1.append(u1_ref[at, :] * g1)
                slope0.append(s_ref[chunk, 0, at, :] * g0)
                g0 = g0 + g1 * c_ref[chunk, 1, at, :]
                g1 = g1 + scale * c_ref[chunk, 2, at, :]
            keep(pair, 0, slope0[::-1])
            keep(pair, 1, slope1[::-1])
            return g1, g0

        lax.fori_loop(0, rows // (2 * SUB), bwd, (adjoint1, adjoint0), unroll=8)

    main = jnp.dot(xt_ref[...], sh_ref[...], preferred_element_type=f32)
    rest = jnp.dot(xt_ref[:chans, :], sl_ref[...], preferred_element_type=f32)
    grad = main[:chans] + main[chans:] + rest
    each = chans // n_tm
    for chunk in range(chunks):
        for level in range(3):
            at = (3 * chunk + level) * wide
            for d in range(n_tm):
                gp_ref[d, level, :, chunk * wide : (chunk + 1) * wide] = grad[
                    each * d : each * (d + 1), at : at + wide
                ]

    main = lax.dot_general(sh_ref[...], w_ref[...], NT, preferred_element_type=f32)
    rest = lax.dot_general(sl_ref[...], w_ref[:chans, :], NT, preferred_element_type=f32)
    acc_ref[...] = main[:, :chans] + main[:, chans:] + rest

    def one(k, _):
        even, odd = pair_rows(acc_ref[tile(2 * k), :], acc_ref[tile(2 * k + 1), :])
        flat_ref[0, tile(k), :] = even
        flat_ref[1, tile(k), :] = odd
        return 0

    lax.fori_loop(0, rows // (2 * SUB), one, 0, unroll=8)
    piece = rows // 2 // n_freq
    for j in range(n_freq):
        at = pl.ds(pl.multiple_of(jnp.bitwise_xor(z, j) * piece, piece), piece)
        gk_ref[j] = flat_ref[core, at, :]
        gs_ref[j] = flat_ref[1 - core, at, :]


def swap(value, axis, distance):
    count = lax.axis_size(axis)
    return lax.ppermute(value, axis, [(i, i ^ distance) for i in range(count)])


def resident(value):
    return pltpu.with_memory_space_constraint(value, pltpu.HBM)


def on_device(increments, projections, phases, groups):
    steps, batch, chans = increments.shape
    freqs = phases.shape[1]
    n_tm, n_freq = lax.axis_size("tm"), lax.axis_size("freq")
    amplitude = math.sqrt(2.0 / (steps * n_tm))
    rows = 2 * steps * batch
    mine = freqs // 2
    wide = min(WIDE, mine)
    chunks = mine // wide
    each = chans // n_tm
    chips = n_tm // 2
    x = increments.reshape(rows // 2, chans)
    p = jnp.transpose(projections, (1, 0, 2))
    y = swap(x, "tm", 1)
    x, weights, turns, weight = call(
        prepare_kernel,
        "prepare",
        1.9,
        [STAY] * 4,
        [
            pltpu.VMEM((rows // 2, chans), f32),
            pltpu.VMEM((2 * chans, 3 * mine), bf16),
            pltpu.VMEM((4 * chans, 3 * mine), bf16),
            pltpu.VMEM((SUB, mine), f32),
        ],
        [
            pltpu.VMEM((chunks, 3, chans, wide), f32),
            pltpu.VMEM((3, freqs), f32),
            pltpu.SMEM((batch,), jnp.int32),
            pltpu.SemaphoreType.DMA((3 + chunks,)),
        ],
        resident(x),
        resident(p),
        resident(phases),
        resident(groups),
    )

    def waves_body(*refs):
        waves_kernel(amplitude, wide, *refs)

    cosines, sines, local, own, flat = call(
        waves_body,
        "waves",
        8.0,
        [VECTORS] * 3,
        [
            pltpu.VMEM((chunks, 3, rows, wide), f32),
            pltpu.VMEM((chunks, 3, rows, wide), f32),
            pltpu.VMEM((6 * SUB, mine), f32),
            jax.ShapeDtypeStruct((3 * SUB, mine), f32),
            pltpu.VMEM((rows, chans), f32),
        ],
        [pltpu.VMEM((rows, 4 * chans), bf16), pltpu.VMEM((rows, 3 * mine), f32)],
        x,
        y,
        turns,
    )
    got = [own] + [swap(own, "tm", 2 * d) for d in range(1, chips)]
    (xt,) = call(
        turn_kernel, "turn", 0.8, [VECTORS], [pltpu.VMEM((2 * chans, rows), bf16)], [], flat
    )

    def grads_body(*refs):
        grads_kernel((n_tm, n_freq, wide), *refs)

    gshape = jax.ShapeDtypeStruct((n_freq, rows // 2 // n_freq, chans), f32)
    parts, kept, sent = call(
        grads_body,
        "grads",
        7.0,
        [VECTORS] * (6 + chips),
        [jax.ShapeDtypeStruct((n_tm, 3, each, mine), f32), gshape, gshape],
        [
            pltpu.VMEM((rows, 3 * mine), bf16),
            pltpu.VMEM((rows, 3 * mine), bf16),
            pltpu.VMEM((chips, 3 * SUB, mine), f32),
            pltpu.VMEM((rows, wide), f32),
            pltpu.VMEM((rows, chans), f32),
            pltpu.VMEM((2, rows // 2, chans), f32),
        ],
        cosines,
        sines,
        local,
        xt,
        weights,
        weight,
        *got,
    )

    pieces = kept + swap(sent, "tm", 1)
    result = pieces[0]
    for j in range(1, n_freq):
        result = result + swap(pieces[j], "freq", j)
    grad_increments = result.reshape(steps // n_freq, batch, chans)
    parts = lax.all_to_all(parts, "tm", 0, 0, tiled=True)
    total = jnp.sum(parts.reshape(chips, 2, 3, each, mine), axis=0)
    grad_projections = jnp.transpose(total, (2, 1, 0, 3)).reshape(each, 3, freqs)
    return (grad_increments, grad_projections)


def solution(mesh):
    placed = (P("tm", None, None), P(None, None, "freq"), P(None, "freq"), P())
    return jax.shard_map(
        on_device,
        mesh=mesh,
        in_specs=placed,
        out_specs=(P(("tm", "freq"), None, None), P("tm", None, "freq")),
        check_vma=False,
    )
```

time: 47.5 us -> 42.1 us (0.89)
  Pallas kernels: 19.4 us -> 15.6 us
  waiting for transfers between devices: 12.2 us -> 11.3 us
  other arithmetic: 1.47 us -> 0.74 us
    pallas_call x2 -> x4, Pallas kernels: 19.4 us -> 15.6 us  [call(): pl.pallas_call(body, in_specs=ins, out_specs=[VECTORS] * len(outs), out_s...]
    ppermute x8, waiting for transfers between devices: 11.2 us -> 10.4 us  [swap(): return lax.ppermute(value, axis, [(i, i ^ distance) for i in range(count)])]
    concatenate x1 -> x0, other arithmetic: 0.73 us -> none  [on_device(): place = jnp.concatenate([here, groups])]
  transfers between devices with their start and end apart: 9 -> 9, of which waited for: 8 -> 7; matrix products, arithmetic and copies ran while one was open for 3% -> 2% of each run, Pallas kernels for 0% -> 4%
where the time goes in v4:
time: 42.1 us; the launch traced here: 41.8 us
  Pallas kernels  15.6 us (37%)
  starting transfers between devices  12.8 us (30%)
  waiting for transfers between devices  11.3 us (27%)
  other arithmetic  0.74 us (2%)
  local copies, waits for them, and re-layouts  0.71 us (2%)
  between operations  0.7 us (2%)
    pallas_call x4, Pallas kernels, call(): pl.pallas_call(body, in_specs=ins, out_specs=[VECTORS] * len(outs), out_s...  15.6 us
    ppermute x8, waiting for transfers between devices, swap(): return lax.ppermute(value, axis, [(i, i ^ distance) for i in range(count)])  10.4 us
    ppermute x8, starting transfers between devices, swap(): return lax.ppermute(value, axis, [(i, i ^ distance) for i in range(count)])  9.22 us
    all_to_all x1, starting transfers between devices, on_device(): parts = lax.all_to_all(parts, 'tm', 0, 0, tiled=True)  3.55 us
    all_to_all x1, waiting for transfers between devices, on_device(): parts = lax.all_to_all(parts, 'tm', 0, 0, tiled=True)  0.93 us
  transfers between devices with their start and end apart: 9, of which 7 were waited for; matrix products, arithmetic and copies ran while one was open for 2% of the time, Pallas kernels for 4%

profile of v4, /device:TPU:0, one launch (start us, length us, event | category | flops | bytes accessed | tf_op | source)
XLA Modules:
  0.0 41.8 jit_solution(17873980402958428583)
XLA Ops:
  0.6 0.5 %collective-permute-start = (f32[512,128]{1,0:T(8,128)}, f32[512,128]{1,0:T(8,128)S(1)}, u32[]{:S(2)}, u32[]{:S(2)}) collective-permute-start(f32[512,128]{1,0:T(8,128)} %bitcast.26), channel_id=1, source_target_pairs={{0,4},{4,0},{8,12},{12,8},{16,20},{20,16},{24,28},{28,24},{1,5},{5... | collective-permute-start | bytes 786440 | tf_op jit(solution)/shard_map/ppermute | solution.py:328
  1.1 1.4 %prepare.1 = (f32[512,128]{1,0:T(8,128)S(1)}, bf16[256,1536]{1,0:T(8,128)(2,1)S(1)}, bf16[512,1536]{1,0:T(8,128)(2,1)S(1)}, f32[8,512]{1,0:T(8,128)S(1)}) custom-call(f32[512,128]{1,0:T(8,128)} %bitcast.27, f32[3,128,1024]{2,1,0:T(8,128)} %bitcast.25, f32[3,1024]{1,0:T(4,128)} %ph_hbm.1, s32[4]{0:T(128)} %g_hbm.1), custom_call_target="tpu_custom_call" | custom-call | flops 2090000000 | bytes 5700000 | tf_op jit(solution)/shard_map/prepare/pallas_call | solution.py:57
  2.6 0.0 collective-permute-done.refs_1_
  2.6 7.9 %waves.1 = (f32[2,3,1024,256]{3,2,1,0:T(8,128)S(1)}, f32[2,3,1024,256]{3,2,1,0:T(8,128)S(1)}, f32[48,512]{1,0:T(8,128)S(1)}, f32[24,512]{1,0:T(8,128)S(1)}, f32[1024,128]{1,0:T(8,128)S(1)}) custom-call(f32[512,128]{1,0:T(8,128)S(1)} %get-tuple-element.14.refs_0_, f32[512,128]{1,0:T(8,128)S(1)} %collective-permute-done.refs_1_, ...), custom_call_target="tpu_custom_call" | custom-call | flops 8800000000 | bytes 24000000 | tf_op jit(solution)/shard_map/waves/pallas_call | solution.py:57
  10.4 3.8 %collective-permute-start.3 = (f32[24,512]{1,0:T(8,128)S(1)}, f32[24,512]{1,0:T(8,128)S(1)}, u32[]{:S(2)}, u32[]{:S(2)}) collective-permute-start(f32[24,512]{1,0:T(8,128)S(1)} %get-tuple-element.22.refs_6_), channel_id=1, source_target_pairs={{0,24},{4,28},{8,16},{12,20},{16,8},{20,12},{24,0},{28,4},{1,25},{... | collective-permute-start | bytes 147464 | tf_op jit(solution)/shard_map/ppermute | solution.py:328
  14.3 0.5 %collective-permute-start.2 = (f32[24,512]{1,0:T(8,128)S(1)}, f32[24,512]{1,0:T(8,128)S(1)}, u32[]{:S(2)}, u32[]{:S(2)}) collective-permute-start(f32[24,512]{1,0:T(8,128)S(1)} %get-tuple-element.22.refs_6_), channel_id=1, source_target_pairs={{0,16},{4,20},{8,24},{12,28},{16,0},{20,4},{24,8},{28,12},{1,17},{... | collective-permute-start | bytes 147464 | tf_op jit(solution)/shard_map/ppermute | solution.py:328
  14.8 0.1 collective-permute-start.1
  14.9 0.2 turn.1.refs_3_
  15.1 1.2 %collective-permute-done.3.refs_9_ = f32[24,512]{1,0:T(8,128)S(1)} collective-permute-done((f32[24,512]{1,0:T(8,128)S(1)}, f32[24,512]{1,0:T(8,128)S(1)}, u32[]{:S(2)}, u32[]{:S(2)}) %collective-permute-start.3) | collective-permute-done | bytes 49184 | tf_op jit(solution)/shard_map/ppermute | solution.py:328
  16.4 2.0 %collective-permute-done.2.refs_8_ = f32[24,512]{1,0:T(8,128)S(1)} collective-permute-done((f32[24,512]{1,0:T(8,128)S(1)}, f32[24,512]{1,0:T(8,128)S(1)}, u32[]{:S(2)}, u32[]{:S(2)}) %collective-permute-start.2) | collective-permute-done | bytes 49184 | tf_op jit(solution)/shard_map/ppermute | solution.py:328
  18.4 0.5 %collective-permute-done.1.refs_7_ = f32[24,512]{1,0:T(8,128)S(1)} collective-permute-done((f32[24,512]{1,0:T(8,128)S(1)}, f32[24,512]{1,0:T(8,128)S(1)}, u32[]{:S(2)}, u32[]{:S(2)}) %collective-permute-start.1) | collective-permute-done | bytes 49184 | tf_op jit(solution)/shard_map/ppermute | solution.py:328
  18.9 6.1 %grads.1 = (f32[8,3,16,512]{3,2,1,0:T(8,128)}, f32[4,128,128]{2,1,0:T(8,128)S(1)}, f32[4,128,128]{2,1,0:T(8,128)S(1)}) custom-call(f32[2,3,1024,256]{3,2,1,0:T(8,128)S(1)} %get-tuple-element.16.refs_0_, f32[2,3,1024,256]{3,2,1,0:T(8,128)S(1)} %get-tuple-element.17.refs_1_, f32[48,512]{1,0:T(8,128)S(1)} %get-tuple-element.18.refs_2_, ...), custom_call_target="tpu_custom_call" | custom-call | flops 7699999744 | bytes 21000000 | tf_op jit(solution)/shard_map/grads/pallas_call | solution.py:57
  25.0 0.0 collective-permute-start.4
  25.0 3.5 %all-to-all-start = ((f32[8,3,16,512]{3,2,1,0:T(8,128)}), f32[8,3,16,512]{3,2,1,0:T(8,128)S(1)}, u32[]{:S(2)}, u32[]{:S(2)}) async-start(f32[8,3,16,512]{3,2,1,0:T(8,128)} %get-tuple-element.25), calls=%async_computation | async-start | bytes 1572864 | tf_op jit(solution)/shard_map/all_to_all | solution.py:429
  28.6 1.6 %collective-permute-start.5 = (f32[128,128]{1,0:T(8,128)S(1)}, f32[128,128]{1,0:T(8,128)S(1)}, u32[]{:S(2)}, u32[]{:S(2)}) collective-permute-start(f32[128,128]{1,0:T(8,128)S(1)} %get-tuple-element.26), channel_id=1, source_target_pairs={{0,1},{1,0},{2,3},{3,2},{4,5},{5,4},{6,7},{7,6},{8,9},{9,8},{10,11... | collective-permute-start | bytes 196616 | tf_op jit(solution)/shard_map/ppermute | solution.py:328
  30.2 2.5 %collective-permute-start.7 = (f32[128,128]{1,0:T(8,128)S(1)}, f32[128,128]{1,0:T(8,128)S(1)}, u32[]{:S(2)}, u32[]{:S(2)}) collective-permute-start(f32[128,128]{1,0:T(8,128)S(1)} %get-tuple-element.27), channel_id=1, source_target_pairs={{0,3},{1,2},{2,1},{3,0},{4,7},{5,6},{6,5},{7,4},{8,11},{9,10},{10,... | collective-permute-start | bytes 196616 | tf_op jit(solution)/shard_map/ppermute | solution.py:328
  32.7 0.1 collective-permute-start.6
  32.8 0.3 collective-permute-done.5
  33.1 3.9 %collective-permute-done.7 = f32[128,128]{1,0:T(8,128)S(1)} collective-permute-done((f32[128,128]{1,0:T(8,128)S(1)}, f32[128,128]{1,0:T(8,128)S(1)}, u32[]{:S(2)}, u32[]{:S(2)}) %collective-permute-start.7) | collective-permute-done | bytes 65568 | tf_op jit(solution)/shard_map/ppermute | solution.py:328
  37.0 2.5 %collective-permute-done.6 = f32[128,128]{1,0:T(8,128)S(1)} collective-permute-done((f32[128,128]{1,0:T(8,128)S(1)}, f32[128,128]{1,0:T(8,128)S(1)}, u32[]{:S(2)}, u32[]{:S(2)}) %collective-permute-start.6) | collective-permute-done | bytes 65568 | tf_op jit(solution)/shard_map/ppermute | solution.py:328
  39.5 0.6 %fusion.2 = f32[128,128]{1,0:T(8,128)} fusion(f32[128,128]{1,0:T(8,128)S(1)} %collective-permute-done.7, f32[128,128]{1,0:T(8,128)S(1)} %collective-permute-done.6, f32[128,128]{1,0:T(8,128)S(1)} %collective-permute-done.5, f32[4,128,128]{2,1,0:T(8,128)S(1)} %add.12), kind=kLoop, calls=%fused_computation.6 | loop fusion | flops 49152 | bytes 327680 | tf_op jit(solution)/shard_map/add | solution.py:427
  40.1 0.9 %all-to-all-done = f32[8,3,16,512]{3,2,1,0:T(8,128)S(1)} async-done(((f32[8,3,16,512]{3,2,1,0:T(8,128)}), f32[8,3,16,512]{3,2,1,0:T(8,128)S(1)}, u32[]{:S(2)}, u32[]{:S(2)}) %all-to-all-start) | async-done | bytes 786464 | tf_op jit(solution)/shard_map/all_to_all | solution.py:429
  41.1 0.1 reduce_sum.9
  41.1 0.7 %copy.7 = f32[2,3,2,8,512]{4,3,0,2,1:T(8,128)} copy(f32[2,3,2,8,512]{4,3,2,1,0:T(8,128)S(1)} %bitcast.22) | data formatting | bytes 393216 | tf_op jit(solution)/shard_map/reshape | solution.py:431
  (3 shorter events, 0.0 us)
Async XLA Ops:
  0.6 1.9 %collective-permute-start = (f32[512,128]{1,0:T(8,128)}, f32[512,128]{1,0:T(8,128)S(1)}, u32[]{:S(2)}, u32[]{:S(2)}) collective-permute-start(f32[512,128]{1,0:T(8,128)} %bitcast.26), channel_id=1, source_target_pairs={{0,4},{4,0},{8,12},{12,8},{16,20},{20,16},{24,28},{28,24},{1,5},{5... | collective-permute-start | bytes 786440 | tf_op jit(solution)/shard_map/ppermute | solution.py:328
  10.4 5.9 %collective-permute-start.3 = (f32[24,512]{1,0:T(8,128)S(1)}, f32[24,512]{1,0:T(8,128)S(1)}, u32[]{:S(2)}, u32[]{:S(2)}) collective-permute-start(f32[24,512]{1,0:T(8,128)S(1)} %get-tuple-element.22.refs_6_), channel_id=1, source_target_pairs={{0,24},{4,28},{8,16},{12,20},{16,8},{20,12},{24,0},{28,4},{1,25},{... | collective-permute-start | bytes 147464 | tf_op jit(solution)/shard_map/ppermute | solution.py:328
  14.3 4.1 %collective-permute-start.2 = (f32[24,512]{1,0:T(8,128)S(1)}, f32[24,512]{1,0:T(8,128)S(1)}, u32[]{:S(2)}, u32[]{:S(2)}) collective-permute-start(f32[24,512]{1,0:T(8,128)S(1)} %get-tuple-element.22.refs_6_), channel_id=1, source_target_pairs={{0,16},{4,20},{8,24},{12,28},{16,0},{20,4},{24,8},{28,12},{1,17},{... | collective-permute-start | bytes 147464 | tf_op jit(solution)/shard_map/ppermute | solution.py:328
  14.8 4.1 %collective-permute-start.1 = (f32[24,512]{1,0:T(8,128)S(1)}, f32[24,512]{1,0:T(8,128)S(1)}, u32[]{:S(2)}, u32[]{:S(2)}) collective-permute-start(f32[24,512]{1,0:T(8,128)S(1)} %get-tuple-element.22.refs_6_), channel_id=1, source_target_pairs={{0,8},{4,12},{8,0},{12,4},{16,24},{20,28},{24,16},{28,20},{1,9},{5... | collective-permute-start | bytes 147464 | tf_op jit(solution)/shard_map/ppermute | solution.py:328
  25.0 3.6 %collective-permute-start.4 = (f32[4,128,128]{2,1,0:T(8,128)S(1)}, f32[4,128,128]{2,1,0:T(8,128)S(1)}, u32[]{:S(2)}, u32[]{:S(2)}) collective-permute-start(f32[4,128,128]{2,1,0:T(8,128)S(1)} %get-tuple-element.24), channel_id=1, source_target_pairs={{0,4},{4,0},{8,12},{12,8},{16,20},{20,16},{24,28},{28,24},{1,5},{5... | collective-permute-start | bytes 786440 | tf_op jit(solution)/shard_map/ppermute | solution.py:328
  25.0 16.1 %all-to-all-start = ((f32[8,3,16,512]{3,2,1,0:T(8,128)}), f32[8,3,16,512]{3,2,1,0:T(8,128)S(1)}, u32[]{:S(2)}, u32[]{:S(2)}) async-start(f32[8,3,16,512]{3,2,1,0:T(8,128)} %get-tuple-element.25), calls=%async_computation | async-start | bytes 1572864 | tf_op jit(solution)/shard_map/all_to_all | solution.py:429
  28.6 4.5 %collective-permute-start.5 = (f32[128,128]{1,0:T(8,128)S(1)}, f32[128,128]{1,0:T(8,128)S(1)}, u32[]{:S(2)}, u32[]{:S(2)}) collective-permute-start(f32[128,128]{1,0:T(8,128)S(1)} %get-tuple-element.26), channel_id=1, source_target_pairs={{0,1},{1,0},{2,3},{3,2},{4,5},{5,4},{6,7},{7,6},{8,9},{9,8},{10,11... | collective-permute-start | bytes 196616 | tf_op jit(solution)/shard_map/ppermute | solution.py:328
  30.2 6.7 %collective-permute-start.7 = (f32[128,128]{1,0:T(8,128)S(1)}, f32[128,128]{1,0:T(8,128)S(1)}, u32[]{:S(2)}, u32[]{:S(2)}) collective-permute-start(f32[128,128]{1,0:T(8,128)S(1)} %get-tuple-element.27), channel_id=1, source_target_pairs={{0,3},{1,2},{2,1},{3,0},{4,7},{5,6},{6,5},{7,4},{8,11},{9,10},{10,... | collective-permute-start | bytes 196616 | tf_op jit(solution)/shard_map/ppermute | solution.py:328
  32.7 6.8 %collective-permute-start.6 = (f32[128,128]{1,0:T(8,128)S(1)}, f32[128,128]{1,0:T(8,128)S(1)}, u32[]{:S(2)}, u32[]{:S(2)}) collective-permute-start(f32[128,128]{1,0:T(8,128)S(1)} %get-tuple-element.28), channel_id=1, source_target_pairs={{0,2},{1,3},{2,0},{3,1},{4,6},{5,7},{6,4},{7,5},{8,10},{9,11},{10,... | collective-permute-start | bytes 196616 | tf_op jit(solution)/shard_map/ppermute | solution.py:328

commit v5 on v4

--- a/solution.py
+++ b/solution.py
@@ -193,16 +193,8 @@
             snd_ref[HALF * k : HALF * (k + 1), here] = both[k]
 
 
-def grads_kernel(sizes, c_ref, s_ref, loc_ref, xt_ref, w_ref, weight_ref, *refs):
-    n_tm, n_freq, wide = sizes
-    chips = n_tm // 2
-    got, refs = refs[:chips], refs[chips:]
-    gp_ref, gk_ref, gs_ref, sh_ref, sl_ref, all_ref, u1_ref, acc_ref, flat_ref = refs
-    rows, chans = acc_ref.shape
-    chunks = c_ref.shape[0]
-    me = lax.axis_index("tm")
-    core, chip, z = me & 1, me >> 1, lax.axis_index("freq")
-
+def compose(chips, loc_ref, weight_ref, got, all_ref):
+    chip = lax.axis_index("tm") >> 1
     for d in range(chips):
         all_ref[jnp.bitwise_xor(chip, d)] = got[d][...]
 
@@ -244,7 +236,7 @@
     tail2 = tall(t2 + b2, t2)
     tail1 = tall(t1 + b1, t1)
     tail12 = tall(t12 + b12 + b1 * t2, t12)
-    starts = (
+    return (
         d2,
         tall(e1, e1 + a0),
         tall(e2, e2 + a01 + e1 * a1),
@@ -252,62 +244,107 @@
         d0 + d1 * tail1 + d2 * tail12,
     )
 
-    for chunk in range(chunks):
-        scale, front1, front2, adjoint1, adjoint0 = [
-            v[:, chunk * wide : (chunk + 1) * wide] for v in starts
-        ]
-
-        def keep(pair, level, slopes):
-            high, low = split(tall(*slopes))
-            at = (3 * chunk + level) * wide
-            sh_ref[tile(pair, 2), at : at + wide] = high
-            sl_ref[tile(pair, 2), at : at + wide] = low
-
-        def fwd(pair, carry):
-            f1, f2 = carry
-            slopes = []
-            for which in range(2):
-                at = tile(2 * pair + which)
-                u1_ref[at, :] = s_ref[chunk, 1, at, :] * f1
-                slopes.append(s_ref[chunk, 2, at, :] * (scale * f2))
-                f2 = f2 + f1 * c_ref[chunk, 1, at, :]
-                f1 = f1 + c_ref[chunk, 0, at, :]
-            keep(pair, 2, slopes)
-            return f1, f2
-
-        lax.fori_loop(0, rows // (2 * SUB), fwd, (front1, front2), unroll=8)
-
-        def bwd(step, carry):
-            g1, g0 = carry
-            pair = rows // (2 * SUB) - 1 - step
-            slope0, slope1 = [], []
-            for which in (1, 0):
-                at = tile(2 * pair + which)
-                slope1.append(u1_ref[at, :] * g1)
-                slope0.append(s_ref[chunk, 0, at, :] * g0)
-                g0 = g0 + g1 * c_ref[chunk, 1, at, :]
-                g1 = g1 + scale * c_ref[chunk, 2, at, :]
-            keep(pair, 0, slope0[::-1])
-            keep(pair, 1, slope1[::-1])
-            return g1, g0
-
-        lax.fori_loop(0, rows // (2 * SUB), bwd, (adjoint1, adjoint0), unroll=8)
-
+
+def slopes(chunk, wide, starts_ref, c_ref, s_ref, u1_ref, sh_ref, sl_ref):
+    rows = u1_ref.shape[0]
+    scale, front1, front2, adjoint1, adjoint0 = [
+        starts_ref[SUB * k : SUB * (k + 1), chunk * wide : (chunk + 1) * wide] for k in range(5)
+    ]
+
+    def keep(pair, level, values):
+        high, low = split(tall(*values))
+        sh_ref[tile(pair, 2), level * wide : (level + 1) * wide] = high
+        sl_ref[tile(pair, 2), level * wide : (level + 1) * wide] = low
+
+    def fwd(pair, carry):
+        f1, f2 = carry
+        slope2 = []
+        for which in range(2):
+            at = tile(2 * pair + which)
+            u1_ref[at, :] = s_ref[chunk, 1, at, :] * f1
+            slope2.append(s_ref[chunk, 2, at, :] * (scale * f2))
+            f2 = f2 + f1 * c_ref[chunk, 1, at, :]
+            f1 = f1 + c_ref[chunk, 0, at, :]
+        keep(pair, 2, slope2)
+        return f1, f2
+
+    lax.fori_loop(0, rows // (2 * SUB), fwd, (front1, front2), unroll=8)
+
+    def bwd(step, carry):
+        g1, g0 = carry
+        pair = rows // (2 * SUB) - 1 - step
+        slope0, slope1 = [], []
+        for which in (1, 0):
+            at = tile(2 * pair + which)
+            slope1.append(u1_ref[at, :] * g1)
+            slope0.append(s_ref[chunk, 0, at, :] * g0)
+            g0 = g0 + g1 * c_ref[chunk, 1, at, :]
+            g1 = g1 + scale * c_ref[chunk, 2, at, :]
+        keep(pair, 0, slope0[::-1])
+        keep(pair, 1, slope1[::-1])
+        return g1, g0
+
+    lax.fori_loop(0, rows // (2 * SUB), bwd, (adjoint1, adjoint0), unroll=8)
+
+
+def frequency_grads(bit, wide, xt_ref, sh_ref, sl_ref, gp_ref, keep_ref, send_ref):
+    n_tm, _, each, _ = gp_ref.shape
+    chans = n_tm * each
     main = jnp.dot(xt_ref[...], sh_ref[...], preferred_element_type=f32)
     rest = jnp.dot(xt_ref[:chans, :], sl_ref[...], preferred_element_type=f32)
     grad = main[:chans] + main[chans:] + rest
-    each = chans // n_tm
-    for chunk in range(chunks):
-        for level in range(3):
-            at = (3 * chunk + level) * wide
-            for d in range(n_tm):
-                gp_ref[d, level, :, chunk * wide : (chunk + 1) * wide] = grad[
-                    each * d : each * (d + 1), at : at + wide
-                ]
-
-    main = lax.dot_general(sh_ref[...], w_ref[...], NT, preferred_element_type=f32)
-    rest = lax.dot_general(sl_ref[...], w_ref[:chans, :], NT, preferred_element_type=f32)
-    acc_ref[...] = main[:, :chans] + main[:, chans:] + rest
+    for level in range(3):
+        for d in range(n_tm):
+            gp_ref[d, level] = grad[each * d : each * (d + 1), level * wide : (level + 1) * wide]
+    me = lax.axis_index("tm")
+    near = [j for j in range(n_tm // 2) if not j & bit]
+    for k, j in enumerate(near):
+        for core in range(2):
+            keep_ref[k, core] = gp_ref[jnp.bitwise_xor(me, 2 * j + core)]
+            send_ref[k, core] = gp_ref[jnp.bitwise_xor(me, 2 * (j | bit) + core)]
+
+
+def increment_grads(w_ref, at, sh_ref, sl_ref):
+    chans = w_ref.shape[0] // 2
+    cols = slice(at, at + sh_ref.shape[1])
+    main = lax.dot_general(sh_ref[...], w_ref[:, cols], NT, preferred_element_type=f32)
+    rest = lax.dot_general(sl_ref[...], w_ref[:chans, cols], NT, preferred_element_type=f32)
+    return main[:, :chans] + main[:, chans:] + rest
+
+
+def grads_kernel(sizes, chunk, bit, c_ref, s_ref, xt_ref, w_ref, *refs):
+    n_freq, chips, chunks, wide = sizes
+    first, last = chunk == 0, chunk == chunks - 1
+    if first:
+        loc_ref, weight_ref, *refs = refs
+        got, refs = refs[:chips], refs[chips:]
+    else:
+        starts_ref, before_ref, *refs = refs
+    keep_ref, send_ref, *refs = refs
+    if last:
+        gk_ref, gs_ref, *refs = refs
+    else:
+        acc_ref, *refs = refs
+    if first:
+        starts_ref, all_ref, *refs = refs
+    u1_ref, sh_ref, sl_ref, gp_ref, *refs = refs
+    if last:
+        acc_ref, flat_ref = refs
+    if first:
+        for k, value in enumerate(compose(chips, loc_ref, weight_ref, got, all_ref)):
+            starts_ref[SUB * k : SUB * (k + 1), :] = value
+
+    slopes(chunk, wide, starts_ref, c_ref, s_ref, u1_ref, sh_ref, sl_ref)
+    frequency_grads(bit, wide, xt_ref, sh_ref, sl_ref, gp_ref, keep_ref, send_ref)
+    total = increment_grads(w_ref, 3 * wide * chunk, sh_ref, sl_ref)
+    if not first:
+        total = total + before_ref[...]
+    acc_ref[...] = total
+    if not last:
+        return
+
+    rows, chans = acc_ref.shape
+    core, z = lax.axis_index("tm") & 1, lax.axis_index("freq")
 
     def one(k, _):
         even, odd = pair_rows(acc_ref[tile(2 * k), :], acc_ref[tile(2 * k + 1), :])
@@ -394,41 +431,69 @@
         turn_kernel, "turn", 0.8, [VECTORS], [pltpu.VMEM((2 * chans, rows), bf16)], [], flat
     )
 
-    def grads_body(*refs):
-        grads_kernel((n_tm, n_freq, wide), *refs)
-
+    bits = [1 << k for k in range(chips.bit_length() - 1)]
+    bshape = jax.ShapeDtypeStruct((chips // 2, 2, 3, each, wide), f32)
     gshape = jax.ShapeDtypeStruct((n_freq, rows // 2 // n_freq, chans), f32)
-    parts, kept, sent = call(
-        grads_body,
-        "grads",
-        7.0,
-        [VECTORS] * (6 + chips),
-        [jax.ShapeDtypeStruct((n_tm, 3, each, mine), f32), gshape, gshape],
-        [
-            pltpu.VMEM((rows, 3 * mine), bf16),
-            pltpu.VMEM((rows, 3 * mine), bf16),
-            pltpu.VMEM((chips, 3 * SUB, mine), f32),
+    total = pltpu.VMEM((rows, chans), f32)
+    starts = pltpu.VMEM((5 * SUB, mine), f32)
+    sums = []
+    for chunk in range(chunks):
+        order = bits if chunk % 2 == 0 else bits[::-1]
+        first, last = chunk == 0, chunk == chunks - 1
+
+        def grads_body(*refs, chunk=chunk, bit=order[0]):
+            grads_kernel((n_freq, chips, chunks, wide), chunk, bit, *refs)
+
+        operands = [cosines, sines, xt, weights]
+        operands += [local, weight, *got] if first else [entries, before]
+        scratch = [pltpu.VMEM((chips, 3 * SUB, mine), f32)] if first else []
+        scratch += [
             pltpu.VMEM((rows, wide), f32),
-            pltpu.VMEM((rows, chans), f32),
-            pltpu.VMEM((2, rows // 2, chans), f32),
-        ],
-        cosines,
-        sines,
-        local,
-        xt,
-        weights,
-        weight,
-        *got,
-    )
-
-    pieces = kept + swap(sent, "tm", 1)
-    result = pieces[0]
-    for j in range(1, n_freq):
-        result = result + swap(pieces[j], "freq", j)
-    grad_increments = result.reshape(steps // n_freq, batch, chans)
-    parts = lax.all_to_all(parts, "tm", 0, 0, tiled=True)
-    total = jnp.sum(parts.reshape(chips, 2, 3, each, mine), axis=0)
-    grad_projections = jnp.transpose(total, (2, 1, 0, 3)).reshape(each, 3, freqs)
+            pltpu.VMEM((rows, 3 * wide), bf16),
+            pltpu.VMEM((rows, 3 * wide), bf16),
+            pltpu.VMEM((n_tm, 3, each, wide), f32),
+        ]
+        scratch += [total, pltpu.VMEM((2, rows // 2, chans), f32)] if last else []
+        outs = call(
+            grads_body,
+            f"grads{chunk}",
+            3.5,
+            [VECTORS] * len(operands),
+            [bshape] * 2 + ([gshape] * 2 if last else [total]) + ([starts] if first else []),
+            scratch,
+            *operands,
+        )
+        kept, sent = outs[:2]
+        if last:
+            mine_kept, mine_sent = outs[2:4]
+        else:
+            before = outs[2]
+        if first:
+            entries = outs[-1]
+        sums.append((kept, sent, order))
+
+    pieces = mine_kept + swap(mine_sent, "tm", 1)
+    done = []
+    for kept, sent, order in sums:
+        blocks = kept + swap(sent, "tm", 2 * order[0])
+        for k, bit in enumerate(order[1:]):
+            left = order[k + 1 :]
+            place = sum(1 for b in left if b < bit)
+            halves = blocks.reshape((-1, 2, 1 << place) + blocks.shape[1:])
+            shape = (-1,) + blocks.shape[1:]
+            mate = swap(halves[:, 1].reshape(shape), "tm", 2 * bit)
+            blocks = halves[:, 0].reshape(shape) + mate
+        done.append(blocks[0])
+    for bit in [1 << k for k in range(n_freq.bit_length() - 1)]:
+        halves = pieces.reshape((-1, 2) + pieces.shape[1:])
+        pieces = halves[:, 0] + swap(halves[:, 1], "freq", bit)
+    grad_increments = pieces.reshape(steps // n_freq, batch, chans)
+
+    here = jnp.concatenate([blocks[0] for blocks in done], axis=-1)
+    away = swap(jnp.concatenate([blocks[1] for blocks in done], axis=-1), "tm", 1)
+    even = lax.axis_index("tm") & 1 == 0
+    low, high = jnp.where(even, here, away), jnp.where(even, away, here)
+    grad_projections = jnp.transpose(jnp.concatenate([low, high], axis=-1), (1, 0, 2))
     return (grad_increments, grad_projections)
 
 

time: 42.1 us -> 45.5 us (1.081)
  waiting for transfers between devices: 11.3 us -> 15.8 us
  other arithmetic: 0.74 us -> 1.5 us
  Pallas kernels: 15.6 us -> 14.9 us
  local copies, waits for them, and re-layouts: 0.71 us -> 0.05 us
  starting transfers between devices: 12.8 us -> 12.2 us
    ppermute x8 -> x12, waiting for transfers between devices: 10.4 us -> 15.8 us  [swap(): return lax.ppermute(value, axis, [(i, i ^ distance) for i in range(count)])]
    all_to_all x1 -> x0, starting transfers between devices: 3.55 us -> none  [on_device(): parts = lax.all_to_all(parts, 'tm', 0, 0, tiled=True)]
    ppermute x8 -> x12, starting transfers between devices: 9.22 us -> 12.2 us  [swap(): return lax.ppermute(value, axis, [(i, i ^ distance) for i in range(count)])]
    all_to_all x1 -> x0, waiting for transfers between devices: 0.93 us -> none  [on_device(): parts = lax.all_to_all(parts, 'tm', 0, 0, tiled=True)]
    pallas_call x4 -> x5, Pallas kernels: 15.6 us -> 14.9 us  [call(): pl.pallas_call(body, in_specs=ins, out_specs=[VECTORS] * len(outs), out_s...]
    reshape x1 -> x0, local copies, waits for them, and re-layouts: 0.69 us -> none  [on_device(): jnp.transpose(total, (2, 1, 0, 3)).reshape(each, 3, freqs)]
    transpose x0 -> x1, other arithmetic: none -> 0.69 us  [on_device(): jnp.transpose(jnp.concatenate([low, high], axis=-1), (1, 0, 2))]
  transfers between devices with their start and end apart: 9 -> 12, of which waited for: 7 -> 8; matrix products, arithmetic and copies ran while one was open for 2% -> 2% of each run, Pallas kernels for 4% -> 9%
where the time goes in v5:
time: 45.5 us; the launch traced here: 45.2 us
  waiting for transfers between devices  15.8 us (35%)
  Pallas kernels  14.9 us (33%)
  starting transfers between devices  12.2 us (27%)
  other arithmetic  1.5 us (3%)
  between operations  0.78 us (2%)
    ppermute x12, waiting for transfers between devices, swap(): return lax.ppermute(value, axis, [(i, i ^ distance) for i in range(count)])  15.8 us
    pallas_call x5, Pallas kernels, call(): pl.pallas_call(body, in_specs=ins, out_specs=[VECTORS] * len(outs), out_s...  14.9 us
    ppermute x12, starting transfers between devices, swap(): return lax.ppermute(value, axis, [(i, i ^ distance) for i in range(count)])  12.2 us
  transfers between devices with their start and end apart: 12, of which 8 were waited for; matrix products, arithmetic and copies ran while one was open for 2% of the time, Pallas kernels for 9%

profile of v5, /device:TPU:0, one launch (start us, length us, event | category | flops | bytes accessed | tf_op | source)
XLA Modules:
  0.0 45.2 jit_solution(12211103586581158814)
XLA Ops:
  0.6 0.5 %collective-permute-start = (f32[512,128]{1,0:T(8,128)}, f32[512,128]{1,0:T(8,128)S(1)}, u32[]{:S(2)}, u32[]{:S(2)}) collective-permute-start(f32[512,128]{1,0:T(8,128)} %bitcast.55), channel_id=1, source_target_pairs={{0,4},{4,0},{8,12},{12,8},{16,20},{20,16},{24,28},{28,24},{1,5},{5... | collective-permute-start | bytes 786440 | tf_op jit(solution)/shard_map/ppermute | solution.py:365
  1.1 1.4 %prepare.1 = (f32[512,128]{1,0:T(8,128)S(1)}, bf16[256,1536]{1,0:T(8,128)(2,1)S(1)}, bf16[512,1536]{1,0:T(8,128)(2,1)S(1)}, f32[8,512]{1,0:T(8,128)S(1)}) custom-call(f32[512,128]{1,0:T(8,128)} %bitcast.56, f32[3,128,1024]{2,1,0:T(8,128)} %bitcast.54, f32[3,1024]{1,0:T(4,128)} %ph_hbm.1, s32[4]{0:T(128)} %g_hbm.1), custom_call_target="tpu_custom_call" | custom-call | flops 2090000000 | bytes 5700000 | tf_op jit(solution)/shard_map/prepare/pallas_call | solution.py:57
  2.6 7.9 %waves.1 = (f32[2,3,1024,256]{3,2,1,0:T(8,128)S(1)}, f32[2,3,1024,256]{3,2,1,0:T(8,128)S(1)}, f32[48,512]{1,0:T(8,128)S(1)}, f32[24,512]{1,0:T(8,128)S(1)}, f32[1024,128]{1,0:T(8,128)S(1)}) custom-call(f32[512,128]{1,0:T(8,128)S(1)} %get-tuple-element.19.refs_0_, f32[512,128]{1,0:T(8,128)S(1)} %collective-permute-done.refs_1_, ...), custom_call_target="tpu_custom_call" | custom-call | flops 8800000000 | bytes 24000000 | tf_op jit(solution)/shard_map/waves/pallas_call | solution.py:57
  10.4 2.9 %collective-permute-start.1 = (f32[24,512]{1,0:T(8,128)S(1)}, f32[24,512]{1,0:T(8,128)S(1)}, u32[]{:S(2)}, u32[]{:S(2)}) collective-permute-start(f32[24,512]{1,0:T(8,128)S(1)} %get-tuple-element.27.refs_6_), channel_id=1, source_target_pairs={{0,8},{4,12},{8,0},{12,4},{16,24},{20,28},{24,16},{28,20},{1,9},{5... | collective-permute-start | bytes 147464 | tf_op jit(solution)/shard_map/ppermute | solution.py:365
  13.3 1.5 %collective-permute-start.2 = (f32[24,512]{1,0:T(8,128)S(1)}, f32[24,512]{1,0:T(8,128)S(1)}, u32[]{:S(2)}, u32[]{:S(2)}) collective-permute-start(f32[24,512]{1,0:T(8,128)S(1)} %get-tuple-element.27.refs_6_), channel_id=1, source_target_pairs={{0,16},{4,20},{8,24},{12,28},{16,0},{20,4},{24,8},{28,12},{1,17},{... | collective-permute-start | bytes 147464 | tf_op jit(solution)/shard_map/ppermute | solution.py:365
  14.8 0.2 turn.1.refs_2_
  15.1 0.3 collective-permute-done.1.refs_7_
  15.4 2.0 %collective-permute-done.2.refs_8_ = f32[24,512]{1,0:T(8,128)S(1)} collective-permute-done((f32[24,512]{1,0:T(8,128)S(1)}, f32[24,512]{1,0:T(8,128)S(1)}, u32[]{:S(2)}, u32[]{:S(2)}) %collective-permute-start.2) | collective-permute-done | bytes 49184 | tf_op jit(solution)/shard_map/ppermute | solution.py:365
  17.4 2.4 %collective-permute-done.3.refs_9_ = f32[24,512]{1,0:T(8,128)S(1)} collective-permute-done((f32[24,512]{1,0:T(8,128)S(1)}, f32[24,512]{1,0:T(8,128)S(1)}, u32[]{:S(2)}, u32[]{:S(2)}) %collective-permute-start.3) | collective-permute-done | bytes 49184 | tf_op jit(solution)/shard_map/ppermute | solution.py:365
  19.8 2.7 %grads0.1 = (f32[2,2,3,16,256]{4,3,2,1,0:T(8,128)S(1)}, f32[2,2,3,16,256]{4,3,2,1,0:T(8,128)S(1)}, f32[1024,128]{1,0:T(8,128)S(1)}, f32[40,512]{1,0:T(8,128)S(1)}) custom-call(f32[2,3,1024,256]{3,2,1,0:T(8,128)S(1)} %get-tuple-element.21.refs_0_, f32[2,3,1024,256]{3,2,1,0:T(8,128)S(1)} %get-tuple-element.22.refs_1_, bf16[256,1024]{1,0:T(8,128)(2,1)S(1)} %turn.1.refs_2_, ...), custom_call_target="tpu_custom_call" | custom-call | flops 3849999872 | bytes 10500000 | tf_op jit(solution)/shard_map/grads0/pallas_call | solution.py:57
  22.5 0.6 %collective-permute-start.7 = (f32[2,2,3,16,256]{4,3,2,1,0:T(8,128)S(1)}, f32[2,2,3,16,256]{4,3,2,1,0:T(8,128)S(1)}, u32[]{:S(2)}, u32[]{:S(2)}) collective-permute-start(f32[2,2,3,16,256]{4,3,2,1,0:T(8,128)S(1)} %get-tuple-element.33), channel_id=1, source_target_pairs={{0,8},{4,12},{8,0},{12,4},{16,24},{20,28},{24,16},{28,20},{1,9},{5... | collective-permute-start | bytes 589832 | tf_op jit(solution)/shard_map/ppermute | solution.py:365
  23.1 2.7 %grads1.1 = (f32[2,2,3,16,256]{4,3,2,1,0:T(8,128)S(1)}, f32[2,2,3,16,256]{4,3,2,1,0:T(8,128)S(1)}, f32[4,128,128]{2,1,0:T(8,128)S(1)}, f32[4,128,128]{2,1,0:T(8,128)S(1)}) custom-call(f32[2,3,1024,256]{3,2,1,0:T(8,128)S(1)} %get-tuple-element.21.refs_0_, f32[2,3,1024,256]{3,2,1,0:T(8,128)S(1)} %get-tuple-element.22.refs_1_, ...), custom_call_target="tpu_custom_call" | custom-call | flops 3849999872 | bytes 10500000 | tf_op jit(solution)/shard_map/grads1/pallas_call | solution.py:57
  25.8 0.1 collective-permute-start.9
  26.0 2.3 %collective-permute-done.7 = f32[2,2,3,16,256]{4,3,2,1,0:T(8,128)S(1)} collective-permute-done((f32[2,2,3,16,256]{4,3,2,1,0:T(8,128)S(1)}, f32[2,2,3,16,256]{4,3,2,1,0:T(8,128)S(1)}, u32[]{:S(2)}, u32[]{:S(2)}) %collective-permute-start.7) | collective-permute-done | bytes 196640 | tf_op jit(solution)/shard_map/ppermute | solution.py:365
  28.3 0.6 %collective-permute-start.8 = (f32[1,2,3,16,256]{4,3,2,1,0:T(8,128)S(1)}, f32[1,2,3,16,256]{4,3,2,1,0:T(8,128)S(1)}, u32[]{:S(2)}, u32[]{:S(2)}) collective-permute-start(f32[1,2,3,16,256]{4,3,2,1,0:T(8,128)S(1)} %slice_bitcast_fusion.4), channel_id=1, source_target_pairs={{0,16},{4,20},{8,24},{12,28},{16,0},{20,4},{24,8},{28,12},{1,17},{... | collective-permute-start | bytes 294920 | tf_op jit(solution)/shard_map/ppermute | solution.py:365
  28.9 3.7 %collective-permute-done.9 = f32[2,2,3,16,256]{4,3,2,1,0:T(8,128)S(1)} collective-permute-done((f32[2,2,3,16,256]{4,3,2,1,0:T(8,128)S(1)}, f32[2,2,3,16,256]{4,3,2,1,0:T(8,128)S(1)}, u32[]{:S(2)}, u32[]{:S(2)}) %collective-permute-start.9) | collective-permute-done | bytes 196640 | tf_op jit(solution)/shard_map/ppermute | solution.py:365
  32.6 1.6 %collective-permute-start.10 = (f32[1,2,3,16,256]{4,3,2,1,0:T(8,128)S(1)}, f32[1,2,3,16,256]{4,3,2,1,0:T(8,128)S(1)}, u32[]{:S(2)}, u32[]{:S(2)}) collective-permute-start(f32[1,2,3,16,256]{4,3,2,1,0:T(8,128)S(1)} %slice_bitcast_fusion.2), channel_id=1, source_target_pairs={{0,8},{4,12},{8,0},{12,4},{16,24},{20,28},{24,16},{28,20},{1,9},{5... | collective-permute-start | bytes 294920 | tf_op jit(solution)/shard_map/ppermute | solution.py:365
  34.3 1.6 %collective-permute-start.5 = (f32[2,128,128]{2,1,0:T(8,128)S(1)}, f32[2,128,128]{2,1,0:T(8,128)S(1)}, u32[]{:S(2)}, u32[]{:S(2)}) collective-permute-start(f32[2,128,128]{2,1,0:T(8,128)S(1)} %slice_bitcast_fusion), channel_id=1, source_target_pairs={{0,1},{1,0},{2,3},{3,2},{4,5},{5,4},{6,7},{7,6},{8,9},{9,8},{10,11... | collective-permute-start | bytes 393224 | tf_op jit(solution)/shard_map/ppermute | solution.py:365
  36.0 1.3 %collective-permute-done.10 = f32[1,2,3,16,256]{4,3,2,1,0:T(8,128)S(1)} collective-permute-done((f32[1,2,3,16,256]{4,3,2,1,0:T(8,128)S(1)}, f32[1,2,3,16,256]{4,3,2,1,0:T(8,128)S(1)}, u32[]{:S(2)}, u32[]{:S(2)}) %collective-permute-start.10) | collective-permute-done | bytes 98336 | tf_op jit(solution)/shard_map/ppermute | solution.py:365
  37.4 1.9 %collective-permute-done.5 = f32[2,128,128]{2,1,0:T(8,128)S(1)} collective-permute-done((f32[2,128,128]{2,1,0:T(8,128)S(1)}, f32[2,128,128]{2,1,0:T(8,128)S(1)}, u32[]{:S(2)}, u32[]{:S(2)}) %collective-permute-start.5) | collective-permute-done | bytes 131104 | tf_op jit(solution)/shard_map/ppermute | solution.py:365
  39.4 2.7 %collective-permute-start.6 = (f32[1,128,128]{2,1,0:T(8,128)S(1)}, f32[1,128,128]{2,1,0:T(8,128)S(1)}, u32[]{:S(2)}, u32[]{:S(2)}) collective-permute-start(f32[1,128,128]{2,1,0:T(8,128)S(1)} %slice_bitcast_fusion.6), channel_id=1, source_target_pairs={{0,2},{1,3},{2,0},{3,1},{4,6},{5,7},{6,4},{7,5},{8,10},{9,11},{10,... | collective-permute-start | bytes 196616 | tf_op jit(solution)/shard_map/ppermute | solution.py:365
  42.0 0.7 %maximum_bitcast_fusion = f32[16,3,1024]{2,0,1:T(8,128)} fusion(f32[3,16,512]{2,1,0:T(8,128)S(1)} %get-tuple-element.39, f32[3,16,512]{2,1,0:T(8,128)S(1)} %get-tuple-element.38), kind=kLoop, calls=%fused_computation | loop fusion | flops 49152 | bytes 393216 | tf_op jit(solution)/shard_map/transpose | solution.py:496
  42.7 1.9 %collective-permute-done.6 = f32[1,128,128]{2,1,0:T(8,128)S(1)} collective-permute-done((f32[1,128,128]{2,1,0:T(8,128)S(1)}, f32[1,128,128]{2,1,0:T(8,128)S(1)}, u32[]{:S(2)}, u32[]{:S(2)}) %collective-permute-start.6) | collective-permute-done | bytes 65568 | tf_op jit(solution)/shard_map/ppermute | solution.py:365
  44.6 0.6 %fusion.6 = f32[1,128,128]{2,1,0:T(8,128)} fusion(f32[1,128,128]{2,1,0:T(8,128)S(1)} %collective-permute-done.6, f32[1,2,128,128]{3,2,1,0:T(8,128)S(1)} %fusion.1), kind=kLoop, calls=%fused_computation.20 | loop fusion | flops 16384 | bytes 196608 | tf_op jit(solution)/shard_map/add | solution.py:489
  (21 shorter events, 0.4 us)
Async XLA Ops:
  0.6 1.9 %collective-permute-start = (f32[512,128]{1,0:T(8,128)}, f32[512,128]{1,0:T(8,128)S(1)}, u32[]{:S(2)}, u32[]{:S(2)}) collective-permute-start(f32[512,128]{1,0:T(8,128)} %bitcast.55), channel_id=1, source_target_pairs={{0,4},{4,0},{8,12},{12,8},{16,20},{20,16},{24,28},{28,24},{1,5},{5... | collective-permute-start | bytes 786440 | tf_op jit(solution)/shard_map/ppermute | solution.py:365
  10.4 5.0 %collective-permute-start.1 = (f32[24,512]{1,0:T(8,128)S(1)}, f32[24,512]{1,0:T(8,128)S(1)}, u32[]{:S(2)}, u32[]{:S(2)}) collective-permute-start(f32[24,512]{1,0:T(8,128)S(1)} %get-tuple-element.27.refs_6_), channel_id=1, source_target_pairs={{0,8},{4,12},{8,0},{12,4},{16,24},{20,28},{24,16},{28,20},{1,9},{5... | collective-permute-start | bytes 147464 | tf_op jit(solution)/shard_map/ppermute | solution.py:365
  13.3 4.1 %collective-permute-start.2 = (f32[24,512]{1,0:T(8,128)S(1)}, f32[24,512]{1,0:T(8,128)S(1)}, u32[]{:S(2)}, u32[]{:S(2)}) collective-permute-start(f32[24,512]{1,0:T(8,128)S(1)} %get-tuple-element.27.refs_6_), channel_id=1, source_target_pairs={{0,16},{4,20},{8,24},{12,28},{16,0},{20,4},{24,8},{28,12},{1,17},{... | collective-permute-start | bytes 147464 | tf_op jit(solution)/shard_map/ppermute | solution.py:365
  14.8 5.0 %collective-permute-start.3 = (f32[24,512]{1,0:T(8,128)S(1)}, f32[24,512]{1,0:T(8,128)S(1)}, u32[]{:S(2)}, u32[]{:S(2)}) collective-permute-start(f32[24,512]{1,0:T(8,128)S(1)} %get-tuple-element.27.refs_6_), channel_id=1, source_target_pairs={{0,24},{4,28},{8,16},{12,20},{16,8},{20,12},{24,0},{28,4},{1,25},{... | collective-permute-start | bytes 147464 | tf_op jit(solution)/shard_map/ppermute | solution.py:365
  22.5 5.7 %collective-permute-start.7 = (f32[2,2,3,16,256]{4,3,2,1,0:T(8,128)S(1)}, f32[2,2,3,16,256]{4,3,2,1,0:T(8,128)S(1)}, u32[]{:S(2)}, u32[]{:S(2)}) collective-permute-start(f32[2,2,3,16,256]{4,3,2,1,0:T(8,128)S(1)} %get-tuple-element.33), channel_id=1, source_target_pairs={{0,8},{4,12},{8,0},{12,4},{16,24},{20,28},{24,16},{28,20},{1,9},{5... | collective-permute-start | bytes 589832 | tf_op jit(solution)/shard_map/ppermute | solution.py:365
  25.8 6.7 %collective-permute-start.9 = (f32[2,2,3,16,256]{4,3,2,1,0:T(8,128)S(1)}, f32[2,2,3,16,256]{4,3,2,1,0:T(8,128)S(1)}, u32[]{:S(2)}, u32[]{:S(2)}) collective-permute-start(f32[2,2,3,16,256]{4,3,2,1,0:T(8,128)S(1)} %get-tuple-element.35), channel_id=1, source_target_pairs={{0,16},{4,20},{8,24},{12,28},{16,0},{20,4},{24,8},{28,12},{1,17},{... | collective-permute-start | bytes 589832 | tf_op jit(solution)/shard_map/ppermute | solution.py:365
  25.9 8.3 %collective-permute-start.4 = (f32[4,128,128]{2,1,0:T(8,128)S(1)}, f32[4,128,128]{2,1,0:T(8,128)S(1)}, u32[]{:S(2)}, u32[]{:S(2)}) collective-permute-start(f32[4,128,128]{2,1,0:T(8,128)S(1)} %get-tuple-element.31), channel_id=1, source_target_pairs={{0,4},{4,0},{8,12},{12,8},{16,20},{20,16},{24,28},{28,24},{1,5},{5... | collective-permute-start | bytes 786440 | tf_op jit(solution)/shard_map/ppermute | solution.py:365
  28.3 7.6 %collective-permute-start.8 = (f32[1,2,3,16,256]{4,3,2,1,0:T(8,128)S(1)}, f32[1,2,3,16,256]{4,3,2,1,0:T(8,128)S(1)}, u32[]{:S(2)}, u32[]{:S(2)}) collective-permute-start(f32[1,2,3,16,256]{4,3,2,1,0:T(8,128)S(1)} %slice_bitcast_fusion.4), channel_id=1, source_target_pairs={{0,16},{4,20},{8,24},{12,28},{16,0},{20,4},{24,8},{28,12},{1,17},{... | collective-permute-start | bytes 294920 | tf_op jit(solution)/shard_map/ppermute | solution.py:365
  32.6 4.7 %collective-permute-start.10 = (f32[1,2,3,16,256]{4,3,2,1,0:T(8,128)S(1)}, f32[1,2,3,16,256]{4,3,2,1,0:T(8,128)S(1)}, u32[]{:S(2)}, u32[]{:S(2)}) collective-permute-start(f32[1,2,3,16,256]{4,3,2,1,0:T(8,128)S(1)} %slice_bitcast_fusion.2), channel_id=1, source_target_pairs={{0,8},{4,12},{8,0},{12,4},{16,24},{20,28},{24,16},{28,20},{1,9},{5... | collective-permute-start | bytes 294920 | tf_op jit(solution)/shard_map/ppermute | solution.py:365
  34.3 5.0 %collective-permute-start.5 = (f32[2,128,128]{2,1,0:T(8,128)S(1)}, f32[2,128,128]{2,1,0:T(8,128)S(1)}, u32[]{:S(2)}, u32[]{:S(2)}) collective-permute-start(f32[2,128,128]{2,1,0:T(8,128)S(1)} %slice_bitcast_fusion), channel_id=1, source_target_pairs={{0,1},{1,0},{2,3},{3,2},{4,5},{5,4},{6,7},{7,6},{8,9},{9,8},{10,11... | collective-permute-start | bytes 393224 | tf_op jit(solution)/shard_map/ppermute | solution.py:365
  37.3 4.7 %collective-permute-start.11 = (f32[3,16,512]{2,1,0:T(8,128)S(1)}, f32[3,16,512]{2,1,0:T(8,128)S(1)}, u32[]{:S(2)}, u32[]{:S(2)}) collective-permute-start(f32[3,16,512]{2,1,0:T(8,128)S(1)} %pad_maximum_fusion.1), channel_id=1, source_target_pairs={{0,4},{4,0},{8,12},{12,8},{16,20},{20,16},{24,28},{28,24},{1,5},{5... | collective-permute-start | bytes 294920 | tf_op jit(solution)/shard_map/ppermute | solution.py:365
  39.4 5.2 %collective-permute-start.6 = (f32[1,128,128]{2,1,0:T(8,128)S(1)}, f32[1,128,128]{2,1,0:T(8,128)S(1)}, u32[]{:S(2)}, u32[]{:S(2)}) collective-permute-start(f32[1,128,128]{2,1,0:T(8,128)S(1)} %slice_bitcast_fusion.6), channel_id=1, source_target_pairs={{0,2},{1,3},{2,0},{3,1},{4,6},{5,7},{6,4},{7,5},{8,10},{9,11},{10,... | collective-permute-start | bytes 196616 | tf_op jit(solution)/shard_map/ppermute | solution.py:365

commit v6 on v5

--- a/solution.py
+++ b/solution.py
@@ -123,7 +123,7 @@
 
 
 def waves_kernel(amplitude, wide, x_ref, y_ref, r_ref, *rest):
-    c_ref, s_ref, loc_ref, snd_ref, flat_ref, xs_ref, ang_ref = rest
+    c_ref, s_ref, loc_ref, snd_ref, flat_ref, xs_ref, ang0_ref, ang1_ref = rest
     rows, chans = flat_ref.shape
     chunks = c_ref.shape[0]
     core = lax.axis_index("tm") & 1
@@ -151,32 +151,49 @@
     def _():
         pairs(y_ref, x_ref)
 
-    ang_ref[...] = jnp.dot(xs_ref[...], r_ref[...], preferred_element_type=f32)
-    zero = jnp.zeros((SUB, wide), f32)
-    for chunk in range(chunks):
-        here = slice(chunk * wide, (chunk + 1) * wide)
-
-        def step(i, carry):
+    block = ang0_ref.shape[0]
+    blocks = rows // block
+
+    def turns(item, ang_ref):
+        at = pl.ds(pl.multiple_of(lax.rem(item, blocks) * block, block), block)
+        cols = pl.ds(pl.multiple_of(lax.div(item, blocks) * (3 * wide), 3 * wide), 3 * wide)
+        ang_ref[...] = jnp.dot(xs_ref[at, :], r_ref[:, cols], preferred_element_type=f32)
+
+    def sums_over(chunk, base, ang_ref, carry):
+        for k in range(block // SUB):
             s0, s1, s2, s01, s12, s012 = carry
+            at = pl.ds(pl.multiple_of(base + k * SUB, SUB), SUB)
             cosines = []
             for level in range(3):
-                at = (3 * chunk + level) * wide
-                turn = ang_ref[tile(i), at : at + wide]
+                turn = ang_ref[k * SUB : (k + 1) * SUB, level * wide : (level + 1) * wide]
                 r = turn - ((turn + MAGIC) - MAGIC)
                 z = r * r
                 sine = r * horner(z, sin_coefs)
                 cosine = horner(z, cos_coefs)
                 wave = amplitude - sine * sine
-                c_ref[chunk, level, tile(i), :] = wave
-                s_ref[chunk, level, tile(i), :] = sine * cosine
+                c_ref[chunk, level, at, :] = wave
+                s_ref[chunk, level, at, :] = sine * cosine
                 cosines.append(wave)
             c0, c1, c2 = cosines
             s012 = s012 + s01 * c2
             s12 = s12 + s1 * c2
             s01 = s01 + s0 * c1
-            return (s0 + c0, s1 + c1, s2 + c2, s01, s12, s012)
-
-        sums = lax.fori_loop(0, rows // SUB, step, (zero,) * 6, unroll=16)
+            carry = (s0 + c0, s1 + c1, s2 + c2, s01, s12, s012)
+        return carry
+
+    zero = jnp.zeros((SUB, wide), f32)
+    turns(jnp.int32(0), ang0_ref)
+    for chunk in range(chunks):
+        here = slice(chunk * wide, (chunk + 1) * wide)
+
+        def step(i, carry):
+            item = chunk * blocks + 2 * i
+            turns(item + 1, ang1_ref)
+            carry = sums_over(chunk, 2 * i * block, ang0_ref, carry)
+            turns(jnp.minimum(item + 2, chunks * blocks - 1), ang0_ref)
+            return sums_over(chunk, (2 * i + 1) * block, ang1_ref, carry)
+
+        sums = lax.fori_loop(0, blocks // 2, step, (zero,) * 6)
         for k in range(6):
             loc_ref[SUB * k : SUB * (k + 1), here] = sums[k]
         a0, a1, a2, a01, a12, a012 = [v[:HALF] for v in sums]
@@ -312,36 +329,40 @@
     return main[:, :chans] + main[:, chans:] + rest
 
 
-def grads_kernel(sizes, chunk, bit, c_ref, s_ref, xt_ref, w_ref, *refs):
+def grads_kernel(sizes, chunk, bit, c_ref, s_ref, *refs):
     n_freq, chips, chunks, wide = sizes
     first, last = chunk == 0, chunk == chunks - 1
     if first:
         loc_ref, weight_ref, *refs = refs
         got, refs = refs[:chips], refs[chips:]
     else:
-        starts_ref, before_ref, *refs = refs
-    keep_ref, send_ref, *refs = refs
+        starts_ref, *refs = refs
+    if last:
+        w_ref, *refs = refs
+        before, refs = refs[: 2 * chunk], refs[2 * chunk :]
+    else:
+        xt_ref, keep_ref, send_ref, *refs = refs
+    sh_ref, sl_ref, *refs = refs
     if last:
         gk_ref, gs_ref, *refs = refs
-    else:
-        acc_ref, *refs = refs
     if first:
         starts_ref, all_ref, *refs = refs
-    u1_ref, sh_ref, sl_ref, gp_ref, *refs = refs
-    if last:
-        acc_ref, flat_ref = refs
+    u1_ref, *refs = refs
     if first:
         for k, value in enumerate(compose(chips, loc_ref, weight_ref, got, all_ref)):
             starts_ref[SUB * k : SUB * (k + 1), :] = value
 
     slopes(chunk, wide, starts_ref, c_ref, s_ref, u1_ref, sh_ref, sl_ref)
-    frequency_grads(bit, wide, xt_ref, sh_ref, sl_ref, gp_ref, keep_ref, send_ref)
+    if not last:
+        (gp_ref,) = refs
+        frequency_grads(bit, wide, xt_ref, sh_ref, sl_ref, gp_ref, keep_ref, send_ref)
+        return
+
+    acc_ref, flat_ref = refs
     total = increment_grads(w_ref, 3 * wide * chunk, sh_ref, sl_ref)
-    if not first:
-        total = total + before_ref[...]
+    for k in range(chunk):
+        total = total + increment_grads(w_ref, 3 * wide * k, before[2 * k], before[2 * k + 1])
     acc_ref[...] = total
-    if not last:
-        return
 
     rows, chans = acc_ref.shape
     core, z = lax.axis_index("tm") & 1, lax.axis_index("freq")
@@ -358,6 +379,19 @@
         at = pl.ds(pl.multiple_of(jnp.bitwise_xor(z, j) * piece, piece), piece)
         gk_ref[j] = flat_ref[core, at, :]
         gs_ref[j] = flat_ref[1 - core, at, :]
+
+
+def join_kernel(n_freq, early, places, kept_ref, other_ref, *refs):
+    blocks, refs = refs[: 2 * early], refs[2 * early :]
+    for j in range(n_freq):
+        refs[j][...] = kept_ref[j] + other_ref[j]
+    for k in range(early):
+        near_ref, far_ref = refs[n_freq + 2 * k : n_freq + 2 * k + 2]
+        size, bit = near_ref.shape[0], 1 << places[k]
+        for j in range(size):
+            at = (j // bit) * (2 * bit) + j % bit
+            near_ref[j] = blocks[2 * k][at] + blocks[2 * k + 1][at]
+            far_ref[j] = blocks[2 * k][at + bit] + blocks[2 * k + 1][at + bit]
 
 
 def swap(value, axis, distance):
@@ -421,7 +455,7 @@
             jax.ShapeDtypeStruct((3 * SUB, mine), f32),
             pltpu.VMEM((rows, chans), f32),
         ],
-        [pltpu.VMEM((rows, 4 * chans), bf16), pltpu.VMEM((rows, 3 * mine), f32)],
+        [pltpu.VMEM((rows, 4 * chans), bf16)] + [pltpu.VMEM((rows // 4, 3 * wide), f32)] * 2,
         x,
         y,
         turns,
@@ -432,62 +466,86 @@
     )
 
     bits = [1 << k for k in range(chips.bit_length() - 1)]
+    orders = [bits if chunk % 2 == 0 else bits[::-1] for chunk in range(chunks)]
     bshape = jax.ShapeDtypeStruct((chips // 2, 2, 3, each, wide), f32)
     gshape = jax.ShapeDtypeStruct((n_freq, rows // 2 // n_freq, chans), f32)
-    total = pltpu.VMEM((rows, chans), f32)
-    starts = pltpu.VMEM((5 * SUB, mine), f32)
-    sums = []
+    gp = pltpu.VMEM((n_tm, 3, each, wide), f32)
+    early, parts = [], []
     for chunk in range(chunks):
-        order = bits if chunk % 2 == 0 else bits[::-1]
         first, last = chunk == 0, chunk == chunks - 1
 
-        def grads_body(*refs, chunk=chunk, bit=order[0]):
-            grads_kernel((n_freq, chips, chunks, wide), chunk, bit, *refs)
-
-        operands = [cosines, sines, xt, weights]
-        operands += [local, weight, *got] if first else [entries, before]
+        def grads_body(*refs, chunk=chunk):
+            grads_kernel((n_freq, chips, chunks, wide), chunk, orders[chunk][0], *refs)
+
+        operands = [cosines, sines] + ([local, weight, *got] if first else [entries])
+        operands += [weights, *parts] if last else [xt]
+        outs = [] if last else [bshape] * 2
+        outs += [pltpu.VMEM((rows, 3 * wide), bf16)] * 2
+        outs += [gshape] * 2 if last else []
+        outs += [pltpu.VMEM((5 * SUB, mine), f32)] if first else []
         scratch = [pltpu.VMEM((chips, 3 * SUB, mine), f32)] if first else []
-        scratch += [
-            pltpu.VMEM((rows, wide), f32),
-            pltpu.VMEM((rows, 3 * wide), bf16),
-            pltpu.VMEM((rows, 3 * wide), bf16),
-            pltpu.VMEM((n_tm, 3, each, wide), f32),
-        ]
-        scratch += [total, pltpu.VMEM((2, rows // 2, chans), f32)] if last else []
+        scratch += [pltpu.VMEM((rows, wide), f32)]
+        if last:
+            scratch += [pltpu.VMEM((rows, chans), f32), pltpu.VMEM((2, rows // 2, chans), f32)]
+        else:
+            scratch += [gp]
         outs = call(
-            grads_body,
-            f"grads{chunk}",
-            3.5,
-            [VECTORS] * len(operands),
-            [bshape] * 2 + ([gshape] * 2 if last else [total]) + ([starts] if first else []),
-            scratch,
-            *operands,
+            grads_body, f"grads{chunk}", 2.5, [VECTORS] * len(operands), outs, scratch, *operands
         )
-        kept, sent = outs[:2]
-        if last:
-            mine_kept, mine_sent = outs[2:4]
-        else:
-            before = outs[2]
         if first:
             entries = outs[-1]
-        sums.append((kept, sent, order))
-
-    pieces = mine_kept + swap(mine_sent, "tm", 1)
+        if last:
+            high, low, kept, sent = outs[:4]
+        else:
+            early += [outs[0], swap(outs[1], "tm", 2 * orders[chunk][0])]
+            parts += outs[2:4]
+
+    other = swap(sent, "tm", 1)
+
+    def last_body(*refs):
+        frequency_grads(orders[-1][0], wide, *refs[:3], refs[5], *refs[3:5])
+
+    near, far = call(
+        last_body, "last", 0.8, [VECTORS] * 3, [bshape] * 2, [gp], xt, high, low
+    )
+    near_sum = near + swap(far, "tm", 2 * orders[-1][0])
+
+    def place(order, step):
+        return sum(1 for b in order[step:] if b < order[step])
+
+    def join_body(*refs):
+        join_kernel(n_freq, chunks - 1, [place(order, 1) for order in orders[:-1]], *refs)
+
+    half = jax.ShapeDtypeStruct((chips // 4,) + bshape.shape[1:], f32)
+    joined = call(
+        join_body,
+        "join",
+        0.2,
+        [VECTORS] * (2 + len(early)),
+        [jax.ShapeDtypeStruct(gshape.shape[1:], f32)] * n_freq + [half] * len(early),
+        [],
+        kept,
+        other,
+        *early,
+    )
+    result = joined[0]
+    for j in range(1, n_freq):
+        result = result + swap(joined[j], "freq", j)
+    grad_increments = result.reshape(steps // n_freq, batch, chans)
+
     done = []
-    for kept, sent, order in sums:
-        blocks = kept + swap(sent, "tm", 2 * order[0])
-        for k, bit in enumerate(order[1:]):
-            left = order[k + 1 :]
-            place = sum(1 for b in left if b < bit)
-            halves = blocks.reshape((-1, 2, 1 << place) + blocks.shape[1:])
+    for chunk, order in enumerate(orders):
+        if chunk < chunks - 1:
+            kept, sent = joined[n_freq + 2 * chunk : n_freq + 2 * chunk + 2]
+            blocks, step = kept + swap(sent, "tm", 2 * order[1]), 2
+        else:
+            blocks, step = near_sum, 1
+        for k in range(step, len(order)):
+            halves = blocks.reshape((-1, 2, 1 << place(order, k)) + blocks.shape[1:])
             shape = (-1,) + blocks.shape[1:]
-            mate = swap(halves[:, 1].reshape(shape), "tm", 2 * bit)
+            mate = swap(halves[:, 1].reshape(shape), "tm", 2 * order[k])
             blocks = halves[:, 0].reshape(shape) + mate
         done.append(blocks[0])
-    for bit in [1 << k for k in range(n_freq.bit_length() - 1)]:
-        halves = pieces.reshape((-1, 2) + pieces.shape[1:])
-        pieces = halves[:, 0] + swap(halves[:, 1], "freq", bit)
-    grad_increments = pieces.reshape(steps // n_freq, batch, chans)
 
     here = jnp.concatenate([blocks[0] for blocks in done], axis=-1)
     away = swap(jnp.concatenate([blocks[1] for blocks in done], axis=-1), "tm", 1)

time: 45.5 us -> 46.8 us (1.029)
  waiting for transfers between devices: 15.8 us -> 17.3 us
    ppermute x12 -> x13, waiting for transfers between devices: 15.8 us -> 17.3 us  [swap(): return lax.ppermute(value, axis, [(i, i ^ distance) for i in range(count)])]
    pallas_call x5 -> x7, Pallas kernels: 14.9 us -> 14.7 us  [call(): pl.pallas_call(body, in_specs=ins, out_specs=[VECTORS] * len(outs), out_s...]
    ppermute x12 -> x13, starting transfers between devices: 12.2 us -> 12.3 us  [swap(): return lax.ppermute(value, axis, [(i, i ^ distance) for i in range(count)])]
  transfers between devices with their start and end apart: 12 -> 13, of which waited for: 8 -> 8; matrix products, arithmetic and copies ran while one was open for 2% -> 2% of each run, Pallas kernels for 9% -> 4%
where the time goes in v6:
time: 46.8 us; the launch traced here: 46.6 us
  waiting for transfers between devices  17.3 us (37%)
  Pallas kernels  14.7 us (31%)
  starting transfers between devices  12.3 us (26%)
  other arithmetic  1.42 us (3%)
  between operations  0.77 us (2%)
    ppermute x13, waiting for transfers between devices, swap(): return lax.ppermute(value, axis, [(i, i ^ distance) for i in range(count)])  17.3 us
    pallas_call x7, Pallas kernels, call(): pl.pallas_call(body, in_specs=ins, out_specs=[VECTORS] * len(outs), out_s...  14.7 us
    ppermute x13, starting transfers between devices, swap(): return lax.ppermute(value, axis, [(i, i ^ distance) for i in range(count)])  12.3 us
  transfers between devices with their start and end apart: 13, of which 8 were waited for; matrix products, arithmetic and copies ran while one was open for 2% of the time, Pallas kernels for 4%

profile of v6, /device:TPU:0, one launch (start us, length us, event | category | flops | bytes accessed | tf_op | source)
XLA Modules:
  0.0 46.6 jit_solution(17683923332312648658)
XLA Ops:
  0.6 0.5 %collective-permute-start = (f32[512,128]{1,0:T(8,128)}, f32[512,128]{1,0:T(8,128)S(1)}, u32[]{:S(2)}, u32[]{:S(2)}) collective-permute-start(f32[512,128]{1,0:T(8,128)} %bitcast.26), channel_id=1, source_target_pairs={{0,4},{4,0},{8,12},{12,8},{16,20},{20,16},{24,28},{28,24},{1,5},{5... | collective-permute-start | bytes 786440 | tf_op jit(solution)/shard_map/ppermute | solution.py:399
  1.1 1.4 %prepare.1 = (f32[512,128]{1,0:T(8,128)S(1)}, bf16[256,1536]{1,0:T(8,128)(2,1)S(1)}, bf16[512,1536]{1,0:T(8,128)(2,1)S(1)}, f32[8,512]{1,0:T(8,128)S(1)}) custom-call(f32[512,128]{1,0:T(8,128)} %bitcast.27, f32[3,128,1024]{2,1,0:T(8,128)} %bitcast.25, f32[3,1024]{1,0:T(4,128)} %ph_hbm.1, s32[4]{0:T(128)} %g_hbm.1), custom_call_target="tpu_custom_call" | custom-call | flops 2090000000 | bytes 5700000 | tf_op jit(solution)/shard_map/prepare/pallas_call | solution.py:57
  2.6 7.5 %waves.1 = (f32[2,3,1024,256]{3,2,1,0:T(8,128)S(1)}, f32[2,3,1024,256]{3,2,1,0:T(8,128)S(1)}, f32[48,512]{1,0:T(8,128)S(1)}, f32[24,512]{1,0:T(8,128)S(1)}, f32[1024,128]{1,0:T(8,128)S(1)}) custom-call(f32[512,128]{1,0:T(8,128)S(1)} %get-tuple-element.28.refs_0_, f32[512,128]{1,0:T(8,128)S(1)} %collective-permute-done.refs_1_, ...), custom_call_target="tpu_custom_call" | custom-call | flops 8800000000 | bytes 24000000 | tf_op jit(solution)/shard_map/waves/pallas_call | solution.py:57
  10.1 2.9 %collective-permute-start.1 = (f32[24,512]{1,0:T(8,128)S(1)}, f32[24,512]{1,0:T(8,128)S(1)}, u32[]{:S(2)}, u32[]{:S(2)}) collective-permute-start(f32[24,512]{1,0:T(8,128)S(1)} %get-tuple-element.34.refs_4_), channel_id=1, source_target_pairs={{0,8},{4,12},{8,0},{12,4},{16,24},{20,28},{24,16},{28,20},{1,9},{5... | collective-permute-start | bytes 147464 | tf_op jit(solution)/shard_map/ppermute | solution.py:399
  12.9 1.5 %collective-permute-start.2 = (f32[24,512]{1,0:T(8,128)S(1)}, f32[24,512]{1,0:T(8,128)S(1)}, u32[]{:S(2)}, u32[]{:S(2)}) collective-permute-start(f32[24,512]{1,0:T(8,128)S(1)} %get-tuple-element.34.refs_4_), channel_id=1, source_target_pairs={{0,16},{4,20},{8,24},{12,28},{16,0},{20,4},{24,8},{28,12},{1,17},{... | collective-permute-start | bytes 147464 | tf_op jit(solution)/shard_map/ppermute | solution.py:399
  14.7 0.4 collective-permute-done.1.refs_5_
  15.1 2.0 %collective-permute-done.2.refs_6_ = f32[24,512]{1,0:T(8,128)S(1)} collective-permute-done((f32[24,512]{1,0:T(8,128)S(1)}, f32[24,512]{1,0:T(8,128)S(1)}, u32[]{:S(2)}, u32[]{:S(2)}) %collective-permute-start.2) | collective-permute-done | bytes 49184 | tf_op jit(solution)/shard_map/ppermute | solution.py:399
  17.0 2.4 %collective-permute-done.3.refs_7_ = f32[24,512]{1,0:T(8,128)S(1)} collective-permute-done((f32[24,512]{1,0:T(8,128)S(1)}, f32[24,512]{1,0:T(8,128)S(1)}, u32[]{:S(2)}, u32[]{:S(2)}) %collective-permute-start.3) | collective-permute-done | bytes 49184 | tf_op jit(solution)/shard_map/ppermute | solution.py:399
  19.5 1.9 %grads0.1 = (f32[2,2,3,16,256]{4,3,2,1,0:T(8,128)S(1)}, f32[2,2,3,16,256]{4,3,2,1,0:T(8,128)S(1)}, bf16[1024,768]{1,0:T(8,128)(2,1)S(1)}, bf16[1024,768]{1,0:T(8,128)(2,1)S(1)}, f32[40,512]{1,0:T(8,128)S(1)}) custom-call(f32[2,3,1024,256]{3,2,1,0:T(8,128)S(1)} %get-tuple-element.30.refs_0_, f32[2,3,1024,256]{3,2,1,0:T(8,128)S(1)} %get-tuple-element.31.refs_1_, ...), custom_call_target="tpu_custom_call" | custom-call | flops 2750000128 | bytes 7500000 | tf_op jit(solution)/shard_map/grads0/pallas_call | solution.py:57
  21.4 2.9 %grads1.1 = (bf16[1024,768]{1,0:T(8,128)(2,1)S(1)}, bf16[1024,768]{1,0:T(8,128)(2,1)S(1)}, f32[4,128,128]{2,1,0:T(8,128)S(1)}, f32[4,128,128]{2,1,0:T(8,128)S(1)}) custom-call(f32[2,3,1024,256]{3,2,1,0:T(8,128)S(1)} %get-tuple-element.30.refs_0_, f32[2,3,1024,256]{3,2,1,0:T(8,128)S(1)} %get-tuple-element.31.refs_1_, ...), custom_call_target="tpu_custom_call" | custom-call | flops 2750000128 | bytes 7500000 | tf_op jit(solution)/shard_map/grads1/pallas_call | solution.py:57
  24.2 0.8 %last.1 = (f32[2,2,3,16,256]{4,3,2,1,0:T(8,128)S(1)}, f32[2,2,3,16,256]{4,3,2,1,0:T(8,128)S(1)}) custom-call(bf16[256,1024]{1,0:T(8,128)(2,1)S(1)} %turn.1.refs_8_.refs_0_, bf16[1024,768]{1,0:T(8,128)(2,1)S(1)} %get-tuple-element.50.refs_1_, bf16[1024,768]{1,0:T(8,128)(2,1)S(1)} %get-tuple-element.51.refs_2_), custom_call_target="tpu_custom_call" | custom-call | flops 880000000 | bytes 2400000 | tf_op jit(solution)/shard_map/last/pallas_call | solution.py:57
  25.1 0.5 %collective-permute-start.10 = (f32[2,2,3,16,256]{4,3,2,1,0:T(8,128)S(1)}, f32[2,2,3,16,256]{4,3,2,1,0:T(8,128)S(1)}, u32[]{:S(2)}, u32[]{:S(2)}) collective-permute-start(f32[2,2,3,16,256]{4,3,2,1,0:T(8,128)S(1)} %get-tuple-element.53), channel_id=1, source_target_pairs={{0,16},{4,20},{8,24},{12,28},{16,0},{20,4},{24,8},{28,12},{1,17},{... | collective-permute-start | bytes 589832 | tf_op jit(solution)/shard_map/ppermute | solution.py:399
  25.8 5.0 %collective-permute-done.10 = f32[2,2,3,16,256]{4,3,2,1,0:T(8,128)S(1)} collective-permute-done((f32[2,2,3,16,256]{4,3,2,1,0:T(8,128)S(1)}, f32[2,2,3,16,256]{4,3,2,1,0:T(8,128)S(1)}, u32[]{:S(2)}, u32[]{:S(2)}) %collective-permute-start.10) | collective-permute-done | bytes 196640 | tf_op jit(solution)/shard_map/ppermute | solution.py:399
  30.8 0.6 %collective-permute-start.11 = (f32[1,2,3,16,256]{4,3,2,1,0:T(8,128)S(1)}, f32[1,2,3,16,256]{4,3,2,1,0:T(8,128)S(1)}, u32[]{:S(2)}, u32[]{:S(2)}) collective-permute-start(f32[1,2,3,16,256]{4,3,2,1,0:T(8,128)S(1)} %slice_bitcast_fusion), channel_id=1, source_target_pairs={{0,8},{4,12},{8,0},{12,4},{16,24},{20,28},{24,16},{28,20},{1,9},{5... | collective-permute-start | bytes 294920 | tf_op jit(solution)/shard_map/ppermute | solution.py:399
  31.4 1.9 %collective-permute-done.5.refs_3_ = f32[2,2,3,16,256]{4,3,2,1,0:T(8,128)S(1)} collective-permute-done((f32[2,2,3,16,256]{4,3,2,1,0:T(8,128)S(1)}, f32[2,2,3,16,256]{4,3,2,1,0:T(8,128)S(1)}, u32[]{:S(2)}, u32[]{:S(2)}) %collective-permute-start.5) | collective-permute-done | bytes 196640 | tf_op jit(solution)/shard_map/ppermute | solution.py:399
  33.4 1.6 %collective-permute-start.9 = (f32[1,2,3,16,256]{4,3,2,1,0:T(8,128)S(1)}, f32[1,2,3,16,256]{4,3,2,1,0:T(8,128)S(1)}, u32[]{:S(2)}, u32[]{:S(2)}) collective-permute-start(f32[1,2,3,16,256]{4,3,2,1,0:T(8,128)S(1)} %get-tuple-element.49), channel_id=1, source_target_pairs={{0,16},{4,20},{8,24},{12,28},{16,0},{20,4},{24,8},{28,12},{1,17},{... | collective-permute-start | bytes 294920 | tf_op jit(solution)/shard_map/ppermute | solution.py:399
  35.0 1.6 %collective-permute-start.6 = (f32[128,128]{1,0:T(8,128)S(1)}, f32[128,128]{1,0:T(8,128)S(1)}, u32[]{:S(2)}, u32[]{:S(2)}) collective-permute-start(f32[128,128]{1,0:T(8,128)S(1)} %get-tuple-element.45), channel_id=1, source_target_pairs={{0,1},{1,0},{2,3},{3,2},{4,5},{5,4},{6,7},{7,6},{8,9},{9,8},{10,11... | collective-permute-start | bytes 196616 | tf_op jit(solution)/shard_map/ppermute | solution.py:399
  36.5 2.6 %collective-permute-start.7 = (f32[128,128]{1,0:T(8,128)S(1)}, f32[128,128]{1,0:T(8,128)S(1)}, u32[]{:S(2)}, u32[]{:S(2)}) collective-permute-start(f32[128,128]{1,0:T(8,128)S(1)} %get-tuple-element.46), channel_id=1, source_target_pairs={{0,2},{1,3},{2,0},{3,1},{4,6},{5,7},{6,4},{7,5},{8,10},{9,11},{10,... | collective-permute-start | bytes 196616 | tf_op jit(solution)/shard_map/ppermute | solution.py:399
  39.1 0.2 collective-permute-start.8
  39.5 0.3 collective-permute-done.6
  39.9 3.2 %collective-permute-done.7 = f32[128,128]{1,0:T(8,128)S(1)} collective-permute-done((f32[128,128]{1,0:T(8,128)S(1)}, f32[128,128]{1,0:T(8,128)S(1)}, u32[]{:S(2)}, u32[]{:S(2)}) %collective-permute-start.7) | collective-permute-done | bytes 65568 | tf_op jit(solution)/shard_map/ppermute | solution.py:399
  43.1 2.1 %collective-permute-done.8 = f32[128,128]{1,0:T(8,128)S(1)} collective-permute-done((f32[128,128]{1,0:T(8,128)S(1)}, f32[128,128]{1,0:T(8,128)S(1)}, u32[]{:S(2)}, u32[]{:S(2)}) %collective-permute-start.8) | collective-permute-done | bytes 65568 | tf_op jit(solution)/shard_map/ppermute | solution.py:399
  45.2 0.6 %add_add_fusion = f32[128,128]{1,0:T(8,128)} fusion(f32[128,128]{1,0:T(8,128)S(1)} %collective-permute-done.8, f32[128,128]{1,0:T(8,128)S(1)} %collective-permute-done.7, f32[128,128]{1,0:T(8,128)S(1)} %get-tuple-element.44, f32[128,128]{1,0:T(8,128)S(1)} %collective-permute-done.6), kind=kLoop, calls=%fused_computation.10 | loop fusion | flops 49152 | bytes 327680 | tf_op jit(solution)/shard_map/add | solution.py:533
  45.9 0.7 %maximum_bitcast_fusion = f32[16,3,1024]{2,0,1:T(8,128)} fusion(f32[3,16,512]{2,1,0:T(8,128)S(1)} %get-tuple-element.57, f32[3,16,512]{2,1,0:T(8,128)S(1)} %get-tuple-element.56), kind=kLoop, calls=%fused_computation | loop fusion | flops 49152 | bytes 393216 | tf_op jit(solution)/shard_map/transpose | solution.py:554
  (19 shorter events, 0.7 us)
Async XLA Ops:
  0.6 1.9 %collective-permute-start = (f32[512,128]{1,0:T(8,128)}, f32[512,128]{1,0:T(8,128)S(1)}, u32[]{:S(2)}, u32[]{:S(2)}) collective-permute-start(f32[512,128]{1,0:T(8,128)} %bitcast.26), channel_id=1, source_target_pairs={{0,4},{4,0},{8,12},{12,8},{16,20},{20,16},{24,28},{28,24},{1,5},{5... | collective-permute-start | bytes 786440 | tf_op jit(solution)/shard_map/ppermute | solution.py:399
  10.1 5.0 %collective-permute-start.1 = (f32[24,512]{1,0:T(8,128)S(1)}, f32[24,512]{1,0:T(8,128)S(1)}, u32[]{:S(2)}, u32[]{:S(2)}) collective-permute-start(f32[24,512]{1,0:T(8,128)S(1)} %get-tuple-element.34.refs_4_), channel_id=1, source_target_pairs={{0,8},{4,12},{8,0},{12,4},{16,24},{20,28},{24,16},{28,20},{1,9},{5... | collective-permute-start | bytes 147464 | tf_op jit(solution)/shard_map/ppermute | solution.py:399
  12.9 4.1 %collective-permute-start.2 = (f32[24,512]{1,0:T(8,128)S(1)}, f32[24,512]{1,0:T(8,128)S(1)}, u32[]{:S(2)}, u32[]{:S(2)}) collective-permute-start(f32[24,512]{1,0:T(8,128)S(1)} %get-tuple-element.34.refs_4_), channel_id=1, source_target_pairs={{0,16},{4,20},{8,24},{12,28},{16,0},{20,4},{24,8},{28,12},{1,17},{... | collective-permute-start | bytes 147464 | tf_op jit(solution)/shard_map/ppermute | solution.py:399
  14.5 5.0 %collective-permute-start.3 = (f32[24,512]{1,0:T(8,128)S(1)}, f32[24,512]{1,0:T(8,128)S(1)}, u32[]{:S(2)}, u32[]{:S(2)}) collective-permute-start(f32[24,512]{1,0:T(8,128)S(1)} %get-tuple-element.34.refs_4_), channel_id=1, source_target_pairs={{0,24},{4,28},{8,16},{12,20},{16,8},{20,12},{24,0},{28,4},{1,25},{... | collective-permute-start | bytes 147464 | tf_op jit(solution)/shard_map/ppermute | solution.py:399
  25.1 5.7 %collective-permute-start.10 = (f32[2,2,3,16,256]{4,3,2,1,0:T(8,128)S(1)}, f32[2,2,3,16,256]{4,3,2,1,0:T(8,128)S(1)}, u32[]{:S(2)}, u32[]{:S(2)}) collective-permute-start(f32[2,2,3,16,256]{4,3,2,1,0:T(8,128)S(1)} %get-tuple-element.53), channel_id=1, source_target_pairs={{0,16},{4,20},{8,24},{12,28},{16,0},{20,4},{24,8},{28,12},{1,17},{... | collective-permute-start | bytes 589832 | tf_op jit(solution)/shard_map/ppermute | solution.py:399
  25.6 7.7 %collective-permute-start.4 = (f32[4,128,128]{2,1,0:T(8,128)S(1)}, f32[4,128,128]{2,1,0:T(8,128)S(1)}, u32[]{:S(2)}, u32[]{:S(2)}) collective-permute-start(f32[4,128,128]{2,1,0:T(8,128)S(1)} %get-tuple-element.41), channel_id=1, source_target_pairs={{0,4},{4,0},{8,12},{12,8},{16,20},{20,16},{24,28},{28,24},{1,5},{5... | collective-permute-start | bytes 786440 | tf_op jit(solution)/shard_map/ppermute | solution.py:399
  25.6 7.7 %collective-permute-start.5 = (f32[2,2,3,16,256]{4,3,2,1,0:T(8,128)S(1)}, f32[2,2,3,16,256]{4,3,2,1,0:T(8,128)S(1)}, u32[]{:S(2)}, u32[]{:S(2)}) collective-permute-start(f32[2,2,3,16,256]{4,3,2,1,0:T(8,128)S(1)} %get-tuple-element.43), channel_id=1, source_target_pairs={{0,8},{4,12},{8,0},{12,4},{16,24},{20,28},{24,16},{28,20},{1,9},{5... | collective-permute-start | bytes 589832 | tf_op jit(solution)/shard_map/ppermute | solution.py:399
  30.8 8.5 %collective-permute-start.11 = (f32[1,2,3,16,256]{4,3,2,1,0:T(8,128)S(1)}, f32[1,2,3,16,256]{4,3,2,1,0:T(8,128)S(1)}, u32[]{:S(2)}, u32[]{:S(2)}) collective-permute-start(f32[1,2,3,16,256]{4,3,2,1,0:T(8,128)S(1)} %slice_bitcast_fusion), channel_id=1, source_target_pairs={{0,8},{4,12},{8,0},{12,4},{16,24},{20,28},{24,16},{28,20},{1,9},{5... | collective-permute-start | bytes 294920 | tf_op jit(solution)/shard_map/ppermute | solution.py:399
  33.4 6.0 %collective-permute-start.9 = (f32[1,2,3,16,256]{4,3,2,1,0:T(8,128)S(1)}, f32[1,2,3,16,256]{4,3,2,1,0:T(8,128)S(1)}, u32[]{:S(2)}, u32[]{:S(2)}) collective-permute-start(f32[1,2,3,16,256]{4,3,2,1,0:T(8,128)S(1)} %get-tuple-element.49), channel_id=1, source_target_pairs={{0,16},{4,20},{8,24},{12,28},{16,0},{20,4},{24,8},{28,12},{1,17},{... | collective-permute-start | bytes 294920 | tf_op jit(solution)/shard_map/ppermute | solution.py:399
  35.0 4.9 %collective-permute-start.6 = (f32[128,128]{1,0:T(8,128)S(1)}, f32[128,128]{1,0:T(8,128)S(1)}, u32[]{:S(2)}, u32[]{:S(2)}) collective-permute-start(f32[128,128]{1,0:T(8,128)S(1)} %get-tuple-element.45), channel_id=1, source_target_pairs={{0,1},{1,0},{2,3},{3,2},{4,5},{5,4},{6,7},{7,6},{8,9},{9,8},{10,11... | collective-permute-start | bytes 196616 | tf_op jit(solution)/shard_map/ppermute | solution.py:399
  36.5 6.6 %collective-permute-start.7 = (f32[128,128]{1,0:T(8,128)S(1)}, f32[128,128]{1,0:T(8,128)S(1)}, u32[]{:S(2)}, u32[]{:S(2)}) collective-permute-start(f32[128,128]{1,0:T(8,128)S(1)} %get-tuple-element.46), channel_id=1, source_target_pairs={{0,2},{1,3},{2,0},{3,1},{4,6},{5,7},{6,4},{7,5},{8,10},{9,11},{10,... | collective-permute-start | bytes 196616 | tf_op jit(solution)/shard_map/ppermute | solution.py:399
  39.1 6.1 %collective-permute-start.8 = (f32[128,128]{1,0:T(8,128)S(1)}, f32[128,128]{1,0:T(8,128)S(1)}, u32[]{:S(2)}, u32[]{:S(2)}) collective-permute-start(f32[128,128]{1,0:T(8,128)S(1)} %get-tuple-element.47), channel_id=1, source_target_pairs={{0,3},{1,2},{2,1},{3,0},{4,7},{5,6},{6,5},{7,4},{8,11},{9,10},{10,... | collective-permute-start | bytes 196616 | tf_op jit(solution)/shard_map/ppermute | solution.py:399
  39.5 6.4 %collective-permute-start.12 = (f32[3,16,512]{2,1,0:T(8,128)S(1)}, f32[3,16,512]{2,1,0:T(8,128)S(1)}, u32[]{:S(2)}, u32[]{:S(2)}) collective-permute-start(f32[3,16,512]{2,1,0:T(8,128)S(1)} %pad_maximum_fusion.1), channel_id=1, source_target_pairs={{0,4},{4,0},{8,12},{12,8},{16,20},{20,16},{24,28},{28,24},{1,5},{5... | collective-permute-start | bytes 294920 | tf_op jit(solution)/shard_map/ppermute | solution.py:399

commit v7 on v4

--- a/solution.py
+++ b/solution.py
@@ -21,7 +21,7 @@
     0.2196967986036905,
 )
 NT = (((1,), (1,)), ((), ()))
-PARAMS = pltpu.CompilerParams(vmem_limit_bytes=24 * 1024 * 1024)
+PARAMS = pltpu.CompilerParams(vmem_limit_bytes=20 * 1024 * 1024)
 VECTORS = pl.BlockSpec(memory_space=pltpu.VMEM)
 STAY = pl.BlockSpec(memory_space=pltpu.HBM)
 
@@ -123,13 +123,12 @@
 
 
 def waves_kernel(amplitude, wide, x_ref, y_ref, r_ref, *rest):
-    c_ref, s_ref, loc_ref, snd_ref, flat_ref, xs_ref, ang_ref = rest
+    c_ref, half_ref, z_ref, loc_ref, snd_ref, flat_ref, xs_ref, ang0_ref, ang1_ref = rest
     rows, chans = flat_ref.shape
     chunks = c_ref.shape[0]
     core = lax.axis_index("tm") & 1
     root = math.sqrt(2.0 * amplitude)
     sin_coefs = [root * coef for coef in SIN]
-    cos_coefs = [-root * coef for coef in COS]
     lane = lax.broadcasted_iota(jnp.int32, (2 * SUB, chans), 1)
     ones = jnp.where(lane < 3, 1.0, 0.0).astype(bf16)
 
@@ -151,32 +150,49 @@
     def _():
         pairs(y_ref, x_ref)
 
-    ang_ref[...] = jnp.dot(xs_ref[...], r_ref[...], preferred_element_type=f32)
-    zero = jnp.zeros((SUB, wide), f32)
-    for chunk in range(chunks):
-        here = slice(chunk * wide, (chunk + 1) * wide)
-
-        def step(i, carry):
+    block = ang0_ref.shape[0]
+    blocks = rows // block
+
+    def turns(item, ang_ref):
+        at = pl.ds(pl.multiple_of(lax.rem(item, blocks) * block, block), block)
+        cols = pl.ds(pl.multiple_of(lax.div(item, blocks) * (3 * wide), 3 * wide), 3 * wide)
+        ang_ref[...] = jnp.dot(xs_ref[at, :], r_ref[:, cols], preferred_element_type=f32)
+
+    def sums_over(chunk, base, ang_ref, carry):
+        for k in range(block // SUB):
             s0, s1, s2, s01, s12, s012 = carry
+            at = pl.ds(pl.multiple_of(base + k * SUB, SUB), SUB)
             cosines = []
             for level in range(3):
-                at = (3 * chunk + level) * wide
-                turn = ang_ref[tile(i), at : at + wide]
+                turn = ang_ref[k * SUB : (k + 1) * SUB, level * wide : (level + 1) * wide]
                 r = turn - ((turn + MAGIC) - MAGIC)
                 z = r * r
                 sine = r * horner(z, sin_coefs)
-                cosine = horner(z, cos_coefs)
                 wave = amplitude - sine * sine
-                c_ref[chunk, level, tile(i), :] = wave
-                s_ref[chunk, level, tile(i), :] = sine * cosine
+                c_ref[chunk, level, at, :] = wave
+                half_ref[chunk, level, at, :] = sine
+                z_ref[chunk, level, at, :] = z
                 cosines.append(wave)
             c0, c1, c2 = cosines
             s012 = s012 + s01 * c2
             s12 = s12 + s1 * c2
             s01 = s01 + s0 * c1
-            return (s0 + c0, s1 + c1, s2 + c2, s01, s12, s012)
-
-        sums = lax.fori_loop(0, rows // SUB, step, (zero,) * 6, unroll=16)
+            carry = (s0 + c0, s1 + c1, s2 + c2, s01, s12, s012)
+        return carry
+
+    zero = jnp.zeros((SUB, wide), f32)
+    turns(jnp.int32(0), ang0_ref)
+    for chunk in range(chunks):
+        here = slice(chunk * wide, (chunk + 1) * wide)
+
+        def step(i, carry):
+            item = chunk * blocks + 2 * i
+            turns(item + 1, ang1_ref)
+            carry = sums_over(chunk, 2 * i * block, ang0_ref, carry)
+            turns(jnp.minimum(item + 2, chunks * blocks - 1), ang0_ref)
+            return sums_over(chunk, (2 * i + 1) * block, ang1_ref, carry)
+
+        sums = lax.fori_loop(0, blocks // 2, step, (zero,) * 6)
         for k in range(6):
             loc_ref[SUB * k : SUB * (k + 1), here] = sums[k]
         a0, a1, a2, a01, a12, a012 = [v[:HALF] for v in sums]
@@ -193,16 +209,22 @@
             snd_ref[HALF * k : HALF * (k + 1), here] = both[k]
 
 
-def grads_kernel(sizes, c_ref, s_ref, loc_ref, xt_ref, w_ref, weight_ref, *refs):
-    n_tm, n_freq, wide = sizes
-    chips = n_tm // 2
-    got, refs = refs[:chips], refs[chips:]
-    gp_ref, gk_ref, gs_ref, sh_ref, sl_ref, all_ref, u1_ref, acc_ref, flat_ref = refs
-    rows, chans = acc_ref.shape
-    chunks = c_ref.shape[0]
-    me = lax.axis_index("tm")
-    core, chip, z = me & 1, me >> 1, lax.axis_index("freq")
-
+def sines_kernel(amplitude, half_ref, z_ref, s_ref):
+    chunks, levels, rows, _ = s_ref.shape
+    coefs = [-math.sqrt(2.0 * amplitude) * coef for coef in COS]
+    for chunk in range(chunks):
+        for level in range(levels):
+
+            def step(i, _):
+                value = horner(z_ref[chunk, level, tile(i), :], coefs)
+                s_ref[chunk, level, tile(i), :] = half_ref[chunk, level, tile(i), :] * value
+                return 0
+
+            lax.fori_loop(0, rows // SUB, step, 0, unroll=16)
+
+
+def compose(chips, loc_ref, weight_ref, got, all_ref):
+    chip = lax.axis_index("tm") >> 1
     for d in range(chips):
         all_ref[jnp.bitwise_xor(chip, d)] = got[d][...]
 
@@ -244,7 +266,7 @@
     tail2 = tall(t2 + b2, t2)
     tail1 = tall(t1 + b1, t1)
     tail12 = tall(t12 + b12 + b1 * t2, t12)
-    starts = (
+    return (
         d2,
         tall(e1, e1 + a0),
         tall(e2, e2 + a01 + e1 * a1),
@@ -252,58 +274,77 @@
         d0 + d1 * tail1 + d2 * tail12,
     )
 
-    for chunk in range(chunks):
-        scale, front1, front2, adjoint1, adjoint0 = [
-            v[:, chunk * wide : (chunk + 1) * wide] for v in starts
-        ]
-
-        def keep(pair, level, slopes):
-            high, low = split(tall(*slopes))
-            at = (3 * chunk + level) * wide
-            sh_ref[tile(pair, 2), at : at + wide] = high
-            sl_ref[tile(pair, 2), at : at + wide] = low
-
-        def fwd(pair, carry):
-            f1, f2 = carry
-            slopes = []
-            for which in range(2):
-                at = tile(2 * pair + which)
-                u1_ref[at, :] = s_ref[chunk, 1, at, :] * f1
-                slopes.append(s_ref[chunk, 2, at, :] * (scale * f2))
-                f2 = f2 + f1 * c_ref[chunk, 1, at, :]
-                f1 = f1 + c_ref[chunk, 0, at, :]
-            keep(pair, 2, slopes)
-            return f1, f2
-
-        lax.fori_loop(0, rows // (2 * SUB), fwd, (front1, front2), unroll=8)
-
-        def bwd(step, carry):
-            g1, g0 = carry
-            pair = rows // (2 * SUB) - 1 - step
-            slope0, slope1 = [], []
-            for which in (1, 0):
-                at = tile(2 * pair + which)
-                slope1.append(u1_ref[at, :] * g1)
-                slope0.append(s_ref[chunk, 0, at, :] * g0)
-                g0 = g0 + g1 * c_ref[chunk, 1, at, :]
-                g1 = g1 + scale * c_ref[chunk, 2, at, :]
-            keep(pair, 0, slope0[::-1])
-            keep(pair, 1, slope1[::-1])
-            return g1, g0
-
-        lax.fori_loop(0, rows // (2 * SUB), bwd, (adjoint1, adjoint0), unroll=8)
+
+def slopes(chunk, wide, starts, c_ref, s_ref, u1_ref, sh_ref, sl_ref):
+    rows = u1_ref.shape[0]
+    scale, front1, front2, adjoint1, adjoint0 = [
+        v[:, chunk * wide : (chunk + 1) * wide] for v in starts
+    ]
+
+    def keep(pair, level, values):
+        high, low = split(tall(*values))
+        at = (3 * chunk + level) * wide
+        sh_ref[tile(pair, 2), at : at + wide] = high
+        sl_ref[tile(pair, 2), at : at + wide] = low
+
+    def fwd(pair, carry):
+        f1, f2 = carry
+        slope2 = []
+        for which in range(2):
+            at = tile(2 * pair + which)
+            u1_ref[at, :] = s_ref[chunk, 1, at, :] * f1
+            slope2.append(s_ref[chunk, 2, at, :] * (scale * f2))
+            f2 = f2 + f1 * c_ref[chunk, 1, at, :]
+            f1 = f1 + c_ref[chunk, 0, at, :]
+        keep(pair, 2, slope2)
+        return f1, f2
+
+    lax.fori_loop(0, rows // (2 * SUB), fwd, (front1, front2), unroll=8)
+
+    def bwd(step, carry):
+        g1, g0 = carry
+        pair = rows // (2 * SUB) - 1 - step
+        slope0, slope1 = [], []
+        for which in (1, 0):
+            at = tile(2 * pair + which)
+            slope1.append(u1_ref[at, :] * g1)
+            slope0.append(s_ref[chunk, 0, at, :] * g0)
+            g0 = g0 + g1 * c_ref[chunk, 1, at, :]
+            g1 = g1 + scale * c_ref[chunk, 2, at, :]
+        keep(pair, 0, slope0[::-1])
+        keep(pair, 1, slope1[::-1])
+        return g1, g0
+
+    lax.fori_loop(0, rows // (2 * SUB), bwd, (adjoint1, adjoint0), unroll=8)
+
+
+def grads_kernel(sizes, c_ref, s_ref, loc_ref, xt_ref, w_ref, weight_ref, *refs):
+    n_tm, n_freq, wide = sizes
+    chips = n_tm // 2
+    got, refs = refs[:chips], refs[chips:]
+    blocks, refs = refs[:chips], refs[chips:]
+    gk_ref, gs_ref, sh_ref, sl_ref, gp_ref, all_ref, u1_ref, acc_ref, flat_ref = refs
+    rows, chans = acc_ref.shape
+    each = chans // n_tm
+    me = lax.axis_index("tm")
+    core, z = me & 1, lax.axis_index("freq")
+
+    starts = compose(chips, loc_ref, weight_ref, got, all_ref)
+    for chunk in range(c_ref.shape[0]):
+        slopes(chunk, wide, starts, c_ref, s_ref, u1_ref, sh_ref, sl_ref)
 
     main = jnp.dot(xt_ref[...], sh_ref[...], preferred_element_type=f32)
     rest = jnp.dot(xt_ref[:chans, :], sl_ref[...], preferred_element_type=f32)
     grad = main[:chans] + main[chans:] + rest
-    each = chans // n_tm
-    for chunk in range(chunks):
+    for chunk in range(c_ref.shape[0]):
         for level in range(3):
             at = (3 * chunk + level) * wide
             for d in range(n_tm):
                 gp_ref[d, level, :, chunk * wide : (chunk + 1) * wide] = grad[
                     each * d : each * (d + 1), at : at + wide
                 ]
+    for d in range(n_tm):
+        blocks[d // 2][d % 2] = gp_ref[jnp.bitwise_xor(me, d)]
 
     main = lax.dot_general(sh_ref[...], w_ref[...], NT, preferred_element_type=f32)
     rest = lax.dot_general(sl_ref[...], w_ref[:chans, :], NT, preferred_element_type=f32)
@@ -372,19 +413,24 @@
     def waves_body(*refs):
         waves_kernel(amplitude, wide, *refs)
 
-    cosines, sines, local, own, flat = call(
+    def sines_body(*refs):
+        sines_kernel(amplitude, *refs)
+
+    big = pltpu.VMEM((chunks, 3, rows, wide), f32)
+    cosines, halves, squares, local, own, flat = call(
         waves_body,
         "waves",
         8.0,
         [VECTORS] * 3,
         [
-            pltpu.VMEM((chunks, 3, rows, wide), f32),
-            pltpu.VMEM((chunks, 3, rows, wide), f32),
+            big,
+            big,
+            big,
             pltpu.VMEM((6 * SUB, mine), f32),
             jax.ShapeDtypeStruct((3 * SUB, mine), f32),
             pltpu.VMEM((rows, chans), f32),
         ],
-        [pltpu.VMEM((rows, 4 * chans), bf16), pltpu.VMEM((rows, 3 * mine), f32)],
+        [pltpu.VMEM((rows, 4 * chans), bf16)] + [pltpu.VMEM((rows // 4, 3 * wide), f32)] * 2,
         x,
         y,
         turns,
@@ -394,19 +440,23 @@
         turn_kernel, "turn", 0.8, [VECTORS], [pltpu.VMEM((2 * chans, rows), bf16)], [], flat
     )
 
+    (sines,) = call(sines_body, "sines", 2.4, [VECTORS] * 2, [big], [], halves, squares)
+
     def grads_body(*refs):
         grads_kernel((n_tm, n_freq, wide), *refs)
 
+    bshape = jax.ShapeDtypeStruct((2, 3, each, mine), f32)
     gshape = jax.ShapeDtypeStruct((n_freq, rows // 2 // n_freq, chans), f32)
-    parts, kept, sent = call(
+    *blocks, kept, sent = call(
         grads_body,
         "grads",
-        7.0,
+        6.0,
         [VECTORS] * (6 + chips),
-        [jax.ShapeDtypeStruct((n_tm, 3, each, mine), f32), gshape, gshape],
+        [bshape] * chips + [gshape] * 2,
         [
             pltpu.VMEM((rows, 3 * mine), bf16),
             pltpu.VMEM((rows, 3 * mine), bf16),
+            pltpu.VMEM((n_tm, 3, each, mine), f32),
             pltpu.VMEM((chips, 3 * SUB, mine), f32),
             pltpu.VMEM((rows, wide), f32),
             pltpu.VMEM((rows, chans), f32),
@@ -422,13 +472,20 @@
     )
 
     pieces = kept + swap(sent, "tm", 1)
+    others = [swap(pieces[j], "freq", j) for j in range(1, n_freq)]
+    others[0], blocks[0] = lax.optimization_barrier((others[0], blocks[0]))
+    total = blocks[0]
+    for d in range(chips - 1, 0, -1):
+        total = total + swap(blocks[d], "tm", 2 * d)
     result = pieces[0]
-    for j in range(1, n_freq):
-        result = result + swap(pieces[j], "freq", j)
+    for other in others:
+        result = result + other
     grad_increments = result.reshape(steps // n_freq, batch, chans)
-    parts = lax.all_to_all(parts, "tm", 0, 0, tiled=True)
-    total = jnp.sum(parts.reshape(chips, 2, 3, each, mine), axis=0)
-    grad_projections = jnp.transpose(total, (2, 1, 0, 3)).reshape(each, 3, freqs)
+
+    here, away = total[0], swap(total[1], "tm", 1)
+    even = lax.axis_index("tm") & 1 == 0
+    low, high = jnp.where(even, here, away), jnp.where(even, away, here)
+    grad_projections = jnp.transpose(jnp.concatenate([low, high], axis=-1), (1, 0, 2))
     return (grad_increments, grad_projections)
 
 

time: 42.1 us -> 38.9 us (0.924)
  waiting for transfers between devices: 11.3 us -> 4.6 us
  starting transfers between devices: 12.8 us -> 16.9 us
  other arithmetic: 0.74 us -> 1.46 us
  local copies, waits for them, and re-layouts: 0.71 us -> 0.02 us
  Pallas kernels: 15.6 us -> 15 us
    ppermute x8 -> x12, starting transfers between devices: 9.22 us -> 16.9 us  [swap(): return lax.ppermute(value, axis, [(i, i ^ distance) for i in range(count)])]
    ppermute x8 -> x12, waiting for transfers between devices: 10.4 us -> 4.6 us  [swap(): return lax.ppermute(value, axis, [(i, i ^ distance) for i in range(count)])]
    all_to_all x1 -> x0, starting transfers between devices: 3.55 us -> none  [on_device(): parts = lax.all_to_all(parts, 'tm', 0, 0, tiled=True)]
    all_to_all x1 -> x0, waiting for transfers between devices: 0.93 us -> none  [on_device(): parts = lax.all_to_all(parts, 'tm', 0, 0, tiled=True)]
    transpose x0 -> x1, other arithmetic: none -> 0.69 us  [on_device(): jnp.transpose(jnp.concatenate([low, high], axis=-1), (1, 0, 2))]
    reshape x1 -> x0, local copies, waits for them, and re-layouts: 0.69 us -> none  [on_device(): jnp.transpose(total, (2, 1, 0, 3)).reshape(each, 3, freqs)]
    pallas_call x4 -> x5, Pallas kernels: 15.6 us -> 15 us  [call(): pl.pallas_call(body, in_specs=ins, out_specs=[VECTORS] * len(outs), out_s...]
  transfers between devices with their start and end apart: 9 -> 12, of which waited for: 7 -> 4; matrix products, arithmetic and copies ran while one was open for 2% -> 2% of each run, Pallas kernels for 4% -> 10%
where the time goes in v7:
time: 38.9 us; the launch traced here: 38.6 us
  starting transfers between devices  16.9 us (43%)
  Pallas kernels  15 us (39%)
  waiting for transfers between devices  4.6 us (12%)
  other arithmetic  1.46 us (4%)
  between operations  0.75 us (2%)
    ppermute x12, starting transfers between devices, swap(): return lax.ppermute(value, axis, [(i, i ^ distance) for i in range(count)])  16.9 us
    pallas_call x5, Pallas kernels, call(): pl.pallas_call(body, in_specs=ins, out_specs=[VECTORS] * len(outs), out_s...  15 us
    ppermute x12, waiting for transfers between devices, swap(): return lax.ppermute(value, axis, [(i, i ^ distance) for i in range(count)])  4.6 us
  transfers between devices with their start and end apart: 12, of which 4 were waited for; matrix products, arithmetic and copies ran while one was open for 2% of the time, Pallas kernels for 10%

profile of v7, /device:TPU:0, one launch (start us, length us, event | category | flops | bytes accessed | tf_op | source)
XLA Modules:
  0.0 38.6 jit_solution(3981807873265087682)
XLA Ops:
  0.6 0.5 %collective-permute-start = (f32[512,128]{1,0:T(8,128)}, f32[512,128]{1,0:T(8,128)S(1)}, u32[]{:S(2)}, u32[]{:S(2)}) collective-permute-start(f32[512,128]{1,0:T(8,128)} %bitcast.29), channel_id=1, source_target_pairs={{0,4},{4,0},{8,12},{12,8},{16,20},{20,16},{24,28},{28,24},{1,5},{5... | collective-permute-start | bytes 786440 | tf_op jit(solution)/shard_map/ppermute | solution.py:369
  1.1 1.4 %prepare.1 = (f32[512,128]{1,0:T(8,128)S(1)}, bf16[256,1536]{1,0:T(8,128)(2,1)S(1)}, bf16[512,1536]{1,0:T(8,128)(2,1)S(1)}, f32[8,512]{1,0:T(8,128)S(1)}) custom-call(f32[512,128]{1,0:T(8,128)} %bitcast.30, f32[3,128,1024]{2,1,0:T(8,128)} %bitcast.28, f32[3,1024]{1,0:T(4,128)} %ph_hbm.1, s32[4]{0:T(128)} %g_hbm.1), custom_call_target="tpu_custom_call" | custom-call | flops 2090000000 | bytes 5700000 | tf_op jit(solution)/shard_map/prepare/pallas_call | solution.py:57
  2.6 5.8 %waves.1 = (f32[2,3,1024,256]{3,2,1,0:T(8,128)S(1)}, f32[2,3,1024,256]{3,2,1,0:T(8,128)S(1)}, f32[2,3,1024,256]{3,2,1,0:T(8,128)S(1)}, f32[48,512]{1,0:T(8,128)S...) custom-call(f32[512,128]{1,0:T(8,128)S(1)} %get-tuple-element.20.refs_0_, ...), custom_call_target="tpu_custom_call" | custom-call | flops 8800000000 | bytes 24000000 | tf_op jit(solution)/shard_map/waves/pallas_call | solution.py:57
  8.4 2.9 %collective-permute-start.1 = (f32[24,512]{1,0:T(8,128)S(1)}, f32[24,512]{1,0:T(8,128)S(1)}, u32[]{:S(2)}, u32[]{:S(2)}) collective-permute-start(f32[24,512]{1,0:T(8,128)S(1)} %get-tuple-element.29.refs_6_), channel_id=1, source_target_pairs={{0,8},{4,12},{8,0},{12,4},{16,24},{20,28},{24,16},{28,20},{1,9},{5... | collective-permute-start | bytes 147464 | tf_op jit(solution)/shard_map/ppermute | solution.py:369
  11.2 1.5 %collective-permute-start.2 = (f32[24,512]{1,0:T(8,128)S(1)}, f32[24,512]{1,0:T(8,128)S(1)}, u32[]{:S(2)}, u32[]{:S(2)}) collective-permute-start(f32[24,512]{1,0:T(8,128)S(1)} %get-tuple-element.29.refs_6_), channel_id=1, source_target_pairs={{0,16},{4,20},{8,24},{12,28},{16,0},{20,4},{24,8},{28,12},{1,17},{... | collective-permute-start | bytes 147464 | tf_op jit(solution)/shard_map/ppermute | solution.py:369
  12.7 0.0 collective-permute-start.3
  12.8 2.3 %sines.1.refs_1_ = f32[2,3,1024,256]{3,2,1,0:T(8,128)S(1)} custom-call(f32[2,3,1024,256]{3,2,1,0:T(8,128)S(1)} %get-tuple-element.23.refs_0_, f32[2,3,1024,256]{3,2,1,0:T(8,128)S(1)} %get-tuple-element.24.refs_1_), custom_call_target="tpu_custom_call" | custom-call | flops 2640000000 | bytes 7200000 | tf_op jit(solution)/shard_map/sines/pallas_call | solution.py:57
  15.1 0.2 turn.1.refs_3_
  15.3 2.4 %collective-permute-done.3.refs_9_ = f32[24,512]{1,0:T(8,128)S(1)} collective-permute-done((f32[24,512]{1,0:T(8,128)S(1)}, f32[24,512]{1,0:T(8,128)S(1)}, u32[]{:S(2)}, u32[]{:S(2)}) %collective-permute-start.3) | collective-permute-done | bytes 49184 | tf_op jit(solution)/shard_map/ppermute | solution.py:369
  17.7 5.2 %grads.1 = (f32[2,3,16,512]{3,2,1,0:T(8,128)S(1)}, f32[2,3,16,512]{3,2,1,0:T(8,128)S(1)}, f32[2,3,16,512]{3,2,1,0:T(8,128)S(1)}, f32[2,3,16,512]{3,2,1,0:T(8,128...) custom-call(f32[2,3,1024,256]{3,2,1,0:T(8,128)S(1)} %get-tuple-element.22.refs_0_, ...), custom_call_target="tpu_custom_call" | custom-call | flops 6600000000 | bytes 18000000 | tf_op jit(solution)/shard_map/grads/pallas_call | solution.py:57
  23.0 0.1 collective-permute-start.4
  23.1 0.6 %collective-permute-start.10 = (f32[2,3,16,512]{3,2,1,0:T(8,128)S(1)}, f32[2,3,16,512]{3,2,1,0:T(8,128)S(1)}, u32[]{:S(2)}, u32[]{:S(2)}) collective-permute-start(f32[2,3,16,512]{3,2,1,0:T(8,128)S(1)} %get-tuple-element.37), channel_id=1, source_target_pairs={{0,8},{4,12},{8,0},{12,4},{16,24},{20,28},{24,16},{28,20},{1,9},{5... | collective-permute-start | bytes 589832 | tf_op jit(solution)/shard_map/ppermute | solution.py:369
  23.7 1.4 %collective-permute-start.8 = (f32[2,3,16,512]{3,2,1,0:T(8,128)S(1)}, f32[2,3,16,512]{3,2,1,0:T(8,128)S(1)}, u32[]{:S(2)}, u32[]{:S(2)}) collective-permute-start(f32[2,3,16,512]{3,2,1,0:T(8,128)S(1)} %get-tuple-element.35), channel_id=1, source_target_pairs={{0,24},{4,28},{8,16},{12,20},{16,8},{20,12},{24,0},{28,4},{1,25},{... | collective-permute-start | bytes 589832 | tf_op jit(solution)/shard_map/ppermute | solution.py:369
  25.1 1.5 %collective-permute-start.9 = (f32[2,3,16,512]{3,2,1,0:T(8,128)S(1)}, f32[2,3,16,512]{3,2,1,0:T(8,128)S(1)}, u32[]{:S(2)}, u32[]{:S(2)}) collective-permute-start(f32[2,3,16,512]{3,2,1,0:T(8,128)S(1)} %get-tuple-element.36), channel_id=1, source_target_pairs={{0,16},{4,20},{8,24},{12,28},{16,0},{20,4},{24,8},{28,12},{1,17},{... | collective-permute-start | bytes 589832 | tf_op jit(solution)/shard_map/ppermute | solution.py:369
  26.7 1.6 %collective-permute-start.5 = (f32[128,128]{1,0:T(8,128)S(1)}, f32[128,128]{1,0:T(8,128)S(1)}, u32[]{:S(2)}, u32[]{:S(2)}) collective-permute-start(f32[128,128]{1,0:T(8,128)S(1)} %get-tuple-element.40), channel_id=1, source_target_pairs={{0,1},{1,0},{2,3},{3,2},{4,5},{5,4},{6,7},{7,6},{8,9},{9,8},{10,11... | collective-permute-start | bytes 196616 | tf_op jit(solution)/shard_map/ppermute | solution.py:369
  28.3 2.6 %collective-permute-start.6 = (f32[128,128]{1,0:T(8,128)S(1)}, f32[128,128]{1,0:T(8,128)S(1)}, u32[]{:S(2)}, u32[]{:S(2)}) collective-permute-start(f32[128,128]{1,0:T(8,128)S(1)} %get-tuple-element.42), channel_id=1, source_target_pairs={{0,2},{1,3},{2,0},{3,1},{4,6},{5,7},{6,4},{7,5},{8,10},{9,11},{10,... | collective-permute-start | bytes 196616 | tf_op jit(solution)/shard_map/ppermute | solution.py:369
  30.9 0.1 collective-permute-done.5
  31.0 4.0 %collective-permute-start.7 = (f32[128,128]{1,0:T(8,128)S(1)}, f32[128,128]{1,0:T(8,128)S(1)}, u32[]{:S(2)}, u32[]{:S(2)}) collective-permute-start(f32[128,128]{1,0:T(8,128)S(1)} %get-tuple-element.41), channel_id=1, source_target_pairs={{0,3},{1,2},{2,1},{3,0},{4,7},{5,6},{6,5},{7,4},{8,11},{9,10},{10,... | collective-permute-start | bytes 196616 | tf_op jit(solution)/shard_map/ppermute | solution.py:369
  35.0 1.0 %collective-permute-done.9 = f32[2,3,16,512]{3,2,1,0:T(8,128)S(1)} collective-permute-done((f32[2,3,16,512]{3,2,1,0:T(8,128)S(1)}, f32[2,3,16,512]{3,2,1,0:T(8,128)S(1)}, u32[]{:S(2)}, u32[]{:S(2)}) %collective-permute-start.9) | collective-permute-done | bytes 196640 | tf_op jit(solution)/shard_map/ppermute | solution.py:369
  36.0 0.1 add_add_fusion
  36.1 0.1 collective-permute-start.11
  36.2 1.1 %collective-permute-done.7 = f32[128,128]{1,0:T(8,128)S(1)} collective-permute-done((f32[128,128]{1,0:T(8,128)S(1)}, f32[128,128]{1,0:T(8,128)S(1)}, u32[]{:S(2)}, u32[]{:S(2)}) %collective-permute-start.7) | collective-permute-done | bytes 65568 | tf_op jit(solution)/shard_map/ppermute | solution.py:369
  37.3 0.7 %fusion.4 = f32[128,128]{1,0:T(8,128)} fusion(f32[128,128]{1,0:T(8,128)S(1)} %collective-permute-done.7, f32[128,128]{1,0:T(8,128)S(1)} %collective-permute-done.6, f32[128,128]{1,0:T(8,128)S(1)} %collective-permute-done.5, f32[4,128,128]{2,1,0:T(8,128)S(1)} %add.21), kind=kLoop, calls=%fused_computation.12 | loop fusion | flops 49152 | bytes 327680 | tf_op jit(solution)/shard_map/add | solution.py:482
  38.0 0.7 %maximum_bitcast_fusion = f32[16,3,1024]{2,0,1:T(8,128)} fusion(f32[3,16,512]{2,1,0:T(8,128)S(1)} %get-tuple-element.39, f32[3,16,512]{2,1,0:T(8,128)S(1)} %get-tuple-element.38), kind=kLoop, calls=%fused_computation | loop fusion | flops 49152 | bytes 393216 | tf_op jit(solution)/shard_map/transpose | solution.py:488
  (12 shorter events, 0.1 us)
Async XLA Ops:
  0.6 1.9 %collective-permute-start = (f32[512,128]{1,0:T(8,128)}, f32[512,128]{1,0:T(8,128)S(1)}, u32[]{:S(2)}, u32[]{:S(2)}) collective-permute-start(f32[512,128]{1,0:T(8,128)} %bitcast.29), channel_id=1, source_target_pairs={{0,4},{4,0},{8,12},{12,8},{16,20},{20,16},{24,28},{28,24},{1,5},{5... | collective-permute-start | bytes 786440 | tf_op jit(solution)/shard_map/ppermute | solution.py:369
  8.4 6.9 %collective-permute-start.1 = (f32[24,512]{1,0:T(8,128)S(1)}, f32[24,512]{1,0:T(8,128)S(1)}, u32[]{:S(2)}, u32[]{:S(2)}) collective-permute-start(f32[24,512]{1,0:T(8,128)S(1)} %get-tuple-element.29.refs_6_), channel_id=1, source_target_pairs={{0,8},{4,12},{8,0},{12,4},{16,24},{20,28},{24,16},{28,20},{1,9},{5... | collective-permute-start | bytes 147464 | tf_op jit(solution)/shard_map/ppermute | solution.py:369
  11.2 4.1 %collective-permute-start.2 = (f32[24,512]{1,0:T(8,128)S(1)}, f32[24,512]{1,0:T(8,128)S(1)}, u32[]{:S(2)}, u32[]{:S(2)}) collective-permute-start(f32[24,512]{1,0:T(8,128)S(1)} %get-tuple-element.29.refs_6_), channel_id=1, source_target_pairs={{0,16},{4,20},{8,24},{12,28},{16,0},{20,4},{24,8},{28,12},{1,17},{... | collective-permute-start | bytes 147464 | tf_op jit(solution)/shard_map/ppermute | solution.py:369
  12.7 5.0 %collective-permute-start.3 = (f32[24,512]{1,0:T(8,128)S(1)}, f32[24,512]{1,0:T(8,128)S(1)}, u32[]{:S(2)}, u32[]{:S(2)}) collective-permute-start(f32[24,512]{1,0:T(8,128)S(1)} %get-tuple-element.29.refs_6_), channel_id=1, source_target_pairs={{0,24},{4,28},{8,16},{12,20},{16,8},{20,12},{24,0},{28,4},{1,25},{... | collective-permute-start | bytes 147464 | tf_op jit(solution)/shard_map/ppermute | solution.py:369
  23.0 3.6 %collective-permute-start.4 = (f32[4,128,128]{2,1,0:T(8,128)S(1)}, f32[4,128,128]{2,1,0:T(8,128)S(1)}, u32[]{:S(2)}, u32[]{:S(2)}) collective-permute-start(f32[4,128,128]{2,1,0:T(8,128)S(1)} %get-tuple-element.31), channel_id=1, source_target_pairs={{0,4},{4,0},{8,12},{12,8},{16,20},{20,16},{24,28},{28,24},{1,5},{5... | collective-permute-start | bytes 786440 | tf_op jit(solution)/shard_map/ppermute | solution.py:369
  23.1 12.0 %collective-permute-start.10 = (f32[2,3,16,512]{3,2,1,0:T(8,128)S(1)}, f32[2,3,16,512]{3,2,1,0:T(8,128)S(1)}, u32[]{:S(2)}, u32[]{:S(2)}) collective-permute-start(f32[2,3,16,512]{3,2,1,0:T(8,128)S(1)} %get-tuple-element.37), channel_id=1, source_target_pairs={{0,8},{4,12},{8,0},{12,4},{16,24},{20,28},{24,16},{28,20},{1,9},{5... | collective-permute-start | bytes 589832 | tf_op jit(solution)/shard_map/ppermute | solution.py:369
  23.7 11.4 %collective-permute-start.8 = (f32[2,3,16,512]{3,2,1,0:T(8,128)S(1)}, f32[2,3,16,512]{3,2,1,0:T(8,128)S(1)}, u32[]{:S(2)}, u32[]{:S(2)}) collective-permute-start(f32[2,3,16,512]{3,2,1,0:T(8,128)S(1)} %get-tuple-element.35), channel_id=1, source_target_pairs={{0,24},{4,28},{8,16},{12,20},{16,8},{20,12},{24,0},{28,4},{1,25},{... | collective-permute-start | bytes 589832 | tf_op jit(solution)/shard_map/ppermute | solution.py:369
  25.1 10.9 %collective-permute-start.9 = (f32[2,3,16,512]{3,2,1,0:T(8,128)S(1)}, f32[2,3,16,512]{3,2,1,0:T(8,128)S(1)}, u32[]{:S(2)}, u32[]{:S(2)}) collective-permute-start(f32[2,3,16,512]{3,2,1,0:T(8,128)S(1)} %get-tuple-element.36), channel_id=1, source_target_pairs={{0,16},{4,20},{8,24},{12,28},{16,0},{20,4},{24,8},{28,12},{1,17},{... | collective-permute-start | bytes 589832 | tf_op jit(solution)/shard_map/ppermute | solution.py:369
  26.7 4.3 %collective-permute-start.5 = (f32[128,128]{1,0:T(8,128)S(1)}, f32[128,128]{1,0:T(8,128)S(1)}, u32[]{:S(2)}, u32[]{:S(2)}) collective-permute-start(f32[128,128]{1,0:T(8,128)S(1)} %get-tuple-element.40), channel_id=1, source_target_pairs={{0,1},{1,0},{2,3},{3,2},{4,5},{5,4},{6,7},{7,6},{8,9},{9,8},{10,11... | collective-permute-start | bytes 196616 | tf_op jit(solution)/shard_map/ppermute | solution.py:369
  28.3 7.8 %collective-permute-start.6 = (f32[128,128]{1,0:T(8,128)S(1)}, f32[128,128]{1,0:T(8,128)S(1)}, u32[]{:S(2)}, u32[]{:S(2)}) collective-permute-start(f32[128,128]{1,0:T(8,128)S(1)} %get-tuple-element.42), channel_id=1, source_target_pairs={{0,2},{1,3},{2,0},{3,1},{4,6},{5,7},{6,4},{7,5},{8,10},{9,11},{10,... | collective-permute-start | bytes 196616 | tf_op jit(solution)/shard_map/ppermute | solution.py:369
  31.0 6.2 %collective-permute-start.7 = (f32[128,128]{1,0:T(8,128)S(1)}, f32[128,128]{1,0:T(8,128)S(1)}, u32[]{:S(2)}, u32[]{:S(2)}) collective-permute-start(f32[128,128]{1,0:T(8,128)S(1)} %get-tuple-element.41), channel_id=1, source_target_pairs={{0,3},{1,2},{2,1},{3,0},{4,7},{5,6},{6,5},{7,4},{8,11},{9,10},{10,... | collective-permute-start | bytes 196616 | tf_op jit(solution)/shard_map/ppermute | solution.py:369
  36.1 1.9 %collective-permute-start.11 = (f32[3,16,512]{2,1,0:T(8,128)S(1)}, f32[3,16,512]{2,1,0:T(8,128)S(1)}, u32[]{:S(2)}, u32[]{:S(2)}) collective-permute-start(f32[3,16,512]{2,1,0:T(8,128)S(1)} %slice_bitcast_fusion), channel_id=1, source_target_pairs={{0,4},{4,0},{8,12},{12,8},{16,20},{20,16},{24,28},{28,24},{1,5},{5... | collective-permute-start | bytes 294920 | tf_op jit(solution)/shard_map/ppermute | solution.py:369

commit v8 on v7

--- a/solution.py
+++ b/solution.py
@@ -209,48 +209,67 @@
             snd_ref[HALF * k : HALF * (k + 1), here] = both[k]
 
 
-def sines_kernel(amplitude, half_ref, z_ref, s_ref):
-    chunks, levels, rows, _ = s_ref.shape
+def sines_kernel(amplitude, chunk, half_ref, z_ref, s_ref):
+    levels, rows, _ = s_ref.shape
     coefs = [-math.sqrt(2.0 * amplitude) * coef for coef in COS]
-    for chunk in range(chunks):
-        for level in range(levels):
-
-            def step(i, _):
-                value = horner(z_ref[chunk, level, tile(i), :], coefs)
-                s_ref[chunk, level, tile(i), :] = half_ref[chunk, level, tile(i), :] * value
-                return 0
-
-            lax.fori_loop(0, rows // SUB, step, 0, unroll=16)
-
-
-def compose(chips, loc_ref, weight_ref, got, all_ref):
+    for level in range(levels):
+
+        def step(i, _):
+            value = horner(z_ref[chunk, level, tile(i), :], coefs)
+            s_ref[level, tile(i), :] = half_ref[chunk, level, tile(i), :] * value
+            return 0
+
+        lax.fori_loop(0, rows // SUB, step, 0, unroll=16)
+
+
+def parts_of(ref):
+    return [ref[HALF * k : HALF * (k + 1), :] for k in range(6)]
+
+
+def chain(early, late):
+    a0, a1, a2, a01, a12, a012 = early
+    b0, b1, b2, b01, b12, b012 = late
+    return (
+        a0 + b0,
+        a1 + b1,
+        a2 + b2,
+        a01 + b01 + a0 * b1,
+        a12 + b12 + a1 * b2,
+        a012 + b012 + a0 * b12 + a01 * b2,
+    )
+
+
+def ordered(flag, mine, other):
+    early = [jnp.where(flag, b, a) for a, b in zip(mine, other)]
+    late = [jnp.where(flag, a, b) for a, b in zip(mine, other)]
+    return early, late
+
+
+def chain_kernel(bit, own_ref, other_ref, out_ref):
+    flag = (lax.axis_index("tm") >> 1) & bit != 0
+    both = chain(*ordered(flag, parts_of(own_ref), parts_of(other_ref)))
+    for k in range(6):
+        out_ref[HALF * k : HALF * (k + 1), :] = both[k]
+
+
+def compose(loc_ref, weight_ref, own_ref, got):
     chip = lax.axis_index("tm") >> 1
-    for d in range(chips):
-        all_ref[jnp.bitwise_xor(chip, d)] = got[d][...]
-
     weight = weight_ref[:HALF]
     zero = jnp.zeros(weight.shape, f32)
-
-    def sums_of(j):
-        return [all_ref[j, HALF * k : HALF * (k + 1), :] for k in range(6)]
-
-    def forward(j, carry):
-        p0, p01, p012 = carry
-        b0, b1, b2, b01, b12, b012 = sums_of(j)
-        p012 = p012 + b012 + p0 * b12 + p01 * b2
-        p01 = p01 + b01 + p0 * b1
-        return (p0 + b0, p01, p012)
-
-    def backward(step, carry):
-        t1, t2, t12 = carry
-        b0, b1, b2, b01, b12, b012 = sums_of(chips - 1 - step)
-        t12 = t12 + b12 + b1 * t2
-        return (t1 + b1, t2 + b2, t12)
-
-    entry = lax.fori_loop(0, chip, forward, (zero,) * 3)
-    e1, e2 = entry[:2]
-    totals = lax.fori_loop(chip, chips, forward, entry)
-    t1, t2, t12 = lax.fori_loop(0, chips - 1 - chip, backward, (zero,) * 3)
+    own = parts_of(own_ref)
+    before, after = [zero] * 6, [zero] * 6
+    for k, ref in enumerate(got):
+        other = parts_of(ref)
+        flag = chip & (1 << k) != 0
+        first = [jnp.where(flag, v, 0.0) for v in other]
+        second = [jnp.where(flag, 0.0, v) for v in other]
+        before = chain(first, before)
+        after = chain(after, second)
+    p0, p1, p2, p01, p12, p012 = before
+    e1, e2 = p0, p01
+    _, t1, t2, _, t12, _ = after
+    whole = chain(chain(before, own), after)
+    totals = (whole[0], whole[3], whole[5])
     seeds = [2.0 * weight * jnp.sum(weight * total, axis=0, keepdims=True) for total in totals]
 
     def local(k):
@@ -292,8 +311,8 @@
         slope2 = []
         for which in range(2):
             at = tile(2 * pair + which)
-            u1_ref[at, :] = s_ref[chunk, 1, at, :] * f1
-            slope2.append(s_ref[chunk, 2, at, :] * (scale * f2))
+            u1_ref[at, :] = s_ref[1, at, :] * f1
+            slope2.append(s_ref[2, at, :] * (scale * f2))
             f2 = f2 + f1 * c_ref[chunk, 1, at, :]
             f1 = f1 + c_ref[chunk, 0, at, :]
         keep(pair, 2, slope2)
@@ -308,7 +327,7 @@
         for which in (1, 0):
             at = tile(2 * pair + which)
             slope1.append(u1_ref[at, :] * g1)
-            slope0.append(s_ref[chunk, 0, at, :] * g0)
+            slope0.append(s_ref[0, at, :] * g0)
             g0 = g0 + g1 * c_ref[chunk, 1, at, :]
             g1 = g1 + scale * c_ref[chunk, 2, at, :]
         keep(pair, 0, slope0[::-1])
@@ -318,19 +337,20 @@
     lax.fori_loop(0, rows // (2 * SUB), bwd, (adjoint1, adjoint0), unroll=8)
 
 
-def grads_kernel(sizes, c_ref, s_ref, loc_ref, xt_ref, w_ref, weight_ref, *refs):
-    n_tm, n_freq, wide = sizes
-    chips = n_tm // 2
-    got, refs = refs[:chips], refs[chips:]
-    blocks, refs = refs[:chips], refs[chips:]
-    gk_ref, gs_ref, sh_ref, sl_ref, gp_ref, all_ref, u1_ref, acc_ref, flat_ref = refs
+def grads_kernel(sizes, c_ref, loc_ref, xt_ref, w_ref, weight_ref, *refs):
+    n_tm, n_freq, wide, levels = sizes
+    chunks = c_ref.shape[0]
+    sines, refs = refs[:chunks], refs[chunks:]
+    own_ref, got, refs = refs[0], refs[1 : 1 + levels], refs[1 + levels :]
+    blocks, refs = refs[: n_tm // 2], refs[n_tm // 2 :]
+    gk_ref, gs_ref, sh_ref, sl_ref, gp_ref, u1_ref, acc_ref, flat_ref = refs
     rows, chans = acc_ref.shape
     each = chans // n_tm
     me = lax.axis_index("tm")
     core, z = me & 1, lax.axis_index("freq")
 
-    starts = compose(chips, loc_ref, weight_ref, got, all_ref)
-    for chunk in range(c_ref.shape[0]):
+    starts = compose(loc_ref, weight_ref, own_ref, got)
+    for chunk, s_ref in enumerate(sines):
         slopes(chunk, wide, starts, c_ref, s_ref, u1_ref, sh_ref, sl_ref)
 
     main = jnp.dot(xt_ref[...], sh_ref[...], preferred_element_type=f32)
@@ -413,9 +433,6 @@
     def waves_body(*refs):
         waves_kernel(amplitude, wide, *refs)
 
-    def sines_body(*refs):
-        sines_kernel(amplitude, *refs)
-
     big = pltpu.VMEM((chunks, 3, rows, wide), f32)
     cosines, halves, squares, local, own, flat = call(
         waves_body,
@@ -435,15 +452,53 @@
         y,
         turns,
     )
-    got = [own] + [swap(own, "tm", 2 * d) for d in range(1, chips)]
     (xt,) = call(
         turn_kernel, "turn", 0.8, [VECTORS], [pltpu.VMEM((2 * chans, rows), bf16)], [], flat
     )
 
-    (sines,) = call(sines_body, "sines", 2.4, [VECTORS] * 2, [big], [], halves, squares)
+    def sines_of(chunk):
+        def sines_body(*refs):
+            sines_kernel(amplitude, chunk, *refs)
+
+        return call(
+            sines_body,
+            f"sines{chunk}",
+            1.2,
+            [VECTORS] * 2,
+            [pltpu.VMEM((3, rows, wide), f32)],
+            [],
+            halves,
+            squares,
+        )[0]
+
+    levels = chips.bit_length() - 1
+    got, sines, current = [], [], own
+    for k in range(levels):
+        other = swap(current, "tm", 2 << k)
+        if k < levels - 1:
+
+            def chain_body(*refs, bit=1 << k):
+                chain_kernel(bit, *refs)
+
+            if len(sines) < chunks:
+                sines.append(sines_of(len(sines)))
+                other, sines[-1] = lax.optimization_barrier((other, sines[-1]))
+            (current,) = call(
+                chain_body,
+                "chain",
+                0.1,
+                [VECTORS] * 2,
+                [jax.ShapeDtypeStruct(own.shape, f32)],
+                [],
+                current,
+                other,
+            )
+            halves, current = lax.optimization_barrier((halves, current))
+        got.append(other)
+    sines += [sines_of(k) for k in range(len(sines), chunks)]
 
     def grads_body(*refs):
-        grads_kernel((n_tm, n_freq, wide), *refs)
+        grads_kernel((n_tm, n_freq, wide, levels), *refs)
 
     bshape = jax.ShapeDtypeStruct((2, 3, each, mine), f32)
     gshape = jax.ShapeDtypeStruct((n_freq, rows // 2 // n_freq, chans), f32)
@@ -451,23 +506,23 @@
         grads_body,
         "grads",
         6.0,
-        [VECTORS] * (6 + chips),
+        [VECTORS] * (6 + chunks + levels),
         [bshape] * chips + [gshape] * 2,
         [
             pltpu.VMEM((rows, 3 * mine), bf16),
             pltpu.VMEM((rows, 3 * mine), bf16),
             pltpu.VMEM((n_tm, 3, each, mine), f32),
-            pltpu.VMEM((chips, 3 * SUB, mine), f32),
             pltpu.VMEM((rows, wide), f32),
             pltpu.VMEM((rows, chans), f32),
             pltpu.VMEM((2, rows // 2, chans), f32),
         ],
         cosines,
-        sines,
         local,
         xt,
         weights,
         weight,
+        *sines,
+        own,
         *got,
     )
 

time: 38.9 us -> 38.5 us (0.990)
  waiting for transfers between devices: 4.6 us -> 4.06 us
    ppermute x12 -> x11, waiting for transfers between devices: 4.6 us -> 4.06 us  [swap(): return lax.ppermute(value, axis, [(i, i ^ distance) for i in range(count)])]
    ppermute x12 -> x11, starting transfers between devices: 16.9 us -> 17 us  [swap(): return lax.ppermute(value, axis, [(i, i ^ distance) for i in range(count)])]
    pallas_call x5 -> x7, Pallas kernels: 15 us -> 14.9 us  [call(): pl.pallas_call(body, in_specs=ins, out_specs=[VECTORS] * len(outs), out_s...]
  transfers between devices with their start and end apart: 12 -> 11, of which waited for: 4 -> 5; matrix products, arithmetic and copies ran while one was open for 2% -> 2% of each run, Pallas kernels for 10% -> 10%
where the time goes in v8:
time: 38.5 us; the launch traced here: 38.2 us
  starting transfers between devices  17 us (44%)
  Pallas kernels  14.9 us (39%)
  waiting for transfers between devices  4.06 us (11%)
  other arithmetic  1.46 us (4%)
  between operations  0.74 us (2%)
    ppermute x11, starting transfers between devices, swap(): return lax.ppermute(value, axis, [(i, i ^ distance) for i in range(count)])  17 us
    pallas_call x7, Pallas kernels, call(): pl.pallas_call(body, in_specs=ins, out_specs=[VECTORS] * len(outs), out_s...  14.9 us
    ppermute x11, waiting for transfers between devices, swap(): return lax.ppermute(value, axis, [(i, i ^ distance) for i in range(count)])  4.06 us
  transfers between devices with their start and end apart: 11, of which 5 were waited for; matrix products, arithmetic and copies ran while one was open for 2% of the time, Pallas kernels for 10%

profile of v8, /device:TPU:0, one launch (start us, length us, event | category | flops | bytes accessed | tf_op | source)
XLA Modules:
  0.0 38.2 jit_solution(6118334353467578852)
XLA Ops:
  0.6 0.5 %collective-permute-start = (f32[512,128]{1,0:T(8,128)}, f32[512,128]{1,0:T(8,128)S(1)}, u32[]{:S(2)}, u32[]{:S(2)}) collective-permute-start(f32[512,128]{1,0:T(8,128)} %bitcast.29), channel_id=1, source_target_pairs={{0,4},{4,0},{8,12},{12,8},{16,20},{20,16},{24,28},{28,24},{1,5},{5... | collective-permute-start | bytes 786440 | tf_op jit(solution)/shard_map/ppermute | solution.py:389
  1.1 1.4 %prepare.1 = (f32[512,128]{1,0:T(8,128)S(1)}, bf16[256,1536]{1,0:T(8,128)(2,1)S(1)}, bf16[512,1536]{1,0:T(8,128)(2,1)S(1)}, f32[8,512]{1,0:T(8,128)S(1)}) custom-call(f32[512,128]{1,0:T(8,128)} %bitcast.30, f32[3,128,1024]{2,1,0:T(8,128)} %bitcast.28, f32[3,1024]{1,0:T(4,128)} %ph_hbm.1, s32[4]{0:T(128)} %g_hbm.1), custom_call_target="tpu_custom_call" | custom-call | flops 2090000000 | bytes 5700000 | tf_op jit(solution)/shard_map/prepare/pallas_call | solution.py:57
  2.6 5.8 %waves.1 = (f32[2,3,1024,256]{3,2,1,0:T(8,128)S(1)}, f32[2,3,1024,256]{3,2,1,0:T(8,128)S(1)}, f32[2,3,1024,256]{3,2,1,0:T(8,128)S(1)}, f32[48,512]{1,0:T(8,128)S...) custom-call(f32[512,128]{1,0:T(8,128)S(1)} %get-tuple-element.24.refs_0_, ...), custom_call_target="tpu_custom_call" | custom-call | flops 8800000000 | bytes 24000000 | tf_op jit(solution)/shard_map/waves/pallas_call | solution.py:57
  8.4 2.9 %collective-permute-start.1 = (f32[24,512]{1,0:T(8,128)S(1)}, f32[24,512]{1,0:T(8,128)S(1)}, u32[]{:S(2)}, u32[]{:S(2)}) collective-permute-start(f32[24,512]{1,0:T(8,128)S(1)} %get-tuple-element.31.refs_0_.refs_7_), channel_id=1, source_target_pairs={{0,8},{4,12},{8,0},{12,4},{16,24},{20,28},{24,16},{28,20},{1,9},{5... | collective-permute-start | bytes 147464 | tf_op jit(solution)/shard_map/ppermute | solution.py:389
  11.2 1.2 %sines0.1.refs_5_ = f32[3,1024,256]{2,1,0:T(8,128)S(1)} custom-call(f32[2,3,1024,256]{3,2,1,0:T(8,128)S(1)} %get-tuple-element.36.refs_0_, f32[2,3,1024,256]{3,2,1,0:T(8,128)S(1)} %get-tuple-element.33.refs_1_), custom_call_target="tpu_custom_call" | custom-call | flops 1320000000 | bytes 3600000 | tf_op jit(solution)/shard_map/sines0/pallas_call | solution.py:57
  12.4 0.2 turn.1.refs_2_
  12.6 0.7 %collective-permute-done.1.refs_1_.refs_8_ = f32[24,512]{1,0:T(8,128)S(1)} collective-permute-done((f32[24,512]{1,0:T(8,128)S(1)}, f32[24,512]{1,0:T(8,128)S(1)}, u32[]{:S(2)}, u32[]{:S(2)}) %collective-permute-start.1) | collective-permute-done | bytes 49184 | tf_op jit(solution)/shard_map/ppermute | solution.py:389
  13.4 2.1 %collective-permute-start.2 = (f32[24,512]{1,0:T(8,128)S(1)}, f32[24,512]{1,0:T(8,128)S(1)}, u32[]{:S(2)}, u32[]{:S(2)}) collective-permute-start(f32[24,512]{1,0:T(8,128)S(1)} %chain.1), channel_id=1, source_target_pairs={{0,16},{4,20},{8,24},{12,28},{16,0},{20,4},{24,8},{28,12},{1,17},{... | collective-permute-start | bytes 147464 | tf_op jit(solution)/shard_map/ppermute | solution.py:389
  15.4 1.2 %sines1.1.refs_6_ = f32[3,1024,256]{2,1,0:T(8,128)S(1)} custom-call(f32[2,3,1024,256]{3,2,1,0:T(8,128)S(1)} %get-tuple-element.36.refs_0_, f32[2,3,1024,256]{3,2,1,0:T(8,128)S(1)} %get-tuple-element.33.refs_1_), custom_call_target="tpu_custom_call" | custom-call | flops 1320000000 | bytes 3600000 | tf_op jit(solution)/shard_map/sines1/pallas_call | solution.py:57
  16.6 0.9 %collective-permute-done.2.refs_9_ = f32[24,512]{1,0:T(8,128)S(1)} collective-permute-done((f32[24,512]{1,0:T(8,128)S(1)}, f32[24,512]{1,0:T(8,128)S(1)}, u32[]{:S(2)}, u32[]{:S(2)}) %collective-permute-start.2) | collective-permute-done | bytes 49184 | tf_op jit(solution)/shard_map/ppermute | solution.py:389
  17.5 5.2 %grads.1 = (f32[2,3,16,512]{3,2,1,0:T(8,128)S(1)}, f32[2,3,16,512]{3,2,1,0:T(8,128)S(1)}, f32[2,3,16,512]{3,2,1,0:T(8,128)S(1)}, f32[2,3,16,512]{3,2,1,0:T(8,128...) custom-call(f32[2,3,1024,256]{3,2,1,0:T(8,128)S(1)} %get-tuple-element.26.refs_0_, ...), custom_call_target="tpu_custom_call" | custom-call | flops 6600000000 | bytes 18000000 | tf_op jit(solution)/shard_map/grads/pallas_call | solution.py:57
  22.7 0.1 collective-permute-start.3
  22.8 2.1 %collective-permute-start.9 = (f32[2,3,16,512]{3,2,1,0:T(8,128)S(1)}, f32[2,3,16,512]{3,2,1,0:T(8,128)S(1)}, u32[]{:S(2)}, u32[]{:S(2)}) collective-permute-start(f32[2,3,16,512]{3,2,1,0:T(8,128)S(1)} %get-tuple-element.45), channel_id=1, source_target_pairs={{0,8},{4,12},{8,0},{12,4},{16,24},{20,28},{24,16},{28,20},{1,9},{5... | collective-permute-start | bytes 589832 | tf_op jit(solution)/shard_map/ppermute | solution.py:389
  24.9 1.5 %collective-permute-start.8 = (f32[2,3,16,512]{3,2,1,0:T(8,128)S(1)}, f32[2,3,16,512]{3,2,1,0:T(8,128)S(1)}, u32[]{:S(2)}, u32[]{:S(2)}) collective-permute-start(f32[2,3,16,512]{3,2,1,0:T(8,128)S(1)} %get-tuple-element.44), channel_id=1, source_target_pairs={{0,16},{4,20},{8,24},{12,28},{16,0},{20,4},{24,8},{28,12},{1,17},{... | collective-permute-start | bytes 589832 | tf_op jit(solution)/shard_map/ppermute | solution.py:389
  26.5 2.1 %collective-permute-start.4 = (f32[128,128]{1,0:T(8,128)S(1)}, f32[128,128]{1,0:T(8,128)S(1)}, u32[]{:S(2)}, u32[]{:S(2)}) collective-permute-start(f32[128,128]{1,0:T(8,128)S(1)} %get-tuple-element.48), channel_id=1, source_target_pairs={{0,1},{1,0},{2,3},{3,2},{4,5},{5,4},{6,7},{7,6},{8,9},{9,8},{10,11... | collective-permute-start | bytes 196616 | tf_op jit(solution)/shard_map/ppermute | solution.py:389
  28.6 2.5 %collective-permute-start.6 = (f32[128,128]{1,0:T(8,128)S(1)}, f32[128,128]{1,0:T(8,128)S(1)}, u32[]{:S(2)}, u32[]{:S(2)}) collective-permute-start(f32[128,128]{1,0:T(8,128)S(1)} %get-tuple-element.49), channel_id=1, source_target_pairs={{0,3},{1,2},{2,1},{3,0},{4,7},{5,6},{6,5},{7,4},{8,11},{9,10},{10,... | collective-permute-start | bytes 196616 | tf_op jit(solution)/shard_map/ppermute | solution.py:389
  31.1 3.2 %collective-permute-start.5 = (f32[128,128]{1,0:T(8,128)S(1)}, f32[128,128]{1,0:T(8,128)S(1)}, u32[]{:S(2)}, u32[]{:S(2)}) collective-permute-start(f32[128,128]{1,0:T(8,128)S(1)} %get-tuple-element.50), channel_id=1, source_target_pairs={{0,2},{1,3},{2,0},{3,1},{4,6},{5,7},{6,4},{7,5},{8,10},{9,11},{10,... | collective-permute-start | bytes 196616 | tf_op jit(solution)/shard_map/ppermute | solution.py:389
  34.3 1.8 %collective-permute-done.8 = f32[2,3,16,512]{3,2,1,0:T(8,128)S(1)} collective-permute-done((f32[2,3,16,512]{3,2,1,0:T(8,128)S(1)}, f32[2,3,16,512]{3,2,1,0:T(8,128)S(1)}, u32[]{:S(2)}, u32[]{:S(2)}) %collective-permute-start.8) | collective-permute-done | bytes 196640 | tf_op jit(solution)/shard_map/ppermute | solution.py:389
  36.0 0.1 add_add_fusion
  36.1 0.1 collective-permute-start.10
  36.2 0.3 collective-permute-done.5
  36.6 0.7 %fusion.4 = f32[128,128]{1,0:T(8,128)} fusion(f32[128,128]{1,0:T(8,128)S(1)} %collective-permute-done.6, f32[128,128]{1,0:T(8,128)S(1)} %collective-permute-done.5, f32[128,128]{1,0:T(8,128)S(1)} %collective-permute-done.4, f32[4,128,128]{2,1,0:T(8,128)S(1)} %add.21), kind=kLoop, calls=%fused_computation.12 | loop fusion | flops 49152 | bytes 327680 | tf_op jit(solution)/shard_map/add | solution.py:537
  37.2 0.3 collective-permute-done.10
  37.5 0.7 %maximum_bitcast_fusion = f32[16,3,1024]{2,0,1:T(8,128)} fusion(f32[3,16,512]{2,1,0:T(8,128)S(1)} %get-tuple-element.47, f32[3,16,512]{2,1,0:T(8,128)S(1)} %get-tuple-element.46), kind=kLoop, calls=%fused_computation | loop fusion | flops 49152 | bytes 393216 | tf_op jit(solution)/shard_map/transpose | solution.py:543
  (12 shorter events, 0.1 us)
Async XLA Ops:
  0.6 1.9 %collective-permute-start = (f32[512,128]{1,0:T(8,128)}, f32[512,128]{1,0:T(8,128)S(1)}, u32[]{:S(2)}, u32[]{:S(2)}) collective-permute-start(f32[512,128]{1,0:T(8,128)} %bitcast.29), channel_id=1, source_target_pairs={{0,4},{4,0},{8,12},{12,8},{16,20},{20,16},{24,28},{28,24},{1,5},{5... | collective-permute-start | bytes 786440 | tf_op jit(solution)/shard_map/ppermute | solution.py:389
  8.4 5.0 %collective-permute-start.1 = (f32[24,512]{1,0:T(8,128)S(1)}, f32[24,512]{1,0:T(8,128)S(1)}, u32[]{:S(2)}, u32[]{:S(2)}) collective-permute-start(f32[24,512]{1,0:T(8,128)S(1)} %get-tuple-element.31.refs_0_.refs_7_), channel_id=1, source_target_pairs={{0,8},{4,12},{8,0},{12,4},{16,24},{20,28},{24,16},{28,20},{1,9},{5... | collective-permute-start | bytes 147464 | tf_op jit(solution)/shard_map/ppermute | solution.py:389
  13.4 4.2 %collective-permute-start.2 = (f32[24,512]{1,0:T(8,128)S(1)}, f32[24,512]{1,0:T(8,128)S(1)}, u32[]{:S(2)}, u32[]{:S(2)}) collective-permute-start(f32[24,512]{1,0:T(8,128)S(1)} %chain.1), channel_id=1, source_target_pairs={{0,16},{4,20},{8,24},{12,28},{16,0},{20,4},{24,8},{28,12},{1,17},{... | collective-permute-start | bytes 147464 | tf_op jit(solution)/shard_map/ppermute | solution.py:389
  22.7 3.7 %collective-permute-start.3 = (f32[4,128,128]{2,1,0:T(8,128)S(1)}, f32[4,128,128]{2,1,0:T(8,128)S(1)}, u32[]{:S(2)}, u32[]{:S(2)}) collective-permute-start(f32[4,128,128]{2,1,0:T(8,128)S(1)} %get-tuple-element.39), channel_id=1, source_target_pairs={{0,4},{4,0},{8,12},{12,8},{16,20},{20,16},{24,28},{28,24},{1,5},{5... | collective-permute-start | bytes 786440 | tf_op jit(solution)/shard_map/ppermute | solution.py:389
  22.8 11.5 %collective-permute-start.9 = (f32[2,3,16,512]{3,2,1,0:T(8,128)S(1)}, f32[2,3,16,512]{3,2,1,0:T(8,128)S(1)}, u32[]{:S(2)}, u32[]{:S(2)}) collective-permute-start(f32[2,3,16,512]{3,2,1,0:T(8,128)S(1)} %get-tuple-element.45), channel_id=1, source_target_pairs={{0,8},{4,12},{8,0},{12,4},{16,24},{20,28},{24,16},{28,20},{1,9},{5... | collective-permute-start | bytes 589832 | tf_op jit(solution)/shard_map/ppermute | solution.py:389
  24.9 11.2 %collective-permute-start.8 = (f32[2,3,16,512]{3,2,1,0:T(8,128)S(1)}, f32[2,3,16,512]{3,2,1,0:T(8,128)S(1)}, u32[]{:S(2)}, u32[]{:S(2)}) collective-permute-start(f32[2,3,16,512]{3,2,1,0:T(8,128)S(1)} %get-tuple-element.44), channel_id=1, source_target_pairs={{0,16},{4,20},{8,24},{12,28},{16,0},{20,4},{24,8},{28,12},{1,17},{... | collective-permute-start | bytes 589832 | tf_op jit(solution)/shard_map/ppermute | solution.py:389
  26.4 9.7 %collective-permute-start.7 = (f32[2,3,16,512]{3,2,1,0:T(8,128)S(1)}, f32[2,3,16,512]{3,2,1,0:T(8,128)S(1)}, u32[]{:S(2)}, u32[]{:S(2)}) collective-permute-start(f32[2,3,16,512]{3,2,1,0:T(8,128)S(1)} %get-tuple-element.43), channel_id=1, source_target_pairs={{0,24},{4,28},{8,16},{12,20},{16,8},{20,12},{24,0},{28,4},{1,25},{... | collective-permute-start | bytes 589832 | tf_op jit(solution)/shard_map/ppermute | solution.py:389
  26.5 4.6 %collective-permute-start.4 = (f32[128,128]{1,0:T(8,128)S(1)}, f32[128,128]{1,0:T(8,128)S(1)}, u32[]{:S(2)}, u32[]{:S(2)}) collective-permute-start(f32[128,128]{1,0:T(8,128)S(1)} %get-tuple-element.48), channel_id=1, source_target_pairs={{0,1},{1,0},{2,3},{3,2},{4,5},{5,4},{6,7},{7,6},{8,9},{9,8},{10,11... | collective-permute-start | bytes 196616 | tf_op jit(solution)/shard_map/ppermute | solution.py:389
  28.6 7.6 %collective-permute-start.6 = (f32[128,128]{1,0:T(8,128)S(1)}, f32[128,128]{1,0:T(8,128)S(1)}, u32[]{:S(2)}, u32[]{:S(2)}) collective-permute-start(f32[128,128]{1,0:T(8,128)S(1)} %get-tuple-element.49), channel_id=1, source_target_pairs={{0,3},{1,2},{2,1},{3,0},{4,7},{5,6},{6,5},{7,4},{8,11},{9,10},{10,... | collective-permute-start | bytes 196616 | tf_op jit(solution)/shard_map/ppermute | solution.py:389
  31.1 5.5 %collective-permute-start.5 = (f32[128,128]{1,0:T(8,128)S(1)}, f32[128,128]{1,0:T(8,128)S(1)}, u32[]{:S(2)}, u32[]{:S(2)}) collective-permute-start(f32[128,128]{1,0:T(8,128)S(1)} %get-tuple-element.50), channel_id=1, source_target_pairs={{0,2},{1,3},{2,0},{3,1},{4,6},{5,7},{6,4},{7,5},{8,10},{9,11},{10,... | collective-permute-start | bytes 196616 | tf_op jit(solution)/shard_map/ppermute | solution.py:389
  36.1 1.4 %collective-permute-start.10 = (f32[3,16,512]{2,1,0:T(8,128)S(1)}, f32[3,16,512]{2,1,0:T(8,128)S(1)}, u32[]{:S(2)}, u32[]{:S(2)}) collective-permute-start(f32[3,16,512]{2,1,0:T(8,128)S(1)} %slice_bitcast_fusion), channel_id=1, source_target_pairs={{0,4},{4,0},{8,12},{12,8},{16,20},{20,16},{24,28},{28,24},{1,5},{5... | collective-permute-start | bytes 294920 | tf_op jit(solution)/shard_map/ppermute | solution.py:389

commit v9 on v7

--- a/solution.py
+++ b/solution.py
@@ -223,34 +223,48 @@
             lax.fori_loop(0, rows // SUB, step, 0, unroll=16)
 
 
-def compose(chips, loc_ref, weight_ref, got, all_ref):
+def parts_of(ref):
+    return [ref[HALF * k : HALF * (k + 1), :] for k in range(6)]
+
+
+def chain(early, late):
+    a0, a1, a2, a01, a12, a012 = early
+    b0, b1, b2, b01, b12, b012 = late
+    return (
+        a0 + b0,
+        a1 + b1,
+        a2 + b2,
+        a01 + b01 + a0 * b1,
+        a12 + b12 + a1 * b2,
+        a012 + b012 + a0 * b12 + a01 * b2,
+    )
+
+
+def ordered(flag, mine, other):
+    early = [jnp.where(flag, b, a) for a, b in zip(mine, other)]
+    late = [jnp.where(flag, a, b) for a, b in zip(mine, other)]
+    return early, late
+
+
+def compose(loc_ref, weight_ref, own_ref, got):
     chip = lax.axis_index("tm") >> 1
-    for d in range(chips):
-        all_ref[jnp.bitwise_xor(chip, d)] = got[d][...]
-
     weight = weight_ref[:HALF]
     zero = jnp.zeros(weight.shape, f32)
-
-    def sums_of(j):
-        return [all_ref[j, HALF * k : HALF * (k + 1), :] for k in range(6)]
-
-    def forward(j, carry):
-        p0, p01, p012 = carry
-        b0, b1, b2, b01, b12, b012 = sums_of(j)
-        p012 = p012 + b012 + p0 * b12 + p01 * b2
-        p01 = p01 + b01 + p0 * b1
-        return (p0 + b0, p01, p012)
-
-    def backward(step, carry):
-        t1, t2, t12 = carry
-        b0, b1, b2, b01, b12, b012 = sums_of(chips - 1 - step)
-        t12 = t12 + b12 + b1 * t2
-        return (t1 + b1, t2 + b2, t12)
-
-    entry = lax.fori_loop(0, chip, forward, (zero,) * 3)
-    e1, e2 = entry[:2]
-    totals = lax.fori_loop(chip, chips, forward, entry)
-    t1, t2, t12 = lax.fori_loop(0, chips - 1 - chip, backward, (zero,) * 3)
+    blocks = [parts_of(ref) for ref in (own_ref, *got)]
+    before, after = [zero] * 6, [zero] * 6
+    for k in range(len(got).bit_length()):
+        other = blocks[1]
+        flag = chip & (1 << k) != 0
+        first = [jnp.where(flag, v, 0.0) for v in other]
+        second = [jnp.where(flag, 0.0, v) for v in other]
+        before = chain(first, before)
+        after = chain(after, second)
+        blocks = [chain(*ordered(flag, a, b)) for a, b in zip(blocks[::2], blocks[1::2])]
+    p0, p1, p2, p01, p12, p012 = before
+    e1, e2 = p0, p01
+    _, t1, t2, _, t12, _ = after
+    whole = blocks[0]
+    totals = (whole[0], whole[3], whole[5])
     seeds = [2.0 * weight * jnp.sum(weight * total, axis=0, keepdims=True) for total in totals]
 
     def local(k):
@@ -318,33 +332,15 @@
     lax.fori_loop(0, rows // (2 * SUB), bwd, (adjoint1, adjoint0), unroll=8)
 
 
-def grads_kernel(sizes, c_ref, s_ref, loc_ref, xt_ref, w_ref, weight_ref, *refs):
-    n_tm, n_freq, wide = sizes
-    chips = n_tm // 2
-    got, refs = refs[:chips], refs[chips:]
-    blocks, refs = refs[:chips], refs[chips:]
-    gk_ref, gs_ref, sh_ref, sl_ref, gp_ref, all_ref, u1_ref, acc_ref, flat_ref = refs
+def increments_kernel(sizes, c_ref, s_ref, loc_ref, w_ref, weight_ref, own_ref, *refs):
+    chips, n_freq, wide = sizes
+    got, refs = refs[: chips - 1], refs[chips - 1 :]
+    gk_ref, gs_ref, sh_ref, sl_ref, u1_ref, acc_ref, flat_ref = refs
     rows, chans = acc_ref.shape
-    each = chans // n_tm
-    me = lax.axis_index("tm")
-    core, z = me & 1, lax.axis_index("freq")
-
-    starts = compose(chips, loc_ref, weight_ref, got, all_ref)
+    core, z = lax.axis_index("tm") & 1, lax.axis_index("freq")
+    starts = compose(loc_ref, weight_ref, own_ref, got)
     for chunk in range(c_ref.shape[0]):
         slopes(chunk, wide, starts, c_ref, s_ref, u1_ref, sh_ref, sl_ref)
-
-    main = jnp.dot(xt_ref[...], sh_ref[...], preferred_element_type=f32)
-    rest = jnp.dot(xt_ref[:chans, :], sl_ref[...], preferred_element_type=f32)
-    grad = main[:chans] + main[chans:] + rest
-    for chunk in range(c_ref.shape[0]):
-        for level in range(3):
-            at = (3 * chunk + level) * wide
-            for d in range(n_tm):
-                gp_ref[d, level, :, chunk * wide : (chunk + 1) * wide] = grad[
-                    each * d : each * (d + 1), at : at + wide
-                ]
-    for d in range(n_tm):
-        blocks[d // 2][d % 2] = gp_ref[jnp.bitwise_xor(me, d)]
 
     main = lax.dot_general(sh_ref[...], w_ref[...], NT, preferred_element_type=f32)
     rest = lax.dot_general(sl_ref[...], w_ref[:chans, :], NT, preferred_element_type=f32)
@@ -362,6 +358,29 @@
         at = pl.ds(pl.multiple_of(jnp.bitwise_xor(z, j) * piece, piece), piece)
         gk_ref[j] = flat_ref[core, at, :]
         gs_ref[j] = flat_ref[1 - core, at, :]
+
+
+def frequencies_kernel(sizes, bits, xt_ref, sh_ref, sl_ref, *refs):
+    n_tm, wide = sizes
+    chips, chunks = n_tm // 2, len(bits)
+    blocks, gp_ref = refs[: 2 * chunks], refs[2 * chunks]
+    chans = xt_ref.shape[0] // 2
+    each = chans // n_tm
+    me = lax.axis_index("tm")
+    main = jnp.dot(xt_ref[...], sh_ref[...], preferred_element_type=f32)
+    rest = jnp.dot(xt_ref[:chans, :], sl_ref[...], preferred_element_type=f32)
+    grad = main[:chans] + main[chans:] + rest
+    for chunk in range(chunks):
+        for level in range(3):
+            at = (3 * chunk + level) * wide
+            for d in range(n_tm):
+                gp_ref[chunk, d, level] = grad[each * d : each * (d + 1), at : at + wide]
+        keep_ref, send_ref = blocks[2 * chunk : 2 * chunk + 2]
+        bit = bits[chunk]
+        for k, j in enumerate([j for j in range(chips) if not j & bit]):
+            for side in range(2):
+                keep_ref[k, side] = gp_ref[chunk, jnp.bitwise_xor(me, 2 * j + side)]
+                send_ref[k, side] = gp_ref[chunk, jnp.bitwise_xor(me, 2 * (j | bit) + side)]
 
 
 def swap(value, axis, distance):
@@ -413,9 +432,6 @@
     def waves_body(*refs):
         waves_kernel(amplitude, wide, *refs)
 
-    def sines_body(*refs):
-        sines_kernel(amplitude, *refs)
-
     big = pltpu.VMEM((chunks, 3, rows, wide), f32)
     cosines, halves, squares, local, own, flat = call(
         waves_body,
@@ -435,29 +451,27 @@
         y,
         turns,
     )
-    got = [own] + [swap(own, "tm", 2 * d) for d in range(1, chips)]
     (xt,) = call(
         turn_kernel, "turn", 0.8, [VECTORS], [pltpu.VMEM((2 * chans, rows), bf16)], [], flat
     )
 
+    def sines_body(*refs):
+        sines_kernel(amplitude, *refs)
+
+    got = [swap(own, "tm", 2 * d) for d in range(1, chips)]
     (sines,) = call(sines_body, "sines", 2.4, [VECTORS] * 2, [big], [], halves, squares)
 
-    def grads_body(*refs):
-        grads_kernel((n_tm, n_freq, wide), *refs)
-
-    bshape = jax.ShapeDtypeStruct((2, 3, each, mine), f32)
+    def increments_body(*refs):
+        increments_kernel((chips, n_freq, wide), *refs)
+
     gshape = jax.ShapeDtypeStruct((n_freq, rows // 2 // n_freq, chans), f32)
-    *blocks, kept, sent = call(
-        grads_body,
-        "grads",
-        6.0,
-        [VECTORS] * (6 + chips),
-        [bshape] * chips + [gshape] * 2,
+    kept, sent, high, low = call(
+        increments_body,
+        "increments",
+        3.8,
+        [VECTORS] * (5 + chips),
+        [gshape] * 2 + [pltpu.VMEM((rows, 3 * mine), bf16)] * 2,
         [
-            pltpu.VMEM((rows, 3 * mine), bf16),
-            pltpu.VMEM((rows, 3 * mine), bf16),
-            pltpu.VMEM((n_tm, 3, each, mine), f32),
-            pltpu.VMEM((chips, 3 * SUB, mine), f32),
             pltpu.VMEM((rows, wide), f32),
             pltpu.VMEM((rows, chans), f32),
             pltpu.VMEM((2, rows // 2, chans), f32),
@@ -465,23 +479,49 @@
         cosines,
         sines,
         local,
-        xt,
         weights,
         weight,
+        own,
         *got,
     )
 
+    bits = [1 << k for k in range(chips.bit_length() - 1)]
+    orders = [bits if chunk % 2 == 0 else bits[::-1] for chunk in range(chunks)]
+
+    def frequencies_body(*refs):
+        frequencies_kernel((n_tm, wide), [order[0] for order in orders], *refs)
+
+    bshape = jax.ShapeDtypeStruct((chips // 2, 2, 3, each, wide), f32)
+    blocks = call(
+        frequencies_body,
+        "frequencies",
+        1.5,
+        [VECTORS] * 3,
+        [bshape] * (2 * chunks),
+        [pltpu.VMEM((chunks, n_tm, 3, each, wide), f32)],
+        xt,
+        high,
+        low,
+    )
     pieces = kept + swap(sent, "tm", 1)
+    pieces, *blocks = lax.optimization_barrier((pieces, *blocks))
     others = [swap(pieces[j], "freq", j) for j in range(1, n_freq)]
-    others[0], blocks[0] = lax.optimization_barrier((others[0], blocks[0]))
-    total = blocks[0]
-    for d in range(chips - 1, 0, -1):
-        total = total + swap(blocks[d], "tm", 2 * d)
     result = pieces[0]
     for other in others:
         result = result + other
     grad_increments = result.reshape(steps // n_freq, batch, chans)
 
+    sums = [
+        blocks[2 * k] + swap(blocks[2 * k + 1], "tm", 2 * order[0]) for k, order in enumerate(orders)
+    ]
+    for step in range(1, len(bits)):
+        for k, order in enumerate(orders):
+            place = sum(1 for bit in order[step:] if bit < order[step])
+            halves = sums[k].reshape((-1, 2, 1 << place) + bshape.shape[1:])
+            shape = (-1,) + bshape.shape[1:]
+            mate = swap(halves[:, 1].reshape(shape), "tm", 2 * order[step])
+            sums[k] = halves[:, 0].reshape(shape) + mate
+    total = jnp.concatenate([value[0] for value in sums], axis=-1)
     here, away = total[0], swap(total[1], "tm", 1)
     even = lax.axis_index("tm") & 1 == 0
     low, high = jnp.where(even, here, away), jnp.where(even, away, here)

time: 38.9 us -> 45.4 us (1.17)
  local copies, waits for them, and re-layouts: 0.02 us -> 5.37 us
  starting transfers between devices: 16.9 us -> 12.1 us
  waiting for transfers between devices: 4.6 us -> 8.72 us
  other arithmetic: 1.46 us -> 2.43 us
  Pallas kernels: 15 us -> 15.7 us
    unnamed x0 -> x8, local copies, waits for them, and re-layouts: none -> 5.34 us
    ppermute x12 -> x13, starting transfers between devices: 16.9 us -> 12.1 us  [swap(): return lax.ppermute(value, axis, [(i, i ^ distance) for i in range(count)])]
    ppermute x12 -> x13, waiting for transfers between devices: 4.6 us -> 8.72 us  [swap(): return lax.ppermute(value, axis, [(i, i ^ distance) for i in range(count)])]
    add x1, other arithmetic: 0.05 us -> 0.98 us  [on_device(): pieces = kept + swap(sent, 'tm', 1)]
    pallas_call x5 -> x6, Pallas kernels: 15 us -> 15.7 us  [call(): pl.pallas_call(body, in_specs=ins, out_specs=[VECTORS] * len(outs), out_s...]
  transfers between devices with their start and end apart: 12 -> 13, of which waited for: 4 -> 6; matrix products, arithmetic and copies ran while one was open for 2% -> 2% of each run, Pallas kernels for 10% -> 12%
where the time goes in v9:
time: 45.4 us; the launch traced here: 45.1 us
  Pallas kernels  15.7 us (35%)
  starting transfers between devices  12.1 us (27%)
  waiting for transfers between devices  8.72 us (19%)
  local copies, waits for them, and re-layouts  5.37 us (12%)
  other arithmetic  2.43 us (5%)
  between operations  0.81 us (2%)
    pallas_call x6, Pallas kernels, call(): pl.pallas_call(body, in_specs=ins, out_specs=[VECTORS] * len(outs), out_s...  15.7 us
    ppermute x13, starting transfers between devices, swap(): return lax.ppermute(value, axis, [(i, i ^ distance) for i in range(count)])  12.1 us
    ppermute x13, waiting for transfers between devices, swap(): return lax.ppermute(value, axis, [(i, i ^ distance) for i in range(count)])  8.72 us
    unnamed x8, local copies, waits for them, and re-layouts  5.34 us
    add x1, other arithmetic, on_device(): pieces = kept + swap(sent, 'tm', 1)  0.98 us
  transfers between devices with their start and end apart: 13, of which 6 were waited for; matrix products, arithmetic and copies ran while one was open for 2% of the time, Pallas kernels for 12%

profile of v9, /device:TPU:0, one launch (start us, length us, event | category | flops | bytes accessed | tf_op | source)
XLA Modules:
  0.0 45.1 jit_solution(17844367643460799582)
XLA Ops:
  1.1 1.4 %prepare.1 = (f32[512,128]{1,0:T(8,128)S(1)}, bf16[256,1536]{1,0:T(8,128)(2,1)S(1)}, bf16[512,1536]{1,0:T(8,128)(2,1)S(1)}, f32[8,512]{1,0:T(8,128)S(1)}) custom-call(f32[512,128]{1,0:T(8,128)} %bitcast.55, f32[3,128,1024]{2,1,0:T(8,128)} %bitcast.53, f32[3,1024]{1,0:T(4,128)} %ph_hbm.1, s32[4]{0:T(128)} %g_hbm.1), custom_call_target="tpu_custom_call" | custom-call | flops 2090000000 | bytes 5700000 | tf_op jit(solution)/shard_map/prepare/pallas_call | solution.py:57
  2.6 5.8 %waves.1 = (f32[2,3,1024,256]{3,2,1,0:T(8,128)S(1)}, f32[2,3,1024,256]{3,2,1,0:T(8,128)S(1)}, f32[2,3,1024,256]{3,2,1,0:T(8,128)S(1)}, f32[48,512]{1,0:T(8,128)S...) custom-call(f32[512,128]{1,0:T(8,128)S(1)} %get-tuple-element.25.refs_0_, ...), custom_call_target="tpu_custom_call" | custom-call | flops 8800000000 | bytes 24000000 | tf_op jit(solution)/shard_map/waves/pallas_call | solution.py:57
  8.4 0.8 %copy-done.2 = f32[1024,128]{1,0:T(8,128)} copy-done((f32[1024,128]{1,0:T(8,128)}, f32[1024,128]{1,0:T(8,128)S(1)}, u32[]{:S(2)}) %copy-start.2) | copy-done | bytes 524312
  9.1 2.8 %collective-permute-start.1 = (f32[24,512]{1,0:T(8,128)S(1)}, f32[24,512]{1,0:T(8,128)S(1)}, u32[]{:S(2)}, u32[]{:S(2)}) collective-permute-start(f32[24,512]{1,0:T(8,128)S(1)} %get-tuple-element.33.refs_5_), channel_id=1, source_target_pairs={{0,8},{4,12},{8,0},{12,4},{16,24},{20,28},{24,16},{28,20},{1,9},{5... | collective-permute-start | bytes 147464 | tf_op jit(solution)/shard_map/ppermute | solution.py:388
  11.9 1.5 %collective-permute-start.2 = (f32[24,512]{1,0:T(8,128)S(1)}, f32[24,512]{1,0:T(8,128)S(1)}, u32[]{:S(2)}, u32[]{:S(2)}) collective-permute-start(f32[24,512]{1,0:T(8,128)S(1)} %get-tuple-element.33.refs_5_), channel_id=1, source_target_pairs={{0,16},{4,20},{8,24},{12,28},{16,0},{20,4},{24,8},{28,12},{1,17},{... | collective-permute-start | bytes 147464 | tf_op jit(solution)/shard_map/ppermute | solution.py:388
  13.5 2.3 %sines.1.refs_1_ = f32[2,3,1024,256]{3,2,1,0:T(8,128)S(1)} custom-call(f32[2,3,1024,256]{3,2,1,0:T(8,128)S(1)} %get-tuple-element.28.refs_0_, f32[2,3,1024,256]{3,2,1,0:T(8,128)S(1)} %get-tuple-element.29.refs_1_), custom_call_target="tpu_custom_call" | custom-call | flops 2640000000 | bytes 7200000 | tf_op jit(solution)/shard_map/sines/pallas_call | solution.py:57
  16.0 2.4 %collective-permute-done.3.refs_8_ = f32[24,512]{1,0:T(8,128)S(1)} collective-permute-done((f32[24,512]{1,0:T(8,128)S(1)}, f32[24,512]{1,0:T(8,128)S(1)}, u32[]{:S(2)}, u32[]{:S(2)}) %collective-permute-start.3) | collective-permute-done | bytes 49184 | tf_op jit(solution)/shard_map/ppermute | solution.py:388
  18.5 4.6 %increments.1 = (f32[4,128,128]{2,1,0:T(8,128)S(1)}, f32[4,128,128]{2,1,0:T(8,128)}, bf16[1024,1536]{1,0:T(8,128)(2,1)S(1)}, bf16[1024,1536]{1,0:T(8,128)(2,1)S(1)}) custom-call(f32[2,3,1024,256]{3,2,1,0:T(8,128)S(1)} %get-tuple-element.27.refs_0_, f32[2,3,1024,256]{3,2,1,0:T(8,128)S(1)} %sines.1.refs_1_, f32[48,512]{1,0:T(8,128)S(1)} %get-tuple-element.30.refs_2_, ...), custom_call_target="tpu_custom_call" | custom-call | flops 4180000000 | bytes 11400000 | tf_op jit(solution)/shard_map/increments/pallas_call | solution.py:57
  23.1 1.6 %copy-done = bf16[1024,1536]{1,0:T(8,128)(2,1)} copy-done((bf16[1024,1536]{1,0:T(8,128)(2,1)}, bf16[1024,1536]{1,0:T(8,128)(2,1)S(1)}, u32[]{:S(2)}) %copy-start) | copy-done | bytes 3145752
  24.7 1.0 %copy-done.3 = f32[1024,128]{1,0:T(8,128)S(1)} copy-done((f32[1024,128]{1,0:T(8,128)S(1)}, f32[1024,128]{1,0:T(8,128)}, u32[]{:S(2)}) %copy-start.3) | copy-done | bytes 524312
  26.0 1.9 %copy-done.1 = bf16[1024,1536]{1,0:T(8,128)(2,1)S(1)} copy-done((bf16[1024,1536]{1,0:T(8,128)(2,1)S(1)}, bf16[1024,1536]{1,0:T(8,128)(2,1)}, u32[]{:S(2)}) %copy-start.1) | copy-done | bytes 3145752
  27.9 1.4 %frequencies.1 = (f32[2,2,3,16,256]{4,3,2,1,0:T(8,128)S(1)}, f32[2,2,3,16,256]{4,3,2,1,0:T(8,128)S(1)}, f32[2,2,3,16,256]{4,3,2,1,0:T(8,128)S(1)}, f32[2,2,3,16,256]{4,3,2,1,0:T(8,128)S(1)}) custom-call(bf16[256,1024]{1,0:T(8,128)(2,1)S(1)} %turn.1.refs_0_, bf16[1024,1536]{1,0:T(8,128)(2,1)S(1)} %get-tuple-element.37.refs_1_, bf16[1024,1536]{1,0:T(8,128)(2,1)S(1)} %copy-done.1), custom_call_target="tpu_custom_call" | custom-call | flops 1650000000 | bytes 4500000 | tf_op jit(solution)/shard_map/frequencies/pallas_call | solution.py:57
  29.3 1.0 %add.24 = f32[4,128,128]{2,1,0:T(8,128)S(1)} add(f32[4,128,128]{2,1,0:T(8,128)S(1)} %get-tuple-element.34, f32[4,128,128]{2,1,0:T(8,128)} %collective-permute-done.4) | non-fusion elementwise | flops 65536 | bytes 786432 | tf_op jit(solution)/shard_map/add | solution.py:506
  30.3 0.6 %collective-permute-start.8 = (f32[2,2,3,16,256]{4,3,2,1,0:T(8,128)S(1)}, f32[2,2,3,16,256]{4,3,2,1,0:T(8,128)S(1)}, u32[]{:S(2)}, u32[]{:S(2)}) collective-permute-start(f32[2,2,3,16,256]{4,3,2,1,0:T(8,128)S(1)} %get-tuple-element.45), channel_id=1, source_target_pairs={{0,8},{4,12},{8,0},{12,4},{16,24},{20,28},{24,16},{28,20},{1,9},{5... | collective-permute-start | bytes 589832 | tf_op jit(solution)/shard_map/ppermute | solution.py:388
  31.2 1.8 %collective-permute-start.5 = (f32[128,128]{1,0:T(8,128)S(1)}, f32[128,128]{1,0:T(8,128)S(1)}, u32[]{:S(2)}, u32[]{:S(2)}) collective-permute-start(f32[128,128]{1,0:T(8,128)S(1)} %get-tuple-element.52), channel_id=1, source_target_pairs={{0,1},{1,0},{2,3},{3,2},{4,5},{5,4},{6,7},{7,6},{8,9},{9,8},{10,11... | collective-permute-start | bytes 196616 | tf_op jit(solution)/shard_map/ppermute | solution.py:388
  33.0 2.6 %collective-permute-start.6 = (f32[128,128]{1,0:T(8,128)S(1)}, f32[128,128]{1,0:T(8,128)S(1)}, u32[]{:S(2)}, u32[]{:S(2)}) collective-permute-start(f32[128,128]{1,0:T(8,128)S(1)} %get-tuple-element.54), channel_id=1, source_target_pairs={{0,2},{1,3},{2,0},{3,1},{4,6},{5,7},{6,4},{7,5},{8,10},{9,11},{10,... | collective-permute-start | bytes 196616 | tf_op jit(solution)/shard_map/ppermute | solution.py:388
  35.7 2.0 %collective-permute-done.8 = f32[2,2,3,16,256]{4,3,2,1,0:T(8,128)S(1)} collective-permute-done((f32[2,2,3,16,256]{4,3,2,1,0:T(8,128)S(1)}, f32[2,2,3,16,256]{4,3,2,1,0:T(8,128)S(1)}, u32[]{:S(2)}, u32[]{:S(2)}) %collective-permute-start.8) | collective-permute-done | bytes 196640 | tf_op jit(solution)/shard_map/ppermute | solution.py:388
  37.7 0.6 %collective-permute-start.9 = (f32[1,2,3,16,256]{4,3,2,1,0:T(8,128)S(1)}, f32[1,2,3,16,256]{4,3,2,1,0:T(8,128)S(1)}, u32[]{:S(2)}, u32[]{:S(2)}) collective-permute-start(f32[1,2,3,16,256]{4,3,2,1,0:T(8,128)S(1)} %slice_bitcast_fusion.2), channel_id=1, source_target_pairs={{0,16},{4,20},{8,24},{12,28},{16,0},{20,4},{24,8},{28,12},{1,17},{... | collective-permute-start | bytes 294920 | tf_op jit(solution)/shard_map/ppermute | solution.py:388
  38.3 1.2 %collective-permute-start.11 = (f32[1,2,3,16,256]{4,3,2,1,0:T(8,128)S(1)}, f32[1,2,3,16,256]{4,3,2,1,0:T(8,128)S(1)}, u32[]{:S(2)}, u32[]{:S(2)}) collective-permute-start(f32[1,2,3,16,256]{4,3,2,1,0:T(8,128)S(1)} %slice_bitcast_fusion), channel_id=1, source_target_pairs={{0,8},{4,12},{8,0},{12,4},{16,24},{20,28},{24,16},{28,20},{1,9},{5... | collective-permute-start | bytes 294920 | tf_op jit(solution)/shard_map/ppermute | solution.py:388
  39.5 2.9 %collective-permute-done.9 = f32[1,2,3,16,256]{4,3,2,1,0:T(8,128)S(1)} collective-permute-done((f32[1,2,3,16,256]{4,3,2,1,0:T(8,128)S(1)}, f32[1,2,3,16,256]{4,3,2,1,0:T(8,128)S(1)}, u32[]{:S(2)}, u32[]{:S(2)}) %collective-permute-start.9) | collective-permute-done | bytes 98336 | tf_op jit(solution)/shard_map/ppermute | solution.py:388
  42.4 0.6 %collective-permute-done.11 = f32[1,2,3,16,256]{4,3,2,1,0:T(8,128)S(1)} collective-permute-done((f32[1,2,3,16,256]{4,3,2,1,0:T(8,128)S(1)}, f32[1,2,3,16,256]{4,3,2,1,0:T(8,128)S(1)}, u32[]{:S(2)}, u32[]{:S(2)}) %collective-permute-start.11) | collective-permute-done | bytes 98336 | tf_op jit(solution)/shard_map/ppermute | solution.py:388
  43.2 0.6 %fusion.8 = f32[128,128]{1,0:T(8,128)} fusion(f32[128,128]{1,0:T(8,128)S(1)} %collective-permute-done.7, f32[128,128]{1,0:T(8,128)S(1)} %collective-permute-done.6, f32[128,128]{1,0:T(8,128)S(1)} %collective-permute-done.5, f32[4,128,128]{2,1,0:T(8,128)S(1)} %add.24), kind=kLoop, calls=%fused_computation.20 | loop fusion | flops 49152 | bytes 327680 | tf_op jit(solution)/shard_map/add | solution.py:511
  43.8 0.6 %collective-permute-done.12 = f32[3,16,512]{2,1,0:T(8,128)S(1)} collective-permute-done((f32[3,16,512]{2,1,0:T(8,128)S(1)}, f32[3,16,512]{2,1,0:T(8,128)S(1)}, u32[]{:S(2)}, u32[]{:S(2)}) %collective-permute-start.12) | collective-permute-done | bytes 98336 | tf_op jit(solution)/shard_map/ppermute | solution.py:388
  44.4 0.7 %maximum_bitcast_fusion = f32[16,3,1024]{2,0,1:T(8,128)} fusion(f32[3,16,512]{2,1,0:T(8,128)S(1)} %get-tuple-element.51, f32[3,16,512]{2,1,0:T(8,128)S(1)} %get-tuple-element.50), kind=kLoop, calls=%fused_computation.2 | loop fusion | flops 49152 | bytes 393216 | tf_op jit(solution)/shard_map/transpose | solution.py:528
  (28 shorter events, 1.6 us)
Async XLA Ops:
  0.6 1.9 %collective-permute-start = (f32[512,128]{1,0:T(8,128)}, f32[512,128]{1,0:T(8,128)S(1)}, u32[]{:S(2)}, u32[]{:S(2)}) collective-permute-start(f32[512,128]{1,0:T(8,128)} %bitcast.54), channel_id=1, source_target_pairs={{0,4},{4,0},{8,12},{12,8},{16,20},{20,16},{24,28},{28,24},{1,5},{5... | collective-permute-start | bytes 786440 | tf_op jit(solution)/shard_map/ppermute | solution.py:388
  8.4 0.8 %copy-start.2 = (f32[1024,128]{1,0:T(8,128)}, f32[1024,128]{1,0:T(8,128)S(1)}, u32[]{:S(2)}) copy-start(f32[1024,128]{1,0:T(8,128)S(1)} %get-tuple-element.36.flat_ref) | copy-start | bytes 1572868
  9.1 6.7 %collective-permute-start.1 = (f32[24,512]{1,0:T(8,128)S(1)}, f32[24,512]{1,0:T(8,128)S(1)}, u32[]{:S(2)}, u32[]{:S(2)}) collective-permute-start(f32[24,512]{1,0:T(8,128)S(1)} %get-tuple-element.33.refs_5_), channel_id=1, source_target_pairs={{0,8},{4,12},{8,0},{12,4},{16,24},{20,28},{24,16},{28,20},{1,9},{5... | collective-permute-start | bytes 147464 | tf_op jit(solution)/shard_map/ppermute | solution.py:388
  11.9 4.1 %collective-permute-start.2 = (f32[24,512]{1,0:T(8,128)S(1)}, f32[24,512]{1,0:T(8,128)S(1)}, u32[]{:S(2)}, u32[]{:S(2)}) collective-permute-start(f32[24,512]{1,0:T(8,128)S(1)} %get-tuple-element.33.refs_5_), channel_id=1, source_target_pairs={{0,16},{4,20},{8,24},{12,28},{16,0},{20,4},{24,8},{28,12},{1,17},{... | collective-permute-start | bytes 147464 | tf_op jit(solution)/shard_map/ppermute | solution.py:388
  13.5 5.0 %collective-permute-start.3 = (f32[24,512]{1,0:T(8,128)S(1)}, f32[24,512]{1,0:T(8,128)S(1)}, u32[]{:S(2)}, u32[]{:S(2)}) collective-permute-start(f32[24,512]{1,0:T(8,128)S(1)} %get-tuple-element.33.refs_5_), channel_id=1, source_target_pairs={{0,24},{4,28},{8,16},{12,20},{16,8},{20,12},{24,0},{28,4},{1,25},{... | collective-permute-start | bytes 147464 | tf_op jit(solution)/shard_map/ppermute | solution.py:388
  23.1 1.6 %copy-start = (bf16[1024,1536]{1,0:T(8,128)(2,1)}, bf16[1024,1536]{1,0:T(8,128)(2,1)S(1)}, u32[]{:S(2)}) copy-start(bf16[1024,1536]{1,0:T(8,128)(2,1)S(1)} %get-tuple-element.38.refs_2_) | copy-start | bytes 9437188
  24.7 4.6 %collective-permute-start.4 = (f32[4,128,128]{2,1,0:T(8,128)}, f32[4,128,128]{2,1,0:T(8,128)}, u32[]{:S(2)}, u32[]{:S(2)}) collective-permute-start(f32[4,128,128]{2,1,0:T(8,128)} %get-tuple-element.35), channel_id=1, source_target_pairs={{0,4},{4,0},{8,12},{12,8},{16,20},{20,16},{24,28},{28,24},{1,5},{5... | collective-permute-start | bytes 786440 | tf_op jit(solution)/shard_map/ppermute | solution.py:388
  24.7 1.0 %copy-start.3 = (f32[1024,128]{1,0:T(8,128)S(1)}, f32[1024,128]{1,0:T(8,128)}, u32[]{:S(2)}) copy-start(f32[1024,128]{1,0:T(8,128)} %copy-done.2) | copy-start | bytes 1572868
  26.0 1.9 %copy-start.1 = (bf16[1024,1536]{1,0:T(8,128)(2,1)S(1)}, bf16[1024,1536]{1,0:T(8,128)(2,1)}, u32[]{:S(2)}) copy-start(bf16[1024,1536]{1,0:T(8,128)(2,1)} %copy-done) | copy-start | bytes 9437188
  30.3 7.4 %collective-permute-start.8 = (f32[2,2,3,16,256]{4,3,2,1,0:T(8,128)S(1)}, f32[2,2,3,16,256]{4,3,2,1,0:T(8,128)S(1)}, u32[]{:S(2)}, u32[]{:S(2)}) collective-permute-start(f32[2,2,3,16,256]{4,3,2,1,0:T(8,128)S(1)} %get-tuple-element.45), channel_id=1, source_target_pairs={{0,8},{4,12},{8,0},{12,4},{16,24},{20,28},{24,16},{28,20},{1,9},{5... | collective-permute-start | bytes 589832 | tf_op jit(solution)/shard_map/ppermute | solution.py:388
  30.9 7.4 %collective-permute-start.10 = (f32[2,2,3,16,256]{4,3,2,1,0:T(8,128)S(1)}, f32[2,2,3,16,256]{4,3,2,1,0:T(8,128)S(1)}, u32[]{:S(2)}, u32[]{:S(2)}) collective-permute-start(f32[2,2,3,16,256]{4,3,2,1,0:T(8,128)S(1)} %get-tuple-element.47), channel_id=1, source_target_pairs={{0,16},{4,20},{8,24},{12,28},{16,0},{20,4},{24,8},{28,12},{1,17},{... | collective-permute-start | bytes 589832 | tf_op jit(solution)/shard_map/ppermute | solution.py:388
  31.2 11.9 %collective-permute-start.5 = (f32[128,128]{1,0:T(8,128)S(1)}, f32[128,128]{1,0:T(8,128)S(1)}, u32[]{:S(2)}, u32[]{:S(2)}) collective-permute-start(f32[128,128]{1,0:T(8,128)S(1)} %get-tuple-element.52), channel_id=1, source_target_pairs={{0,1},{1,0},{2,3},{3,2},{4,5},{5,4},{6,7},{7,6},{8,9},{9,8},{10,11... | collective-permute-start | bytes 196616 | tf_op jit(solution)/shard_map/ppermute | solution.py:388
  33.0 10.1 %collective-permute-start.6 = (f32[128,128]{1,0:T(8,128)S(1)}, f32[128,128]{1,0:T(8,128)S(1)}, u32[]{:S(2)}, u32[]{:S(2)}) collective-permute-start(f32[128,128]{1,0:T(8,128)S(1)} %get-tuple-element.54), channel_id=1, source_target_pairs={{0,2},{1,3},{2,0},{3,1},{4,6},{5,7},{6,4},{7,5},{8,10},{9,11},{10,... | collective-permute-start | bytes 196616 | tf_op jit(solution)/shard_map/ppermute | solution.py:388
  35.6 7.5 %collective-permute-start.7 = (f32[128,128]{1,0:T(8,128)S(1)}, f32[128,128]{1,0:T(8,128)S(1)}, u32[]{:S(2)}, u32[]{:S(2)}) collective-permute-start(f32[128,128]{1,0:T(8,128)S(1)} %get-tuple-element.53), channel_id=1, source_target_pairs={{0,3},{1,2},{2,1},{3,0},{4,7},{5,6},{6,5},{7,4},{8,11},{9,10},{10,... | collective-permute-start | bytes 196616 | tf_op jit(solution)/shard_map/ppermute | solution.py:388
  37.7 4.7 %collective-permute-start.9 = (f32[1,2,3,16,256]{4,3,2,1,0:T(8,128)S(1)}, f32[1,2,3,16,256]{4,3,2,1,0:T(8,128)S(1)}, u32[]{:S(2)}, u32[]{:S(2)}) collective-permute-start(f32[1,2,3,16,256]{4,3,2,1,0:T(8,128)S(1)} %slice_bitcast_fusion.2), channel_id=1, source_target_pairs={{0,16},{4,20},{8,24},{12,28},{16,0},{20,4},{24,8},{28,12},{1,17},{... | collective-permute-start | bytes 294920 | tf_op jit(solution)/shard_map/ppermute | solution.py:388
  38.3 4.7 %collective-permute-start.11 = (f32[1,2,3,16,256]{4,3,2,1,0:T(8,128)S(1)}, f32[1,2,3,16,256]{4,3,2,1,0:T(8,128)S(1)}, u32[]{:S(2)}, u32[]{:S(2)}) collective-permute-start(f32[1,2,3,16,256]{4,3,2,1,0:T(8,128)S(1)} %slice_bitcast_fusion), channel_id=1, source_target_pairs={{0,8},{4,12},{8,0},{12,4},{16,24},{20,28},{24,16},{28,20},{1,9},{5... | collective-permute-start | bytes 294920 | tf_op jit(solution)/shard_map/ppermute | solution.py:388
  43.0 1.4 %collective-permute-start.12 = (f32[3,16,512]{2,1,0:T(8,128)S(1)}, f32[3,16,512]{2,1,0:T(8,128)S(1)}, u32[]{:S(2)}, u32[]{:S(2)}) collective-permute-start(f32[3,16,512]{2,1,0:T(8,128)S(1)} %fusion.2), channel_id=1, source_target_pairs={{0,4},{4,0},{8,12},{12,8},{16,20},{20,16},{24,28},{28,24},{1,5},{5... | collective-permute-start | bytes 294920 | tf_op jit(solution)/shard_map/ppermute | solution.py:388

commit v10 on v7

--- a/solution.py
+++ b/solution.py
@@ -21,7 +21,7 @@
     0.2196967986036905,
 )
 NT = (((1,), (1,)), ((), ()))
-PARAMS = pltpu.CompilerParams(vmem_limit_bytes=20 * 1024 * 1024)
+PARAMS = pltpu.CompilerParams(vmem_limit_bytes=16 * 1024 * 1024)
 VECTORS = pl.BlockSpec(memory_space=pltpu.VMEM)
 STAY = pl.BlockSpec(memory_space=pltpu.HBM)
 
@@ -223,34 +223,48 @@
             lax.fori_loop(0, rows // SUB, step, 0, unroll=16)
 
 
-def compose(chips, loc_ref, weight_ref, got, all_ref):
+def parts_of(ref):
+    return [ref[HALF * k : HALF * (k + 1), :] for k in range(6)]
+
+
+def chain(early, late):
+    a0, a1, a2, a01, a12, a012 = early
+    b0, b1, b2, b01, b12, b012 = late
+    return (
+        a0 + b0,
+        a1 + b1,
+        a2 + b2,
+        a01 + b01 + a0 * b1,
+        a12 + b12 + a1 * b2,
+        a012 + b012 + a0 * b12 + a01 * b2,
+    )
+
+
+def ordered(flag, mine, other):
+    early = [jnp.where(flag, b, a) for a, b in zip(mine, other)]
+    late = [jnp.where(flag, a, b) for a, b in zip(mine, other)]
+    return early, late
+
+
+def compose(loc_ref, weight_ref, own_ref, got):
     chip = lax.axis_index("tm") >> 1
-    for d in range(chips):
-        all_ref[jnp.bitwise_xor(chip, d)] = got[d][...]
-
     weight = weight_ref[:HALF]
     zero = jnp.zeros(weight.shape, f32)
-
-    def sums_of(j):
-        return [all_ref[j, HALF * k : HALF * (k + 1), :] for k in range(6)]
-
-    def forward(j, carry):
-        p0, p01, p012 = carry
-        b0, b1, b2, b01, b12, b012 = sums_of(j)
-        p012 = p012 + b012 + p0 * b12 + p01 * b2
-        p01 = p01 + b01 + p0 * b1
-        return (p0 + b0, p01, p012)
-
-    def backward(step, carry):
-        t1, t2, t12 = carry
-        b0, b1, b2, b01, b12, b012 = sums_of(chips - 1 - step)
-        t12 = t12 + b12 + b1 * t2
-        return (t1 + b1, t2 + b2, t12)
-
-    entry = lax.fori_loop(0, chip, forward, (zero,) * 3)
-    e1, e2 = entry[:2]
-    totals = lax.fori_loop(chip, chips, forward, entry)
-    t1, t2, t12 = lax.fori_loop(0, chips - 1 - chip, backward, (zero,) * 3)
+    blocks = [parts_of(ref) for ref in (own_ref, *got)]
+    before, after = [zero] * 6, [zero] * 6
+    for k in range(len(got).bit_length()):
+        other = blocks[1]
+        flag = chip & (1 << k) != 0
+        first = [jnp.where(flag, v, 0.0) for v in other]
+        second = [jnp.where(flag, 0.0, v) for v in other]
+        before = chain(first, before)
+        after = chain(after, second)
+        blocks = [chain(*ordered(flag, a, b)) for a, b in zip(blocks[::2], blocks[1::2])]
+    p0, p1, p2, p01, p12, p012 = before
+    e1, e2 = p0, p01
+    _, t1, t2, _, t12, _ = after
+    whole = blocks[0]
+    totals = (whole[0], whole[3], whole[5])
     seeds = [2.0 * weight * jnp.sum(weight * total, axis=0, keepdims=True) for total in totals]
 
     def local(k):
@@ -318,18 +332,17 @@
     lax.fori_loop(0, rows // (2 * SUB), bwd, (adjoint1, adjoint0), unroll=8)
 
 
-def grads_kernel(sizes, c_ref, s_ref, loc_ref, xt_ref, w_ref, weight_ref, *refs):
+def grads_kernel(sizes, c_ref, s_ref, loc_ref, xt_ref, w_ref, weight_ref, own_ref, *refs):
     n_tm, n_freq, wide = sizes
-    chips = n_tm // 2
-    got, refs = refs[:chips], refs[chips:]
-    blocks, refs = refs[:chips], refs[chips:]
-    gk_ref, gs_ref, sh_ref, sl_ref, gp_ref, all_ref, u1_ref, acc_ref, flat_ref = refs
+    got, refs = refs[: n_tm // 2 - 1], refs[n_tm // 2 - 1 :]
+    blocks, refs = refs[: n_tm // 2], refs[n_tm // 2 :]
+    gk_ref, gs_ref, sh_ref, sl_ref, gp_ref, u1_ref, acc_ref, flat_ref = refs
     rows, chans = acc_ref.shape
     each = chans // n_tm
     me = lax.axis_index("tm")
     core, z = me & 1, lax.axis_index("freq")
 
-    starts = compose(chips, loc_ref, weight_ref, got, all_ref)
+    starts = compose(loc_ref, weight_ref, own_ref, got)
     for chunk in range(c_ref.shape[0]):
         slopes(chunk, wide, starts, c_ref, s_ref, u1_ref, sh_ref, sl_ref)
 
@@ -413,9 +426,6 @@
     def waves_body(*refs):
         waves_kernel(amplitude, wide, *refs)
 
-    def sines_body(*refs):
-        sines_kernel(amplitude, *refs)
-
     big = pltpu.VMEM((chunks, 3, rows, wide), f32)
     cosines, halves, squares, local, own, flat = call(
         waves_body,
@@ -435,11 +445,14 @@
         y,
         turns,
     )
-    got = [own] + [swap(own, "tm", 2 * d) for d in range(1, chips)]
     (xt,) = call(
         turn_kernel, "turn", 0.8, [VECTORS], [pltpu.VMEM((2 * chans, rows), bf16)], [], flat
     )
 
+    def sines_body(*refs):
+        sines_kernel(amplitude, *refs)
+
+    got = [swap(own, "tm", 2 * d) for d in range(1, chips)]
     (sines,) = call(sines_body, "sines", 2.4, [VECTORS] * 2, [big], [], halves, squares)
 
     def grads_body(*refs):
@@ -457,7 +470,6 @@
             pltpu.VMEM((rows, 3 * mine), bf16),
             pltpu.VMEM((rows, 3 * mine), bf16),
             pltpu.VMEM((n_tm, 3, each, mine), f32),
-            pltpu.VMEM((chips, 3 * SUB, mine), f32),
             pltpu.VMEM((rows, wide), f32),
             pltpu.VMEM((rows, chans), f32),
             pltpu.VMEM((2, rows // 2, chans), f32),
@@ -468,6 +480,7 @@
         xt,
         weights,
         weight,
+        own,
         *got,
     )
 

time: 38.9 us -> 38.9 us (level)
  no operation moved by 1% of the time
where the time goes in v10:
time: 38.9 us; the launch traced here: 38.6 us
  starting transfers between devices  16.9 us (43%)
  Pallas kernels  14.9 us (38%)
  waiting for transfers between devices  4.6 us (12%)
  other arithmetic  1.46 us (4%)
  between operations  0.75 us (2%)
    ppermute x12, starting transfers between devices, swap(): return lax.ppermute(value, axis, [(i, i ^ distance) for i in range(count)])  16.9 us
    pallas_call x5, Pallas kernels, call(): pl.pallas_call(body, in_specs=ins, out_specs=[VECTORS] * len(outs), out_s...  14.9 us
    ppermute x12, waiting for transfers between devices, swap(): return lax.ppermute(value, axis, [(i, i ^ distance) for i in range(count)])  4.6 us
  transfers between devices with their start and end apart: 12, of which 4 were waited for; matrix products, arithmetic and copies ran while one was open for 2% of the time, Pallas kernels for 10%

profile of v10, /device:TPU:0, one launch (start us, length us, event | category | flops | bytes accessed | tf_op | source)
XLA Modules:
  0.0 38.6 jit_solution(5802603658418301886)
XLA Ops:
  0.6 0.5 %collective-permute-start = (f32[512,128]{1,0:T(8,128)}, f32[512,128]{1,0:T(8,128)S(1)}, u32[]{:S(2)}, u32[]{:S(2)}) collective-permute-start(f32[512,128]{1,0:T(8,128)} %bitcast.29), channel_id=1, source_target_pairs={{0,4},{4,0},{8,12},{12,8},{16,20},{20,16},{24,28},{28,24},{1,5},{5... | collective-permute-start | bytes 786440 | tf_op jit(solution)/shard_map/ppermute | solution.py:382
  1.1 1.4 %prepare.1 = (f32[512,128]{1,0:T(8,128)S(1)}, bf16[256,1536]{1,0:T(8,128)(2,1)S(1)}, bf16[512,1536]{1,0:T(8,128)(2,1)S(1)}, f32[8,512]{1,0:T(8,128)S(1)}) custom-call(f32[512,128]{1,0:T(8,128)} %bitcast.30, f32[3,128,1024]{2,1,0:T(8,128)} %bitcast.28, f32[3,1024]{1,0:T(4,128)} %ph_hbm.1, s32[4]{0:T(128)} %g_hbm.1), custom_call_target="tpu_custom_call" | custom-call | flops 2090000000 | bytes 5700000 | tf_op jit(solution)/shard_map/prepare/pallas_call | solution.py:57
  2.6 5.8 %waves.1 = (f32[2,3,1024,256]{3,2,1,0:T(8,128)S(1)}, f32[2,3,1024,256]{3,2,1,0:T(8,128)S(1)}, f32[2,3,1024,256]{3,2,1,0:T(8,128)S(1)}, f32[48,512]{1,0:T(8,128)S...) custom-call(f32[512,128]{1,0:T(8,128)S(1)} %get-tuple-element.20.refs_0_, ...), custom_call_target="tpu_custom_call" | custom-call | flops 8800000000 | bytes 24000000 | tf_op jit(solution)/shard_map/waves/pallas_call | solution.py:57
  8.4 2.9 %collective-permute-start.1 = (f32[24,512]{1,0:T(8,128)S(1)}, f32[24,512]{1,0:T(8,128)S(1)}, u32[]{:S(2)}, u32[]{:S(2)}) collective-permute-start(f32[24,512]{1,0:T(8,128)S(1)} %get-tuple-element.29.refs_6_), channel_id=1, source_target_pairs={{0,8},{4,12},{8,0},{12,4},{16,24},{20,28},{24,16},{28,20},{1,9},{5... | collective-permute-start | bytes 147464 | tf_op jit(solution)/shard_map/ppermute | solution.py:382
  11.2 1.5 %collective-permute-start.2 = (f32[24,512]{1,0:T(8,128)S(1)}, f32[24,512]{1,0:T(8,128)S(1)}, u32[]{:S(2)}, u32[]{:S(2)}) collective-permute-start(f32[24,512]{1,0:T(8,128)S(1)} %get-tuple-element.29.refs_6_), channel_id=1, source_target_pairs={{0,16},{4,20},{8,24},{12,28},{16,0},{20,4},{24,8},{28,12},{1,17},{... | collective-permute-start | bytes 147464 | tf_op jit(solution)/shard_map/ppermute | solution.py:382
  12.7 0.0 collective-permute-start.3
  12.8 2.3 %sines.1.refs_1_ = f32[2,3,1024,256]{3,2,1,0:T(8,128)S(1)} custom-call(f32[2,3,1024,256]{3,2,1,0:T(8,128)S(1)} %get-tuple-element.23.refs_0_, f32[2,3,1024,256]{3,2,1,0:T(8,128)S(1)} %get-tuple-element.24.refs_1_), custom_call_target="tpu_custom_call" | custom-call | flops 2640000000 | bytes 7200000 | tf_op jit(solution)/shard_map/sines/pallas_call | solution.py:57
  15.1 0.2 turn.1.refs_3_
  15.3 2.4 %collective-permute-done.3.refs_9_ = f32[24,512]{1,0:T(8,128)S(1)} collective-permute-done((f32[24,512]{1,0:T(8,128)S(1)}, f32[24,512]{1,0:T(8,128)S(1)}, u32[]{:S(2)}, u32[]{:S(2)}) %collective-permute-start.3) | collective-permute-done | bytes 49184 | tf_op jit(solution)/shard_map/ppermute | solution.py:382
  17.7 5.2 %grads.1 = (f32[2,3,16,512]{3,2,1,0:T(8,128)S(1)}, f32[2,3,16,512]{3,2,1,0:T(8,128)S(1)}, f32[2,3,16,512]{3,2,1,0:T(8,128)S(1)}, f32[2,3,16,512]{3,2,1,0:T(8,128...) custom-call(f32[2,3,1024,256]{3,2,1,0:T(8,128)S(1)} %get-tuple-element.22.refs_0_, ...), custom_call_target="tpu_custom_call" | custom-call | flops 6600000000 | bytes 18000000 | tf_op jit(solution)/shard_map/grads/pallas_call | solution.py:57
  23.0 0.1 collective-permute-start.4
  23.0 0.6 %collective-permute-start.10 = (f32[2,3,16,512]{3,2,1,0:T(8,128)S(1)}, f32[2,3,16,512]{3,2,1,0:T(8,128)S(1)}, u32[]{:S(2)}, u32[]{:S(2)}) collective-permute-start(f32[2,3,16,512]{3,2,1,0:T(8,128)S(1)} %get-tuple-element.37), channel_id=1, source_target_pairs={{0,8},{4,12},{8,0},{12,4},{16,24},{20,28},{24,16},{28,20},{1,9},{5... | collective-permute-start | bytes 589832 | tf_op jit(solution)/shard_map/ppermute | solution.py:382
  23.6 1.4 %collective-permute-start.8 = (f32[2,3,16,512]{3,2,1,0:T(8,128)S(1)}, f32[2,3,16,512]{3,2,1,0:T(8,128)S(1)}, u32[]{:S(2)}, u32[]{:S(2)}) collective-permute-start(f32[2,3,16,512]{3,2,1,0:T(8,128)S(1)} %get-tuple-element.35), channel_id=1, source_target_pairs={{0,24},{4,28},{8,16},{12,20},{16,8},{20,12},{24,0},{28,4},{1,25},{... | collective-permute-start | bytes 589832 | tf_op jit(solution)/shard_map/ppermute | solution.py:382
  25.1 1.5 %collective-permute-start.9 = (f32[2,3,16,512]{3,2,1,0:T(8,128)S(1)}, f32[2,3,16,512]{3,2,1,0:T(8,128)S(1)}, u32[]{:S(2)}, u32[]{:S(2)}) collective-permute-start(f32[2,3,16,512]{3,2,1,0:T(8,128)S(1)} %get-tuple-element.36), channel_id=1, source_target_pairs={{0,16},{4,20},{8,24},{12,28},{16,0},{20,4},{24,8},{28,12},{1,17},{... | collective-permute-start | bytes 589832 | tf_op jit(solution)/shard_map/ppermute | solution.py:382
  26.7 1.6 %collective-permute-start.5 = (f32[128,128]{1,0:T(8,128)S(1)}, f32[128,128]{1,0:T(8,128)S(1)}, u32[]{:S(2)}, u32[]{:S(2)}) collective-permute-start(f32[128,128]{1,0:T(8,128)S(1)} %get-tuple-element.40), channel_id=1, source_target_pairs={{0,1},{1,0},{2,3},{3,2},{4,5},{5,4},{6,7},{7,6},{8,9},{9,8},{10,11... | collective-permute-start | bytes 196616 | tf_op jit(solution)/shard_map/ppermute | solution.py:382
  28.3 2.6 %collective-permute-start.6 = (f32[128,128]{1,0:T(8,128)S(1)}, f32[128,128]{1,0:T(8,128)S(1)}, u32[]{:S(2)}, u32[]{:S(2)}) collective-permute-start(f32[128,128]{1,0:T(8,128)S(1)} %get-tuple-element.42), channel_id=1, source_target_pairs={{0,2},{1,3},{2,0},{3,1},{4,6},{5,7},{6,4},{7,5},{8,10},{9,11},{10,... | collective-permute-start | bytes 196616 | tf_op jit(solution)/shard_map/ppermute | solution.py:382
  30.9 0.1 collective-permute-done.5
  31.0 4.0 %collective-permute-start.7 = (f32[128,128]{1,0:T(8,128)S(1)}, f32[128,128]{1,0:T(8,128)S(1)}, u32[]{:S(2)}, u32[]{:S(2)}) collective-permute-start(f32[128,128]{1,0:T(8,128)S(1)} %get-tuple-element.41), channel_id=1, source_target_pairs={{0,3},{1,2},{2,1},{3,0},{4,7},{5,6},{6,5},{7,4},{8,11},{9,10},{10,... | collective-permute-start | bytes 196616 | tf_op jit(solution)/shard_map/ppermute | solution.py:382
  35.0 1.0 %collective-permute-done.9 = f32[2,3,16,512]{3,2,1,0:T(8,128)S(1)} collective-permute-done((f32[2,3,16,512]{3,2,1,0:T(8,128)S(1)}, f32[2,3,16,512]{3,2,1,0:T(8,128)S(1)}, u32[]{:S(2)}, u32[]{:S(2)}) %collective-permute-start.9) | collective-permute-done | bytes 196640 | tf_op jit(solution)/shard_map/ppermute | solution.py:382
  36.0 0.1 add_add_fusion
  36.1 0.1 collective-permute-start.11
  36.1 1.1 %collective-permute-done.7 = f32[128,128]{1,0:T(8,128)S(1)} collective-permute-done((f32[128,128]{1,0:T(8,128)S(1)}, f32[128,128]{1,0:T(8,128)S(1)}, u32[]{:S(2)}, u32[]{:S(2)}) %collective-permute-start.7) | collective-permute-done | bytes 65568 | tf_op jit(solution)/shard_map/ppermute | solution.py:382
  37.2 0.7 %fusion.4 = f32[128,128]{1,0:T(8,128)} fusion(f32[128,128]{1,0:T(8,128)S(1)} %collective-permute-done.7, f32[128,128]{1,0:T(8,128)S(1)} %collective-permute-done.6, f32[128,128]{1,0:T(8,128)S(1)} %collective-permute-done.5, f32[4,128,128]{2,1,0:T(8,128)S(1)} %add.21), kind=kLoop, calls=%fused_computation.12 | loop fusion | flops 49152 | bytes 327680 | tf_op jit(solution)/shard_map/add | solution.py:495
  37.9 0.7 %maximum_bitcast_fusion = f32[16,3,1024]{2,0,1:T(8,128)} fusion(f32[3,16,512]{2,1,0:T(8,128)S(1)} %get-tuple-element.39, f32[3,16,512]{2,1,0:T(8,128)S(1)} %get-tuple-element.38), kind=kLoop, calls=%fused_computation | loop fusion | flops 49152 | bytes 393216 | tf_op jit(solution)/shard_map/transpose | solution.py:501
  (12 shorter events, 0.1 us)
Async XLA Ops:
  0.6 1.9 %collective-permute-start = (f32[512,128]{1,0:T(8,128)}, f32[512,128]{1,0:T(8,128)S(1)}, u32[]{:S(2)}, u32[]{:S(2)}) collective-permute-start(f32[512,128]{1,0:T(8,128)} %bitcast.29), channel_id=1, source_target_pairs={{0,4},{4,0},{8,12},{12,8},{16,20},{20,16},{24,28},{28,24},{1,5},{5... | collective-permute-start | bytes 786440 | tf_op jit(solution)/shard_map/ppermute | solution.py:382
  8.4 6.9 %collective-permute-start.1 = (f32[24,512]{1,0:T(8,128)S(1)}, f32[24,512]{1,0:T(8,128)S(1)}, u32[]{:S(2)}, u32[]{:S(2)}) collective-permute-start(f32[24,512]{1,0:T(8,128)S(1)} %get-tuple-element.29.refs_6_), channel_id=1, source_target_pairs={{0,8},{4,12},{8,0},{12,4},{16,24},{20,28},{24,16},{28,20},{1,9},{5... | collective-permute-start | bytes 147464 | tf_op jit(solution)/shard_map/ppermute | solution.py:382
  11.2 4.1 %collective-permute-start.2 = (f32[24,512]{1,0:T(8,128)S(1)}, f32[24,512]{1,0:T(8,128)S(1)}, u32[]{:S(2)}, u32[]{:S(2)}) collective-permute-start(f32[24,512]{1,0:T(8,128)S(1)} %get-tuple-element.29.refs_6_), channel_id=1, source_target_pairs={{0,16},{4,20},{8,24},{12,28},{16,0},{20,4},{24,8},{28,12},{1,17},{... | collective-permute-start | bytes 147464 | tf_op jit(solution)/shard_map/ppermute | solution.py:382
  12.7 5.0 %collective-permute-start.3 = (f32[24,512]{1,0:T(8,128)S(1)}, f32[24,512]{1,0:T(8,128)S(1)}, u32[]{:S(2)}, u32[]{:S(2)}) collective-permute-start(f32[24,512]{1,0:T(8,128)S(1)} %get-tuple-element.29.refs_6_), channel_id=1, source_target_pairs={{0,24},{4,28},{8,16},{12,20},{16,8},{20,12},{24,0},{28,4},{1,25},{... | collective-permute-start | bytes 147464 | tf_op jit(solution)/shard_map/ppermute | solution.py:382
  23.0 3.6 %collective-permute-start.4 = (f32[4,128,128]{2,1,0:T(8,128)S(1)}, f32[4,128,128]{2,1,0:T(8,128)S(1)}, u32[]{:S(2)}, u32[]{:S(2)}) collective-permute-start(f32[4,128,128]{2,1,0:T(8,128)S(1)} %get-tuple-element.31), channel_id=1, source_target_pairs={{0,4},{4,0},{8,12},{12,8},{16,20},{20,16},{24,28},{28,24},{1,5},{5... | collective-permute-start | bytes 786440 | tf_op jit(solution)/shard_map/ppermute | solution.py:382
  23.0 12.0 %collective-permute-start.10 = (f32[2,3,16,512]{3,2,1,0:T(8,128)S(1)}, f32[2,3,16,512]{3,2,1,0:T(8,128)S(1)}, u32[]{:S(2)}, u32[]{:S(2)}) collective-permute-start(f32[2,3,16,512]{3,2,1,0:T(8,128)S(1)} %get-tuple-element.37), channel_id=1, source_target_pairs={{0,8},{4,12},{8,0},{12,4},{16,24},{20,28},{24,16},{28,20},{1,9},{5... | collective-permute-start | bytes 589832 | tf_op jit(solution)/shard_map/ppermute | solution.py:382
  23.6 11.4 %collective-permute-start.8 = (f32[2,3,16,512]{3,2,1,0:T(8,128)S(1)}, f32[2,3,16,512]{3,2,1,0:T(8,128)S(1)}, u32[]{:S(2)}, u32[]{:S(2)}) collective-permute-start(f32[2,3,16,512]{3,2,1,0:T(8,128)S(1)} %get-tuple-element.35), channel_id=1, source_target_pairs={{0,24},{4,28},{8,16},{12,20},{16,8},{20,12},{24,0},{28,4},{1,25},{... | collective-permute-start | bytes 589832 | tf_op jit(solution)/shard_map/ppermute | solution.py:382
  25.1 10.9 %collective-permute-start.9 = (f32[2,3,16,512]{3,2,1,0:T(8,128)S(1)}, f32[2,3,16,512]{3,2,1,0:T(8,128)S(1)}, u32[]{:S(2)}, u32[]{:S(2)}) collective-permute-start(f32[2,3,16,512]{3,2,1,0:T(8,128)S(1)} %get-tuple-element.36), channel_id=1, source_target_pairs={{0,16},{4,20},{8,24},{12,28},{16,0},{20,4},{24,8},{28,12},{1,17},{... | collective-permute-start | bytes 589832 | tf_op jit(solution)/shard_map/ppermute | solution.py:382
  26.7 4.3 %collective-permute-start.5 = (f32[128,128]{1,0:T(8,128)S(1)}, f32[128,128]{1,0:T(8,128)S(1)}, u32[]{:S(2)}, u32[]{:S(2)}) collective-permute-start(f32[128,128]{1,0:T(8,128)S(1)} %get-tuple-element.40), channel_id=1, source_target_pairs={{0,1},{1,0},{2,3},{3,2},{4,5},{5,4},{6,7},{7,6},{8,9},{9,8},{10,11... | collective-permute-start | bytes 196616 | tf_op jit(solution)/shard_map/ppermute | solution.py:382
  28.3 7.8 %collective-permute-start.6 = (f32[128,128]{1,0:T(8,128)S(1)}, f32[128,128]{1,0:T(8,128)S(1)}, u32[]{:S(2)}, u32[]{:S(2)}) collective-permute-start(f32[128,128]{1,0:T(8,128)S(1)} %get-tuple-element.42), channel_id=1, source_target_pairs={{0,2},{1,3},{2,0},{3,1},{4,6},{5,7},{6,4},{7,5},{8,10},{9,11},{10,... | collective-permute-start | bytes 196616 | tf_op jit(solution)/shard_map/ppermute | solution.py:382
  31.0 6.2 %collective-permute-start.7 = (f32[128,128]{1,0:T(8,128)S(1)}, f32[128,128]{1,0:T(8,128)S(1)}, u32[]{:S(2)}, u32[]{:S(2)}) collective-permute-start(f32[128,128]{1,0:T(8,128)S(1)} %get-tuple-element.41), channel_id=1, source_target_pairs={{0,3},{1,2},{2,1},{3,0},{4,7},{5,6},{6,5},{7,4},{8,11},{9,10},{10,... | collective-permute-start | bytes 196616 | tf_op jit(solution)/shard_map/ppermute | solution.py:382
  36.1 1.8 %collective-permute-start.11 = (f32[3,16,512]{2,1,0:T(8,128)S(1)}, f32[3,16,512]{2,1,0:T(8,128)S(1)}, u32[]{:S(2)}, u32[]{:S(2)}) collective-permute-start(f32[3,16,512]{2,1,0:T(8,128)S(1)} %slice_bitcast_fusion), channel_id=1, source_target_pairs={{0,4},{4,0},{8,12},{12,8},{16,20},{20,16},{24,28},{28,24},{1,5},{5... | collective-permute-start | bytes 294920 | tf_op jit(solution)/shard_map/ppermute | solution.py:382

commit v11 on v10

--- a/solution.py
+++ b/solution.py
@@ -485,6 +485,7 @@
     )
 
     pieces = kept + swap(sent, "tm", 1)
+    pieces, blocks[1] = lax.optimization_barrier((pieces, blocks[1]))
     others = [swap(pieces[j], "freq", j) for j in range(1, n_freq)]
     others[0], blocks[0] = lax.optimization_barrier((others[0], blocks[0]))
     total = blocks[0]

time: 38.9 us -> 38.9 us (level)
  no operation moved by 1% of the time
where the time goes in v11:
time: 38.9 us; the launch traced here: 38.7 us
  starting transfers between devices  16.9 us (43%)
  Pallas kernels  14.9 us (38%)
  waiting for transfers between devices  4.6 us (12%)
  other arithmetic  1.46 us (4%)
  between operations  0.74 us (2%)
    ppermute x12, starting transfers between devices, swap(): return lax.ppermute(value, axis, [(i, i ^ distance) for i in range(count)])  16.9 us
    pallas_call x5, Pallas kernels, call(): pl.pallas_call(body, in_specs=ins, out_specs=[VECTORS] * len(outs), out_s...  14.9 us
    ppermute x12, waiting for transfers between devices, swap(): return lax.ppermute(value, axis, [(i, i ^ distance) for i in range(count)])  4.6 us
  transfers between devices with their start and end apart: 12, of which 4 were waited for; matrix products, arithmetic and copies ran while one was open for 2% of the time, Pallas kernels for 10%

profile of v11, /device:TPU:0, one launch (start us, length us, event | category | flops | bytes accessed | tf_op | source)
XLA Modules:
  0.0 38.7 jit_solution(17549420913827207429)
XLA Ops:
  0.6 0.5 %collective-permute-start = (f32[512,128]{1,0:T(8,128)}, f32[512,128]{1,0:T(8,128)S(1)}, u32[]{:S(2)}, u32[]{:S(2)}) collective-permute-start(f32[512,128]{1,0:T(8,128)} %bitcast.27), channel_id=1, source_target_pairs={{0,4},{4,0},{8,12},{12,8},{16,20},{20,16},{24,28},{28,24},{1,5},{5... | collective-permute-start | bytes 786440 | tf_op jit(solution)/shard_map/ppermute | solution.py:382
  1.1 1.4 %prepare.1 = (f32[512,128]{1,0:T(8,128)S(1)}, bf16[256,1536]{1,0:T(8,128)(2,1)S(1)}, bf16[512,1536]{1,0:T(8,128)(2,1)S(1)}, f32[8,512]{1,0:T(8,128)S(1)}) custom-call(f32[512,128]{1,0:T(8,128)} %bitcast.28, f32[3,128,1024]{2,1,0:T(8,128)} %bitcast.26, f32[3,1024]{1,0:T(4,128)} %ph_hbm.1, s32[4]{0:T(128)} %g_hbm.1), custom_call_target="tpu_custom_call" | custom-call | flops 2090000000 | bytes 5700000 | tf_op jit(solution)/shard_map/prepare/pallas_call | solution.py:57
  2.6 5.8 %waves.1 = (f32[2,3,1024,256]{3,2,1,0:T(8,128)S(1)}, f32[2,3,1024,256]{3,2,1,0:T(8,128)S(1)}, f32[2,3,1024,256]{3,2,1,0:T(8,128)S(1)}, f32[48,512]{1,0:T(8,128)S...) custom-call(f32[512,128]{1,0:T(8,128)S(1)} %get-tuple-element.22.refs_0_, ...), custom_call_target="tpu_custom_call" | custom-call | flops 8800000000 | bytes 24000000 | tf_op jit(solution)/shard_map/waves/pallas_call | solution.py:57
  8.4 2.9 %collective-permute-start.1 = (f32[24,512]{1,0:T(8,128)S(1)}, f32[24,512]{1,0:T(8,128)S(1)}, u32[]{:S(2)}, u32[]{:S(2)}) collective-permute-start(f32[24,512]{1,0:T(8,128)S(1)} %get-tuple-element.31.refs_6_), channel_id=1, source_target_pairs={{0,8},{4,12},{8,0},{12,4},{16,24},{20,28},{24,16},{28,20},{1,9},{5... | collective-permute-start | bytes 147464 | tf_op jit(solution)/shard_map/ppermute | solution.py:382
  11.2 1.5 %collective-permute-start.2 = (f32[24,512]{1,0:T(8,128)S(1)}, f32[24,512]{1,0:T(8,128)S(1)}, u32[]{:S(2)}, u32[]{:S(2)}) collective-permute-start(f32[24,512]{1,0:T(8,128)S(1)} %get-tuple-element.31.refs_6_), channel_id=1, source_target_pairs={{0,16},{4,20},{8,24},{12,28},{16,0},{20,4},{24,8},{28,12},{1,17},{... | collective-permute-start | bytes 147464 | tf_op jit(solution)/shard_map/ppermute | solution.py:382
  12.7 0.0 collective-permute-start.3
  12.8 2.3 %sines.1.refs_1_ = f32[2,3,1024,256]{3,2,1,0:T(8,128)S(1)} custom-call(f32[2,3,1024,256]{3,2,1,0:T(8,128)S(1)} %get-tuple-element.25.refs_0_, f32[2,3,1024,256]{3,2,1,0:T(8,128)S(1)} %get-tuple-element.26.refs_1_), custom_call_target="tpu_custom_call" | custom-call | flops 2640000000 | bytes 7200000 | tf_op jit(solution)/shard_map/sines/pallas_call | solution.py:57
  15.1 0.2 turn.1.refs_3_
  15.3 2.4 %collective-permute-done.3.refs_9_ = f32[24,512]{1,0:T(8,128)S(1)} collective-permute-done((f32[24,512]{1,0:T(8,128)S(1)}, f32[24,512]{1,0:T(8,128)S(1)}, u32[]{:S(2)}, u32[]{:S(2)}) %collective-permute-start.3) | collective-permute-done | bytes 49184 | tf_op jit(solution)/shard_map/ppermute | solution.py:382
  17.7 5.2 %grads.1 = (f32[2,3,16,512]{3,2,1,0:T(8,128)S(1)}, f32[2,3,16,512]{3,2,1,0:T(8,128)S(1)}, f32[2,3,16,512]{3,2,1,0:T(8,128)S(1)}, f32[2,3,16,512]{3,2,1,0:T(8,128...) custom-call(f32[2,3,1024,256]{3,2,1,0:T(8,128)S(1)} %get-tuple-element.24.refs_0_, ...), custom_call_target="tpu_custom_call" | custom-call | flops 6600000000 | bytes 18000000 | tf_op jit(solution)/shard_map/grads/pallas_call | solution.py:57
  23.0 0.1 collective-permute-start.4
  23.0 0.6 %collective-permute-start.8 = (f32[2,3,16,512]{3,2,1,0:T(8,128)S(1)}, f32[2,3,16,512]{3,2,1,0:T(8,128)S(1)}, u32[]{:S(2)}, u32[]{:S(2)}) collective-permute-start(f32[2,3,16,512]{3,2,1,0:T(8,128)S(1)} %get-tuple-element.39), channel_id=1, source_target_pairs={{0,24},{4,28},{8,16},{12,20},{16,8},{20,12},{24,0},{28,4},{1,25},{... | collective-permute-start | bytes 589832 | tf_op jit(solution)/shard_map/ppermute | solution.py:382
  23.6 1.5 %collective-permute-start.9 = (f32[2,3,16,512]{3,2,1,0:T(8,128)S(1)}, f32[2,3,16,512]{3,2,1,0:T(8,128)S(1)}, u32[]{:S(2)}, u32[]{:S(2)}) collective-permute-start(f32[2,3,16,512]{3,2,1,0:T(8,128)S(1)} %get-tuple-element.40), channel_id=1, source_target_pairs={{0,16},{4,20},{8,24},{12,28},{16,0},{20,4},{24,8},{28,12},{1,17},{... | collective-permute-start | bytes 589832 | tf_op jit(solution)/shard_map/ppermute | solution.py:382
  25.1 1.6 %collective-permute-start.10 = (f32[2,3,16,512]{3,2,1,0:T(8,128)S(1)}, f32[2,3,16,512]{3,2,1,0:T(8,128)S(1)}, u32[]{:S(2)}, u32[]{:S(2)}) collective-permute-start(f32[2,3,16,512]{3,2,1,0:T(8,128)S(1)} %get-tuple-element.41), channel_id=1, source_target_pairs={{0,8},{4,12},{8,0},{12,4},{16,24},{20,28},{24,16},{28,20},{1,9},{5... | collective-permute-start | bytes 589832 | tf_op jit(solution)/shard_map/ppermute | solution.py:382
  26.7 1.6 %collective-permute-start.5 = (f32[128,128]{1,0:T(8,128)S(1)}, f32[128,128]{1,0:T(8,128)S(1)}, u32[]{:S(2)}, u32[]{:S(2)}) collective-permute-start(f32[128,128]{1,0:T(8,128)S(1)} %get-tuple-element.44), channel_id=1, source_target_pairs={{0,1},{1,0},{2,3},{3,2},{4,5},{5,4},{6,7},{7,6},{8,9},{9,8},{10,11... | collective-permute-start | bytes 196616 | tf_op jit(solution)/shard_map/ppermute | solution.py:382
  28.4 2.6 %collective-permute-start.6 = (f32[128,128]{1,0:T(8,128)S(1)}, f32[128,128]{1,0:T(8,128)S(1)}, u32[]{:S(2)}, u32[]{:S(2)}) collective-permute-start(f32[128,128]{1,0:T(8,128)S(1)} %get-tuple-element.46), channel_id=1, source_target_pairs={{0,2},{1,3},{2,0},{3,1},{4,6},{5,7},{6,4},{7,5},{8,10},{9,11},{10,... | collective-permute-start | bytes 196616 | tf_op jit(solution)/shard_map/ppermute | solution.py:382
  31.0 0.1 collective-permute-done.5
  31.1 4.0 %collective-permute-start.7 = (f32[128,128]{1,0:T(8,128)S(1)}, f32[128,128]{1,0:T(8,128)S(1)}, u32[]{:S(2)}, u32[]{:S(2)}) collective-permute-start(f32[128,128]{1,0:T(8,128)S(1)} %get-tuple-element.45), channel_id=1, source_target_pairs={{0,3},{1,2},{2,1},{3,0},{4,7},{5,6},{6,5},{7,4},{8,11},{9,10},{10,... | collective-permute-start | bytes 196616 | tf_op jit(solution)/shard_map/ppermute | solution.py:382
  35.1 0.1 add_add_fusion
  35.2 0.1 collective-permute-start.11
  35.2 0.1 collective-permute-done.6
  35.3 2.0 %collective-permute-done.7 = f32[128,128]{1,0:T(8,128)S(1)} collective-permute-done((f32[128,128]{1,0:T(8,128)S(1)}, f32[128,128]{1,0:T(8,128)S(1)}, u32[]{:S(2)}, u32[]{:S(2)}) %collective-permute-start.7) | collective-permute-done | bytes 65568 | tf_op jit(solution)/shard_map/ppermute | solution.py:382
  37.3 0.7 %fusion.3 = f32[128,128]{1,0:T(8,128)} fusion(f32[128,128]{1,0:T(8,128)S(1)} %collective-permute-done.7, f32[128,128]{1,0:T(8,128)S(1)} %collective-permute-done.6, f32[128,128]{1,0:T(8,128)S(1)} %collective-permute-done.5, f32[4,128,128]{2,1,0:T(8,128)S(1)} %add.21), kind=kLoop, calls=%fused_computation.8 | loop fusion | flops 49152 | bytes 327680 | tf_op jit(solution)/shard_map/add | solution.py:496
  38.0 0.7 %maximum_bitcast_fusion = f32[16,3,1024]{2,0,1:T(8,128)} fusion(f32[3,16,512]{2,1,0:T(8,128)S(1)} %get-tuple-element.43, f32[3,16,512]{2,1,0:T(8,128)S(1)} %get-tuple-element.42), kind=kLoop, calls=%fused_computation | loop fusion | flops 49152 | bytes 393216 | tf_op jit(solution)/shard_map/transpose | solution.py:502
  (12 shorter events, 0.1 us)
Async XLA Ops:
  0.6 1.9 %collective-permute-start = (f32[512,128]{1,0:T(8,128)}, f32[512,128]{1,0:T(8,128)S(1)}, u32[]{:S(2)}, u32[]{:S(2)}) collective-permute-start(f32[512,128]{1,0:T(8,128)} %bitcast.27), channel_id=1, source_target_pairs={{0,4},{4,0},{8,12},{12,8},{16,20},{20,16},{24,28},{28,24},{1,5},{5... | collective-permute-start | bytes 786440 | tf_op jit(solution)/shard_map/ppermute | solution.py:382
  8.4 6.9 %collective-permute-start.1 = (f32[24,512]{1,0:T(8,128)S(1)}, f32[24,512]{1,0:T(8,128)S(1)}, u32[]{:S(2)}, u32[]{:S(2)}) collective-permute-start(f32[24,512]{1,0:T(8,128)S(1)} %get-tuple-element.31.refs_6_), channel_id=1, source_target_pairs={{0,8},{4,12},{8,0},{12,4},{16,24},{20,28},{24,16},{28,20},{1,9},{5... | collective-permute-start | bytes 147464 | tf_op jit(solution)/shard_map/ppermute | solution.py:382
  11.2 4.1 %collective-permute-start.2 = (f32[24,512]{1,0:T(8,128)S(1)}, f32[24,512]{1,0:T(8,128)S(1)}, u32[]{:S(2)}, u32[]{:S(2)}) collective-permute-start(f32[24,512]{1,0:T(8,128)S(1)} %get-tuple-element.31.refs_6_), channel_id=1, source_target_pairs={{0,16},{4,20},{8,24},{12,28},{16,0},{20,4},{24,8},{28,12},{1,17},{... | collective-permute-start | bytes 147464 | tf_op jit(solution)/shard_map/ppermute | solution.py:382
  12.7 5.0 %collective-permute-start.3 = (f32[24,512]{1,0:T(8,128)S(1)}, f32[24,512]{1,0:T(8,128)S(1)}, u32[]{:S(2)}, u32[]{:S(2)}) collective-permute-start(f32[24,512]{1,0:T(8,128)S(1)} %get-tuple-element.31.refs_6_), channel_id=1, source_target_pairs={{0,24},{4,28},{8,16},{12,20},{16,8},{20,12},{24,0},{28,4},{1,25},{... | collective-permute-start | bytes 147464 | tf_op jit(solution)/shard_map/ppermute | solution.py:382
  23.0 2.1 %collective-permute-start.4 = (f32[4,128,128]{2,1,0:T(8,128)S(1)}, f32[4,128,128]{2,1,0:T(8,128)S(1)}, u32[]{:S(2)}, u32[]{:S(2)}) collective-permute-start(f32[4,128,128]{2,1,0:T(8,128)S(1)} %get-tuple-element.33), channel_id=1, source_target_pairs={{0,4},{4,0},{8,12},{12,8},{16,20},{20,16},{24,28},{28,24},{1,5},{5... | collective-permute-start | bytes 786440 | tf_op jit(solution)/shard_map/ppermute | solution.py:382
  23.0 12.0 %collective-permute-start.8 = (f32[2,3,16,512]{3,2,1,0:T(8,128)S(1)}, f32[2,3,16,512]{3,2,1,0:T(8,128)S(1)}, u32[]{:S(2)}, u32[]{:S(2)}) collective-permute-start(f32[2,3,16,512]{3,2,1,0:T(8,128)S(1)} %get-tuple-element.39), channel_id=1, source_target_pairs={{0,24},{4,28},{8,16},{12,20},{16,8},{20,12},{24,0},{28,4},{1,25},{... | collective-permute-start | bytes 589832 | tf_op jit(solution)/shard_map/ppermute | solution.py:382
  23.6 11.5 %collective-permute-start.9 = (f32[2,3,16,512]{3,2,1,0:T(8,128)S(1)}, f32[2,3,16,512]{3,2,1,0:T(8,128)S(1)}, u32[]{:S(2)}, u32[]{:S(2)}) collective-permute-start(f32[2,3,16,512]{3,2,1,0:T(8,128)S(1)} %get-tuple-element.40), channel_id=1, source_target_pairs={{0,16},{4,20},{8,24},{12,28},{16,0},{20,4},{24,8},{28,12},{1,17},{... | collective-permute-start | bytes 589832 | tf_op jit(solution)/shard_map/ppermute | solution.py:382
  25.1 9.9 %collective-permute-start.10 = (f32[2,3,16,512]{3,2,1,0:T(8,128)S(1)}, f32[2,3,16,512]{3,2,1,0:T(8,128)S(1)}, u32[]{:S(2)}, u32[]{:S(2)}) collective-permute-start(f32[2,3,16,512]{3,2,1,0:T(8,128)S(1)} %get-tuple-element.41), channel_id=1, source_target_pairs={{0,8},{4,12},{8,0},{12,4},{16,24},{20,28},{24,16},{28,20},{1,9},{5... | collective-permute-start | bytes 589832 | tf_op jit(solution)/shard_map/ppermute | solution.py:382
  26.7 4.3 %collective-permute-start.5 = (f32[128,128]{1,0:T(8,128)S(1)}, f32[128,128]{1,0:T(8,128)S(1)}, u32[]{:S(2)}, u32[]{:S(2)}) collective-permute-start(f32[128,128]{1,0:T(8,128)S(1)} %get-tuple-element.44), channel_id=1, source_target_pairs={{0,1},{1,0},{2,3},{3,2},{4,5},{5,4},{6,7},{7,6},{8,9},{9,8},{10,11... | collective-permute-start | bytes 196616 | tf_op jit(solution)/shard_map/ppermute | solution.py:382
  28.4 6.9 %collective-permute-start.6 = (f32[128,128]{1,0:T(8,128)S(1)}, f32[128,128]{1,0:T(8,128)S(1)}, u32[]{:S(2)}, u32[]{:S(2)}) collective-permute-start(f32[128,128]{1,0:T(8,128)S(1)} %get-tuple-element.46), channel_id=1, source_target_pairs={{0,2},{1,3},{2,0},{3,1},{4,6},{5,7},{6,4},{7,5},{8,10},{9,11},{10,... | collective-permute-start | bytes 196616 | tf_op jit(solution)/shard_map/ppermute | solution.py:382
  31.1 6.2 %collective-permute-start.7 = (f32[128,128]{1,0:T(8,128)S(1)}, f32[128,128]{1,0:T(8,128)S(1)}, u32[]{:S(2)}, u32[]{:S(2)}) collective-permute-start(f32[128,128]{1,0:T(8,128)S(1)} %get-tuple-element.45), channel_id=1, source_target_pairs={{0,3},{1,2},{2,1},{3,0},{4,7},{5,6},{6,5},{7,4},{8,11},{9,10},{10,... | collective-permute-start | bytes 196616 | tf_op jit(solution)/shard_map/ppermute | solution.py:382
  35.2 2.8 %collective-permute-start.11 = (f32[3,16,512]{2,1,0:T(8,128)S(1)}, f32[3,16,512]{2,1,0:T(8,128)S(1)}, u32[]{:S(2)}, u32[]{:S(2)}) collective-permute-start(f32[3,16,512]{2,1,0:T(8,128)S(1)} %slice_bitcast_fusion), channel_id=1, source_target_pairs={{0,4},{4,0},{8,12},{12,8},{16,20},{20,16},{24,28},{28,24},{1,5},{5... | collective-permute-start | bytes 294920 | tf_op jit(solution)/shard_map/ppermute | solution.py:382

commit v12 on v8

--- a/solution.py
+++ b/solution.py
@@ -140,7 +140,7 @@
             xs_ref[tile(k, 2), :] = jnp.concatenate([high, low, high, ones], axis=1)
             return 0
 
-        lax.fori_loop(0, rows // (2 * SUB), one, 0, unroll=8)
+        lax.fori_loop(0, rows // (2 * SUB), one, 0, unroll=16)
 
     @pl.when(core == 0)
     def _():
@@ -318,7 +318,7 @@
         keep(pair, 2, slope2)
         return f1, f2
 
-    lax.fori_loop(0, rows // (2 * SUB), fwd, (front1, front2), unroll=8)
+    lax.fori_loop(0, rows // (2 * SUB), fwd, (front1, front2), unroll=16)
 
     def bwd(step, carry):
         g1, g0 = carry
@@ -334,7 +334,7 @@
         keep(pair, 1, slope1[::-1])
         return g1, g0
 
-    lax.fori_loop(0, rows // (2 * SUB), bwd, (adjoint1, adjoint0), unroll=8)
+    lax.fori_loop(0, rows // (2 * SUB), bwd, (adjoint1, adjoint0), unroll=16)
 
 
 def grads_kernel(sizes, c_ref, loc_ref, xt_ref, w_ref, weight_ref, *refs):
@@ -376,7 +376,7 @@
         flat_ref[1, tile(k), :] = odd
         return 0
 
-    lax.fori_loop(0, rows // (2 * SUB), one, 0, unroll=8)
+    lax.fori_loop(0, rows // (2 * SUB), one, 0, unroll=16)
     piece = rows // 2 // n_freq
     for j in range(n_freq):
         at = pl.ds(pl.multiple_of(jnp.bitwise_xor(z, j) * piece, piece), piece)

time: 38.5 us -> 38.6 us (level)
  no operation moved by 1% of the time
where the time goes in v12:
time: 38.6 us; the launch traced here: 38.3 us
  starting transfers between devices  17 us (44%)
  Pallas kernels  15 us (39%)
  waiting for transfers between devices  4.06 us (11%)
  other arithmetic  1.46 us (4%)
  between operations  0.74 us (2%)
    ppermute x11, starting transfers between devices, swap(): return lax.ppermute(value, axis, [(i, i ^ distance) for i in range(count)])  17 us
    pallas_call x7, Pallas kernels, call(): pl.pallas_call(body, in_specs=ins, out_specs=[VECTORS] * len(outs), out_s...  15 us
    ppermute x11, waiting for transfers between devices, swap(): return lax.ppermute(value, axis, [(i, i ^ distance) for i in range(count)])  4.06 us
  transfers between devices with their start and end apart: 11, of which 5 were waited for; matrix products, arithmetic and copies ran while one was open for 2% of the time, Pallas kernels for 10%

profile of v12, /device:TPU:0, one launch (start us, length us, event | category | flops | bytes accessed | tf_op | source)
XLA Modules:
  0.0 38.3 jit_solution(11994646041224652100)
XLA Ops:
  0.6 0.5 %collective-permute-start = (f32[512,128]{1,0:T(8,128)}, f32[512,128]{1,0:T(8,128)S(1)}, u32[]{:S(2)}, u32[]{:S(2)}) collective-permute-start(f32[512,128]{1,0:T(8,128)} %bitcast.29), channel_id=1, source_target_pairs={{0,4},{4,0},{8,12},{12,8},{16,20},{20,16},{24,28},{28,24},{1,5},{5... | collective-permute-start | bytes 786440 | tf_op jit(solution)/shard_map/ppermute | solution.py:389
  1.1 1.4 %prepare.1 = (f32[512,128]{1,0:T(8,128)S(1)}, bf16[256,1536]{1,0:T(8,128)(2,1)S(1)}, bf16[512,1536]{1,0:T(8,128)(2,1)S(1)}, f32[8,512]{1,0:T(8,128)S(1)}) custom-call(f32[512,128]{1,0:T(8,128)} %bitcast.30, f32[3,128,1024]{2,1,0:T(8,128)} %bitcast.28, f32[3,1024]{1,0:T(4,128)} %ph_hbm.1, s32[4]{0:T(128)} %g_hbm.1), custom_call_target="tpu_custom_call" | custom-call | flops 2090000000 | bytes 5700000 | tf_op jit(solution)/shard_map/prepare/pallas_call | solution.py:57
  2.6 5.8 %waves.1 = (f32[2,3,1024,256]{3,2,1,0:T(8,128)S(1)}, f32[2,3,1024,256]{3,2,1,0:T(8,128)S(1)}, f32[2,3,1024,256]{3,2,1,0:T(8,128)S(1)}, f32[48,512]{1,0:T(8,128)S...) custom-call(f32[512,128]{1,0:T(8,128)S(1)} %get-tuple-element.24.refs_0_, ...), custom_call_target="tpu_custom_call" | custom-call | flops 8800000000 | bytes 24000000 | tf_op jit(solution)/shard_map/waves/pallas_call | solution.py:57
  8.3 2.9 %collective-permute-start.1 = (f32[24,512]{1,0:T(8,128)S(1)}, f32[24,512]{1,0:T(8,128)S(1)}, u32[]{:S(2)}, u32[]{:S(2)}) collective-permute-start(f32[24,512]{1,0:T(8,128)S(1)} %get-tuple-element.31.refs_0_.refs_7_), channel_id=1, source_target_pairs={{0,8},{4,12},{8,0},{12,4},{16,24},{20,28},{24,16},{28,20},{1,9},{5... | collective-permute-start | bytes 147464 | tf_op jit(solution)/shard_map/ppermute | solution.py:389
  11.2 1.2 %sines0.1.refs_5_ = f32[3,1024,256]{2,1,0:T(8,128)S(1)} custom-call(f32[2,3,1024,256]{3,2,1,0:T(8,128)S(1)} %get-tuple-element.36.refs_0_, f32[2,3,1024,256]{3,2,1,0:T(8,128)S(1)} %get-tuple-element.33.refs_1_), custom_call_target="tpu_custom_call" | custom-call | flops 1320000000 | bytes 3600000 | tf_op jit(solution)/shard_map/sines0/pallas_call | solution.py:57
  12.4 0.2 turn.1.refs_2_
  12.6 0.7 %collective-permute-done.1.refs_1_.refs_8_ = f32[24,512]{1,0:T(8,128)S(1)} collective-permute-done((f32[24,512]{1,0:T(8,128)S(1)}, f32[24,512]{1,0:T(8,128)S(1)}, u32[]{:S(2)}, u32[]{:S(2)}) %collective-permute-start.1) | collective-permute-done | bytes 49184 | tf_op jit(solution)/shard_map/ppermute | solution.py:389
  13.3 2.1 %collective-permute-start.2 = (f32[24,512]{1,0:T(8,128)S(1)}, f32[24,512]{1,0:T(8,128)S(1)}, u32[]{:S(2)}, u32[]{:S(2)}) collective-permute-start(f32[24,512]{1,0:T(8,128)S(1)} %chain.1), channel_id=1, source_target_pairs={{0,16},{4,20},{8,24},{12,28},{16,0},{20,4},{24,8},{28,12},{1,17},{... | collective-permute-start | bytes 147464 | tf_op jit(solution)/shard_map/ppermute | solution.py:389
  15.4 1.2 %sines1.1.refs_6_ = f32[3,1024,256]{2,1,0:T(8,128)S(1)} custom-call(f32[2,3,1024,256]{3,2,1,0:T(8,128)S(1)} %get-tuple-element.36.refs_0_, f32[2,3,1024,256]{3,2,1,0:T(8,128)S(1)} %get-tuple-element.33.refs_1_), custom_call_target="tpu_custom_call" | custom-call | flops 1320000000 | bytes 3600000 | tf_op jit(solution)/shard_map/sines1/pallas_call | solution.py:57
  16.6 0.9 %collective-permute-done.2.refs_9_ = f32[24,512]{1,0:T(8,128)S(1)} collective-permute-done((f32[24,512]{1,0:T(8,128)S(1)}, f32[24,512]{1,0:T(8,128)S(1)}, u32[]{:S(2)}, u32[]{:S(2)}) %collective-permute-start.2) | collective-permute-done | bytes 49184 | tf_op jit(solution)/shard_map/ppermute | solution.py:389
  17.5 5.3 %grads.1 = (f32[2,3,16,512]{3,2,1,0:T(8,128)S(1)}, f32[2,3,16,512]{3,2,1,0:T(8,128)S(1)}, f32[2,3,16,512]{3,2,1,0:T(8,128)S(1)}, f32[2,3,16,512]{3,2,1,0:T(8,128...) custom-call(f32[2,3,1024,256]{3,2,1,0:T(8,128)S(1)} %get-tuple-element.26.refs_0_, ...), custom_call_target="tpu_custom_call" | custom-call | flops 6600000000 | bytes 18000000 | tf_op jit(solution)/shard_map/grads/pallas_call | solution.py:57
  22.8 0.1 collective-permute-start.3
  22.9 2.1 %collective-permute-start.9 = (f32[2,3,16,512]{3,2,1,0:T(8,128)S(1)}, f32[2,3,16,512]{3,2,1,0:T(8,128)S(1)}, u32[]{:S(2)}, u32[]{:S(2)}) collective-permute-start(f32[2,3,16,512]{3,2,1,0:T(8,128)S(1)} %get-tuple-element.45), channel_id=1, source_target_pairs={{0,8},{4,12},{8,0},{12,4},{16,24},{20,28},{24,16},{28,20},{1,9},{5... | collective-permute-start | bytes 589832 | tf_op jit(solution)/shard_map/ppermute | solution.py:389
  25.0 1.5 %collective-permute-start.8 = (f32[2,3,16,512]{3,2,1,0:T(8,128)S(1)}, f32[2,3,16,512]{3,2,1,0:T(8,128)S(1)}, u32[]{:S(2)}, u32[]{:S(2)}) collective-permute-start(f32[2,3,16,512]{3,2,1,0:T(8,128)S(1)} %get-tuple-element.44), channel_id=1, source_target_pairs={{0,16},{4,20},{8,24},{12,28},{16,0},{20,4},{24,8},{28,12},{1,17},{... | collective-permute-start | bytes 589832 | tf_op jit(solution)/shard_map/ppermute | solution.py:389
  26.6 2.1 %collective-permute-start.4 = (f32[128,128]{1,0:T(8,128)S(1)}, f32[128,128]{1,0:T(8,128)S(1)}, u32[]{:S(2)}, u32[]{:S(2)}) collective-permute-start(f32[128,128]{1,0:T(8,128)S(1)} %get-tuple-element.48), channel_id=1, source_target_pairs={{0,1},{1,0},{2,3},{3,2},{4,5},{5,4},{6,7},{7,6},{8,9},{9,8},{10,11... | collective-permute-start | bytes 196616 | tf_op jit(solution)/shard_map/ppermute | solution.py:389
  28.7 2.5 %collective-permute-start.6 = (f32[128,128]{1,0:T(8,128)S(1)}, f32[128,128]{1,0:T(8,128)S(1)}, u32[]{:S(2)}, u32[]{:S(2)}) collective-permute-start(f32[128,128]{1,0:T(8,128)S(1)} %get-tuple-element.49), channel_id=1, source_target_pairs={{0,3},{1,2},{2,1},{3,0},{4,7},{5,6},{6,5},{7,4},{8,11},{9,10},{10,... | collective-permute-start | bytes 196616 | tf_op jit(solution)/shard_map/ppermute | solution.py:389
  31.1 3.2 %collective-permute-start.5 = (f32[128,128]{1,0:T(8,128)S(1)}, f32[128,128]{1,0:T(8,128)S(1)}, u32[]{:S(2)}, u32[]{:S(2)}) collective-permute-start(f32[128,128]{1,0:T(8,128)S(1)} %get-tuple-element.50), channel_id=1, source_target_pairs={{0,2},{1,3},{2,0},{3,1},{4,6},{5,7},{6,4},{7,5},{8,10},{9,11},{10,... | collective-permute-start | bytes 196616 | tf_op jit(solution)/shard_map/ppermute | solution.py:389
  34.4 1.8 %collective-permute-done.8 = f32[2,3,16,512]{3,2,1,0:T(8,128)S(1)} collective-permute-done((f32[2,3,16,512]{3,2,1,0:T(8,128)S(1)}, f32[2,3,16,512]{3,2,1,0:T(8,128)S(1)}, u32[]{:S(2)}, u32[]{:S(2)}) %collective-permute-start.8) | collective-permute-done | bytes 196640 | tf_op jit(solution)/shard_map/ppermute | solution.py:389
  36.1 0.1 add_add_fusion
  36.2 0.1 collective-permute-start.10
  36.3 0.3 collective-permute-done.5
  36.7 0.7 %fusion.4 = f32[128,128]{1,0:T(8,128)} fusion(f32[128,128]{1,0:T(8,128)S(1)} %collective-permute-done.6, f32[128,128]{1,0:T(8,128)S(1)} %collective-permute-done.5, f32[128,128]{1,0:T(8,128)S(1)} %collective-permute-done.4, f32[4,128,128]{2,1,0:T(8,128)S(1)} %add.21), kind=kLoop, calls=%fused_computation.12 | loop fusion | flops 49152 | bytes 327680 | tf_op jit(solution)/shard_map/add | solution.py:537
  37.3 0.3 collective-permute-done.10
  37.6 0.7 %maximum_bitcast_fusion = f32[16,3,1024]{2,0,1:T(8,128)} fusion(f32[3,16,512]{2,1,0:T(8,128)S(1)} %get-tuple-element.47, f32[3,16,512]{2,1,0:T(8,128)S(1)} %get-tuple-element.46), kind=kLoop, calls=%fused_computation | loop fusion | flops 49152 | bytes 393216 | tf_op jit(solution)/shard_map/transpose | solution.py:543
  (12 shorter events, 0.1 us)
Async XLA Ops:
  0.6 1.9 %collective-permute-start = (f32[512,128]{1,0:T(8,128)}, f32[512,128]{1,0:T(8,128)S(1)}, u32[]{:S(2)}, u32[]{:S(2)}) collective-permute-start(f32[512,128]{1,0:T(8,128)} %bitcast.29), channel_id=1, source_target_pairs={{0,4},{4,0},{8,12},{12,8},{16,20},{20,16},{24,28},{28,24},{1,5},{5... | collective-permute-start | bytes 786440 | tf_op jit(solution)/shard_map/ppermute | solution.py:389
  8.3 5.0 %collective-permute-start.1 = (f32[24,512]{1,0:T(8,128)S(1)}, f32[24,512]{1,0:T(8,128)S(1)}, u32[]{:S(2)}, u32[]{:S(2)}) collective-permute-start(f32[24,512]{1,0:T(8,128)S(1)} %get-tuple-element.31.refs_0_.refs_7_), channel_id=1, source_target_pairs={{0,8},{4,12},{8,0},{12,4},{16,24},{20,28},{24,16},{28,20},{1,9},{5... | collective-permute-start | bytes 147464 | tf_op jit(solution)/shard_map/ppermute | solution.py:389
  13.3 4.2 %collective-permute-start.2 = (f32[24,512]{1,0:T(8,128)S(1)}, f32[24,512]{1,0:T(8,128)S(1)}, u32[]{:S(2)}, u32[]{:S(2)}) collective-permute-start(f32[24,512]{1,0:T(8,128)S(1)} %chain.1), channel_id=1, source_target_pairs={{0,16},{4,20},{8,24},{12,28},{16,0},{20,4},{24,8},{28,12},{1,17},{... | collective-permute-start | bytes 147464 | tf_op jit(solution)/shard_map/ppermute | solution.py:389
  22.8 3.7 %collective-permute-start.3 = (f32[4,128,128]{2,1,0:T(8,128)S(1)}, f32[4,128,128]{2,1,0:T(8,128)S(1)}, u32[]{:S(2)}, u32[]{:S(2)}) collective-permute-start(f32[4,128,128]{2,1,0:T(8,128)S(1)} %get-tuple-element.39), channel_id=1, source_target_pairs={{0,4},{4,0},{8,12},{12,8},{16,20},{20,16},{24,28},{28,24},{1,5},{5... | collective-permute-start | bytes 786440 | tf_op jit(solution)/shard_map/ppermute | solution.py:389
  22.9 11.5 %collective-permute-start.9 = (f32[2,3,16,512]{3,2,1,0:T(8,128)S(1)}, f32[2,3,16,512]{3,2,1,0:T(8,128)S(1)}, u32[]{:S(2)}, u32[]{:S(2)}) collective-permute-start(f32[2,3,16,512]{3,2,1,0:T(8,128)S(1)} %get-tuple-element.45), channel_id=1, source_target_pairs={{0,8},{4,12},{8,0},{12,4},{16,24},{20,28},{24,16},{28,20},{1,9},{5... | collective-permute-start | bytes 589832 | tf_op jit(solution)/shard_map/ppermute | solution.py:389
  25.0 11.2 %collective-permute-start.8 = (f32[2,3,16,512]{3,2,1,0:T(8,128)S(1)}, f32[2,3,16,512]{3,2,1,0:T(8,128)S(1)}, u32[]{:S(2)}, u32[]{:S(2)}) collective-permute-start(f32[2,3,16,512]{3,2,1,0:T(8,128)S(1)} %get-tuple-element.44), channel_id=1, source_target_pairs={{0,16},{4,20},{8,24},{12,28},{16,0},{20,4},{24,8},{28,12},{1,17},{... | collective-permute-start | bytes 589832 | tf_op jit(solution)/shard_map/ppermute | solution.py:389
  26.5 9.7 %collective-permute-start.7 = (f32[2,3,16,512]{3,2,1,0:T(8,128)S(1)}, f32[2,3,16,512]{3,2,1,0:T(8,128)S(1)}, u32[]{:S(2)}, u32[]{:S(2)}) collective-permute-start(f32[2,3,16,512]{3,2,1,0:T(8,128)S(1)} %get-tuple-element.43), channel_id=1, source_target_pairs={{0,24},{4,28},{8,16},{12,20},{16,8},{20,12},{24,0},{28,4},{1,25},{... | collective-permute-start | bytes 589832 | tf_op jit(solution)/shard_map/ppermute | solution.py:389
  26.6 4.6 %collective-permute-start.4 = (f32[128,128]{1,0:T(8,128)S(1)}, f32[128,128]{1,0:T(8,128)S(1)}, u32[]{:S(2)}, u32[]{:S(2)}) collective-permute-start(f32[128,128]{1,0:T(8,128)S(1)} %get-tuple-element.48), channel_id=1, source_target_pairs={{0,1},{1,0},{2,3},{3,2},{4,5},{5,4},{6,7},{7,6},{8,9},{9,8},{10,11... | collective-permute-start | bytes 196616 | tf_op jit(solution)/shard_map/ppermute | solution.py:389
  28.7 7.6 %collective-permute-start.6 = (f32[128,128]{1,0:T(8,128)S(1)}, f32[128,128]{1,0:T(8,128)S(1)}, u32[]{:S(2)}, u32[]{:S(2)}) collective-permute-start(f32[128,128]{1,0:T(8,128)S(1)} %get-tuple-element.49), channel_id=1, source_target_pairs={{0,3},{1,2},{2,1},{3,0},{4,7},{5,6},{6,5},{7,4},{8,11},{9,10},{10,... | collective-permute-start | bytes 196616 | tf_op jit(solution)/shard_map/ppermute | solution.py:389
  31.1 5.5 %collective-permute-start.5 = (f32[128,128]{1,0:T(8,128)S(1)}, f32[128,128]{1,0:T(8,128)S(1)}, u32[]{:S(2)}, u32[]{:S(2)}) collective-permute-start(f32[128,128]{1,0:T(8,128)S(1)} %get-tuple-element.50), channel_id=1, source_target_pairs={{0,2},{1,3},{2,0},{3,1},{4,6},{5,7},{6,4},{7,5},{8,10},{9,11},{10,... | collective-permute-start | bytes 196616 | tf_op jit(solution)/shard_map/ppermute | solution.py:389
  36.2 1.4 %collective-permute-start.10 = (f32[3,16,512]{2,1,0:T(8,128)S(1)}, f32[3,16,512]{2,1,0:T(8,128)S(1)}, u32[]{:S(2)}, u32[]{:S(2)}) collective-permute-start(f32[3,16,512]{2,1,0:T(8,128)S(1)} %slice_bitcast_fusion), channel_id=1, source_target_pairs={{0,4},{4,0},{8,12},{12,8},{16,20},{20,16},{24,28},{28,24},{1,5},{5... | collective-permute-start | bytes 294920 | tf_op jit(solution)/shard_map/ppermute | solution.py:389
